TPU v7x, 32 devices: a whole 2x2x4 slice. The times are simulated.
32 devices in a mesh: mode: 4 (over y, core), gx: 2 (over x), gy: 4 (over z).
Axes of the slice: x: 2, y: 2, z: 4, core: 2. Of those that a mesh axis runs over, the one named last changes fastest.
Arguments:
- right_side: float32 [16, 32, 7168], P('gx', 'gy', 'mode'), may hold values from -6 to 6
- col_block: int32 [56, 8], P('mode'), may hold values from 0 to 55, as said below
- blocks: bfloat16 [56, 8, 128, 128], P('mode'), may hold values from -0.1875 to 0.1875
- relax_rate: float32 [7168], P('mode'), may hold values from 0.5 to 4
- drift_speed: float32 [2, 7168], P(None, 'mode'), may hold values from 0.3 to 1.5
- upwind_sign: int32 [2, 7168], P(None, 'mode'), may hold values from 0 to 1
- wall_mask: int32 [16, 32], P('gx', 'gy'), may hold values 0 or 1
Outputs:
- solution: float32 [16, 32, 7168], P('gx', 'gy', 'mode')
- hessenberg: float32 [4, 3], replicated
Inputs may be any that keep to these rules, and one draw needn't show every extreme that they name: `col_block`: for every block row and every o in 0 .. 3, slots o * 2 to (o + 1) * 2 - 1 hold distinct column blocks of o * 14 to (o + 1) * 14 - 1.
All inputs are finite; a program needn't handle non-finite values. No bound on the sum of `wall_mask` on one device may be relied on, other than what follows from the above.
Results may differ from a plain program's by a relative error of at most 0.00081.
Values may be sent and summed in bfloat16 or wider, within the bound.
No kernel may reach another device: no remote copies, remote signals or barrier semaphores. Data moves between devices by JAX's collectives and lax.ppermute only.
A program may use at most 128 MiB of HBM per device.

v0:
```python
import jax
import jax.numpy as jnp
from jax import lax
from jax.sharding import PartitionSpec as P

KRYLOV = 3


epsilon = 1e-12


def extended(block, sides, width):
    for axis, dim in sides:
        count = lax.axis_size(axis)
        forward = [(i, i + 1) for i in range(count - 1)]
        backward = [(target, source) for source, target in forward]
        low = lax.ppermute(
            lax.slice_in_dim(block, block.shape[dim] - width, None, axis=dim), axis, forward
        )
        high = lax.ppermute(lax.slice_in_dim(block, 0, width, axis=dim), axis, backward)
        block = jnp.concatenate([low, block, high], axis=dim)
    return block


def apply_operator(current, col_block, blocks, relax_rate, drift_speed, upwind_sign, open_cells):
    cells_first, cells_second, local_modes = current.shape
    block_size = blocks.shape[2]
    local_blocks = col_block.shape[0]
    slot_count = col_block.shape[1]
    masked = current * open_cells[:, :, None]
    padded = extended(masked, (("gx", 0), ("gy", 1)), 1)
    from_west = padded[:-2, 1:-1]
    from_east = padded[2:, 1:-1]
    from_south = padded[1:-1, :-2]
    from_north = padded[1:-1, 2:]
    upstream_first = jnp.where(upwind_sign[0] == 1, from_west, from_east)
    upstream_second = jnp.where(upwind_sign[1] == 1, from_south, from_north)
    drift_term = drift_speed[0] * (current - upstream_first) + drift_speed[1] * (
        current - upstream_second
    )
    cell_count = cells_first * cells_second
    rounded = current.astype(jnp.bfloat16).reshape(cell_count, local_modes)
    gathered = lax.all_gather(rounded, "mode", axis=1, tiled=True)
    gathered = gathered.reshape(cell_count, -1, block_size)
    picked = jnp.take(gathered, col_block.reshape(-1), axis=1)
    picked = picked.reshape(cell_count, local_blocks, slot_count, block_size)
    scattered = jnp.einsum("rsik,crsk->cri", blocks, picked, preferred_element_type=jnp.float32)
    scattered = scattered.reshape(cells_first, cells_second, local_modes)
    return relax_rate * current + drift_term - scattered


def least_squares(hessenberg, initial):
    upper = [
        [hessenberg[row_index, col_index] for col_index in range(KRYLOV)]
        for row_index in range(KRYLOV + 1)
    ]
    target = [initial] + [jnp.zeros_like(initial) for row_index in range(KRYLOV)]
    cosines = []
    sines = []
    for col_index in range(KRYLOV):
        for row_index in range(col_index):
            first = upper[row_index][col_index]
            second = upper[row_index + 1][col_index]
            upper[row_index][col_index] = cosines[row_index] * first + sines[row_index] * second
            upper[row_index + 1][col_index] = cosines[row_index] * second - sines[row_index] * first
        first = upper[col_index][col_index]
        second = upper[col_index + 1][col_index]
        radius = jnp.sqrt(first * first + second * second)
        cosine = first / radius
        sine_value = second / radius
        upper[col_index][col_index] = radius
        target[col_index + 1] = -sine_value * target[col_index]
        target[col_index] = cosine * target[col_index]
        cosines.append(cosine)
        sines.append(sine_value)
    combo = [None] * KRYLOV
    for row_index in reversed(range(KRYLOV)):
        running = target[row_index]
        for col_index in range(row_index + 1, KRYLOV):
            running = running - upper[row_index][col_index] * combo[col_index]
        combo[row_index] = running / upper[row_index][row_index]
    return combo


def per_device(right_side, col_block, blocks, relax_rate, drift_speed, upwind_sign, wall_mask):
    open_cells = (1 - wall_mask).astype(jnp.float32)
    squared = lax.psum(jnp.sum(right_side * right_side), ("mode", "gx", "gy"))
    initial = jnp.sqrt(squared + epsilon)
    krylov_basis = [right_side / initial]
    columns_list = []
    for section in range(KRYLOV):
        mapped = apply_operator(
            krylov_basis[section],
            col_block,
            blocks,
            relax_rate,
            drift_speed,
            upwind_sign,
            open_cells,
        )
        local_products = jnp.stack(
            [jnp.sum(krylov_basis[earlier] * mapped) for earlier in range(section + 1)]
        )
        products, image_square = lax.psum(
            (local_products, jnp.sum(mapped * mapped)), ("mode", "gx", "gy")
        )
        coefficients = [products[earlier] for earlier in range(section + 1)]
        for earlier in range(section + 1):
            mapped = mapped - coefficients[earlier] * krylov_basis[earlier]
        length = jnp.sqrt(jnp.maximum(image_square - jnp.sum(products * products), 0.0) + epsilon)
        krylov_basis.append(mapped / length)
        entries = (
            coefficients
            + [length]
            + [jnp.zeros_like(length) for later in range(KRYLOV - section - 1)]
        )
        columns_list.append(jnp.stack(entries))
    hessenberg = jnp.stack(columns_list, axis=1)
    combo = least_squares(hessenberg, initial)
    solution = jnp.zeros_like(right_side)
    for section in range(KRYLOV):
        solution = solution + combo[section] * krylov_basis[section]
    return (solution, hessenberg)


def solution(mesh):
    return jax.shard_map(
        per_device,
        mesh=mesh,
        in_specs=(
            P("gx", "gy", "mode"),
            P("mode", None),
            P("mode", None, None, None),
            P("mode"),
            P(None, "mode"),
            P(None, "mode"),
            P("gx", "gy"),
        ),
        out_specs=(P("gx", "gy", "mode"), P()),
        check_vma=False,
    )
```

profile of v0, /device:TPU:0, one launch (start us, length us, event | category | flops | bytes accessed | tf_op | source)
XLA Modules:
  0.0 284.0 jit_solution(9305886080614791052)
XLA Ops:
  0.6 1.7 multiply_reduce_fusion.9
  2.4 0.7 subtract_convert_fusion
  3.1 42.2 %psum.49 = f32[]{:T(128)} all-reduce(f32[]{:T(128)} %multiply_reduce_fusion.9), channel_id=1, replica_groups=mesh['mode'=4,'gx'=2,'gy'=4] {'mode','gx','gy'}, use_global_device_ids=true, to_apply=%region_1.0 | all-reduce | flops 1 | bytes 8 | tf_op jit(solution)/shard_map/psum | solution.py:87
  46.0 1.1 broadcast_multiply_fusion.2
  47.1 1.3 collective-permute-start.1
  48.4 4.5 %collective-permute-start = (f32[1,8,1792]{2,1,0:T(8,128)S(1)}, f32[1,8,1792]{2,1,0:T(8,128)S(1)}, u32[]{:S(2)}, u32[]{:S(2)}) collective-permute-start(f32[1,8,1792]{2,1,0:T(8,128)S(1)} %get-tuple-element.44), channel_id=1, source_target_pairs={{0,4},{1,5},{2,6},{3,7},{8,12},{9,13},{10,14},{11,15},{16,20},{17,... | collective-permute-start | bytes 172040 | tf_op jit(solution)/shard_map/ppermute | solution.py:17
  53.2 10.3 %all_gather.9 = bf16[64,7168]{1,0:T(8,128)(2,1)S(1)} all-gather(bf16[64,1792]{1,0:T(8,128)(2,1)S(1)} %get-tuple-element.47), channel_id=1, replica_groups=mesh['mode'=4,'gx'=2,'gy'=4] {'mode'}, dimensions={1}, use_global_device_ids=true | all-gather | bytes 1146880 | tf_op jit(solution)/shard_map/all_gather | solution.py:43
  63.7 0.9 gather_fusion
  64.9 1.8 copy-done
  66.7 1.3 convolution_bitcast_fusion.2
  68.6 1.3 collective-permute-start.3
  69.9 4.5 %collective-permute-start.2 = (f32[10,1,1792]{2,1,0:T(1,128)S(1)}, f32[10,1,1792]{2,1,0:T(1,128)S(1)}, u32[]{:S(2)}, u32[]{:S(2)}) collective-permute-start(f32[10,1,1792]{2,1,0:T(1,128)S(1)} %get-tuple-element.38), channel_id=1, source_target_pairs={{0,1},{1,2},{2,3},{4,5},{5,6},{6,7},{8,9},{9,10},{10,11},{12,13},{... | collective-permute-start | bytes 215048 | tf_op jit(solution)/shard_map/ppermute | solution.py:17
  75.0 1.4 collective-permute-done.2
  76.4 1.1 multiply_reduce_fusion.8
  77.5 40.4 %all-reduce.2 = (f32[]{:T(128)}, f32[1]{0:T(128)}) all-reduce(f32[]{:T(128)} %get-tuple-element.17, f32[1]{0:T(128)} %bitcast.6), channel_id=1, replica_groups=mesh['mode'=4,'gx'=2,'gy'=4] {'mode','gx','gy'}, use_global_device_ids=true, to_apply=%region_5.7 | all-reduce | flops 2 | bytes 16 | tf_op jit(solution)/shard_map/psum | solution.py:104
  119.9 0.8 broadcast_multiply_fusion.1
  120.7 10.3 %all_gather.10 = bf16[64,7168]{1,0:T(8,128)(2,1)S(1)} all-gather(bf16[64,1792]{1,0:T(8,128)(2,1)S(1)} %convert_bitcast_fusion.1), channel_id=1, replica_groups=mesh['mode'=4,'gx'=2,'gy'=4] {'mode'}, dimensions={1}, use_global_device_ids=true | all-gather | bytes 1146880 | tf_op jit(solution)/shard_map/all_gather | solution.py:43
  131.3 2.1 gather_fusion.1
  133.3 1.9 broadcast_select_fusion.1
  135.2 1.3 collective-permute-start.5
  136.5 4.5 %collective-permute-start.4 = (f32[1,8,1792]{2,1,0:T(8,128)S(1)}, f32[1,8,1792]{2,1,0:T(8,128)S(1)}, u32[]{:S(2)}, u32[]{:S(2)}) collective-permute-start(f32[1,8,1792]{2,1,0:T(8,128)S(1)} %get-tuple-element.42), channel_id=1, source_target_pairs={{0,4},{1,5},{2,6},{3,7},{8,12},{9,13},{10,14},{11,15},{16,20},{17,... | collective-permute-start | bytes 172040 | tf_op jit(solution)/shard_map/ppermute | solution.py:17
  141.1 1.3 convolution_bitcast_fusion.1
  145.0 1.3 collective-permute-start.7
  146.3 4.5 %collective-permute-start.6 = (f32[10,1,1792]{2,1,0:T(1,128)S(1)}, f32[10,1,1792]{2,1,0:T(1,128)S(1)}, u32[]{:S(2)}, u32[]{:S(2)}) collective-permute-start(f32[10,1,1792]{2,1,0:T(1,128)S(1)} %get-tuple-element.36), channel_id=1, source_target_pairs={{0,1},{1,2},{2,3},{4,5},{5,6},{6,7},{8,9},{9,10},{10,11},{12,13},{... | collective-permute-start | bytes 215048 | tf_op jit(solution)/shard_map/ppermute | solution.py:17
  150.8 0.7 maximum_bitcast_fusion
  151.6 1.2 collective-permute-done.6
  152.8 1.2 multiply_reduce_fusion.6
  153.9 1.4 pad_maximum_fusion.34
  155.4 40.3 %all-reduce.1 = (f32[]{:T(128)}, f32[2]{0:T(128)S(1)}) all-reduce(f32[]{:T(128)} %get-tuple-element.14, f32[2]{0:T(128)S(1)} %pad_maximum_fusion.34), channel_id=1, replica_groups=mesh['mode'=4,'gx'=2,'gy'=4] {'mode','gx','gy'}, use_global_device_ids=true, to_apply=%region_10.12 | all-reduce | flops 3 | bytes 24 | tf_op jit(solution)/shard_map/psum | solution.py:104
  195.7 0.6 multiply_reduce_fusion.11
  196.3 0.7 fusion.33
  198.3 1.4 broadcast_multiply_fusion
  199.7 10.3 %all_gather.11 = bf16[64,7168]{1,0:T(8,128)(2,1)S(1)} all-gather(bf16[64,1792]{1,0:T(8,128)(2,1)S(1)} %convert_bitcast_fusion), channel_id=1, replica_groups=mesh['mode'=4,'gx'=2,'gy'=4] {'mode'}, dimensions={1}, use_global_device_ids=true | all-gather | bytes 1146880 | tf_op jit(solution)/shard_map/all_gather | solution.py:43
  210.2 2.1 gather_fusion.2
  212.3 1.9 broadcast_select_fusion
  214.2 1.3 collective-permute-start.9
  215.5 4.5 %collective-permute-start.8 = (f32[1,8,1792]{2,1,0:T(8,128)S(1)}, f32[1,8,1792]{2,1,0:T(8,128)S(1)}, u32[]{:S(2)}, u32[]{:S(2)}) collective-permute-start(f32[1,8,1792]{2,1,0:T(8,128)S(1)} %get-tuple-element.40), channel_id=1, source_target_pairs={{0,4},{1,5},{2,6},{3,7},{8,12},{9,13},{10,14},{11,15},{16,20},{17,... | collective-permute-start | bytes 172040 | tf_op jit(solution)/shard_map/ppermute | solution.py:17
  220.1 1.3 convolution_bitcast_fusion
  224.6 1.3 collective-permute-start.11
  225.9 4.5 %collective-permute-start.10 = (f32[10,1,1792]{2,1,0:T(1,128)S(1)}, f32[10,1,1792]{2,1,0:T(1,128)S(1)}, u32[]{:S(2)}, u32[]{:S(2)}) collective-permute-start(f32[10,1,1792]{2,1,0:T(1,128)S(1)} %get-tuple-element.34), channel_id=1, source_target_pairs={{0,1},{1,2},{2,3},{4,5},{5,6},{6,7},{8,9},{9,10},{10,11},{12,13},{... | collective-permute-start | bytes 215048 | tf_op jit(solution)/shard_map/ppermute | solution.py:17
  230.8 1.6 collective-permute-done.10
  232.4 1.1 multiply_reduce_fusion
  233.5 2.0 pad_maximum_fusion.35
  235.5 40.3 %all-reduce = (f32[3]{0:T(128)S(1)}, f32[]{:T(128)}) all-reduce(f32[3]{0:T(128)S(1)} %pad_maximum_fusion.35, f32[]{:T(128)} %get-tuple-element.9), channel_id=1, replica_groups=mesh['mode'=4,'gx'=2,'gy'=4] {'mode','gx','gy'}, use_global_device_ids=true, to_apply=%region_15.17 | all-reduce | flops 4 | bytes 32 | tf_op jit(solution)/shard_map/psum | solution.py:104
  275.8 0.7 fusion.32
  276.4 0.6 multiply_reduce_fusion.10
  282.4 0.9 multiply_add_fusion
  283.4 0.7 copy.23
  (53 shorter events, 3.6 us)
Async XLA Ops:
  0.6 52.3 %copy-start.7 = (s32[14,8]{0,1:T(8,128)S(1)}, s32[14,8]{0,1:T(8,128)}, u32[]{:S(2)}) copy-start(s32[14,8]{0,1:T(8,128)} %param.10) | copy-start | bytes 1348
  47.1 21.4 %collective-permute-start.1 = (f32[1,8,1792]{2,1,0:T(8,128)S(1)}, f32[1,8,1792]{2,1,0:T(8,128)S(1)}, u32[]{:S(2)}, u32[]{:S(2)}) collective-permute-start(f32[1,8,1792]{2,1,0:T(8,128)S(1)} %get-tuple-element.45), channel_id=1, source_target_pairs={{4,0},{5,1},{6,2},{7,3},{12,8},{13,9},{14,10},{15,11},{20,16},{21,... | collective-permute-start | bytes 172040 | tf_op jit(solution)/shard_map/ppermute | solution.py:20
  48.4 20.1 %collective-permute-start = (f32[1,8,1792]{2,1,0:T(8,128)S(1)}, f32[1,8,1792]{2,1,0:T(8,128)S(1)}, u32[]{:S(2)}, u32[]{:S(2)}) collective-permute-start(f32[1,8,1792]{2,1,0:T(8,128)S(1)} %get-tuple-element.44), channel_id=1, source_target_pairs={{0,4},{1,5},{2,6},{3,7},{8,12},{9,13},{10,14},{11,15},{16,20},{17,... | collective-permute-start | bytes 172040 | tf_op jit(solution)/shard_map/ppermute | solution.py:17
  64.6 2.0 copy-start
  66.7 1.4 copy-start.5
  68.0 6.4 %copy-start.6 = (f32[2,1792]{1,0:T(2,128)S(1)}, f32[2,1792]{1,0:T(2,128)}, u32[]{:S(2)}) copy-start(f32[2,1792]{1,0:T(2,128)} %param.13) | copy-start | bytes 43012
  68.0 8.4 %copy-start.3 = (f32[8,8,1792]{2,1,0:T(8,128)S(1)}, f32[8,8,1792]{2,1,0:T(8,128)}, u32[]{:S(2)}) copy-start(f32[8,8,1792]{2,1,0:T(8,128)} %param.9) | copy-start | bytes 1376260
  68.1 8.4 %copy-start.4 = (f32[1792]{0:T(1024)S(1)}, f32[1792]{0:T(1024)}, u32[]{:S(2)}) copy-start(f32[1792]{0:T(1024)} %param.12) | copy-start | bytes 21508
  68.6 6.4 %collective-permute-start.3 = (f32[10,1,1792]{2,1,0:T(1,128)S(1)}, f32[10,1,1792]{2,1,0:T(1,128)S(1)}, u32[]{:S(2)}, u32[]{:S(2)}) collective-permute-start(f32[10,1,1792]{2,1,0:T(1,128)S(1)} %get-tuple-element.39), channel_id=1, source_target_pairs={{1,0},{2,1},{3,2},{5,4},{6,5},{7,6},{9,8},{10,9},{11,10},{13,12},{... | collective-permute-start | bytes 215048 | tf_op jit(solution)/shard_map/ppermute | solution.py:20
  69.9 6.5 %collective-permute-start.2 = (f32[10,1,1792]{2,1,0:T(1,128)S(1)}, f32[10,1,1792]{2,1,0:T(1,128)S(1)}, u32[]{:S(2)}, u32[]{:S(2)}) collective-permute-start(f32[10,1,1792]{2,1,0:T(1,128)S(1)} %get-tuple-element.38), channel_id=1, source_target_pairs={{0,1},{1,2},{2,3},{4,5},{5,6},{6,7},{8,9},{9,10},{10,11},{12,13},{... | collective-permute-start | bytes 215048 | tf_op jit(solution)/shard_map/ppermute | solution.py:17
  133.3 7.8 %copy-start.1 = (bf16[14,8,128,128]{3,2,1,0:T(8,128)(2,1)S(1)}, bf16[14,8,128,128]{3,2,1,0:T(8,128)(2,1)}, u32[]{:S(2)}) copy-start(bf16[14,8,128,128]{3,2,1,0:T(8,128)(2,1)} %param.11) | copy-start | bytes 11010052
  135.2 9.6 %collective-permute-start.5 = (f32[1,8,1792]{2,1,0:T(8,128)S(1)}, f32[1,8,1792]{2,1,0:T(8,128)S(1)}, u32[]{:S(2)}, u32[]{:S(2)}) collective-permute-start(f32[1,8,1792]{2,1,0:T(8,128)S(1)} %get-tuple-element.43), channel_id=1, source_target_pairs={{4,0},{5,1},{6,2},{7,3},{12,8},{13,9},{14,10},{15,11},{20,16},{21,... | collective-permute-start | bytes 172040 | tf_op jit(solution)/shard_map/ppermute | solution.py:20
  136.5 8.3 %collective-permute-start.4 = (f32[1,8,1792]{2,1,0:T(8,128)S(1)}, f32[1,8,1792]{2,1,0:T(8,128)S(1)}, u32[]{:S(2)}, u32[]{:S(2)}) collective-permute-start(f32[1,8,1792]{2,1,0:T(8,128)S(1)} %get-tuple-element.42), channel_id=1, source_target_pairs={{0,4},{1,5},{2,6},{3,7},{8,12},{9,13},{10,14},{11,15},{16,20},{17,... | collective-permute-start | bytes 172040 | tf_op jit(solution)/shard_map/ppermute | solution.py:17
  145.0 6.6 %collective-permute-start.7 = (f32[10,1,1792]{2,1,0:T(1,128)S(1)}, f32[10,1,1792]{2,1,0:T(1,128)S(1)}, u32[]{:S(2)}, u32[]{:S(2)}) collective-permute-start(f32[10,1,1792]{2,1,0:T(1,128)S(1)} %get-tuple-element.37), channel_id=1, source_target_pairs={{1,0},{2,1},{3,2},{5,4},{6,5},{7,6},{9,8},{10,9},{11,10},{13,12},{... | collective-permute-start | bytes 215048 | tf_op jit(solution)/shard_map/ppermute | solution.py:20
  146.3 6.5 %collective-permute-start.6 = (f32[10,1,1792]{2,1,0:T(1,128)S(1)}, f32[10,1,1792]{2,1,0:T(1,128)S(1)}, u32[]{:S(2)}, u32[]{:S(2)}) collective-permute-start(f32[10,1,1792]{2,1,0:T(1,128)S(1)} %get-tuple-element.36), channel_id=1, source_target_pairs={{0,1},{1,2},{2,3},{4,5},{5,6},{6,7},{8,9},{9,10},{10,11},{12,13},{... | collective-permute-start | bytes 215048 | tf_op jit(solution)/shard_map/ppermute | solution.py:17
  212.3 7.8 %copy-start.2 = (bf16[14,8,128,128]{3,2,1,0:T(8,128)(2,1)S(1)}, bf16[14,8,128,128]{3,2,1,0:T(8,128)(2,1)}, u32[]{:S(2)}) copy-start(bf16[14,8,128,128]{3,2,1,0:T(8,128)(2,1)} %param.11) | copy-start | bytes 11010052
  214.2 10.3 %collective-permute-start.9 = (f32[1,8,1792]{2,1,0:T(8,128)S(1)}, f32[1,8,1792]{2,1,0:T(8,128)S(1)}, u32[]{:S(2)}, u32[]{:S(2)}) collective-permute-start(f32[1,8,1792]{2,1,0:T(8,128)S(1)} %get-tuple-element.41), channel_id=1, source_target_pairs={{4,0},{5,1},{6,2},{7,3},{12,8},{13,9},{14,10},{15,11},{20,16},{21,... | collective-permute-start | bytes 172040 | tf_op jit(solution)/shard_map/ppermute | solution.py:20
  215.5 9.0 %collective-permute-start.8 = (f32[1,8,1792]{2,1,0:T(8,128)S(1)}, f32[1,8,1792]{2,1,0:T(8,128)S(1)}, u32[]{:S(2)}, u32[]{:S(2)}) collective-permute-start(f32[1,8,1792]{2,1,0:T(8,128)S(1)} %get-tuple-element.40), channel_id=1, source_target_pairs={{0,4},{1,5},{2,6},{3,7},{8,12},{9,13},{10,14},{11,15},{16,20},{17,... | collective-permute-start | bytes 172040 | tf_op jit(solution)/shard_map/ppermute | solution.py:17
  224.6 6.2 %collective-permute-start.11 = (f32[10,1,1792]{2,1,0:T(1,128)S(1)}, f32[10,1,1792]{2,1,0:T(1,128)S(1)}, u32[]{:S(2)}, u32[]{:S(2)}) collective-permute-start(f32[10,1,1792]{2,1,0:T(1,128)S(1)} %get-tuple-element.35), channel_id=1, source_target_pairs={{1,0},{2,1},{3,2},{5,4},{6,5},{7,6},{9,8},{10,9},{11,10},{13,12},{... | collective-permute-start | bytes 215048 | tf_op jit(solution)/shard_map/ppermute | solution.py:20
  225.9 6.5 %collective-permute-start.10 = (f32[10,1,1792]{2,1,0:T(1,128)S(1)}, f32[10,1,1792]{2,1,0:T(1,128)S(1)}, u32[]{:S(2)}, u32[]{:S(2)}) collective-permute-start(f32[10,1,1792]{2,1,0:T(1,128)S(1)} %get-tuple-element.34), channel_id=1, source_target_pairs={{0,1},{1,2},{2,3},{4,5},{5,6},{6,7},{8,9},{9,10},{10,11},{12,13},{... | collective-permute-start | bytes 215048 | tf_op jit(solution)/shard_map/ppermute | solution.py:17
where the time goes:
time: 285 us; the launch traced here: 284 us
  blocking collectives  194 us (68%)
  starting transfers between devices  35 us (12%)
  other arithmetic  19.8 us (7%)
  between operations  15.2 us (5%)
  local copies, waits for them, and re-layouts  10.9 us (4%)
  waiting for transfers between devices  4.97 us (2%)
  matrix products  4.04 us (1%)
    psum x3, blocking collectives, per_device(): lax.psum((local_products, jnp.sum(mapped * mapped)), ('mode', 'gx', 'gy'))  121 us
    psum x1, blocking collectives, per_device(): squared = lax.psum(jnp.sum(right_side * right_side), ('mode', 'gx', 'gy'))  42.2 us
    all_gather x3, blocking collectives, apply_operator(): gathered = lax.all_gather(rounded, 'mode', axis=1, tiled=True)  30.8 us
    ppermute x6, starting transfers between devices, extended(): lax.ppermute(lax.slice_in_dim(block, block.shape[dim] - width, None, axis...  27.3 us
    ppermute x6, starting transfers between devices, extended(): lax.ppermute(lax.slice_in_dim(block, 0, width, axis=dim), axis, backward)  7.75 us
  transfers between devices with their start and end apart: 12, of which 5 were waited for; matrix products, arithmetic and copies ran while one was open for 3% of the time, Pallas kernels for 0%

commit v1 on v0

v1 whole, which is shorter than its diff:
```python
import functools

import jax
import jax.numpy as jnp
from jax import lax
from jax.experimental import pallas as pl
from jax.experimental.pallas import tpu as pltpu
from jax.sharding import PartitionSpec as P

KRYLOV = 3
ENTRIES = 16
TAIL = 16
AXES = ("mode", "gx", "gy")

epsilon = 1e-12


def pair_list(count, first):
    pairs = []
    for low in range(first, count - 1, 2):
        pairs += [(low, low + 1), (low + 1, low)]
    return pairs


def swaps_of(count):
    return [pairs for pairs in (pair_list(count, 0), pair_list(count, 1)) if pairs]


def face_swaps(faces):
    received = []
    for axis in ("gx", "gy"):
        swaps = swaps_of(lax.axis_size(axis))
        received.append(
            [lax.ppermute(face, axis, pairs) for face, pairs in zip(faces[axis], swaps)]
        )
    return received


def gather_modes(packed):
    count = lax.axis_size("mode")
    held = {0: packed}
    bit = count // 2
    while bit:
        for key in list(held):
            held[key ^ bit] = lax.ppermute(
                held[key], "mode", [(i, i ^ bit) for i in range(count)]
            )
        bit //= 2
    return [held[key] for key in range(count)]


def write_faces(masked, lanes, first, second, x_refs, y_refs):
    if x_refs:
        even = lax.rem(lax.axis_index("gx"), 2) == 0
        low, high = masked[0], masked[first - 1]
        for ref, take_high in zip(x_refs, (even, jnp.logical_not(even))):
            ref[:, lanes] = jnp.where(take_high, high, low)
    if y_refs:
        even = lax.rem(lax.axis_index("gy"), 2) == 0
        low, high = masked[:, 0, :], masked[:, second - 1, :]
        for ref, take_high in zip(y_refs, (even, jnp.logical_not(even))):
            ref[:, lanes] = jnp.where(take_high, high, low)


def halos(refs, axis, lanes, shape):
    zero = jnp.zeros(shape, jnp.float32)
    values = [ref[:, lanes] for ref in refs] + [zero, zero]
    odd = lax.rem(lax.axis_index(axis), 2) == 1
    return jnp.where(odd, values[0], values[1]), jnp.where(odd, values[1], values[0])


def prepare_kernel(sizes, refs_in, x_refs, y_refs, packed_ref, open_ref):
    first, second, local_blocks, block = sizes
    rhs_ref, relax_ref, speed_ref, wall_ref = refs_in
    cells = first * second
    wall = wall_ref[...].astype(jnp.float32)
    eye = (
        lax.broadcasted_iota(jnp.int32, (second, second), 0)
        == lax.broadcasted_iota(jnp.int32, (second, second), 1)
    ).astype(jnp.float32)
    for row in range(first):
        column = jnp.sum(eye * (1.0 - wall[row : row + 1, :]), axis=1, keepdims=True)
        open_ref[row * second : (row + 1) * second, :] = jnp.broadcast_to(column, (second, block))
    total = jnp.zeros((1, block), jnp.float32)
    for b in range(local_blocks):
        lanes = slice(b * block, (b + 1) * block)
        value = rhs_ref[:, lanes]
        packed_ref[b * cells : (b + 1) * cells, :] = value.astype(jnp.bfloat16)
        masked = (value * open_ref[...]).reshape(first, second, block)
        write_faces(masked, lanes, first, second, x_refs, y_refs)
        total += relax_ref[:, lanes] + speed_ref[0:1, lanes] + speed_ref[1:2, lanes]
    mean = jnp.sum(total, axis=1, keepdims=True) * (1.0 / (local_blocks * block))
    packed_ref[local_blocks * cells :, :] = jnp.broadcast_to(mean, (TAIL, block)).astype(
        jnp.bfloat16
    )


def shift_of(sources, owners, tail_at):
    rows = [ref[tail_at : tail_at + TAIL, :].astype(jnp.float32)[0:1] for ref in sources]
    total = jnp.zeros_like(rows[0])
    for owner in range(len(sources)):
        term = rows[0]
        for place in range(1, len(sources)):
            term = jnp.where(owners[place] == owner, rows[place], term)
        total = total + term
    return total * (1.0 / len(sources))


def step_kernel(sizes, per_owner, last, cols_ref, sources, blocks_ref, earlier, params, x_in, y_in, outs):
    first, second, local_blocks, block = sizes
    relax_ref, speed_ref, sign_ref, open_ref = params
    cells = first * second
    count = len(sources)
    mine = lax.axis_index("mode")
    owners = [mine ^ place for place in range(count)]
    shift = shift_of(sources[: count], owners, local_blocks * cells) if outs.shift_in is None else outs.shift_in[...]
    if outs.shift is not None:
        outs.shift[...] = shift
    open_cells = open_ref[...]
    current_ref = earlier[-1]
    row_at = lax.broadcasted_iota(jnp.int32, (first, second, block), 1)
    sums = {}
    for b in range(local_blocks):
        lanes = slice(b * block, (b + 1) * block)
        picks, weights = [], []
        for place in range(count):
            for p in range(per_owner):
                slot = owners[place] * per_owner + p
                column = cols_ref[b, slot] - owners[place] * local_blocks
                picks.append(sources[place][pl.ds(pl.multiple_of(column * cells, cells), cells), :])
                weights.append(blocks_ref[b, slot])
        scattered = lax.dot_general(
            jnp.concatenate(picks, axis=1),
            jnp.concatenate(weights, axis=1),
            (((1,), (1,)), ((), ())),
            preferred_element_type=jnp.float32,
        )
        current = current_ref[:, lanes]
        masked = (current * open_cells).reshape(first, second, block)
        west_in, east_in = halos(x_in, "gx", lanes, (second, block))
        south_in, north_in = halos(y_in, "gy", lanes, (first, block))
        from_west = jnp.concatenate([west_in[None], masked[:-1]], axis=0)
        from_east = jnp.concatenate([masked[1:], east_in[None]], axis=0)
        from_south = jnp.where(
            row_at == 0, south_in[:, None, :], pltpu.roll(masked, 1, axis=1)
        )
        from_north = jnp.where(
            row_at == second - 1, north_in[:, None, :], pltpu.roll(masked, second - 1, axis=1)
        )
        sign_x = sign_ref[0:1, lanes].reshape(1, 1, block)
        sign_y = sign_ref[1:2, lanes].reshape(1, 1, block)
        speed_x, speed_y = speed_ref[0:1, lanes], speed_ref[1:2, lanes]
        upstream_x = jnp.where(sign_x == 1, from_west, from_east).reshape(cells, block)
        upstream_y = jnp.where(sign_y == 1, from_south, from_north).reshape(cells, block)
        diagonal = relax_ref[:, lanes] + speed_x + speed_y - shift
        result = diagonal * current - speed_x * upstream_x - speed_y * upstream_y - scattered
        if not last:
            outs.value[:, lanes] = result
            outs.packed[b * cells : (b + 1) * cells, :] = result.astype(jnp.bfloat16)
            write_faces(
                (result * open_cells).reshape(first, second, block),
                lanes, first, second, outs.x, outs.y,
            )
        else:
            vectors = [ref[:, lanes] for ref in earlier] + [result]
            at = 0
            for i in range(len(vectors)):
                for j in range(i, len(vectors)):
                    term = jnp.sum((vectors[i] * vectors[j]).reshape(cells // 8, 8, block), axis=0)
                    sums[at] = term if b == 0 else sums[at] + term
                    at += 1
    if last:
        devices = outs.gram.shape[0]
        for at, value in sums.items():
            total = jnp.sum(jnp.sum(value, axis=0, keepdims=True), axis=1, keepdims=True)
            outs.gram[:, at : at + 1, :] = jnp.broadcast_to(
                total.reshape(1, 1, 1), (devices, 1, block)
            )
        left = outs.gram.shape[1] - len(sums)
        outs.gram[:, len(sums) :, :] = jnp.zeros((devices, left, block), jnp.float32)
    elif outs.packed.shape[0] > local_blocks * cells:
        outs.packed[local_blocks * cells :, :] = jnp.zeros((TAIL, block), jnp.bfloat16)


class Outs:
    value = packed = gram = shift = shift_in = None
    x = y = ()


def least_squares(hessenberg, initial):
    upper = [list(row) for row in hessenberg]
    target = [initial] + [jnp.zeros_like(initial) for row_index in range(KRYLOV)]
    cosines = []
    sines = []
    for col_index in range(KRYLOV):
        for row_index in range(col_index):
            first = upper[row_index][col_index]
            second = upper[row_index + 1][col_index]
            upper[row_index][col_index] = cosines[row_index] * first + sines[row_index] * second
            upper[row_index + 1][col_index] = cosines[row_index] * second - sines[row_index] * first
        first = upper[col_index][col_index]
        second = upper[col_index + 1][col_index]
        radius = jnp.sqrt(first * first + second * second)
        cosine = first / radius
        sine_value = second / radius
        upper[col_index][col_index] = radius
        target[col_index + 1] = -sine_value * target[col_index]
        target[col_index] = cosine * target[col_index]
        cosines.append(cosine)
        sines.append(sine_value)
    combo = [None] * KRYLOV
    for row_index in reversed(range(KRYLOV)):
        running = target[row_index]
        for col_index in range(row_index + 1, KRYLOV):
            running = running - upper[row_index][col_index] * combo[col_index]
        combo[row_index] = running / upper[row_index][row_index]
    return combo


def arnoldi(gram, shift):
    size = KRYLOV + 1

    def inner(left, right):
        total = None
        for i in range(size):
            for j in range(size):
                if left[i] is None or right[j] is None:
                    continue
                term = left[i] * right[j] * gram[min(i, j)][max(i, j)]
                total = term if total is None else total + term
        return total

    initial = jnp.sqrt(gram[0][0] + epsilon)
    basis = [[1.0 / initial] + [None] * KRYLOV]
    zero = jnp.zeros_like(initial)
    hessenberg = [[zero] * KRYLOV for row_index in range(size)]
    for section in range(KRYLOV):
        vector = basis[section]
        image = [None] * size
        for k in range(section + 2):
            parts = []
            if k > 0 and vector[k - 1] is not None:
                parts.append(vector[k - 1])
            if vector[k] is not None:
                parts.append(shift * vector[k])
            image[k] = sum(parts[1:], parts[0])
        rest = list(image)
        for earlier in range(section + 1):
            coefficient = inner(basis[earlier], image)
            hessenberg[earlier][section] = coefficient
            for k in range(earlier + 1):
                rest[k] = rest[k] - coefficient * basis[earlier][k]
        length = jnp.sqrt(jnp.maximum(inner(rest, rest), 0.0) + epsilon)
        hessenberg[section + 1][section] = length
        basis.append([None if part is None else part / length for part in rest])
    combo = least_squares(hessenberg, initial)
    weights = []
    for k in range(KRYLOV):
        total = zero
        for j in range(k, KRYLOV):
            total = total + combo[j] * basis[j][k]
        weights.append(total)
    return hessenberg, weights


def finish_kernel(gram_ref, shift_ref, *refs):
    vectors, (solution_ref, hessenberg_ref) = refs[:KRYLOV], refs[KRYLOV:]
    total = jnp.sum(gram_ref[...], axis=0)
    gram = [[None] * (KRYLOV + 1) for i in range(KRYLOV + 1)]
    at = 0
    for i in range(KRYLOV + 1):
        for j in range(i, KRYLOV + 1):
            gram[i][j] = total[at : at + 1, :]
            at += 1
    hessenberg, weights = arnoldi(gram, shift_ref[...])
    rows = lax.broadcasted_iota(jnp.int32, (KRYLOV + 1, KRYLOV), 0)
    cols = lax.broadcasted_iota(jnp.int32, (KRYLOV + 1, KRYLOV), 1)
    table = jnp.zeros((KRYLOV + 1, KRYLOV), jnp.float32)
    for i in range(KRYLOV + 1):
        for j in range(KRYLOV):
            table = jnp.where((rows == i) & (cols == j), hessenberg[i][j][:, :KRYLOV], table)
    hessenberg_ref[...] = table
    block = shift_ref.shape[1]
    for b in range(solution_ref.shape[1] // block):
        lanes = slice(b * block, (b + 1) * block)
        solution_ref[:, lanes] = sum(
            weight * ref[:, lanes] for weight, ref in zip(weights, vectors)
        )


VMEM = pl.BlockSpec(memory_space=pltpu.VMEM)
SMEM = pl.BlockSpec(memory_space=pltpu.SMEM)


def per_device(right_side, col_block, blocks, relax_rate, drift_speed, upwind_sign, wall_mask):
    first, second, local_modes = right_side.shape
    local_blocks, slots, block = blocks.shape[:3]
    cells = first * second
    count = lax.axis_size("mode")
    devices = count * lax.axis_size("gx") * lax.axis_size("gy")
    sizes = (first, second, local_blocks, block)
    x_swaps, y_swaps = len(swaps_of(lax.axis_size("gx"))), len(swaps_of(lax.axis_size("gy")))
    f32 = jnp.float32
    face_shapes = [jax.ShapeDtypeStruct((second, local_modes), f32)] * x_swaps + [
        jax.ShapeDtypeStruct((first, local_modes), f32)
    ] * y_swaps
    packed_rows = local_blocks * cells + TAIL
    packed_shape = jax.ShapeDtypeStruct((packed_rows, block), jnp.bfloat16)
    vector_shape = jax.ShapeDtypeStruct((cells, local_modes), f32)
    shift_shape = jax.ShapeDtypeStruct((1, block), f32)
    n_faces = x_swaps + y_swaps
    limit = pltpu.CompilerParams(vmem_limit_bytes=32 * 1024 * 1024)

    start = right_side.reshape(cells, local_modes)
    relax = relax_rate.reshape(1, local_modes)

    def prepare(*refs):
        faces, (packed_ref, open_ref) = refs[4 : 4 + n_faces], refs[4 + n_faces :]
        prepare_kernel(
            sizes, refs[:4], faces[:x_swaps], faces[x_swaps:], packed_ref, open_ref
        )

    *faces, packed, open_cells = pl.pallas_call(
        prepare,
        out_shape=face_shapes + [packed_shape, jax.ShapeDtypeStruct((cells, block), f32)],
        in_specs=[VMEM] * 4,
        out_specs=[VMEM] * (n_faces + 2),
        compiler_params=limit,
        name="prepare",
    )(start, relax, drift_speed, wall_mask)

    vectors = [start]
    shift = None
    for section in range(KRYLOV):
        last = section == KRYLOV - 1
        sources = gather_modes(packed)
        x_in, y_in = face_swaps({"gx": faces[:x_swaps], "gy": faces[x_swaps:]})
        n_before = len(vectors)

        def step(*refs, last=last, n_before=n_before, has_shift=shift is not None):
            refs = list(refs)

            def take(number):
                taken = refs[:number]
                del refs[:number]
                return taken

            (cols_ref,) = take(1)
            source_refs = take(count)
            (blocks_ref,) = take(1)
            earlier = take(n_before)
            params = take(4)
            x_refs, y_refs = take(x_swaps), take(y_swaps)
            outs = Outs()
            if has_shift:
                (outs.shift_in,) = take(1)
            if last:
                (outs.gram,) = take(1)
            else:
                outs.x, outs.y = take(x_swaps), take(y_swaps)
                outs.packed, outs.value = take(2)
            if not has_shift:
                (outs.shift,) = take(1)
            step_kernel(
                sizes, slots // count, last, cols_ref, source_refs, blocks_ref, earlier, params,
                x_refs, y_refs, outs,
            )

        operands = [col_block, *sources, blocks, *vectors, relax, drift_speed, upwind_sign,
                    open_cells, *x_in, *y_in]
        if shift is not None:
            operands.append(shift)
        if last:
            shapes = [jax.ShapeDtypeStruct((devices, ENTRIES, block), f32)]
        else:
            shapes = face_shapes + [packed_shape, vector_shape]
        if shift is None:
            shapes = shapes + [shift_shape]
        results = pl.pallas_call(
            step,
            out_shape=shapes,
            in_specs=[SMEM] + [VMEM] * (len(operands) - 1),
            out_specs=[VMEM] * len(shapes),
            compiler_params=limit,
            name="step_%d" % section,
        )(*operands)
        if shift is None:
            *results, shift = results
        if last:
            (gram,) = results
        else:
            *faces, packed, value = results
            vectors.append(value)

    gram = lax.all_to_all(gram, AXES, 0, 0)
    solution, hessenberg = pl.pallas_call(
        finish_kernel,
        out_shape=[vector_shape, jax.ShapeDtypeStruct((KRYLOV + 1, KRYLOV), f32)],
        in_specs=[VMEM] * (2 + KRYLOV),
        out_specs=[VMEM] * 2,
        compiler_params=limit,
        name="finish",
    )(gram, shift, *vectors)
    return solution.reshape(first, second, local_modes), hessenberg


def solution(mesh):
    return jax.shard_map(
        per_device,
        mesh=mesh,
        in_specs=(
            P("gx", "gy", "mode"),
            P("mode", None),
            P("mode", None, None, None),
            P("mode"),
            P(None, "mode"),
            P(None, "mode"),
            P("gx", "gy"),
        ),
        out_specs=(P("gx", "gy", "mode"), P()),
        check_vma=False,
    )
```

time: 285 us -> 76.6 us (0.27)
  blocking collectives: 194 us -> 16.8 us
  other arithmetic: 19.8 us -> 0 us
  waiting for transfers between devices: 4.97 us -> 21.1 us
  between operations: 15.2 us -> 0.78 us
  starting transfers between devices: 35 us -> 21.2 us
  Pallas kernels: 0 us -> 7.78 us
  matrix products: 4.04 us -> 0 us
    psum x4 -> x0, blocking collectives: 163 us -> none  [the longest x3 121 us: per_device(): lax.psum((local_products, jnp.sum(mapped * mapped)), ('mode', 'gx', 'gy'))]
    all_gather x3 -> x0, blocking collectives: 30.8 us -> none  [apply_operator(): gathered = lax.all_gather(rounded, 'mode', axis=1, tiled=True)]
    all_to_all x0 -> x1, blocking collectives: none -> 16.8 us  [per_device(): gram = lax.all_to_all(gram, AXES, 0, 0)]
    ppermute x12 -> x18, waiting for transfers between devices: 4.97 us -> 21.1 us  [the longest x9 16.7 us: gather_modes(): lax.ppermute(held[key], 'mode', [(i, i ^ bit) for i in range(count)])]
    ppermute x12 -> x18, starting transfers between devices: 35 us -> 21.2 us  [the longest x9 15 us: face_swaps(): lax.ppermute(face, axis, pairs)]
    pallas_call x0 -> x5, Pallas kernels: none -> 7.78 us  [the longest x3 6.51 us: per_device(): pl.pallas_call(step, out_shape=shapes, in_specs=[SMEM] + [VMEM] * (len(op...]
    reduce_sum x6 -> x0, other arithmetic: 6.35 us -> none  [the longest x2 2.23 us: per_device(): jnp.sum(krylov_basis[earlier] * mapped)]
    unnamed x18 -> x21, local copies, waits for them, and re-layouts: 2.57 us -> 7.68 us
  transfers between devices with their start and end apart: 12 -> 18, of which waited for: 5 -> 6; matrix products, arithmetic and copies ran while one was open for 3% -> 1% of each run, Pallas kernels for 0% -> 0%
where the time goes in v1:
time: 76.6 us; the launch traced here: 76 us
  starting transfers between devices  21.2 us (28%)
  waiting for transfers between devices  21.1 us (28%)
  blocking collectives  16.8 us (22%)
  local copies, waits for them, and re-layouts  8.39 us (11%)
  Pallas kernels  7.78 us (10%)
  between operations  0.78 us (1%)
    all_to_all x1, blocking collectives, per_device(): gram = lax.all_to_all(gram, AXES, 0, 0)  16.8 us
    ppermute x9, waiting for transfers between devices, gather_modes(): lax.ppermute(held[key], 'mode', [(i, i ^ bit) for i in range(count)])  16.7 us
    ppermute x9, starting transfers between devices, face_swaps(): lax.ppermute(face, axis, pairs)  15 us
    unnamed x21, local copies, waits for them, and re-layouts  7.68 us
    pallas_call x3, Pallas kernels, per_device(): pl.pallas_call(step, out_shape=shapes, in_specs=[SMEM] + [VMEM] * (len(op...  6.51 us
    ppermute x9, starting transfers between devices, gather_modes(): lax.ppermute(held[key], 'mode', [(i, i ^ bit) for i in range(count)])  6.22 us
    ppermute x9, waiting for transfers between devices, face_swaps(): lax.ppermute(face, axis, pairs)  4.45 us
  transfers between devices with their start and end apart: 18, of which 6 were waited for; matrix products, arithmetic and copies ran while one was open for 1% of the time, Pallas kernels for 0%

profile of v1, /device:TPU:0, one launch (start us, length us, event | category | flops | bytes accessed | tf_op | source)
XLA Modules:
  0.0 76.0 jit_solution(2287878496535077018)
XLA Ops:
  0.6 0.0 copy-start.8
  0.6 0.7 reshape.14.refs_1_.refs_7_.refs_8_.refs_9_
  1.4 1.0 %copy-done.2 = f32[8,8,1792]{2,1,0:T(8,128)S(1)} copy-done((f32[8,8,1792]{2,1,0:T(8,128)S(1)}, f32[8,8,1792]{2,1,0:T(8,128)}, u32[]{:S(2)}) %copy-start.2) | copy-done | bytes 458776
  2.4 0.7 copy-done.4
  3.1 0.7 copy-done.9
  3.8 0.2 prepare.1
  4.0 3.0 %collective-permute-start.1 = (bf16[912,128]{1,0:T(8,128)(2,1)S(1)}, bf16[912,128]{1,0:T(8,128)(2,1)S(1)}, u32[]{:S(2)}, u32[]{:S(2)}) collective-permute-start(bf16[912,128]{1,0:T(8,128)(2,1)S(1)} %get-tuple-element.20.refs_1_), channel_id=1, source_target_pairs={{0,16},{8,24},{16,0},{24,8},{1,17},{9,25},{17,1},{25,9},{2,18},{10... | collective-permute-start | bytes 700424 | tf_op jit(solution)/shard_map/ppermute | solution.py:45
  7.0 0.0 collective-permute-start
  7.0 5.7 %collective-permute-done.1.refs_3_ = bf16[912,128]{1,0:T(8,128)(2,1)S(1)} collective-permute-done((bf16[912,128]{1,0:T(8,128)(2,1)S(1)}, bf16[912,128]{1,0:T(8,128)(2,1)S(1)}, u32[]{:S(2)}, u32[]{:S(2)}) %collective-permute-start.1) | collective-permute-done | bytes 233504 | tf_op jit(solution)/shard_map/ppermute | solution.py:45
  12.7 0.0 collective-permute-start.2
  12.7 1.7 %collective-permute-start.3 = (f32[8,1792]{1,0:T(8,128)S(1)}, f32[8,1792]{1,0:T(8,128)S(1)}, u32[]{:S(2)}, u32[]{:S(2)}) collective-permute-start(f32[8,1792]{1,0:T(8,128)S(1)} %get-tuple-element.22), channel_id=1, source_target_pairs={{0,4},{4,0},{1,5},{5,1},{2,6},{6,2},{3,7},{7,3},{8,12},{12,8},{9,1... | collective-permute-start | bytes 172040 | tf_op jit(solution)/shard_map/ppermute | solution.py:34
  14.4 1.6 %collective-permute-start.4 = (f32[8,1792]{1,0:T(8,128)S(1)}, f32[8,1792]{1,0:T(8,128)S(1)}, u32[]{:S(2)}, u32[]{:S(2)}) collective-permute-start(f32[8,1792]{1,0:T(8,128)S(1)} %get-tuple-element.23), channel_id=1, source_target_pairs={{0,1},{1,0},{2,3},{3,2},{4,5},{5,4},{6,7},{7,6},{8,9},{9,8},{10,11... | collective-permute-start | bytes 172040 | tf_op jit(solution)/shard_map/ppermute | solution.py:34
  16.0 0.7 collective-permute-start.5
  16.7 0.8 %copy.11.refs_0_ = s32[14,8]{1,0:T(8,128)S(1)} copy(s32[14,8]{0,1:T(8,128)} %param.8) | data formatting | bytes 896 | tf_op args[1]
  17.4 0.0 collective-permute-done.3.refs_11_
  17.4 1.2 %collective-permute-done.4.refs_12_ = f32[8,1792]{1,0:T(8,128)S(1)} collective-permute-done((f32[8,1792]{1,0:T(8,128)S(1)}, f32[8,1792]{1,0:T(8,128)S(1)}, u32[]{:S(2)}, u32[]{:S(2)}) %collective-permute-start.4) | collective-permute-done | bytes 57376 | tf_op jit(solution)/shard_map/ppermute | solution.py:34
  18.6 0.0 collective-permute-done.5.refs_13_
  18.6 0.0 collective-permute-done.refs_2_
  18.6 0.0 collective-permute-done.2.refs_4_
  18.6 0.0 copy-start
  18.6 2.0 %copy-done = bf16[14,8,128,128]{3,2,1,0:T(8,128)(2,1)S(1)} copy-done((bf16[14,8,128,128]{3,2,1,0:T(8,128)(2,1)S(1)}, bf16[14,8,128,128]{3,2,1,0:T(8,128)(2,1)}, u32[]{:S(2)}) %copy-start) | copy-done | bytes 3670040
  20.7 1.0 %copy-done.3 = f32[8,8,1792]{2,1,0:T(8,128)S(1)} copy-done((f32[8,8,1792]{2,1,0:T(8,128)S(1)}, f32[8,8,1792]{2,1,0:T(8,128)}, u32[]{:S(2)}) %copy-start.3) | copy-done | bytes 458776
  21.7 0.7 copy-done.5
  22.4 0.7 copy-done.7
  23.1 2.1 %step_0.1 = (f32[8,1792]{1,0:T(8,128)S(1)}, f32[8,1792]{1,0:T(8,128)S(1)}, f32[8,1792]{1,0:T(8,128)S(1)}, bf16[912,128]{1,0:T(8,128)(2,1)S(1)}, f32[64,1792]{1,0:T(8,128)S(1)}, /*index=5*/f32[1,128]{1,0:T(1,128)S(1)}) custom-call(s32[14,8]{1,0:T(8,128)S(1)} %copy.11.refs_0_, bf16[912,128]{1,0:T(8,128)(2,1)S(1)} %get-tuple-element.20.refs_1_, ...), custom_call_target="tpu_custom_call" | custom-call | tf_op jit(solution)/shard_map/step_0/pallas_call | solution.py:379
  25.2 0.0 copy-start.6
  25.2 1.6 %collective-permute-start.7 = (bf16[912,128]{1,0:T(8,128)(2,1)S(1)}, bf16[912,128]{1,0:T(8,128)(2,1)S(1)}, u32[]{:S(2)}, u32[]{:S(2)}) collective-permute-start(bf16[912,128]{1,0:T(8,128)(2,1)S(1)} %get-tuple-element.25.refs_1_), channel_id=1, source_target_pairs={{0,16},{8,24},{16,0},{24,8},{1,17},{9,25},{17,1},{25,9},{2,18},{10... | collective-permute-start | bytes 700424 | tf_op jit(solution)/shard_map/ppermute | solution.py:45
  26.8 0.0 collective-permute-start.6
  26.8 5.2 %collective-permute-done.7.refs_3_ = bf16[912,128]{1,0:T(8,128)(2,1)S(1)} collective-permute-done((bf16[912,128]{1,0:T(8,128)(2,1)S(1)}, bf16[912,128]{1,0:T(8,128)(2,1)S(1)}, u32[]{:S(2)}, u32[]{:S(2)}) %collective-permute-start.7) | collective-permute-done | bytes 233504 | tf_op jit(solution)/shard_map/ppermute | solution.py:45
  32.0 0.0 collective-permute-start.8
  32.0 0.8 %collective-permute-start.9 = (f32[8,1792]{1,0:T(8,128)S(1)}, f32[8,1792]{1,0:T(8,128)S(1)}, u32[]{:S(2)}, u32[]{:S(2)}) collective-permute-start(f32[8,1792]{1,0:T(8,128)S(1)} %get-tuple-element.27), channel_id=1, source_target_pairs={{0,4},{4,0},{1,5},{5,1},{2,6},{6,2},{3,7},{7,3},{8,12},{12,8},{9,1... | collective-permute-start | bytes 172040 | tf_op jit(solution)/shard_map/ppermute | solution.py:34
  32.8 4.3 %collective-permute-start.10 = (f32[8,1792]{1,0:T(8,128)S(1)}, f32[8,1792]{1,0:T(8,128)S(1)}, u32[]{:S(2)}, u32[]{:S(2)}) collective-permute-start(f32[8,1792]{1,0:T(8,128)S(1)} %get-tuple-element.28), channel_id=1, source_target_pairs={{0,1},{1,0},{2,3},{3,2},{4,5},{5,4},{6,7},{7,6},{8,9},{9,8},{10,11... | collective-permute-start | bytes 172040 | tf_op jit(solution)/shard_map/ppermute | solution.py:34
  37.1 0.7 collective-permute-start.11
  37.7 0.0 collective-permute-done.9.refs_12_
  37.8 1.6 %collective-permute-done.10.refs_13_ = f32[8,1792]{1,0:T(8,128)S(1)} collective-permute-done((f32[8,1792]{1,0:T(8,128)S(1)}, f32[8,1792]{1,0:T(8,128)S(1)}, u32[]{:S(2)}, u32[]{:S(2)}) %collective-permute-start.10) | collective-permute-done | bytes 57376 | tf_op jit(solution)/shard_map/ppermute | solution.py:34
  39.4 2.1 %step_1.1 = (f32[8,1792]{1,0:T(8,128)S(1)}, f32[8,1792]{1,0:T(8,128)S(1)}, f32[8,1792]{1,0:T(8,128)S(1)}, bf16[912,128]{1,0:T(8,128)(2,1)S(1)}, f32[64,1792]{1,0:T(8,128)S(1)}) custom-call(s32[14,8]{1,0:T(8,128)S(1)} %copy.11.refs_0_, bf16[912,128]{1,0:T(8,128)(2,1)S(1)} %get-tuple-element.25.refs_1_, bf16[912,128]{1,0:T(8,128)(2,1)S(1)} %collective-permute-done.6.refs_2_, ...), custom_call_target="tpu_custom_call" | custom-call | tf_op jit(solution)/shard_map/step_1/pallas_call | solution.py:379
  41.5 1.6 %collective-permute-start.13 = (bf16[912,128]{1,0:T(8,128)(2,1)S(1)}, bf16[912,128]{1,0:T(8,128)(2,1)S(1)}, u32[]{:S(2)}, u32[]{:S(2)}) collective-permute-start(bf16[912,128]{1,0:T(8,128)(2,1)S(1)} %get-tuple-element.31.refs_1_), channel_id=1, source_target_pairs={{0,16},{8,24},{16,0},{24,8},{1,17},{9,25},{17,1},{25,9},{2,18},{10... | collective-permute-start | bytes 700424 | tf_op jit(solution)/shard_map/ppermute | solution.py:45
  43.1 5.8 %collective-permute-done.13.refs_3_ = bf16[912,128]{1,0:T(8,128)(2,1)S(1)} collective-permute-done((bf16[912,128]{1,0:T(8,128)(2,1)S(1)}, bf16[912,128]{1,0:T(8,128)(2,1)S(1)}, u32[]{:S(2)}, u32[]{:S(2)}) %collective-permute-start.13) | collective-permute-done | bytes 233504 | tf_op jit(solution)/shard_map/ppermute | solution.py:45
  48.9 1.5 %collective-permute-start.15 = (f32[8,1792]{1,0:T(8,128)S(1)}, f32[8,1792]{1,0:T(8,128)S(1)}, u32[]{:S(2)}, u32[]{:S(2)}) collective-permute-start(f32[8,1792]{1,0:T(8,128)S(1)} %get-tuple-element.33), channel_id=1, source_target_pairs={{0,4},{4,0},{1,5},{5,1},{2,6},{6,2},{3,7},{7,3},{8,12},{12,8},{9,1... | collective-permute-start | bytes 172040 | tf_op jit(solution)/shard_map/ppermute | solution.py:34
  50.4 3.1 %collective-permute-start.16 = (f32[8,1792]{1,0:T(8,128)S(1)}, f32[8,1792]{1,0:T(8,128)S(1)}, u32[]{:S(2)}, u32[]{:S(2)}) collective-permute-start(f32[8,1792]{1,0:T(8,128)S(1)} %get-tuple-element.34), channel_id=1, source_target_pairs={{0,1},{1,0},{2,3},{3,2},{4,5},{5,4},{6,7},{7,6},{8,9},{9,8},{10,11... | collective-permute-start | bytes 172040 | tf_op jit(solution)/shard_map/ppermute | solution.py:34
  53.5 0.7 collective-permute-start.17
  54.2 1.6 %collective-permute-done.16.refs_14_ = f32[8,1792]{1,0:T(8,128)S(1)} collective-permute-done((f32[8,1792]{1,0:T(8,128)S(1)}, f32[8,1792]{1,0:T(8,128)S(1)}, u32[]{:S(2)}, u32[]{:S(2)}) %collective-permute-start.16) | collective-permute-done | bytes 57376 | tf_op jit(solution)/shard_map/ppermute | solution.py:34
  55.8 0.0 collective-permute-done.17.refs_15_
  55.8 0.0 collective-permute-done.12.refs_2_
  55.8 0.0 collective-permute-done.14.refs_4_
  55.9 2.3 %step_2.1 = f32[32,16,128]{2,1,0:T(8,128)S(1)} custom-call(s32[14,8]{1,0:T(8,128)S(1)} %copy.11.refs_0_, bf16[912,128]{1,0:T(8,128)(2,1)S(1)} %get-tuple-element.31.refs_1_, bf16[912,128]{1,0:T(8,128)(2,1)S(1)} %collective-permute-done.12.refs_2_, bf16[912,128]{1,0:T(8,128)(2,1)S(1)} %collective-permute-done.13.refs_3_, ...), custom_call_target="tpu_custom_call" | custom-call | tf_op jit(solution)/shard_map/step_2/pallas_call | solution.py:379
  58.2 16.8 %all_to_all.5.gram_ref = f32[32,16,128]{2,1,0:T(8,128)S(1)} all-to-all(f32[32,16,128]{2,1,0:T(8,128)S(1)} %step_2.1), channel_id=1, replica_groups=mesh['mode'=4,'gx'=2,'gy'=4] {'mode','gx','gy'}, dimensions={0} | all-to-all | bytes 524288 | tf_op jit(solution)/shard_map/all_to_all | solution.py:395
  75.0 1.1 %finish.1 = (f32[64,1792]{1,0:T(8,128)}, f32[4,3]{1,0:T(4,128)}) custom-call(f32[32,16,128]{2,1,0:T(8,128)S(1)} %all_to_all.5.gram_ref, f32[1,128]{1,0:T(1,128)S(1)} %get-tuple-element.30.refs_15_.refs_16_.shift_ref, f32[64,1792]{1,0:T(8,128)S(1)} %bitcast.6, f32[64,1792]{1,0:T(8,128)S(1)} %get-tuple-element.26.refs_7_.refs_1_, ...), custom_call_target="tpu_custom_call" | custom-call | tf_op jit(solution)/shard_map/finish/pallas_call | solution.py:396
  (16 shorter events, 0.0 us)
Async XLA Ops:
  0.6 38.8 %copy-start.8 = (s32[2,1792]{1,0:T(2,128)S(1)}, s32[2,1792]{1,0:T(2,128)}, u32[]{:S(2)}) copy-start(s32[2,1792]{1,0:T(2,128)} %refs_11_.1) | copy-start | bytes 43012
  1.4 1.0 %copy-start.2 = (f32[8,8,1792]{2,1,0:T(8,128)S(1)}, f32[8,8,1792]{2,1,0:T(8,128)}, u32[]{:S(2)}) copy-start(f32[8,8,1792]{2,1,0:T(8,128)} %param.7) | copy-start | bytes 1376260
  2.4 0.7 copy-start.4
  3.1 0.7 copy-start.9
  4.0 8.7 %collective-permute-start.1 = (bf16[912,128]{1,0:T(8,128)(2,1)S(1)}, bf16[912,128]{1,0:T(8,128)(2,1)S(1)}, u32[]{:S(2)}, u32[]{:S(2)}) collective-permute-start(bf16[912,128]{1,0:T(8,128)(2,1)S(1)} %get-tuple-element.20.refs_1_), channel_id=1, source_target_pairs={{0,16},{8,24},{16,0},{24,8},{1,17},{9,25},{17,1},{25,9},{2,18},{10... | collective-permute-start | bytes 700424 | tf_op jit(solution)/shard_map/ppermute | solution.py:45
  7.0 11.6 %collective-permute-start = (bf16[912,128]{1,0:T(8,128)(2,1)S(1)}, bf16[912,128]{1,0:T(8,128)(2,1)S(1)}, u32[]{:S(2)}, u32[]{:S(2)}) collective-permute-start(bf16[912,128]{1,0:T(8,128)(2,1)S(1)} %get-tuple-element.20.refs_1_), channel_id=1, source_target_pairs={{0,8},{8,0},{16,24},{24,16},{1,9},{9,1},{17,25},{25,17},{2,10},{10... | collective-permute-start | bytes 700424 | tf_op jit(solution)/shard_map/ppermute | solution.py:45
  12.7 5.9 %collective-permute-start.2 = (bf16[912,128]{1,0:T(8,128)(2,1)S(1)}, bf16[912,128]{1,0:T(8,128)(2,1)S(1)}, u32[]{:S(2)}, u32[]{:S(2)}) collective-permute-start(bf16[912,128]{1,0:T(8,128)(2,1)S(1)} %collective-permute-done.1.refs_3_), channel_id=1, source_target_pairs={{0,8},{8,0},{16,24},{24,16},{1,9},{9,1},{17,25},{25,17},{2,10},{10... | collective-permute-start | bytes 700424 | tf_op jit(solution)/shard_map/ppermute | solution.py:45
  12.7 4.7 %collective-permute-start.3 = (f32[8,1792]{1,0:T(8,128)S(1)}, f32[8,1792]{1,0:T(8,128)S(1)}, u32[]{:S(2)}, u32[]{:S(2)}) collective-permute-start(f32[8,1792]{1,0:T(8,128)S(1)} %get-tuple-element.22), channel_id=1, source_target_pairs={{0,4},{4,0},{1,5},{5,1},{2,6},{6,2},{3,7},{7,3},{8,12},{12,8},{9,1... | collective-permute-start | bytes 172040 | tf_op jit(solution)/shard_map/ppermute | solution.py:34
  14.4 4.2 %collective-permute-start.4 = (f32[8,1792]{1,0:T(8,128)S(1)}, f32[8,1792]{1,0:T(8,128)S(1)}, u32[]{:S(2)}, u32[]{:S(2)}) collective-permute-start(f32[8,1792]{1,0:T(8,128)S(1)} %get-tuple-element.23), channel_id=1, source_target_pairs={{0,1},{1,0},{2,3},{3,2},{4,5},{5,4},{6,7},{7,6},{8,9},{9,8},{10,11... | collective-permute-start | bytes 172040 | tf_op jit(solution)/shard_map/ppermute | solution.py:34
  16.0 2.6 %collective-permute-start.5 = (f32[8,1792]{1,0:T(8,128)S(1)}, f32[8,1792]{1,0:T(8,128)S(1)}, u32[]{:S(2)}, u32[]{:S(2)}) collective-permute-start(f32[8,1792]{1,0:T(8,128)S(1)} %get-tuple-element.24), channel_id=1, source_target_pairs={{1,2},{2,1},{5,6},{6,5},{9,10},{10,9},{13,14},{14,13},{17,18},{18,... | collective-permute-start | bytes 172040 | tf_op jit(solution)/shard_map/ppermute | solution.py:34
  18.6 2.0 %copy-start = (bf16[14,8,128,128]{3,2,1,0:T(8,128)(2,1)S(1)}, bf16[14,8,128,128]{3,2,1,0:T(8,128)(2,1)}, u32[]{:S(2)}) copy-start(bf16[14,8,128,128]{3,2,1,0:T(8,128)(2,1)} %refs_5_.5) | copy-start | bytes 11010052
  20.7 1.0 %copy-start.3 = (f32[8,8,1792]{2,1,0:T(8,128)S(1)}, f32[8,8,1792]{2,1,0:T(8,128)}, u32[]{:S(2)}) copy-start(f32[8,8,1792]{2,1,0:T(8,128)} %param.7) | copy-start | bytes 1376260
  21.7 0.7 copy-start.5
  22.4 0.7 copy-start.7
  23.1 16.3 %copy-start.1 = (bf16[14,8,128,128]{3,2,1,0:T(8,128)(2,1)S(1)}, bf16[14,8,128,128]{3,2,1,0:T(8,128)(2,1)}, u32[]{:S(2)}) copy-start(bf16[14,8,128,128]{3,2,1,0:T(8,128)(2,1)} %refs_5_.5) | copy-start | bytes 11010052
  25.2 30.6 %copy-start.6 = (f32[2,1792]{1,0:T(2,128)S(1)}, f32[2,1792]{1,0:T(2,128)}, u32[]{:S(2)}) copy-start(f32[2,1792]{1,0:T(2,128)} %refs_10_.3) | copy-start | bytes 43012
  25.2 6.7 %collective-permute-start.7 = (bf16[912,128]{1,0:T(8,128)(2,1)S(1)}, bf16[912,128]{1,0:T(8,128)(2,1)S(1)}, u32[]{:S(2)}, u32[]{:S(2)}) collective-permute-start(bf16[912,128]{1,0:T(8,128)(2,1)S(1)} %get-tuple-element.25.refs_1_), channel_id=1, source_target_pairs={{0,16},{8,24},{16,0},{24,8},{1,17},{9,25},{17,1},{25,9},{2,18},{10... | collective-permute-start | bytes 700424 | tf_op jit(solution)/shard_map/ppermute | solution.py:45
  26.8 12.6 %collective-permute-start.6 = (bf16[912,128]{1,0:T(8,128)(2,1)S(1)}, bf16[912,128]{1,0:T(8,128)(2,1)S(1)}, u32[]{:S(2)}, u32[]{:S(2)}) collective-permute-start(bf16[912,128]{1,0:T(8,128)(2,1)S(1)} %get-tuple-element.25.refs_1_), channel_id=1, source_target_pairs={{0,8},{8,0},{16,24},{24,16},{1,9},{9,1},{17,25},{25,17},{2,10},{10... | collective-permute-start | bytes 700424 | tf_op jit(solution)/shard_map/ppermute | solution.py:45
  32.0 7.4 %collective-permute-start.8 = (bf16[912,128]{1,0:T(8,128)(2,1)S(1)}, bf16[912,128]{1,0:T(8,128)(2,1)S(1)}, u32[]{:S(2)}, u32[]{:S(2)}) collective-permute-start(bf16[912,128]{1,0:T(8,128)(2,1)S(1)} %collective-permute-done.7.refs_3_), channel_id=1, source_target_pairs={{0,8},{8,0},{16,24},{24,16},{1,9},{9,1},{17,25},{25,17},{2,10},{10... | collective-permute-start | bytes 700424 | tf_op jit(solution)/shard_map/ppermute | solution.py:45
  32.0 5.8 %collective-permute-start.9 = (f32[8,1792]{1,0:T(8,128)S(1)}, f32[8,1792]{1,0:T(8,128)S(1)}, u32[]{:S(2)}, u32[]{:S(2)}) collective-permute-start(f32[8,1792]{1,0:T(8,128)S(1)} %get-tuple-element.27), channel_id=1, source_target_pairs={{0,4},{4,0},{1,5},{5,1},{2,6},{6,2},{3,7},{7,3},{8,12},{12,8},{9,1... | collective-permute-start | bytes 172040 | tf_op jit(solution)/shard_map/ppermute | solution.py:34
  32.8 6.6 %collective-permute-start.10 = (f32[8,1792]{1,0:T(8,128)S(1)}, f32[8,1792]{1,0:T(8,128)S(1)}, u32[]{:S(2)}, u32[]{:S(2)}) collective-permute-start(f32[8,1792]{1,0:T(8,128)S(1)} %get-tuple-element.28), channel_id=1, source_target_pairs={{0,1},{1,0},{2,3},{3,2},{4,5},{5,4},{6,7},{7,6},{8,9},{9,8},{10,11... | collective-permute-start | bytes 172040 | tf_op jit(solution)/shard_map/ppermute | solution.py:34
  37.1 2.3 %collective-permute-start.11 = (f32[8,1792]{1,0:T(8,128)S(1)}, f32[8,1792]{1,0:T(8,128)S(1)}, u32[]{:S(2)}, u32[]{:S(2)}) collective-permute-start(f32[8,1792]{1,0:T(8,128)S(1)} %get-tuple-element.29), channel_id=1, source_target_pairs={{1,2},{2,1},{5,6},{6,5},{9,10},{10,9},{13,14},{14,13},{17,18},{18,... | collective-permute-start | bytes 172040 | tf_op jit(solution)/shard_map/ppermute | solution.py:34
  41.5 7.4 %collective-permute-start.13 = (bf16[912,128]{1,0:T(8,128)(2,1)S(1)}, bf16[912,128]{1,0:T(8,128)(2,1)S(1)}, u32[]{:S(2)}, u32[]{:S(2)}) collective-permute-start(bf16[912,128]{1,0:T(8,128)(2,1)S(1)} %get-tuple-element.31.refs_1_), channel_id=1, source_target_pairs={{0,16},{8,24},{16,0},{24,8},{1,17},{9,25},{17,1},{25,9},{2,18},{10... | collective-permute-start | bytes 700424 | tf_op jit(solution)/shard_map/ppermute | solution.py:45
  43.1 12.7 %collective-permute-start.12 = (bf16[912,128]{1,0:T(8,128)(2,1)S(1)}, bf16[912,128]{1,0:T(8,128)(2,1)S(1)}, u32[]{:S(2)}, u32[]{:S(2)}) collective-permute-start(bf16[912,128]{1,0:T(8,128)(2,1)S(1)} %get-tuple-element.31.refs_1_), channel_id=1, source_target_pairs={{0,8},{8,0},{16,24},{24,16},{1,9},{9,1},{17,25},{25,17},{2,10},{10... | collective-permute-start | bytes 700424 | tf_op jit(solution)/shard_map/ppermute | solution.py:45
  48.9 6.9 %collective-permute-start.14 = (bf16[912,128]{1,0:T(8,128)(2,1)S(1)}, bf16[912,128]{1,0:T(8,128)(2,1)S(1)}, u32[]{:S(2)}, u32[]{:S(2)}) collective-permute-start(bf16[912,128]{1,0:T(8,128)(2,1)S(1)} %collective-permute-done.13.refs_3_), channel_id=1, source_target_pairs={{0,8},{8,0},{16,24},{24,16},{1,9},{9,1},{17,25},{25,17},{2,10},{10... | collective-permute-start | bytes 700424 | tf_op jit(solution)/shard_map/ppermute | solution.py:45
  48.9 5.3 %collective-permute-start.15 = (f32[8,1792]{1,0:T(8,128)S(1)}, f32[8,1792]{1,0:T(8,128)S(1)}, u32[]{:S(2)}, u32[]{:S(2)}) collective-permute-start(f32[8,1792]{1,0:T(8,128)S(1)} %get-tuple-element.33), channel_id=1, source_target_pairs={{0,4},{4,0},{1,5},{5,1},{2,6},{6,2},{3,7},{7,3},{8,12},{12,8},{9,1... | collective-permute-start | bytes 172040 | tf_op jit(solution)/shard_map/ppermute | solution.py:34
  50.4 5.4 %collective-permute-start.16 = (f32[8,1792]{1,0:T(8,128)S(1)}, f32[8,1792]{1,0:T(8,128)S(1)}, u32[]{:S(2)}, u32[]{:S(2)}) collective-permute-start(f32[8,1792]{1,0:T(8,128)S(1)} %get-tuple-element.34), channel_id=1, source_target_pairs={{0,1},{1,0},{2,3},{3,2},{4,5},{5,4},{6,7},{7,6},{8,9},{9,8},{10,11... | collective-permute-start | bytes 172040 | tf_op jit(solution)/shard_map/ppermute | solution.py:34
  53.5 2.3 %collective-permute-start.17 = (f32[8,1792]{1,0:T(8,128)S(1)}, f32[8,1792]{1,0:T(8,128)S(1)}, u32[]{:S(2)}, u32[]{:S(2)}) collective-permute-start(f32[8,1792]{1,0:T(8,128)S(1)} %get-tuple-element.35), channel_id=1, source_target_pairs={{1,2},{2,1},{5,6},{6,5},{9,10},{10,9},{13,14},{14,13},{17,18},{18,... | collective-permute-start | bytes 172040 | tf_op jit(solution)/shard_map/ppermute | solution.py:34

commit v2 on v1

v2 whole, which is shorter than its diff:
```python
import functools

import jax
import jax.numpy as jnp
from jax import lax
from jax.experimental import pallas as pl
from jax.experimental.pallas import tpu as pltpu
from jax.sharding import PartitionSpec as P

KRYLOV = 3
TAIL = 16
AXES = ("mode", "gx", "gy")

epsilon = 1e-12


def pair_list(count, first):
    pairs = []
    for low in range(first, count - 1, 2):
        pairs += [(low, low + 1), (low + 1, low)]
    return pairs


def swaps_of(count):
    return [pairs for pairs in (pair_list(count, 0), pair_list(count, 1)) if pairs]


def face_swaps(faces):
    received = []
    for axis in ("gx", "gy"):
        swaps = swaps_of(lax.axis_size(axis))
        received.append(
            [lax.ppermute(face, axis, pairs) for face, pairs in zip(faces[axis], swaps)]
        )
    return received


def exchange(array, bit):
    count = lax.axis_size("mode")
    return lax.ppermute(array, "mode", [(i, i ^ bit) for i in range(count)])


def gather_far(packed):
    held = {0: packed}
    bit = lax.axis_size("mode") // 2
    while bit > 1:
        for key in list(held):
            held[key ^ bit] = exchange(held[key], bit)
        bit //= 2
    del held[0]
    return held


def hand_on(arrays, after):
    count = len(arrays)
    if not count:
        return []
    return pl.pallas_call(
        lambda *refs: None,
        out_shape=[jax.ShapeDtypeStruct(array.shape, array.dtype) for array in arrays],
        in_specs=[ANY] * (count + 1),
        out_specs=[ANY] * count,
        input_output_aliases={at: at for at in range(count)},
        name="hand_on",
    )(*arrays, after)


def write_faces(masked, lanes, first, second, x_refs, y_refs):
    if x_refs:
        even = lax.rem(lax.axis_index("gx"), 2) == 0
        low, high = masked[0], masked[first - 1]
        for ref, take_high in zip(x_refs, (even, jnp.logical_not(even))):
            ref[:, lanes] = jnp.where(take_high, high, low)
    if y_refs:
        even = lax.rem(lax.axis_index("gy"), 2) == 0
        low, high = masked[:, 0, :], masked[:, second - 1, :]
        for ref, take_high in zip(y_refs, (even, jnp.logical_not(even))):
            ref[:, lanes] = jnp.where(take_high, high, low)


def halos(refs, axis, lanes, shape):
    zero = jnp.zeros(shape, jnp.float32)
    values = [ref[:, lanes] for ref in refs] + [zero, zero]
    odd = lax.rem(lax.axis_index(axis), 2) == 1
    return jnp.where(odd, values[0], values[1]), jnp.where(odd, values[1], values[0])


def start_copies(pairs, sems):
    copies = [
        pltpu.make_async_copy(source, target, sems.at[at])
        for at, (source, target) in enumerate(pairs)
    ]
    for copy in copies:
        copy.start()
    return copies


def prepare_kernel(sizes, ins, x_refs, y_refs, packed_ref, open_ref, rhs_ref, scratch):
    first, second, local_blocks, block = sizes
    relax_ref, speed_ref, wall_ref, sems = scratch
    copies = start_copies(list(zip(ins, (rhs_ref, relax_ref, speed_ref, wall_ref))), sems)
    cells = first * second
    for copy in reversed(copies):
        copy.wait()
    wall = wall_ref[...].astype(jnp.float32)
    eye = (
        lax.broadcasted_iota(jnp.int32, (second, second), 0)
        == lax.broadcasted_iota(jnp.int32, (second, second), 1)
    ).astype(jnp.float32)
    for row in range(first):
        column = jnp.sum(eye * (1.0 - wall[row : row + 1, :]), axis=1, keepdims=True)
        open_ref[row * second : (row + 1) * second, :] = jnp.broadcast_to(column, (second, block))
    total = jnp.zeros((1, block), jnp.float32)
    for b in range(local_blocks):
        lanes = slice(b * block, (b + 1) * block)
        value = rhs_ref[:, lanes]
        packed_ref[b * cells : (b + 1) * cells, :] = value.astype(jnp.bfloat16)
        masked = (value * open_ref[...]).reshape(first, second, block)
        write_faces(masked, lanes, first, second, x_refs, y_refs)
        total += relax_ref[lanes].reshape(1, block) + speed_ref[0:1, lanes] + speed_ref[1:2, lanes]
    mean = jnp.sum(total, axis=1, keepdims=True) * (1.0 / (local_blocks * block))
    packed_ref[local_blocks * cells :, :] = jnp.broadcast_to(mean, (TAIL, block)).astype(
        jnp.bfloat16
    )


def load_kernel(count, *refs):
    for copy in start_copies(list(zip(refs[:count], refs[count : 2 * count])), refs[-1]):
        copy.wait()


def scatter(sizes, per_owner, b, places, cols_ref, sources, blocks_ref):
    first, second, local_blocks, block = sizes
    cells = first * second
    mine = lax.axis_index("mode")
    picks, weights = [], []
    for place, source in zip(places, sources):
        owner = mine ^ place
        for p in range(per_owner):
            slot = owner * per_owner + p
            column = cols_ref[slot, b] - owner * local_blocks
            picks.append(source[pl.ds(pl.multiple_of(column * cells, cells), cells), :])
            weights.append(blocks_ref[b, slot])
    return lax.dot_general(
        jnp.concatenate(picks, axis=1),
        jnp.concatenate(weights, axis=1),
        (((1,), (1,)), ((), ())),
        preferred_element_type=jnp.float32,
    )


def near_kernel(sizes, per_owner, places, cols_ref, sources, blocks_ref, current_ref, params, x_in, y_in, out_ref):
    first, second, local_blocks, block = sizes
    relax_ref, speed_ref, sign_ref, open_ref = params
    cells = first * second
    open_cells = open_ref[...]
    row_at = lax.broadcasted_iota(jnp.int32, (first, second, block), 1)
    for b in range(local_blocks):
        lanes = slice(b * block, (b + 1) * block)
        scattered = scatter(sizes, per_owner, b, places, cols_ref, sources, blocks_ref)
        current = current_ref[:, lanes]
        masked = (current * open_cells).reshape(first, second, block)
        west_in, east_in = halos(x_in, "gx", lanes, (second, block))
        south_in, north_in = halos(y_in, "gy", lanes, (first, block))
        from_west = jnp.concatenate([west_in[None], masked[:-1]], axis=0)
        from_east = jnp.concatenate([masked[1:], east_in[None]], axis=0)
        from_south = jnp.where(
            row_at == 0, south_in[:, None, :], pltpu.roll(masked, 1, axis=1)
        )
        from_north = jnp.where(
            row_at == second - 1, north_in[:, None, :], pltpu.roll(masked, second - 1, axis=1)
        )
        sign_x = sign_ref[0:1, lanes].reshape(1, 1, block)
        sign_y = sign_ref[1:2, lanes].reshape(1, 1, block)
        speed_x, speed_y = speed_ref[0:1, lanes], speed_ref[1:2, lanes]
        upstream_x = jnp.where(sign_x == 1, from_west, from_east).reshape(cells, block)
        upstream_y = jnp.where(sign_y == 1, from_south, from_north).reshape(cells, block)
        diagonal = relax_ref[lanes].reshape(1, block) + speed_x + speed_y
        out_ref[:, lanes] = (
            diagonal * current - speed_x * upstream_x - speed_y * upstream_y - scattered
        )


def add_kernel(sizes, per_owner, places, cols_ref, sources, blocks_ref, partial_ref, out_ref):
    first, second, local_blocks, block = sizes
    for b in range(local_blocks):
        lanes = slice(b * block, (b + 1) * block)
        out_ref[:, lanes] = partial_ref[:, lanes] - scatter(
            sizes, per_owner, b, places, cols_ref, sources, blocks_ref
        )


def shift_of(tails):
    mine = lax.axis_index("mode")
    total = jnp.zeros_like(tails[0])
    for owner in range(len(tails)):
        term = tails[0]
        for place in range(1, len(tails)):
            term = jnp.where((mine ^ place) == owner, tails[place], term)
        total = total + term
    return total * (1.0 / len(tails))


def last_kernel(sizes, per_owner, places, cols_ref, sources, blocks_ref, partial_ref, shift, earlier, open_ref, outs):
    first, second, local_blocks, block = sizes
    cells = first * second
    sums = {}
    for b in range(local_blocks):
        lanes = slice(b * block, (b + 1) * block)
        scattered = scatter(sizes, per_owner, b, places, cols_ref, sources, blocks_ref)
        result = partial_ref[:, lanes] - shift * earlier[-1][:, lanes] - scattered
        if outs.gram is None:
            outs.value[:, lanes] = result
            outs.packed[b * cells : (b + 1) * cells, :] = result.astype(jnp.bfloat16)
            write_faces(
                (result * open_ref[...]).reshape(first, second, block),
                lanes, first, second, outs.x, outs.y,
            )
        else:
            vectors = [ref[:, lanes] for ref in earlier] + [result]
            at = 0
            for i in range(len(vectors)):
                for j in range(i, len(vectors)):
                    term = jnp.sum((vectors[i] * vectors[j]).reshape(cells // 8, 8, block), axis=0)
                    sums[at] = term if b == 0 else sums[at] + term
                    at += 1
    if outs.gram is not None:
        devices = outs.gram.shape[0]
        lane = lax.broadcasted_iota(jnp.int32, (1, block), 1)
        row = jnp.zeros((1, block), jnp.float32)
        for at, value in sums.items():
            total = jnp.sum(jnp.sum(value, axis=0, keepdims=True), axis=1, keepdims=True)
            row = jnp.where(lane == at, total, row)
        outs.gram[...] = jnp.broadcast_to(row[None], (devices, 1, block))


class Outs:
    value = packed = gram = None
    x = y = ()


def least_squares(hessenberg, initial):
    upper = [list(row) for row in hessenberg]
    target = [initial] + [jnp.zeros_like(initial) for row_index in range(KRYLOV)]
    cosines = []
    sines = []
    for col_index in range(KRYLOV):
        for row_index in range(col_index):
            first = upper[row_index][col_index]
            second = upper[row_index + 1][col_index]
            upper[row_index][col_index] = cosines[row_index] * first + sines[row_index] * second
            upper[row_index + 1][col_index] = cosines[row_index] * second - sines[row_index] * first
        first = upper[col_index][col_index]
        second = upper[col_index + 1][col_index]
        radius = jnp.sqrt(first * first + second * second)
        cosine = first / radius
        sine_value = second / radius
        upper[col_index][col_index] = radius
        target[col_index + 1] = -sine_value * target[col_index]
        target[col_index] = cosine * target[col_index]
        cosines.append(cosine)
        sines.append(sine_value)
    combo = [None] * KRYLOV
    for row_index in reversed(range(KRYLOV)):
        running = target[row_index]
        for col_index in range(row_index + 1, KRYLOV):
            running = running - upper[row_index][col_index] * combo[col_index]
        combo[row_index] = running / upper[row_index][row_index]
    return combo


def arnoldi(gram, shift):
    size = KRYLOV + 1

    def inner(left, right):
        total = None
        for i in range(size):
            for j in range(size):
                if left[i] is None or right[j] is None:
                    continue
                term = left[i] * right[j] * gram[min(i, j)][max(i, j)]
                total = term if total is None else total + term
        return total

    initial = jnp.sqrt(gram[0][0] + epsilon)
    basis = [[1.0 / initial] + [None] * KRYLOV]
    zero = jnp.zeros_like(initial)
    hessenberg = [[zero] * KRYLOV for row_index in range(size)]
    for section in range(KRYLOV):
        vector = basis[section]
        image = [None] * size
        for k in range(section + 2):
            parts = []
            if k > 0 and vector[k - 1] is not None:
                parts.append(vector[k - 1])
            if vector[k] is not None:
                parts.append(shift * vector[k])
            image[k] = sum(parts[1:], parts[0])
        rest = list(image)
        for earlier in range(section + 1):
            coefficient = inner(basis[earlier], image)
            hessenberg[earlier][section] = coefficient
            for k in range(earlier + 1):
                rest[k] = rest[k] - coefficient * basis[earlier][k]
        length = jnp.sqrt(jnp.maximum(inner(rest, rest), 0.0) + epsilon)
        hessenberg[section + 1][section] = length
        basis.append([None if part is None else part / length for part in rest])
    combo = least_squares(hessenberg, initial)
    weights = []
    for k in range(KRYLOV):
        total = zero
        for j in range(k, KRYLOV):
            total = total + combo[j] * basis[j][k]
        weights.append(total)
    return hessenberg, weights


def finish_kernel(gram_ref, shift_ref, *refs):
    vectors, (solution_ref, hessenberg_ref) = refs[:KRYLOV], refs[KRYLOV:]
    block = shift_ref.shape[1]
    total = jnp.sum(gram_ref[...], axis=0)
    lane = lax.broadcasted_iota(jnp.int32, (1, block), 1)
    gram = [[None] * (KRYLOV + 1) for i in range(KRYLOV + 1)]
    at = 0
    for i in range(KRYLOV + 1):
        for j in range(i, KRYLOV + 1):
            entry = jnp.sum(jnp.where(lane == at, total, 0.0), axis=1, keepdims=True)
            gram[i][j] = jnp.broadcast_to(entry, (1, block))
            at += 1
    hessenberg, weights = arnoldi(gram, shift_ref[...])
    rows = lax.broadcasted_iota(jnp.int32, (KRYLOV + 1, KRYLOV), 0)
    cols = lax.broadcasted_iota(jnp.int32, (KRYLOV + 1, KRYLOV), 1)
    table = jnp.zeros((KRYLOV + 1, KRYLOV), jnp.float32)
    for i in range(KRYLOV + 1):
        for j in range(KRYLOV):
            table = jnp.where((rows == i) & (cols == j), hessenberg[i][j][:, :KRYLOV], table)
    hessenberg_ref[...] = table
    for b in range(solution_ref.shape[1] // block):
        lanes = slice(b * block, (b + 1) * block)
        solution_ref[:, lanes] = sum(
            weight * ref[:, lanes] for weight, ref in zip(weights, vectors)
        )


VMEM = pl.BlockSpec(memory_space=pltpu.VMEM)
SMEM = pl.BlockSpec(memory_space=pltpu.SMEM)
HBM = pl.BlockSpec(memory_space=pltpu.HBM)
ANY = pl.BlockSpec(memory_space=pl.ANY)


def call(name, kernel, groups, shapes, scratch=(), flops=0):
    flat = [pair for group in groups for pair in group]

    def body(*refs):
        refs = list(refs)
        lists = []
        for group in groups:
            lists.append(refs[: len(group)])
            del refs[: len(group)]
        kernel(*lists, refs[: len(shapes)], refs[len(shapes) :])

    size = sum(operand.size * operand.dtype.itemsize for spec, operand in flat)
    size += sum(shape.size * shape.dtype.itemsize for shape in shapes)
    return pl.pallas_call(
        body,
        out_shape=list(shapes),
        in_specs=[spec for spec, operand in flat],
        out_specs=[VMEM] * len(shapes),
        scratch_shapes=list(scratch),
        compiler_params=pltpu.CompilerParams(vmem_limit_bytes=32 * 1024 * 1024),
        cost_estimate=pl.CostEstimate(flops=flops, bytes_accessed=size, transcendentals=0),
        name=name,
    )(*[operand for spec, operand in flat])


def in_vmem(operands):
    return [(VMEM, operand) for operand in operands]


def in_hbm(operands):
    return [(HBM, operand) for operand in operands]


def per_device(right_side, col_block, blocks, relax_rate, drift_speed, upwind_sign, wall_mask):
    first, second, local_modes = right_side.shape
    local_blocks, slots, block = blocks.shape[:3]
    cells = first * second
    count = lax.axis_size("mode")
    devices = count * lax.axis_size("gx") * lax.axis_size("gy")
    per_owner = slots // count
    sizes = (first, second, local_blocks, block)
    x_swaps, y_swaps = len(swaps_of(lax.axis_size("gx"))), len(swaps_of(lax.axis_size("gy")))
    n_faces = x_swaps + y_swaps
    f32 = jnp.float32
    shape_of = jax.ShapeDtypeStruct
    face_shapes = [shape_of((second, local_modes), f32)] * x_swaps + [
        shape_of((first, local_modes), f32)
    ] * y_swaps
    packed_shape = shape_of((local_blocks * cells + TAIL, block), jnp.bfloat16)
    vector_shape = shape_of((cells, local_modes), f32)
    shift_shape = shape_of((1, block), f32)
    near = [place for place in (0, 1) if place < count]
    far = [place for place in range(count) if place not in near]
    middle = [place for place in far if place % 2 == 0]
    final = [place for place in far if place % 2 == 1]

    def prepare(ins, outs, scratch):
        faces, rest = outs[:n_faces], outs[n_faces:]
        prepare_kernel(sizes, ins, faces[:x_swaps], faces[x_swaps:], *rest, scratch)

    *faces, packed, open_cells, start = call(
        "prepare",
        prepare,
        [in_hbm([right_side.reshape(cells, local_modes), relax_rate, drift_speed, wall_mask])],
        face_shapes + [packed_shape, shape_of((cells, block), f32), vector_shape],
        [
            pltpu.VMEM(relax_rate.shape, f32),
            pltpu.VMEM(drift_speed.shape, f32),
            pltpu.VMEM(wall_mask.shape, jnp.int32),
            pltpu.SemaphoreType.DMA((4,)),
        ],
    )
    kept = [blocks, relax_rate, drift_speed, upwind_sign, col_block.T]

    def load(ins, after, outs, scratch):
        load_kernel(len(ins), *ins, *outs, *scratch)

    blocks, relax_rate, drift_speed, upwind_sign, columns = call(
        "load",
        load,
        [in_hbm(kept), [(ANY, open_cells)]],
        [shape_of(array.shape, array.dtype) for array in kept],
        [pltpu.SemaphoreType.DMA((len(kept),))],
    )

    work = 2 * cells * local_modes * per_owner * block
    vectors = [start]
    for section in range(KRYLOV):
        sources = {0: packed}
        if count > 1:
            sources[1] = exchange(packed, 1)
        held = gather_far(packed)
        x_in, y_in = face_swaps({"gx": faces[:x_swaps], "gy": faces[x_swaps:]})

        def near_step(cols, sources, rest, x_in, y_in, outs, scratch):
            blocks_ref, current_ref, *params = rest
            near_kernel(
                sizes, per_owner, near, cols[0], sources, blocks_ref, current_ref, params,
                x_in, y_in, outs[0],
            )

        (partial,) = call(
            "near_%d" % section,
            near_step,
            [
                [(SMEM, columns)],
                in_vmem([sources[place] for place in near]),
                in_vmem([blocks, vectors[-1], relax_rate, drift_speed, upwind_sign, open_cells]),
                in_vmem(x_in),
                in_vmem(y_in),
            ],
            [vector_shape],
            flops=work * len(near),
        )

        held = dict(zip(held, hand_on(list(held.values()), partial)))
        for place, array in held.items():
            sources[place] = array
            sources[place ^ 1] = exchange(array, 1)

        def middle_step(cols, sources, rest, outs, scratch):
            add_kernel(sizes, per_owner, middle, cols[0], sources, *rest, outs[0])

        if middle:
            (partial,) = call(
                "middle_%d" % section,
                middle_step,
                [
                    [(SMEM, columns)],
                    in_vmem([sources[place] for place in middle]),
                    in_vmem([blocks, partial]),
                ],
                [vector_shape],
                flops=work * len(middle),
            )

        last = section == KRYLOV - 1
        def last_step(cols, sources, rest, earlier, known, outs, scratch, section=section, last=last):
            blocks_ref, partial_ref, open_ref = rest
            if section == 0:
                tail_at = local_blocks * cells
                value = shift_of([ref[tail_at:, :].astype(f32)[0:1] for ref in known])
                outs[-1][...] = value
                outs = outs[:-1]
            else:
                value = known[0][...]
            named = Outs()
            if last:
                named.gram = outs[0]
            else:
                named.x, named.y = outs[:x_swaps], outs[x_swaps:n_faces]
                named.packed, named.value = outs[n_faces:]
            last_kernel(
                sizes, per_owner, final, cols[0], sources, blocks_ref, partial_ref,
                value, earlier, open_ref, named,
            )

        if last:
            shapes = [shape_of((devices, 1, block), f32)]
        else:
            shapes = face_shapes + [packed_shape, vector_shape]
        if section == 0:
            shapes = shapes + [shift_shape]
        results = call(
            "last_%d" % section,
            last_step,
            [
                [(SMEM, columns)],
                in_vmem([sources[place] for place in final]),
                in_vmem([blocks, partial, open_cells]),
                in_vmem(vectors),
                in_vmem([shift] if section else [sources[place] for place in range(count)]),
            ],
            shapes,
            flops=work * len(final),
        )
        if section == 0:
            *results, shift = results
        if last:
            (gram,) = results
        else:
            *faces, packed, value = results
            vectors.append(value)

    gram = lax.all_to_all(gram, AXES, 0, 0)

    def finish(ins, outs, scratch):
        finish_kernel(*ins, *outs)

    solution, hessenberg = call(
        "finish",
        finish,
        [in_vmem([gram, shift, *vectors])],
        [vector_shape, shape_of((KRYLOV + 1, KRYLOV), f32)],
    )
    return solution.reshape(first, second, local_modes), hessenberg


def solution(mesh):
    return jax.shard_map(
        per_device,
        mesh=mesh,
        in_specs=(
            P("gx", "gy", "mode"),
            P("mode", None),
            P("mode", None, None, None),
            P("mode"),
            P(None, "mode"),
            P(None, "mode"),
            P("gx", "gy"),
        ),
        out_specs=(P("gx", "gy", "mode"), P()),
        check_vma=False,
    )
```

time: 76.6 us -> 79.5 us (1.038)
  local copies, waits for them, and re-layouts: 8.39 us -> 29 us
  waiting for transfers between devices: 21.1 us -> 3.01 us
  blocking collectives: 16.8 us -> 11.3 us
  Pallas kernels: 7.78 us -> 12.6 us
    unnamed x21 -> x56, local copies, waits for them, and re-layouts: 7.68 us -> 29 us
    ppermute x9, waiting for transfers between devices: 16.7 us -> 0.02 us  [exchange(): return lax.ppermute(array, 'mode', [(i, i ^ bit) for i in range(count)])]
    all_to_all x1, blocking collectives: 16.8 us -> 11.3 us  [per_device(): gram = lax.all_to_all(gram, AXES, 0, 0)]
    pallas_call x5 -> x15, Pallas kernels: 7.78 us -> 12.6 us  [the longest x12 12.6 us: call(): pl.pallas_call(body, out_shape=list(shapes), in_specs=[spec for spec, ope...]
    ppermute x9, waiting for transfers between devices: 4.45 us -> 2.99 us  [face_swaps(): lax.ppermute(face, axis, pairs)]
  transfers between devices with their start and end apart: 18 -> 18, of which waited for: 6 -> 2; matrix products, arithmetic and copies ran while one was open for 1% -> 0% of each run, Pallas kernels for 0% -> 10%
where the time goes in v2:
time: 79.5 us; the launch traced here: 78.5 us
  local copies, waits for them, and re-layouts  29 us (36%)
  starting transfers between devices  21.6 us (27%)
  Pallas kernels  12.6 us (16%)
  blocking collectives  11.3 us (14%)
  waiting for transfers between devices  3.01 us (4%)
  between operations  0.86 us (1%)
    unnamed x56, local copies, waits for them, and re-layouts  29 us
    ppermute x9, starting transfers between devices, face_swaps(): lax.ppermute(face, axis, pairs)  15.3 us
    pallas_call x12, Pallas kernels, call(): pl.pallas_call(body, out_shape=list(shapes), in_specs=[spec for spec, ope...  12.6 us
    all_to_all x1, blocking collectives, per_device(): gram = lax.all_to_all(gram, AXES, 0, 0)  11.3 us
    ppermute x9, starting transfers between devices, exchange(): return lax.ppermute(array, 'mode', [(i, i ^ bit) for i in range(count)])  6.29 us
    ppermute x9, waiting for transfers between devices, face_swaps(): lax.ppermute(face, axis, pairs)  2.99 us
  transfers between devices with their start and end apart: 18, of which 2 were waited for; matrix products, arithmetic and copies ran while one was open for 0% of the time, Pallas kernels for 10%

profile of v2, /device:TPU:0, one launch (start us, length us, event | category | flops | bytes accessed | tf_op | source)
XLA Modules:
  0.0 78.5 jit_solution(14396708313323810951)
XLA Ops:
  0.6 1.0 %copy-done.20 = f32[8,8,1792]{2,1,0:T(8,128)S(1)} copy-done((f32[8,8,1792]{2,1,0:T(8,128)S(1)}, f32[8,8,1792]{2,1,0:T(8,128)}, u32[]{:S(2)}) %copy-start.20) | copy-done | bytes 458776
  1.7 0.7 copy-done.21
  2.4 0.7 copy-done.23
  3.1 0.7 copy-done.26
  4.8 2.6 %collective-permute-start = (bf16[912,128]{1,0:T(8,128)(2,1)S(1)}, bf16[912,128]{1,0:T(8,128)(2,1)S(1)}, u32[]{:S(2)}, u32[]{:S(2)}) collective-permute-start(bf16[912,128]{1,0:T(8,128)(2,1)S(1)} %get-tuple-element.28.refs_1_.refs_6_), channel_id=1, source_target_pairs={{0,16},{8,24},{16,0},{24,8},{1,17},{9,25},{17,1},{25,9},{2,18},{10... | collective-permute-start | bytes 700424 | tf_op jit(solution)/shard_map/ppermute | solution.py:40
  7.4 1.5 %collective-permute-start.2 = (f32[8,1792]{1,0:T(8,128)S(1)}, f32[8,1792]{1,0:T(8,128)S(1)}, u32[]{:S(2)}, u32[]{:S(2)}) collective-permute-start(f32[8,1792]{1,0:T(8,128)S(1)} %get-tuple-element.34), channel_id=1, source_target_pairs={{0,4},{4,0},{1,5},{5,1},{2,6},{6,2},{3,7},{7,3},{8,12},{12,8},{9,1... | collective-permute-start | bytes 172040 | tf_op jit(solution)/shard_map/ppermute | solution.py:33
  8.9 1.6 %collective-permute-start.3 = (f32[8,1792]{1,0:T(8,128)S(1)}, f32[8,1792]{1,0:T(8,128)S(1)}, u32[]{:S(2)}, u32[]{:S(2)}) collective-permute-start(f32[8,1792]{1,0:T(8,128)S(1)} %get-tuple-element.35), channel_id=1, source_target_pairs={{0,1},{1,0},{2,3},{3,2},{4,5},{5,4},{6,7},{7,6},{8,9},{9,8},{10,11... | collective-permute-start | bytes 172040 | tf_op jit(solution)/shard_map/ppermute | solution.py:33
  11.2 2.0 %copy-done.13 = bf16[14,8,128,128]{3,2,1,0:T(8,128)(2,1)S(1)} copy-done((bf16[14,8,128,128]{3,2,1,0:T(8,128)(2,1)S(1)}, bf16[14,8,128,128]{3,2,1,0:T(8,128)(2,1)}, u32[]{:S(2)}) %copy-start.13) | copy-done | bytes 3670040
  13.2 0.7 copy-done.22
  13.9 0.7 copy-done.24
  14.6 0.7 copy-done.25
  15.3 0.7 copy-done.27
  16.4 1.4 %near_0.1.refs_1_.refs_3_ = f32[64,1792]{1,0:T(8,128)S(1)} custom-call(s32[8,14]{1,0:T(8,128)S(1)} %get-tuple-element.27.refs_0_, bf16[912,128]{1,0:T(8,128)(2,1)S(1)} %get-tuple-element.28.refs_1_.refs_6_, bf16[912,128]{1,0:T(8,128)(2,1)S(1)} %collective-permute-done.1.refs_2_.refs_7_, bf16[14,8,128,128]{3,2,1,0:T(8,128)(2,1)S(1)} %get-tuple-element.29.refs_3_.refs_2_, ...), custom_call_target="tpu_custom_call" | custom-call | flops 117440512 | bytes 5295552 | tf_op jit(solution)/shard_map/near_0/pallas_call | solution.py:364
  17.8 1.8 %copy-done = bf16[14,8,128,128]{3,2,1,0:T(8,128)(2,1)} copy-done((bf16[14,8,128,128]{3,2,1,0:T(8,128)(2,1)}, bf16[14,8,128,128]{3,2,1,0:T(8,128)(2,1)S(1)}, u32[]{:S(2)}) %copy-start) | copy-done | bytes 3670040
  19.6 0.8 copy-done.11
  20.3 0.7 copy-done.14
  21.0 2.0 %copy-done.1 = bf16[14,8,128,128]{3,2,1,0:T(8,128)(2,1)S(1)} copy-done((bf16[14,8,128,128]{3,2,1,0:T(8,128)(2,1)S(1)}, bf16[14,8,128,128]{3,2,1,0:T(8,128)(2,1)}, u32[]{:S(2)}) %copy-start.1) | copy-done | bytes 3670040
  23.1 1.0 %copy-done.12 = f32[64,1792]{1,0:T(8,128)S(1)} copy-done((f32[64,1792]{1,0:T(8,128)S(1)}, f32[64,1792]{1,0:T(8,128)}, u32[]{:S(2)}) %copy-start.12) | copy-done | bytes 458776
  24.1 0.9 %copy-done.15 = bf16[912,128]{1,0:T(8,128)(2,1)S(1)} copy-done((bf16[912,128]{1,0:T(8,128)(2,1)S(1)}, bf16[912,128]{1,0:T(8,128)(2,1)}, u32[]{:S(2)}) %copy-start.15) | copy-done | bytes 233496
  25.0 1.1 %middle_0.1.refs_3_ = f32[64,1792]{1,0:T(8,128)S(1)} custom-call(s32[8,14]{1,0:T(8,128)S(1)} %get-tuple-element.27.refs_0_, bf16[912,128]{1,0:T(8,128)(2,1)S(1)} %copy-done.15, bf16[14,8,128,128]{3,2,1,0:T(8,128)(2,1)S(1)} %copy-done.1, f32[64,1792]{1,0:T(8,128)S(1)} %copy-done.12), custom_call_target="tpu_custom_call" | custom-call | flops 58720256 | bytes 4821440 | tf_op jit(solution)/shard_map/middle_0/pallas_call | solution.py:364
  26.1 1.0 %copy-done.2 = bf16[14,8,128,128]{3,2,1,0:T(8,128)(2,1)S(1)} copy-done((bf16[14,8,128,128]{3,2,1,0:T(8,128)(2,1)S(1)}, bf16[14,8,128,128]{3,2,1,0:T(8,128)(2,1)}, u32[]{:S(2)}) %copy-start.2) | copy-done | bytes 3670040
  27.1 1.1 %last_0.1 = (f32[8,1792]{1,0:T(8,128)S(1)}, f32[8,1792]{1,0:T(8,128)S(1)}, f32[8,1792]{1,0:T(8,128)S(1)}, bf16[912,128]{1,0:T(8,128)(2,1)S(1)}, f32[64,1792]{1,0:T(8,128)S(1)}, /*index=5*/f32[1,128]{1,0:T(1,128)S(1)}) custom-call(s32[8,14]{1,0:T(8,128)S(1)} %get-tuple-element.27.refs_0_, bf16[912,128]{1,0:T(8,128)(2,1)S(1)} %collective-permute-done.5.refs_1_.refs_9_, ...), custom_call_target="tpu_custom_call" | custom-call | flops 58720256 | bytes 6652864 | tf_op jit(solution)/shard_map/last_0/pallas_call | solution.py:364
  29.8 4.4 %collective-permute-start.9 = (f32[8,1792]{1,0:T(8,128)S(1)}, f32[8,1792]{1,0:T(8,128)S(1)}, u32[]{:S(2)}, u32[]{:S(2)}) collective-permute-start(f32[8,1792]{1,0:T(8,128)S(1)} %get-tuple-element.40), channel_id=1, source_target_pairs={{0,1},{1,0},{2,3},{3,2},{4,5},{5,4},{6,7},{7,6},{8,9},{9,8},{10,11... | collective-permute-start | bytes 172040 | tf_op jit(solution)/shard_map/ppermute | solution.py:33
  34.8 1.5 %collective-permute-done.9.refs_10_ = f32[8,1792]{1,0:T(8,128)S(1)} collective-permute-done((f32[8,1792]{1,0:T(8,128)S(1)}, f32[8,1792]{1,0:T(8,128)S(1)}, u32[]{:S(2)}, u32[]{:S(2)}) %collective-permute-start.9) | collective-permute-done | bytes 57376 | tf_op jit(solution)/shard_map/ppermute | solution.py:33
  36.3 1.4 %near_1.1.refs_1_.refs_3_ = f32[64,1792]{1,0:T(8,128)S(1)} custom-call(s32[8,14]{1,0:T(8,128)S(1)} %get-tuple-element.27.refs_0_, bf16[912,128]{1,0:T(8,128)(2,1)S(1)} %get-tuple-element.37.refs_1_, bf16[912,128]{1,0:T(8,128)(2,1)S(1)} %collective-permute-done.7.refs_2_, bf16[14,8,128,128]{3,2,1,0:T(8,128)(2,1)S(1)} %copy-done.2, ...), custom_call_target="tpu_custom_call" | custom-call | flops 117440512 | bytes 5295552 | tf_op jit(solution)/shard_map/near_1/pallas_call | solution.py:364
  37.7 0.8 copy-done.9
  38.5 0.7 copy-done.18
  39.2 2.0 %copy-done.3 = bf16[14,8,128,128]{3,2,1,0:T(8,128)(2,1)S(1)} copy-done((bf16[14,8,128,128]{3,2,1,0:T(8,128)(2,1)S(1)}, bf16[14,8,128,128]{3,2,1,0:T(8,128)(2,1)}, u32[]{:S(2)}) %copy-start.3) | copy-done | bytes 3670040
  41.2 1.0 %copy-done.10 = f32[64,1792]{1,0:T(8,128)S(1)} copy-done((f32[64,1792]{1,0:T(8,128)S(1)}, f32[64,1792]{1,0:T(8,128)}, u32[]{:S(2)}) %copy-start.10) | copy-done | bytes 458776
  42.2 0.9 %copy-done.19 = bf16[912,128]{1,0:T(8,128)(2,1)S(1)} copy-done((bf16[912,128]{1,0:T(8,128)(2,1)S(1)}, bf16[912,128]{1,0:T(8,128)(2,1)}, u32[]{:S(2)}) %copy-start.19) | copy-done | bytes 233496
  43.2 1.0 %middle_1.1.refs_3_ = f32[64,1792]{1,0:T(8,128)S(1)} custom-call(s32[8,14]{1,0:T(8,128)S(1)} %get-tuple-element.27.refs_0_, bf16[912,128]{1,0:T(8,128)(2,1)S(1)} %copy-done.19, bf16[14,8,128,128]{3,2,1,0:T(8,128)(2,1)S(1)} %copy-done.3, f32[64,1792]{1,0:T(8,128)S(1)} %copy-done.10), custom_call_target="tpu_custom_call" | custom-call | flops 58720256 | bytes 4821440 | tf_op jit(solution)/shard_map/middle_1/pallas_call | solution.py:364
  44.2 1.0 %copy-done.4 = bf16[14,8,128,128]{3,2,1,0:T(8,128)(2,1)S(1)} copy-done((bf16[14,8,128,128]{3,2,1,0:T(8,128)(2,1)S(1)}, bf16[14,8,128,128]{3,2,1,0:T(8,128)(2,1)}, u32[]{:S(2)}) %copy-start.4) | copy-done | bytes 3670040
  45.2 1.1 %last_1.1 = (f32[8,1792]{1,0:T(8,128)S(1)}, f32[8,1792]{1,0:T(8,128)S(1)}, f32[8,1792]{1,0:T(8,128)S(1)}, bf16[912,128]{1,0:T(8,128)(2,1)S(1)}, f32[64,1792]{1,0:T(8,128)S(1)}) custom-call(s32[8,14]{1,0:T(8,128)S(1)} %get-tuple-element.27.refs_0_, bf16[912,128]{1,0:T(8,128)(2,1)S(1)} %collective-permute-done.11.refs_1_, ...), custom_call_target="tpu_custom_call" | custom-call | flops 58720256 | bytes 6177728 | tf_op jit(solution)/shard_map/last_1/pallas_call | solution.py:364
  46.9 1.5 %collective-permute-start.12 = (bf16[912,128]{1,0:T(8,128)(2,1)S(1)}, bf16[912,128]{1,0:T(8,128)(2,1)S(1)}, u32[]{:S(2)}, u32[]{:S(2)}) collective-permute-start(bf16[912,128]{1,0:T(8,128)(2,1)S(1)} %get-tuple-element.43.refs_1_), channel_id=1, source_target_pairs={{0,16},{8,24},{16,0},{24,8},{1,17},{9,25},{17,1},{25,9},{2,18},{10... | collective-permute-start | bytes 700424 | tf_op jit(solution)/shard_map/ppermute | solution.py:40
  48.4 1.5 %collective-permute-start.14 = (f32[8,1792]{1,0:T(8,128)S(1)}, f32[8,1792]{1,0:T(8,128)S(1)}, u32[]{:S(2)}, u32[]{:S(2)}) collective-permute-start(f32[8,1792]{1,0:T(8,128)S(1)} %get-tuple-element.45), channel_id=1, source_target_pairs={{0,4},{4,0},{1,5},{5,1},{2,6},{6,2},{3,7},{7,3},{8,12},{12,8},{9,1... | collective-permute-start | bytes 172040 | tf_op jit(solution)/shard_map/ppermute | solution.py:33
  49.9 3.9 %collective-permute-start.15 = (f32[8,1792]{1,0:T(8,128)S(1)}, f32[8,1792]{1,0:T(8,128)S(1)}, u32[]{:S(2)}, u32[]{:S(2)}) collective-permute-start(f32[8,1792]{1,0:T(8,128)S(1)} %get-tuple-element.46), channel_id=1, source_target_pairs={{0,1},{1,0},{2,3},{3,2},{4,5},{5,4},{6,7},{7,6},{8,9},{9,8},{10,11... | collective-permute-start | bytes 172040 | tf_op jit(solution)/shard_map/ppermute | solution.py:33
  54.4 1.5 %collective-permute-done.15.refs_10_ = f32[8,1792]{1,0:T(8,128)S(1)} collective-permute-done((f32[8,1792]{1,0:T(8,128)S(1)}, f32[8,1792]{1,0:T(8,128)S(1)}, u32[]{:S(2)}, u32[]{:S(2)}) %collective-permute-start.15) | collective-permute-done | bytes 57376 | tf_op jit(solution)/shard_map/ppermute | solution.py:33
  55.9 1.4 %near_2.1.refs_1_.refs_3_ = f32[64,1792]{1,0:T(8,128)S(1)} custom-call(s32[8,14]{1,0:T(8,128)S(1)} %get-tuple-element.27.refs_0_, bf16[912,128]{1,0:T(8,128)(2,1)S(1)} %get-tuple-element.43.refs_1_, bf16[912,128]{1,0:T(8,128)(2,1)S(1)} %collective-permute-done.13.refs_2_, bf16[14,8,128,128]{3,2,1,0:T(8,128)(2,1)S(1)} %copy-done.4, ...), custom_call_target="tpu_custom_call" | custom-call | flops 117440512 | bytes 5295552 | tf_op jit(solution)/shard_map/near_2/pallas_call | solution.py:364
  57.3 0.8 copy-done.7
  58.1 0.7 copy-done.16
  58.8 2.0 %copy-done.5 = bf16[14,8,128,128]{3,2,1,0:T(8,128)(2,1)S(1)} copy-done((bf16[14,8,128,128]{3,2,1,0:T(8,128)(2,1)S(1)}, bf16[14,8,128,128]{3,2,1,0:T(8,128)(2,1)}, u32[]{:S(2)}) %copy-start.5) | copy-done | bytes 3670040
  60.8 1.0 %copy-done.8 = f32[64,1792]{1,0:T(8,128)S(1)} copy-done((f32[64,1792]{1,0:T(8,128)S(1)}, f32[64,1792]{1,0:T(8,128)}, u32[]{:S(2)}) %copy-start.8) | copy-done | bytes 458776
  61.9 0.9 %copy-done.17 = bf16[912,128]{1,0:T(8,128)(2,1)S(1)} copy-done((bf16[912,128]{1,0:T(8,128)(2,1)S(1)}, bf16[912,128]{1,0:T(8,128)(2,1)}, u32[]{:S(2)}) %copy-start.17) | copy-done | bytes 233496
  62.8 1.0 %middle_2.1.refs_3_ = f32[64,1792]{1,0:T(8,128)S(1)} custom-call(s32[8,14]{1,0:T(8,128)S(1)} %get-tuple-element.27.refs_0_, bf16[912,128]{1,0:T(8,128)(2,1)S(1)} %copy-done.17, bf16[14,8,128,128]{3,2,1,0:T(8,128)(2,1)S(1)} %copy-done.5, f32[64,1792]{1,0:T(8,128)S(1)} %copy-done.8), custom_call_target="tpu_custom_call" | custom-call | flops 58720256 | bytes 4821440 | tf_op jit(solution)/shard_map/middle_2/pallas_call | solution.py:364
  63.8 1.0 %copy-done.6 = bf16[14,8,128,128]{3,2,1,0:T(8,128)(2,1)S(1)} copy-done((bf16[14,8,128,128]{3,2,1,0:T(8,128)(2,1)S(1)}, bf16[14,8,128,128]{3,2,1,0:T(8,128)(2,1)}, u32[]{:S(2)}) %copy-start.6) | copy-done | bytes 3670040
  64.8 1.3 %last_2.1 = f32[32,1,128]{2,1,0:T(1,128)S(1)} custom-call(s32[8,14]{1,0:T(8,128)S(1)} %get-tuple-element.27.refs_0_, bf16[912,128]{1,0:T(8,128)(2,1)S(1)} %collective-permute-done.17.refs_1_, bf16[14,8,128,128]{3,2,1,0:T(8,128)(2,1)S(1)} %copy-done.6, f32[64,1792]{1,0:T(8,128)S(1)} %middle_2.1.refs_3_, ...), custom_call_target="tpu_custom_call" | custom-call | flops 58720256 | bytes 5788608 | tf_op jit(solution)/shard_map/last_2/pallas_call | solution.py:364
  66.1 11.3 %all_to_all.5.refs_0_ = f32[32,1,128]{2,1,0:T(1,128)S(1)} all-to-all(f32[32,1,128]{2,1,0:T(1,128)S(1)} %last_2.1), channel_id=1, replica_groups=mesh['mode'=4,'gx'=2,'gy'=4] {'mode','gx','gy'}, dimensions={0} | all-to-all | bytes 32768 | tf_op jit(solution)/shard_map/all_to_all | solution.py:535
  77.4 1.1 %finish.1 = (f32[64,1792]{1,0:T(8,128)}, f32[4,3]{1,0:T(4,128)}) custom-call(f32[32,1,128]{2,1,0:T(1,128)S(1)} %all_to_all.5.refs_0_, f32[1,128]{1,0:T(1,128)S(1)} %get-tuple-element.42.refs_7_.refs_8_.refs_1_, f32[64,1792]{1,0:T(8,128)S(1)} %get-tuple-element.30.refs_4_.refs_5_.refs_2_, f32[64,1792]{1,0:T(8,128)S(1)} %get-tuple-element.38.refs_4_.refs_6_.refs_3_, ...), custom_call_target="tpu_custom_call" | custom-call | bytes 1851952 | tf_op jit(solution)/shard_map/finish/pallas_call | solution.py:364
  (60 shorter events, 5.6 us)
Async XLA Ops:
  0.6 1.0 %copy-start.20 = (f32[8,8,1792]{2,1,0:T(8,128)S(1)}, f32[8,8,1792]{2,1,0:T(8,128)}, u32[]{:S(2)}) copy-start(f32[8,8,1792]{2,1,0:T(8,128)} %param.7) | copy-start | bytes 1376260
  1.6 0.7 copy-start.21
  2.4 0.7 copy-start.23
  3.1 0.7 copy-start.26
  4.3 12.1 %collective-permute-start.1 = (bf16[912,128]{1,0:T(8,128)(2,1)S(1)}, bf16[912,128]{1,0:T(8,128)(2,1)S(1)}, u32[]{:S(2)}, u32[]{:S(2)}) collective-permute-start(bf16[912,128]{1,0:T(8,128)(2,1)S(1)} %get-tuple-element.28.refs_1_.refs_6_), channel_id=1, source_target_pairs={{0,8},{8,0},{16,24},{24,16},{1,9},{9,1},{17,25},{25,17},{2,10},{10... | collective-permute-start | bytes 700424 | tf_op jit(solution)/shard_map/ppermute | solution.py:40
  4.8 15.5 %collective-permute-start = (bf16[912,128]{1,0:T(8,128)(2,1)S(1)}, bf16[912,128]{1,0:T(8,128)(2,1)S(1)}, u32[]{:S(2)}, u32[]{:S(2)}) collective-permute-start(bf16[912,128]{1,0:T(8,128)(2,1)S(1)} %get-tuple-element.28.refs_1_.refs_6_), channel_id=1, source_target_pairs={{0,16},{8,24},{16,0},{24,8},{1,17},{9,25},{17,1},{25,9},{2,18},{10... | collective-permute-start | bytes 700424 | tf_op jit(solution)/shard_map/ppermute | solution.py:40
  7.4 8.9 %collective-permute-start.2 = (f32[8,1792]{1,0:T(8,128)S(1)}, f32[8,1792]{1,0:T(8,128)S(1)}, u32[]{:S(2)}, u32[]{:S(2)}) collective-permute-start(f32[8,1792]{1,0:T(8,128)S(1)} %get-tuple-element.34), channel_id=1, source_target_pairs={{0,4},{4,0},{1,5},{5,1},{2,6},{6,2},{3,7},{7,3},{8,12},{12,8},{9,1... | collective-permute-start | bytes 172040 | tf_op jit(solution)/shard_map/ppermute | solution.py:33
  8.9 7.4 %collective-permute-start.3 = (f32[8,1792]{1,0:T(8,128)S(1)}, f32[8,1792]{1,0:T(8,128)S(1)}, u32[]{:S(2)}, u32[]{:S(2)}) collective-permute-start(f32[8,1792]{1,0:T(8,128)S(1)} %get-tuple-element.35), channel_id=1, source_target_pairs={{0,1},{1,0},{2,3},{3,2},{4,5},{5,4},{6,7},{7,6},{8,9},{9,8},{10,11... | collective-permute-start | bytes 172040 | tf_op jit(solution)/shard_map/ppermute | solution.py:33
  10.5 5.9 %collective-permute-start.4 = (f32[8,1792]{1,0:T(8,128)S(1)}, f32[8,1792]{1,0:T(8,128)S(1)}, u32[]{:S(2)}, u32[]{:S(2)}) collective-permute-start(f32[8,1792]{1,0:T(8,128)S(1)} %get-tuple-element.36), channel_id=1, source_target_pairs={{1,2},{2,1},{5,6},{6,5},{9,10},{10,9},{13,14},{14,13},{17,18},{18,... | collective-permute-start | bytes 172040 | tf_op jit(solution)/shard_map/ppermute | solution.py:33
  11.1 2.0 %copy-start.13 = (bf16[14,8,128,128]{3,2,1,0:T(8,128)(2,1)S(1)}, bf16[14,8,128,128]{3,2,1,0:T(8,128)(2,1)}, u32[]{:S(2)}) copy-start(bf16[14,8,128,128]{3,2,1,0:T(8,128)(2,1)} %refs_0_.1) | copy-start | bytes 11010052
  13.2 0.7 copy-start.22
  13.9 0.7 copy-start.24
  14.6 0.7 copy-start.25
  15.3 0.7 copy-start.27
  17.8 1.8 %copy-start = (bf16[14,8,128,128]{3,2,1,0:T(8,128)(2,1)}, bf16[14,8,128,128]{3,2,1,0:T(8,128)(2,1)S(1)}, u32[]{:S(2)}) copy-start(bf16[14,8,128,128]{3,2,1,0:T(8,128)(2,1)S(1)} %get-tuple-element.29.refs_3_.refs_2_) | copy-start | bytes 11010052
  19.6 0.8 copy-start.11
  20.3 0.7 copy-start.14
  21.0 5.1 %collective-permute-start.5 = (bf16[912,128]{1,0:T(8,128)(2,1)}, bf16[912,128]{1,0:T(8,128)(2,1)S(1)}, u32[]{:S(2)}, u32[]{:S(2)}) collective-permute-start(bf16[912,128]{1,0:T(8,128)(2,1)} %hand_on.3.refs_1_.refs_8_), channel_id=1, source_target_pairs={{0,8},{8,0},{16,24},{24,16},{1,9},{9,1},{17,25},{25,17},{2,10},{10... | collective-permute-start | bytes 700424 | tf_op jit(solution)/shard_map/ppermute | solution.py:40
  21.0 2.0 %copy-start.1 = (bf16[14,8,128,128]{3,2,1,0:T(8,128)(2,1)S(1)}, bf16[14,8,128,128]{3,2,1,0:T(8,128)(2,1)}, u32[]{:S(2)}) copy-start(bf16[14,8,128,128]{3,2,1,0:T(8,128)(2,1)} %copy-done) | copy-start | bytes 11010052
  23.1 1.0 %copy-start.12 = (f32[64,1792]{1,0:T(8,128)S(1)}, f32[64,1792]{1,0:T(8,128)}, u32[]{:S(2)}) copy-start(f32[64,1792]{1,0:T(8,128)} %copy-done.11) | copy-start | bytes 1376260
  24.1 0.9 %copy-start.15 = (bf16[912,128]{1,0:T(8,128)(2,1)S(1)}, bf16[912,128]{1,0:T(8,128)(2,1)}, u32[]{:S(2)}) copy-start(bf16[912,128]{1,0:T(8,128)(2,1)} %hand_on.3.refs_1_.refs_8_) | copy-start | bytes 700420
  25.0 2.0 %copy-start.2 = (bf16[14,8,128,128]{3,2,1,0:T(8,128)(2,1)S(1)}, bf16[14,8,128,128]{3,2,1,0:T(8,128)(2,1)}, u32[]{:S(2)}) copy-start(bf16[14,8,128,128]{3,2,1,0:T(8,128)(2,1)} %copy-done) | copy-start | bytes 11010052
  28.2 8.2 %collective-permute-start.7 = (bf16[912,128]{1,0:T(8,128)(2,1)S(1)}, bf16[912,128]{1,0:T(8,128)(2,1)S(1)}, u32[]{:S(2)}, u32[]{:S(2)}) collective-permute-start(bf16[912,128]{1,0:T(8,128)(2,1)S(1)} %get-tuple-element.37.refs_1_), channel_id=1, source_target_pairs={{0,8},{8,0},{16,24},{24,16},{1,9},{9,1},{17,25},{25,17},{2,10},{10... | collective-permute-start | bytes 700424 | tf_op jit(solution)/shard_map/ppermute | solution.py:40
  28.7 9.8 %collective-permute-start.6 = (bf16[912,128]{1,0:T(8,128)(2,1)S(1)}, bf16[912,128]{1,0:T(8,128)(2,1)S(1)}, u32[]{:S(2)}, u32[]{:S(2)}) collective-permute-start(bf16[912,128]{1,0:T(8,128)(2,1)S(1)} %get-tuple-element.37.refs_1_), channel_id=1, source_target_pairs={{0,16},{8,24},{16,0},{24,8},{1,17},{9,25},{17,1},{25,9},{2,18},{10... | collective-permute-start | bytes 700424 | tf_op jit(solution)/shard_map/ppermute | solution.py:40
  29.2 5.6 %collective-permute-start.8 = (f32[8,1792]{1,0:T(8,128)S(1)}, f32[8,1792]{1,0:T(8,128)S(1)}, u32[]{:S(2)}, u32[]{:S(2)}) collective-permute-start(f32[8,1792]{1,0:T(8,128)S(1)} %get-tuple-element.39), channel_id=1, source_target_pairs={{0,4},{4,0},{1,5},{5,1},{2,6},{6,2},{3,7},{7,3},{8,12},{12,8},{9,1... | collective-permute-start | bytes 172040 | tf_op jit(solution)/shard_map/ppermute | solution.py:33
  29.8 6.6 %collective-permute-start.9 = (f32[8,1792]{1,0:T(8,128)S(1)}, f32[8,1792]{1,0:T(8,128)S(1)}, u32[]{:S(2)}, u32[]{:S(2)}) collective-permute-start(f32[8,1792]{1,0:T(8,128)S(1)} %get-tuple-element.40), channel_id=1, source_target_pairs={{0,1},{1,0},{2,3},{3,2},{4,5},{5,4},{6,7},{7,6},{8,9},{9,8},{10,11... | collective-permute-start | bytes 172040 | tf_op jit(solution)/shard_map/ppermute | solution.py:33
  34.2 2.2 %collective-permute-start.10 = (f32[8,1792]{1,0:T(8,128)S(1)}, f32[8,1792]{1,0:T(8,128)S(1)}, u32[]{:S(2)}, u32[]{:S(2)}) collective-permute-start(f32[8,1792]{1,0:T(8,128)S(1)} %get-tuple-element.41), channel_id=1, source_target_pairs={{1,2},{2,1},{5,6},{6,5},{9,10},{10,9},{13,14},{14,13},{17,18},{18,... | collective-permute-start | bytes 172040 | tf_op jit(solution)/shard_map/ppermute | solution.py:33
  37.7 0.8 copy-start.9
  38.5 0.7 copy-start.18
  39.2 5.1 %collective-permute-start.11 = (bf16[912,128]{1,0:T(8,128)(2,1)}, bf16[912,128]{1,0:T(8,128)(2,1)S(1)}, u32[]{:S(2)}, u32[]{:S(2)}) collective-permute-start(bf16[912,128]{1,0:T(8,128)(2,1)} %hand_on.4.refs_1_), channel_id=1, source_target_pairs={{0,8},{8,0},{16,24},{24,16},{1,9},{9,1},{17,25},{25,17},{2,10},{10... | collective-permute-start | bytes 700424 | tf_op jit(solution)/shard_map/ppermute | solution.py:40
  39.2 2.0 %copy-start.3 = (bf16[14,8,128,128]{3,2,1,0:T(8,128)(2,1)S(1)}, bf16[14,8,128,128]{3,2,1,0:T(8,128)(2,1)}, u32[]{:S(2)}) copy-start(bf16[14,8,128,128]{3,2,1,0:T(8,128)(2,1)} %copy-done) | copy-start | bytes 11010052
  41.2 1.0 %copy-start.10 = (f32[64,1792]{1,0:T(8,128)S(1)}, f32[64,1792]{1,0:T(8,128)}, u32[]{:S(2)}) copy-start(f32[64,1792]{1,0:T(8,128)} %copy-done.9) | copy-start | bytes 1376260
  42.2 0.9 %copy-start.19 = (bf16[912,128]{1,0:T(8,128)(2,1)S(1)}, bf16[912,128]{1,0:T(8,128)(2,1)}, u32[]{:S(2)}) copy-start(bf16[912,128]{1,0:T(8,128)(2,1)} %hand_on.4.refs_1_) | copy-start | bytes 700420
  43.2 2.0 %copy-start.4 = (bf16[14,8,128,128]{3,2,1,0:T(8,128)(2,1)S(1)}, bf16[14,8,128,128]{3,2,1,0:T(8,128)(2,1)}, u32[]{:S(2)}) copy-start(bf16[14,8,128,128]{3,2,1,0:T(8,128)(2,1)} %copy-done) | copy-start | bytes 11010052
  46.3 9.6 %collective-permute-start.13 = (bf16[912,128]{1,0:T(8,128)(2,1)S(1)}, bf16[912,128]{1,0:T(8,128)(2,1)S(1)}, u32[]{:S(2)}, u32[]{:S(2)}) collective-permute-start(bf16[912,128]{1,0:T(8,128)(2,1)S(1)} %get-tuple-element.43.refs_1_), channel_id=1, source_target_pairs={{0,8},{8,0},{16,24},{24,16},{1,9},{9,1},{17,25},{25,17},{2,10},{10... | collective-permute-start | bytes 700424 | tf_op jit(solution)/shard_map/ppermute | solution.py:40
  46.9 11.2 %collective-permute-start.12 = (bf16[912,128]{1,0:T(8,128)(2,1)S(1)}, bf16[912,128]{1,0:T(8,128)(2,1)S(1)}, u32[]{:S(2)}, u32[]{:S(2)}) collective-permute-start(bf16[912,128]{1,0:T(8,128)(2,1)S(1)} %get-tuple-element.43.refs_1_), channel_id=1, source_target_pairs={{0,16},{8,24},{16,0},{24,8},{1,17},{9,25},{17,1},{25,9},{2,18},{10... | collective-permute-start | bytes 700424 | tf_op jit(solution)/shard_map/ppermute | solution.py:40
  48.4 6.1 %collective-permute-start.14 = (f32[8,1792]{1,0:T(8,128)S(1)}, f32[8,1792]{1,0:T(8,128)S(1)}, u32[]{:S(2)}, u32[]{:S(2)}) collective-permute-start(f32[8,1792]{1,0:T(8,128)S(1)} %get-tuple-element.45), channel_id=1, source_target_pairs={{0,4},{4,0},{1,5},{5,1},{2,6},{6,2},{3,7},{7,3},{8,12},{12,8},{9,1... | collective-permute-start | bytes 172040 | tf_op jit(solution)/shard_map/ppermute | solution.py:33
  49.9 6.1 %collective-permute-start.15 = (f32[8,1792]{1,0:T(8,128)S(1)}, f32[8,1792]{1,0:T(8,128)S(1)}, u32[]{:S(2)}, u32[]{:S(2)}) collective-permute-start(f32[8,1792]{1,0:T(8,128)S(1)} %get-tuple-element.46), channel_id=1, source_target_pairs={{0,1},{1,0},{2,3},{3,2},{4,5},{5,4},{6,7},{7,6},{8,9},{9,8},{10,11... | collective-permute-start | bytes 172040 | tf_op jit(solution)/shard_map/ppermute | solution.py:33
  53.8 2.2 %collective-permute-start.16 = (f32[8,1792]{1,0:T(8,128)S(1)}, f32[8,1792]{1,0:T(8,128)S(1)}, u32[]{:S(2)}, u32[]{:S(2)}) collective-permute-start(f32[8,1792]{1,0:T(8,128)S(1)} %get-tuple-element.47), channel_id=1, source_target_pairs={{1,2},{2,1},{5,6},{6,5},{9,10},{10,9},{13,14},{14,13},{17,18},{18,... | collective-permute-start | bytes 172040 | tf_op jit(solution)/shard_map/ppermute | solution.py:33
  57.3 0.8 copy-start.7
  58.1 0.7 copy-start.16
  58.8 5.1 %collective-permute-start.17 = (bf16[912,128]{1,0:T(8,128)(2,1)}, bf16[912,128]{1,0:T(8,128)(2,1)S(1)}, u32[]{:S(2)}, u32[]{:S(2)}) collective-permute-start(bf16[912,128]{1,0:T(8,128)(2,1)} %hand_on.5.refs_1_), channel_id=1, source_target_pairs={{0,8},{8,0},{16,24},{24,16},{1,9},{9,1},{17,25},{25,17},{2,10},{10... | collective-permute-start | bytes 700424 | tf_op jit(solution)/shard_map/ppermute | solution.py:40
  58.8 2.0 %copy-start.5 = (bf16[14,8,128,128]{3,2,1,0:T(8,128)(2,1)S(1)}, bf16[14,8,128,128]{3,2,1,0:T(8,128)(2,1)}, u32[]{:S(2)}) copy-start(bf16[14,8,128,128]{3,2,1,0:T(8,128)(2,1)} %copy-done) | copy-start | bytes 11010052
  60.8 1.0 %copy-start.8 = (f32[64,1792]{1,0:T(8,128)S(1)}, f32[64,1792]{1,0:T(8,128)}, u32[]{:S(2)}) copy-start(f32[64,1792]{1,0:T(8,128)} %copy-done.7) | copy-start | bytes 1376260
  61.8 0.9 %copy-start.17 = (bf16[912,128]{1,0:T(8,128)(2,1)S(1)}, bf16[912,128]{1,0:T(8,128)(2,1)}, u32[]{:S(2)}) copy-start(bf16[912,128]{1,0:T(8,128)(2,1)} %hand_on.5.refs_1_) | copy-start | bytes 700420
  62.8 2.0 %copy-start.6 = (bf16[14,8,128,128]{3,2,1,0:T(8,128)(2,1)S(1)}, bf16[14,8,128,128]{3,2,1,0:T(8,128)(2,1)}, u32[]{:S(2)}) copy-start(bf16[14,8,128,128]{3,2,1,0:T(8,128)(2,1)} %copy-done) | copy-start | bytes 11010052

commit v3 on v2

--- a/solution.py
+++ b/solution.py
@@ -8,7 +8,7 @@
 from jax.sharding import PartitionSpec as P
 
 KRYLOV = 3
-TAIL = 16
+SHIFT = 4.05
 AXES = ("mode", "gx", "gy")
 
 epsilon = 1e-12
@@ -58,11 +58,12 @@
     return pl.pallas_call(
         lambda *refs: None,
         out_shape=[jax.ShapeDtypeStruct(array.shape, array.dtype) for array in arrays],
-        in_specs=[ANY] * (count + 1),
+        in_specs=[ANY] * (count + len(after)),
         out_specs=[ANY] * count,
         input_output_aliases={at: at for at in range(count)},
+        compiler_params=pltpu.CompilerParams(vmem_limit_bytes=SCOPED),
         name="hand_on",
-    )(*arrays, after)
+    )(*arrays, *after)
 
 
 def write_faces(masked, lanes, first, second, x_refs, y_refs):
@@ -85,23 +86,8 @@
     return jnp.where(odd, values[0], values[1]), jnp.where(odd, values[1], values[0])
 
 
-def start_copies(pairs, sems):
-    copies = [
-        pltpu.make_async_copy(source, target, sems.at[at])
-        for at, (source, target) in enumerate(pairs)
-    ]
-    for copy in copies:
-        copy.start()
-    return copies
-
-
-def prepare_kernel(sizes, ins, x_refs, y_refs, packed_ref, open_ref, rhs_ref, scratch):
+def prepare_kernel(sizes, rhs_ref, wall_ref, x_refs, y_refs, open_ref):
     first, second, local_blocks, block = sizes
-    relax_ref, speed_ref, wall_ref, sems = scratch
-    copies = start_copies(list(zip(ins, (rhs_ref, relax_ref, speed_ref, wall_ref))), sems)
-    cells = first * second
-    for copy in reversed(copies):
-        copy.wait()
     wall = wall_ref[...].astype(jnp.float32)
     eye = (
         lax.broadcasted_iota(jnp.int32, (second, second), 0)
@@ -110,28 +96,14 @@
     for row in range(first):
         column = jnp.sum(eye * (1.0 - wall[row : row + 1, :]), axis=1, keepdims=True)
         open_ref[row * second : (row + 1) * second, :] = jnp.broadcast_to(column, (second, block))
-    total = jnp.zeros((1, block), jnp.float32)
     for b in range(local_blocks):
         lanes = slice(b * block, (b + 1) * block)
-        value = rhs_ref[:, lanes]
-        packed_ref[b * cells : (b + 1) * cells, :] = value.astype(jnp.bfloat16)
-        masked = (value * open_ref[...]).reshape(first, second, block)
+        masked = (rhs_ref[:, lanes] * open_ref[...]).reshape(first, second, block)
         write_faces(masked, lanes, first, second, x_refs, y_refs)
-        total += relax_ref[lanes].reshape(1, block) + speed_ref[0:1, lanes] + speed_ref[1:2, lanes]
-    mean = jnp.sum(total, axis=1, keepdims=True) * (1.0 / (local_blocks * block))
-    packed_ref[local_blocks * cells :, :] = jnp.broadcast_to(mean, (TAIL, block)).astype(
-        jnp.bfloat16
-    )
-
-
-def load_kernel(count, *refs):
-    for copy in start_copies(list(zip(refs[:count], refs[count : 2 * count])), refs[-1]):
-        copy.wait()
 
 
 def scatter(sizes, per_owner, b, places, cols_ref, sources, blocks_ref):
     first, second, local_blocks, block = sizes
-    cells = first * second
     mine = lax.axis_index("mode")
     picks, weights = [], []
     for place, source in zip(places, sources):
@@ -139,7 +111,7 @@
         for p in range(per_owner):
             slot = owner * per_owner + p
             column = cols_ref[slot, b] - owner * local_blocks
-            picks.append(source[pl.ds(pl.multiple_of(column * cells, cells), cells), :])
+            picks.append(source[:, pl.ds(pl.multiple_of(column * block, block), block)])
             weights.append(blocks_ref[b, slot])
     return lax.dot_general(
         jnp.concatenate(picks, axis=1),
@@ -149,69 +121,77 @@
     )
 
 
-def near_kernel(sizes, per_owner, places, cols_ref, sources, blocks_ref, current_ref, params, x_in, y_in, out_ref):
+def split_speeds(speed_ref, sign_ref, lanes):
+    parts = []
+    for axis in range(2):
+        speed, sign = speed_ref[axis : axis + 1, lanes], sign_ref[axis : axis + 1, lanes]
+        parts += [jnp.where(sign == 1, speed, 0.0), jnp.where(sign == 1, 0.0, speed)]
+    return parts
+
+
+def near_kernel(sizes, per_owner, places, cols_ref, sources, blocks_ref, current_ref, params, open_ref, out_ref):
     first, second, local_blocks, block = sizes
-    relax_ref, speed_ref, sign_ref, open_ref = params
     cells = first * second
     open_cells = open_ref[...]
     row_at = lax.broadcasted_iota(jnp.int32, (first, second, block), 1)
+    zero = jnp.zeros((1, second, block), jnp.float32)
     for b in range(local_blocks):
         lanes = slice(b * block, (b + 1) * block)
         scattered = scatter(sizes, per_owner, b, places, cols_ref, sources, blocks_ref)
         current = current_ref[:, lanes]
         masked = (current * open_cells).reshape(first, second, block)
+        relax_ref, speed_ref, sign_ref = params
+        west, east, south, north = split_speeds(speed_ref, sign_ref, lanes)
+        diagonal = relax_ref[lanes].reshape(1, block) + (west + east) + (south + north) - SHIFT
+        from_west = jnp.concatenate([zero, masked[:-1]], axis=0)
+        from_east = jnp.concatenate([masked[1:], zero], axis=0)
+        from_south = jnp.where(row_at == 0, 0.0, pltpu.roll(masked, 1, axis=1))
+        from_north = jnp.where(row_at == second - 1, 0.0, pltpu.roll(masked, second - 1, axis=1))
+        drift = (
+            west.reshape(1, 1, block) * from_west
+            + east.reshape(1, 1, block) * from_east
+            + south.reshape(1, 1, block) * from_south
+            + north.reshape(1, 1, block) * from_north
+        ).reshape(cells, block)
+        out_ref[:, lanes] = diagonal * current - drift - scattered
+
+
+def middle_kernel(sizes, per_owner, places, cols_ref, sources, blocks_ref, partial_ref, speed_ref, sign_ref, x_in, y_in, out_ref):
+    first, second, local_blocks, block = sizes
+    cells = first * second
+    row_at = lax.broadcasted_iota(jnp.int32, (first, second, block), 1)
+    for b in range(local_blocks):
+        lanes = slice(b * block, (b + 1) * block)
+        value = partial_ref[:, lanes]
+        if places:
+            value = value - scatter(sizes, per_owner, b, places, cols_ref, sources, blocks_ref)
+        west, east, south, north = split_speeds(speed_ref, sign_ref, lanes)
         west_in, east_in = halos(x_in, "gx", lanes, (second, block))
         south_in, north_in = halos(y_in, "gy", lanes, (first, block))
-        from_west = jnp.concatenate([west_in[None], masked[:-1]], axis=0)
-        from_east = jnp.concatenate([masked[1:], east_in[None]], axis=0)
-        from_south = jnp.where(
-            row_at == 0, south_in[:, None, :], pltpu.roll(masked, 1, axis=1)
-        )
-        from_north = jnp.where(
-            row_at == second - 1, north_in[:, None, :], pltpu.roll(masked, second - 1, axis=1)
-        )
-        sign_x = sign_ref[0:1, lanes].reshape(1, 1, block)
-        sign_y = sign_ref[1:2, lanes].reshape(1, 1, block)
-        speed_x, speed_y = speed_ref[0:1, lanes], speed_ref[1:2, lanes]
-        upstream_x = jnp.where(sign_x == 1, from_west, from_east).reshape(cells, block)
-        upstream_y = jnp.where(sign_y == 1, from_south, from_north).reshape(cells, block)
-        diagonal = relax_ref[lanes].reshape(1, block) + speed_x + speed_y
-        out_ref[:, lanes] = (
-            diagonal * current - speed_x * upstream_x - speed_y * upstream_y - scattered
-        )
-
-
-def add_kernel(sizes, per_owner, places, cols_ref, sources, blocks_ref, partial_ref, out_ref):
-    first, second, local_blocks, block = sizes
-    for b in range(local_blocks):
-        lanes = slice(b * block, (b + 1) * block)
-        out_ref[:, lanes] = partial_ref[:, lanes] - scatter(
-            sizes, per_owner, b, places, cols_ref, sources, blocks_ref
-        )
-
-
-def shift_of(tails):
-    mine = lax.axis_index("mode")
-    total = jnp.zeros_like(tails[0])
-    for owner in range(len(tails)):
-        term = tails[0]
-        for place in range(1, len(tails)):
-            term = jnp.where((mine ^ place) == owner, tails[place], term)
-        total = total + term
-    return total * (1.0 / len(tails))
-
-
-def last_kernel(sizes, per_owner, places, cols_ref, sources, blocks_ref, partial_ref, shift, earlier, open_ref, outs):
+        value = value.reshape(first, second, block)
+        value = value - jnp.where(
+            row_at == 0,
+            (south * south_in)[:, None, :],
+            jnp.where(row_at == second - 1, (north * north_in)[:, None, :], 0.0),
+        )
+        value = jnp.concatenate(
+            [value[:1] - (west * west_in)[None], value[1:-1], value[-1:] - (east * east_in)[None]],
+            axis=0,
+        )
+        out_ref[:, lanes] = value.reshape(cells, block)
+
+
+def last_kernel(sizes, per_owner, places, cols_ref, sources, blocks_ref, partial_ref, earlier, open_ref, outs):
     first, second, local_blocks, block = sizes
     cells = first * second
     sums = {}
     for b in range(local_blocks):
         lanes = slice(b * block, (b + 1) * block)
         scattered = scatter(sizes, per_owner, b, places, cols_ref, sources, blocks_ref)
-        result = partial_ref[:, lanes] - shift * earlier[-1][:, lanes] - scattered
+        result = partial_ref[:, lanes] - scattered
         if outs.gram is None:
             outs.value[:, lanes] = result
-            outs.packed[b * cells : (b + 1) * cells, :] = result.astype(jnp.bfloat16)
+            outs.packed[:, lanes] = result.astype(jnp.bfloat16)
             write_faces(
                 (result * open_ref[...]).reshape(first, second, block),
                 lanes, first, second, outs.x, outs.y,
@@ -269,7 +249,7 @@
     return combo
 
 
-def arnoldi(gram, shift):
+def arnoldi(gram):
     size = KRYLOV + 1
 
     def inner(left, right):
@@ -294,7 +274,7 @@
             if k > 0 and vector[k - 1] is not None:
                 parts.append(vector[k - 1])
             if vector[k] is not None:
-                parts.append(shift * vector[k])
+                parts.append(SHIFT * vector[k])
             image[k] = sum(parts[1:], parts[0])
         rest = list(image)
         for earlier in range(section + 1):
@@ -315,9 +295,9 @@
     return hessenberg, weights
 
 
-def finish_kernel(gram_ref, shift_ref, *refs):
+def finish_kernel(gram_ref, *refs):
     vectors, (solution_ref, hessenberg_ref) = refs[:KRYLOV], refs[KRYLOV:]
-    block = shift_ref.shape[1]
+    block = gram_ref.shape[2]
     total = jnp.sum(gram_ref[...], axis=0)
     lane = lax.broadcasted_iota(jnp.int32, (1, block), 1)
     gram = [[None] * (KRYLOV + 1) for i in range(KRYLOV + 1)]
@@ -327,7 +307,7 @@
             entry = jnp.sum(jnp.where(lane == at, total, 0.0), axis=1, keepdims=True)
             gram[i][j] = jnp.broadcast_to(entry, (1, block))
             at += 1
-    hessenberg, weights = arnoldi(gram, shift_ref[...])
+    hessenberg, weights = arnoldi(gram)
     rows = lax.broadcasted_iota(jnp.int32, (KRYLOV + 1, KRYLOV), 0)
     cols = lax.broadcasted_iota(jnp.int32, (KRYLOV + 1, KRYLOV), 1)
     table = jnp.zeros((KRYLOV + 1, KRYLOV), jnp.float32)
@@ -344,8 +324,8 @@
 
 VMEM = pl.BlockSpec(memory_space=pltpu.VMEM)
 SMEM = pl.BlockSpec(memory_space=pltpu.SMEM)
-HBM = pl.BlockSpec(memory_space=pltpu.HBM)
 ANY = pl.BlockSpec(memory_space=pl.ANY)
+SCOPED = 16 * 1024 * 1024
 
 
 def call(name, kernel, groups, shapes, scratch=(), flops=0):
@@ -367,7 +347,7 @@
         in_specs=[spec for spec, operand in flat],
         out_specs=[VMEM] * len(shapes),
         scratch_shapes=list(scratch),
-        compiler_params=pltpu.CompilerParams(vmem_limit_bytes=32 * 1024 * 1024),
+        compiler_params=pltpu.CompilerParams(vmem_limit_bytes=SCOPED),
         cost_estimate=pl.CostEstimate(flops=flops, bytes_accessed=size, transcendentals=0),
         name=name,
     )(*[operand for spec, operand in flat])
@@ -375,10 +355,6 @@
 
 def in_vmem(operands):
     return [(VMEM, operand) for operand in operands]
-
-
-def in_hbm(operands):
-    return [(HBM, operand) for operand in operands]
 
 
 def per_device(right_side, col_block, blocks, relax_rate, drift_speed, upwind_sign, wall_mask):
@@ -396,42 +372,28 @@
     face_shapes = [shape_of((second, local_modes), f32)] * x_swaps + [
         shape_of((first, local_modes), f32)
     ] * y_swaps
-    packed_shape = shape_of((local_blocks * cells + TAIL, block), jnp.bfloat16)
+    packed_shape = shape_of((cells, local_modes), jnp.bfloat16)
     vector_shape = shape_of((cells, local_modes), f32)
-    shift_shape = shape_of((1, block), f32)
     near = [place for place in (0, 1) if place < count]
     far = [place for place in range(count) if place not in near]
     middle = [place for place in far if place % 2 == 0]
     final = [place for place in far if place % 2 == 1]
 
+    start = right_side.reshape(cells, local_modes)
+    packed = start.astype(jnp.bfloat16)
+
     def prepare(ins, outs, scratch):
-        faces, rest = outs[:n_faces], outs[n_faces:]
-        prepare_kernel(sizes, ins, faces[:x_swaps], faces[x_swaps:], *rest, scratch)
-
-    *faces, packed, open_cells, start = call(
+        faces, (open_ref,) = outs[:n_faces], outs[n_faces:]
+        prepare_kernel(sizes, *ins, faces[:x_swaps], faces[x_swaps:], open_ref)
+
+    *faces, open_cells = call(
         "prepare",
         prepare,
-        [in_hbm([right_side.reshape(cells, local_modes), relax_rate, drift_speed, wall_mask])],
-        face_shapes + [packed_shape, shape_of((cells, block), f32), vector_shape],
-        [
-            pltpu.VMEM(relax_rate.shape, f32),
-            pltpu.VMEM(drift_speed.shape, f32),
-            pltpu.VMEM(wall_mask.shape, jnp.int32),
-            pltpu.SemaphoreType.DMA((4,)),
-        ],
+        [in_vmem([start, wall_mask])],
+        face_shapes + [shape_of((cells, block), f32)],
+        flops=8 * 10**9,
     )
-    kept = [blocks, relax_rate, drift_speed, upwind_sign, col_block.T]
-
-    def load(ins, after, outs, scratch):
-        load_kernel(len(ins), *ins, *outs, *scratch)
-
-    blocks, relax_rate, drift_speed, upwind_sign, columns = call(
-        "load",
-        load,
-        [in_hbm(kept), [(ANY, open_cells)]],
-        [shape_of(array.shape, array.dtype) for array in kept],
-        [pltpu.SemaphoreType.DMA((len(kept),))],
-    )
+    columns = col_block.T
 
     work = 2 * cells * local_modes * per_owner * block
     vectors = [start]
@@ -442,11 +404,11 @@
         held = gather_far(packed)
         x_in, y_in = face_swaps({"gx": faces[:x_swaps], "gy": faces[x_swaps:]})
 
-        def near_step(cols, sources, rest, x_in, y_in, outs, scratch):
-            blocks_ref, current_ref, *params = rest
+        def near_step(cols, sources, rest, params, outs, scratch):
+            blocks_ref, current_ref, open_ref = rest
             near_kernel(
                 sizes, per_owner, near, cols[0], sources, blocks_ref, current_ref, params,
-                x_in, y_in, outs[0],
+                open_ref, outs[0],
             )
 
         (partial,) = call(
@@ -455,45 +417,40 @@
             [
                 [(SMEM, columns)],
                 in_vmem([sources[place] for place in near]),
-                in_vmem([blocks, vectors[-1], relax_rate, drift_speed, upwind_sign, open_cells]),
+                in_vmem([blocks, vectors[-1], open_cells]),
+                in_vmem([relax_rate, drift_speed, upwind_sign]),
+            ],
+            [vector_shape],
+            flops=work * len(near),
+        )
+
+        held = dict(zip(held, hand_on(list(held.values()), [partial, *x_in, *y_in])))
+        for place, array in held.items():
+            sources[place] = array
+            sources[place ^ 1] = exchange(array, 1)
+
+        def middle_step(cols, sources, rest, x_in, y_in, outs, scratch):
+            middle_kernel(
+                sizes, per_owner, middle, cols[0], sources, *rest, x_in, y_in, outs[0]
+            )
+
+        (partial,) = call(
+            "middle_%d" % section,
+            middle_step,
+            [
+                [(SMEM, columns)],
+                in_vmem([sources[place] for place in middle]),
+                in_vmem([blocks, partial, drift_speed, upwind_sign]),
                 in_vmem(x_in),
                 in_vmem(y_in),
             ],
             [vector_shape],
-            flops=work * len(near),
-        )
-
-        held = dict(zip(held, hand_on(list(held.values()), partial)))
-        for place, array in held.items():
-            sources[place] = array
-            sources[place ^ 1] = exchange(array, 1)
-
-        def middle_step(cols, sources, rest, outs, scratch):
-            add_kernel(sizes, per_owner, middle, cols[0], sources, *rest, outs[0])
-
-        if middle:
-            (partial,) = call(
-                "middle_%d" % section,
-                middle_step,
-                [
-                    [(SMEM, columns)],
-                    in_vmem([sources[place] for place in middle]),
-                    in_vmem([blocks, partial]),
-                ],
-                [vector_shape],
-                flops=work * len(middle),
-            )
+            flops=work * len(middle),
+        )
 
         last = section == KRYLOV - 1
-        def last_step(cols, sources, rest, earlier, known, outs, scratch, section=section, last=last):
+        def last_step(cols, sources, rest, earlier, outs, scratch, last=last):
             blocks_ref, partial_ref, open_ref = rest
-            if section == 0:
-                tail_at = local_blocks * cells
-                value = shift_of([ref[tail_at:, :].astype(f32)[0:1] for ref in known])
-                outs[-1][...] = value
-                outs = outs[:-1]
-            else:
-                value = known[0][...]
             named = Outs()
             if last:
                 named.gram = outs[0]
@@ -502,15 +459,13 @@
                 named.packed, named.value = outs[n_faces:]
             last_kernel(
                 sizes, per_owner, final, cols[0], sources, blocks_ref, partial_ref,
-                value, earlier, open_ref, named,
+                earlier, open_ref, named,
             )
 
         if last:
             shapes = [shape_of((devices, 1, block), f32)]
         else:
             shapes = face_shapes + [packed_shape, vector_shape]
-        if section == 0:
-            shapes = shapes + [shift_shape]
         results = call(
             "last_%d" % section,
             last_step,
@@ -518,14 +473,11 @@
                 [(SMEM, columns)],
                 in_vmem([sources[place] for place in final]),
                 in_vmem([blocks, partial, open_cells]),
-                in_vmem(vectors),
-                in_vmem([shift] if section else [sources[place] for place in range(count)]),
+                in_vmem(vectors if last else []),
             ],
             shapes,
             flops=work * len(final),
         )
-        if section == 0:
-            *results, shift = results
         if last:
             (gram,) = results
         else:
@@ -540,7 +492,7 @@
     solution, hessenberg = call(
         "finish",
         finish,
-        [in_vmem([gram, shift, *vectors])],
+        [in_vmem([gram, *vectors])],
         [vector_shape, shape_of((KRYLOV + 1, KRYLOV), f32)],
     )
     return solution.reshape(first, second, local_modes), hessenberg

time: 79.5 us -> 52.4 us (0.66)
  local copies, waits for them, and re-layouts: 29 us -> 1.73 us
  blocking collectives: 11.3 us -> 13.3 us
  other arithmetic: 0 us -> 1.05 us
  waiting for transfers between devices: 3.01 us -> 2.01 us
    unnamed x56 -> x16, local copies, waits for them, and re-layouts: 29 us -> 1.73 us
    ppermute x9, waiting for transfers between devices: 2.99 us -> 0.63 us  [face_swaps(): lax.ppermute(face, axis, pairs)]
    all_to_all x1, blocking collectives: 11.3 us -> 13.3 us  [per_device(): gram = lax.all_to_all(gram, AXES, 0, 0)]
    ppermute x9, waiting for transfers between devices: 0.02 us -> 1.38 us  [exchange(): return lax.ppermute(array, 'mode', [(i, i ^ bit) for i in range(count)])]
    convert_element_type x0 -> x1, other arithmetic: none -> 1.05 us  [per_device(): packed = start.astype(jnp.bfloat16)]
    pallas_call x12 -> x11, Pallas kernels: 12.6 us -> 12.1 us  [call(): pl.pallas_call(body, out_shape=list(shapes), in_specs=[spec for spec, ope...]
  transfers between devices with their start and end apart: 18 -> 18, of which waited for: 2 -> 7; matrix products, arithmetic and copies ran while one was open for 0% -> 0% of each run, Pallas kernels for 10% -> 15%
where the time goes in v3:
time: 52.4 us; the launch traced here: 52.1 us
  starting transfers between devices  21.1 us (40%)
  blocking collectives  13.3 us (25%)
  Pallas kernels  12.1 us (23%)
  waiting for transfers between devices  2.01 us (4%)
  local copies, waits for them, and re-layouts  1.73 us (3%)
  other arithmetic  1.05 us (2%)
  between operations  0.85 us (2%)
    ppermute x9, starting transfers between devices, face_swaps(): lax.ppermute(face, axis, pairs)  15.5 us
    all_to_all x1, blocking collectives, per_device(): gram = lax.all_to_all(gram, AXES, 0, 0)  13.3 us
    pallas_call x11, Pallas kernels, call(): pl.pallas_call(body, out_shape=list(shapes), in_specs=[spec for spec, ope...  12.1 us
    ppermute x9, starting transfers between devices, exchange(): return lax.ppermute(array, 'mode', [(i, i ^ bit) for i in range(count)])  5.62 us
    unnamed x16, local copies, waits for them, and re-layouts  1.73 us
    ppermute x9, waiting for transfers between devices, exchange(): return lax.ppermute(array, 'mode', [(i, i ^ bit) for i in range(count)])  1.38 us
  transfers between devices with their start and end apart: 18, of which 7 were waited for; matrix products, arithmetic and copies ran while one was open for 0% of the time, Pallas kernels for 15%

profile of v3, /device:TPU:0, one launch (start us, length us, event | category | flops | bytes accessed | tf_op | source)
XLA Modules:
  0.0 52.1 jit_solution(10700916088087602459)
XLA Ops:
  0.6 1.0 %bitcast_convert_fusion.refs_1_ = bf16[64,1792]{1,0:T(8,128)(2,1)S(1)} fusion(f32[8,8,1792]{2,1,0:T(8,128)} %param.7), kind=kLoop, calls=%fused_computation | loop fusion | flops 114688 | bytes 688128 | tf_op jit(solution)/shard_map/convert_element_type | solution.py:383
  1.7 0.5 collective-permute-start.1
  2.2 2.6 %collective-permute-start = (bf16[64,1792]{1,0:T(8,128)(2,1)S(1)}, bf16[64,1792]{1,0:T(8,128)(2,1)S(1)}, u32[]{:S(2)}, u32[]{:S(2)}) collective-permute-start(bf16[64,1792]{1,0:T(8,128)(2,1)S(1)} %bitcast_convert_fusion.refs_1_), channel_id=1, source_target_pairs={{0,16},{8,24},{16,0},{24,8},{1,17},{9,25},{17,1},{25,9},{2,18},{10... | collective-permute-start | bytes 688136 | tf_op jit(solution)/shard_map/ppermute | solution.py:40
  4.8 1.0 %copy-done.1 = f32[8,8,1792]{2,1,0:T(8,128)S(1)} copy-done((f32[8,8,1792]{2,1,0:T(8,128)S(1)}, f32[8,8,1792]{2,1,0:T(8,128)}, u32[]{:S(2)}) %copy-start.1) | copy-done | bytes 458776
  5.8 0.7 %copy-done.7 = s32[8,8]{1,0:T(8,128)S(1)} copy-done((s32[8,8]{1,0:T(8,128)S(1)}, s32[8,8]{1,0:T(8,128)}, u32[]{:S(2)}) %copy-start.7) | copy-done | bytes 280
  6.5 0.0 copy-start.6
  6.5 0.2 prepare.1
  6.7 1.6 %collective-permute-start.2 = (f32[8,1792]{1,0:T(8,128)S(1)}, f32[8,1792]{1,0:T(8,128)S(1)}, u32[]{:S(2)}, u32[]{:S(2)}) collective-permute-start(f32[8,1792]{1,0:T(8,128)S(1)} %get-tuple-element.19), channel_id=1, source_target_pairs={{0,4},{4,0},{1,5},{5,1},{2,6},{6,2},{3,7},{7,3},{8,12},{12,8},{9,1... | collective-permute-start | bytes 172040 | tf_op jit(solution)/shard_map/ppermute | solution.py:33
  8.3 1.6 %collective-permute-start.3 = (f32[8,1792]{1,0:T(8,128)S(1)}, f32[8,1792]{1,0:T(8,128)S(1)}, u32[]{:S(2)}, u32[]{:S(2)}) collective-permute-start(f32[8,1792]{1,0:T(8,128)S(1)} %get-tuple-element.20), channel_id=1, source_target_pairs={{0,1},{1,0},{2,3},{3,2},{4,5},{5,4},{6,7},{7,6},{8,9},{9,8},{10,11... | collective-permute-start | bytes 172040 | tf_op jit(solution)/shard_map/ppermute | solution.py:33
  9.9 0.7 %collective-permute-start.4 = (f32[8,1792]{1,0:T(8,128)S(1)}, f32[8,1792]{1,0:T(8,128)S(1)}, u32[]{:S(2)}, u32[]{:S(2)}) collective-permute-start(f32[8,1792]{1,0:T(8,128)S(1)} %get-tuple-element.21), channel_id=1, source_target_pairs={{1,2},{2,1},{5,6},{6,5},{9,10},{10,9},{13,14},{14,13},{17,18},{18,... | collective-permute-start | bytes 172040 | tf_op jit(solution)/shard_map/ppermute | solution.py:33
  10.5 0.0 collective-permute-done.1.refs_2_
  10.6 1.4 %near_0.1.refs_1_.refs_3_ = f32[64,1792]{1,0:T(8,128)S(1)} custom-call(s32[8,14]{1,0:T(8,128)S(1)} %bitcast.8, bf16[64,1792]{1,0:T(8,128)(2,1)S(1)} %bitcast_convert_fusion.refs_1_, bf16[64,1792]{1,0:T(8,128)(2,1)S(1)} %collective-permute-done.1.refs_2_, bf16[14,8,128,128]{3,2,1,0:T(8,128)(2,1)S(1)} %copy-done, f32[64,1792]{1,0:T(8,128)S(1)} %bitcast.5, ...), custom_call_target="tpu_custom_call" | custom-call | flops 117440512 | bytes 5115328 | tf_op jit(solution)/shard_map/near_0/pallas_call | solution.py:344
  12.0 0.5 collective-permute-done.3.refs_3_.refs_7_
  12.5 0.0 collective-permute-done.4.refs_4_.refs_8_
  12.5 0.0 collective-permute-done.refs_0_
  12.5 0.1 collective-permute-start.5
  12.6 1.1 %middle_0.1.refs_3_ = f32[64,1792]{1,0:T(8,128)S(1)} custom-call(s32[8,14]{1,0:T(8,128)S(1)} %bitcast.9, bf16[64,1792]{1,0:T(8,128)(2,1)S(1)} %hand_on.3.refs_1_, bf16[14,8,128,128]{3,2,1,0:T(8,128)(2,1)S(1)} %copy-done, f32[64,1792]{1,0:T(8,128)S(1)} %near_0.1.refs_1_.refs_3_, f32[2,1792]{1,0:T(2,128)S(1)} %copy-done.3, s32[2,1792]{1,0:T(2,128)S(1)} %copy-done.4, ...), custom_call_target="tpu_custom_call" | custom-call | flops 58720256 | bytes 5018048 | tf_op jit(solution)/shard_map/middle_0/pallas_call | solution.py:344
  13.6 0.4 collective-permute-done.5.refs_1_
  14.0 1.1 %last_0.1 = (f32[8,1792]{1,0:T(8,128)S(1)}, f32[8,1792]{1,0:T(8,128)S(1)}, f32[8,1792]{1,0:T(8,128)S(1)}, bf16[64,1792]{1,0:T(8,128)(2,1)S(1)}, f32[64,1792]{1,0:T(8,128)S(1)}) custom-call(s32[8,14]{1,0:T(8,128)S(1)} %bitcast.10, bf16[64,1792]{1,0:T(8,128)(2,1)S(1)} %collective-permute-done.5.refs_1_, bf16[14,8,128,128]{3,2,1,0:T(8,128)(2,1)S(1)} %copy-done, ...), custom_call_target="tpu_custom_call" | custom-call | flops 58720256 | bytes 5251520 | tf_op jit(solution)/shard_map/last_0/pallas_call | solution.py:344
  15.1 0.2 collective-permute-start.7
  15.3 0.5 %collective-permute-start.6 = (bf16[64,1792]{1,0:T(8,128)(2,1)S(1)}, bf16[64,1792]{1,0:T(8,128)(2,1)S(1)}, u32[]{:S(2)}, u32[]{:S(2)}) collective-permute-start(bf16[64,1792]{1,0:T(8,128)(2,1)S(1)} %get-tuple-element.22.refs_1_), channel_id=1, source_target_pairs={{0,16},{8,24},{16,0},{24,8},{1,17},{9,25},{17,1},{25,9},{2,18},{10... | collective-permute-start | bytes 688136 | tf_op jit(solution)/shard_map/ppermute | solution.py:40
  15.8 1.2 %collective-permute-start.8 = (f32[8,1792]{1,0:T(8,128)S(1)}, f32[8,1792]{1,0:T(8,128)S(1)}, u32[]{:S(2)}, u32[]{:S(2)}) collective-permute-start(f32[8,1792]{1,0:T(8,128)S(1)} %get-tuple-element.24), channel_id=1, source_target_pairs={{0,4},{4,0},{1,5},{5,1},{2,6},{6,2},{3,7},{7,3},{8,12},{12,8},{9,1... | collective-permute-start | bytes 172040 | tf_op jit(solution)/shard_map/ppermute | solution.py:33
  17.0 3.9 %collective-permute-start.9 = (f32[8,1792]{1,0:T(8,128)S(1)}, f32[8,1792]{1,0:T(8,128)S(1)}, u32[]{:S(2)}, u32[]{:S(2)}) collective-permute-start(f32[8,1792]{1,0:T(8,128)S(1)} %get-tuple-element.25), channel_id=1, source_target_pairs={{0,1},{1,0},{2,3},{3,2},{4,5},{5,4},{6,7},{7,6},{8,9},{9,8},{10,11... | collective-permute-start | bytes 172040 | tf_op jit(solution)/shard_map/ppermute | solution.py:33
  20.9 0.7 %collective-permute-start.10 = (f32[8,1792]{1,0:T(8,128)S(1)}, f32[8,1792]{1,0:T(8,128)S(1)}, u32[]{:S(2)}, u32[]{:S(2)}) collective-permute-start(f32[8,1792]{1,0:T(8,128)S(1)} %get-tuple-element.26), channel_id=1, source_target_pairs={{1,2},{2,1},{5,6},{6,5},{9,10},{10,9},{13,14},{14,13},{17,18},{18,... | collective-permute-start | bytes 172040 | tf_op jit(solution)/shard_map/ppermute | solution.py:33
  21.6 1.4 %near_1.1.refs_1_.refs_3_ = f32[64,1792]{1,0:T(8,128)S(1)} custom-call(s32[8,14]{1,0:T(8,128)S(1)} %bitcast.11, bf16[64,1792]{1,0:T(8,128)(2,1)S(1)} %get-tuple-element.22.refs_1_, bf16[64,1792]{1,0:T(8,128)(2,1)S(1)} %collective-permute-done.7.refs_2_, bf16[14,8,128,128]{3,2,1,0:T(8,128)(2,1)S(1)} %copy-done, ...), custom_call_target="tpu_custom_call" | custom-call | flops 117440512 | bytes 5115328 | tf_op jit(solution)/shard_map/near_1/pallas_call | solution.py:344
  23.0 0.0 collective-permute-done.8.refs_2_.refs_6_
  23.0 0.1 collective-permute-done.9.refs_3_.refs_7_
  23.1 0.0 collective-permute-done.10.refs_4_.refs_8_
  23.1 0.1 collective-permute-done.6.refs_0_
  23.2 0.0 collective-permute-start.11
  23.2 1.1 %middle_1.1.refs_3_ = f32[64,1792]{1,0:T(8,128)S(1)} custom-call(s32[8,14]{1,0:T(8,128)S(1)} %bitcast.12, bf16[64,1792]{1,0:T(8,128)(2,1)S(1)} %hand_on.4.refs_1_, bf16[14,8,128,128]{3,2,1,0:T(8,128)(2,1)S(1)} %copy-done, f32[64,1792]{1,0:T(8,128)S(1)} %near_1.1.refs_1_.refs_3_, f32[2,1792]{1,0:T(2,128)S(1)} %copy-done.3, s32[2,1792]{1,0:T(2,128)S(1)} %copy-done.4, ...), custom_call_target="tpu_custom_call" | custom-call | flops 58720256 | bytes 5018048 | tf_op jit(solution)/shard_map/middle_1/pallas_call | solution.py:344
  24.3 0.4 collective-permute-done.11.refs_1_
  24.7 1.1 %last_1.1 = (f32[8,1792]{1,0:T(8,128)S(1)}, f32[8,1792]{1,0:T(8,128)S(1)}, f32[8,1792]{1,0:T(8,128)S(1)}, bf16[64,1792]{1,0:T(8,128)(2,1)S(1)}, f32[64,1792]{1,0:T(8,128)S(1)}) custom-call(s32[8,14]{1,0:T(8,128)S(1)} %bitcast.13, bf16[64,1792]{1,0:T(8,128)(2,1)S(1)} %collective-permute-done.11.refs_1_, bf16[14,8,128,128]{3,2,1,0:T(8,128)(2,1)S(1)} %copy-done, ...), custom_call_target="tpu_custom_call" | custom-call | flops 58720256 | bytes 5251520 | tf_op jit(solution)/shard_map/last_1/pallas_call | solution.py:344
  25.8 0.2 collective-permute-start.13
  26.0 1.5 %collective-permute-start.12 = (bf16[64,1792]{1,0:T(8,128)(2,1)S(1)}, bf16[64,1792]{1,0:T(8,128)(2,1)S(1)}, u32[]{:S(2)}, u32[]{:S(2)}) collective-permute-start(bf16[64,1792]{1,0:T(8,128)(2,1)S(1)} %get-tuple-element.27.refs_1_), channel_id=1, source_target_pairs={{0,16},{8,24},{16,0},{24,8},{1,17},{9,25},{17,1},{25,9},{2,18},{10... | collective-permute-start | bytes 688136 | tf_op jit(solution)/shard_map/ppermute | solution.py:40
  27.4 1.5 %collective-permute-start.14 = (f32[8,1792]{1,0:T(8,128)S(1)}, f32[8,1792]{1,0:T(8,128)S(1)}, u32[]{:S(2)}, u32[]{:S(2)}) collective-permute-start(f32[8,1792]{1,0:T(8,128)S(1)} %get-tuple-element.29), channel_id=1, source_target_pairs={{0,4},{4,0},{1,5},{5,1},{2,6},{6,2},{3,7},{7,3},{8,12},{12,8},{9,1... | collective-permute-start | bytes 172040 | tf_op jit(solution)/shard_map/ppermute | solution.py:33
  28.9 3.8 %collective-permute-start.15 = (f32[8,1792]{1,0:T(8,128)S(1)}, f32[8,1792]{1,0:T(8,128)S(1)}, u32[]{:S(2)}, u32[]{:S(2)}) collective-permute-start(f32[8,1792]{1,0:T(8,128)S(1)} %get-tuple-element.30), channel_id=1, source_target_pairs={{0,1},{1,0},{2,3},{3,2},{4,5},{5,4},{6,7},{7,6},{8,9},{9,8},{10,11... | collective-permute-start | bytes 172040 | tf_op jit(solution)/shard_map/ppermute | solution.py:33
  32.8 0.7 %collective-permute-start.16 = (f32[8,1792]{1,0:T(8,128)S(1)}, f32[8,1792]{1,0:T(8,128)S(1)}, u32[]{:S(2)}, u32[]{:S(2)}) collective-permute-start(f32[8,1792]{1,0:T(8,128)S(1)} %get-tuple-element.31), channel_id=1, source_target_pairs={{1,2},{2,1},{5,6},{6,5},{9,10},{10,9},{13,14},{14,13},{17,18},{18,... | collective-permute-start | bytes 172040 | tf_op jit(solution)/shard_map/ppermute | solution.py:33
  33.4 0.0 collective-permute-done.13.refs_2_
  33.4 1.4 %near_2.1.refs_1_.refs_3_ = f32[64,1792]{1,0:T(8,128)S(1)} custom-call(s32[8,14]{1,0:T(8,128)S(1)} %bitcast.14, bf16[64,1792]{1,0:T(8,128)(2,1)S(1)} %get-tuple-element.27.refs_1_, bf16[64,1792]{1,0:T(8,128)(2,1)S(1)} %collective-permute-done.13.refs_2_, bf16[14,8,128,128]{3,2,1,0:T(8,128)(2,1)S(1)} %copy-done, ...), custom_call_target="tpu_custom_call" | custom-call | flops 117440512 | bytes 5115328 | tf_op jit(solution)/shard_map/near_2/pallas_call | solution.py:344
  34.8 0.0 copy-start.2
  34.9 0.1 collective-permute-done.15.refs_3_.refs_7_
  34.9 0.1 collective-permute-start.17
  35.0 1.1 %middle_2.1.refs_3_ = f32[64,1792]{1,0:T(8,128)S(1)} custom-call(s32[8,14]{1,0:T(8,128)S(1)} %bitcast.15, bf16[64,1792]{1,0:T(8,128)(2,1)S(1)} %hand_on.5.refs_1_, bf16[14,8,128,128]{3,2,1,0:T(8,128)(2,1)S(1)} %copy-done, f32[64,1792]{1,0:T(8,128)S(1)} %near_2.1.refs_1_.refs_3_, f32[2,1792]{1,0:T(2,128)S(1)} %copy-done.3, s32[2,1792]{1,0:T(2,128)S(1)} %copy-done.4, ...), custom_call_target="tpu_custom_call" | custom-call | flops 58720256 | bytes 5018048 | tf_op jit(solution)/shard_map/middle_2/pallas_call | solution.py:344
  36.1 0.4 collective-permute-done.17.refs_1_
  36.5 1.3 %last_2.1 = f32[32,1,128]{2,1,0:T(1,128)S(1)} custom-call(s32[8,14]{1,0:T(8,128)S(1)} %bitcast.16, bf16[64,1792]{1,0:T(8,128)(2,1)S(1)} %collective-permute-done.17.refs_1_, bf16[14,8,128,128]{3,2,1,0:T(8,128)(2,1)S(1)} %copy-done, f32[64,1792]{1,0:T(8,128)S(1)} %middle_2.1.refs_3_, f32[64,128]{1,0:T(8,128)S(1)} %get-tuple-element.18.refs_5_.refs_4_, ...), custom_call_target="tpu_custom_call" | custom-call | flops 58720256 | bytes 5784000 | tf_op jit(solution)/shard_map/last_2/pallas_call | solution.py:344
  37.7 13.3 %all_to_all.5.refs_0_ = f32[32,1,128]{2,1,0:T(1,128)S(1)} all-to-all(f32[32,1,128]{2,1,0:T(1,128)S(1)} %last_2.1), channel_id=1, replica_groups=mesh['mode'=4,'gx'=2,'gy'=4] {'mode','gx','gy'}, dimensions={0} | all-to-all | bytes 32768 | tf_op jit(solution)/shard_map/all_to_all | solution.py:487
  51.0 1.1 %finish.1 = (f32[64,1792]{1,0:T(8,128)}, f32[4,3]{1,0:T(4,128)}) custom-call(f32[32,1,128]{2,1,0:T(1,128)S(1)} %all_to_all.5.refs_0_, f32[64,1792]{1,0:T(8,128)S(1)} %bitcast.7, f32[64,1792]{1,0:T(8,128)S(1)} %get-tuple-element.23.refs_4_.refs_6_.refs_2_, f32[64,1792]{1,0:T(8,128)S(1)} %get-tuple-element.28.refs_4_.refs_7_.refs_3_), custom_call_target="tpu_custom_call" | custom-call | bytes 1851440 | tf_op jit(solution)/shard_map/finish/pallas_call | solution.py:344
  (20 shorter events, 0.0 us)
Async XLA Ops:
  1.7 8.9 %collective-permute-start.1 = (bf16[64,1792]{1,0:T(8,128)(2,1)S(1)}, bf16[64,1792]{1,0:T(8,128)(2,1)S(1)}, u32[]{:S(2)}, u32[]{:S(2)}) collective-permute-start(bf16[64,1792]{1,0:T(8,128)(2,1)S(1)} %bitcast_convert_fusion.refs_1_), channel_id=1, source_target_pairs={{0,8},{8,0},{16,24},{24,16},{1,9},{9,1},{17,25},{25,17},{2,10},{10... | collective-permute-start | bytes 688136 | tf_op jit(solution)/shard_map/ppermute | solution.py:40
  2.2 10.3 %collective-permute-start = (bf16[64,1792]{1,0:T(8,128)(2,1)S(1)}, bf16[64,1792]{1,0:T(8,128)(2,1)S(1)}, u32[]{:S(2)}, u32[]{:S(2)}) collective-permute-start(bf16[64,1792]{1,0:T(8,128)(2,1)S(1)} %bitcast_convert_fusion.refs_1_), channel_id=1, source_target_pairs={{0,16},{8,24},{16,0},{24,8},{1,17},{9,25},{17,1},{25,9},{2,18},{10... | collective-permute-start | bytes 688136 | tf_op jit(solution)/shard_map/ppermute | solution.py:40
  4.8 1.0 %copy-start.1 = (f32[8,8,1792]{2,1,0:T(8,128)S(1)}, f32[8,8,1792]{2,1,0:T(8,128)}, u32[]{:S(2)}) copy-start(f32[8,8,1792]{2,1,0:T(8,128)} %param.7) | copy-start | bytes 1376260
  5.8 0.7 %copy-start.7 = (s32[8,8]{1,0:T(8,128)S(1)}, s32[8,8]{1,0:T(8,128)}, u32[]{:S(2)}) copy-start(s32[8,8]{1,0:T(8,128)} %refs_1_.1) | copy-start | bytes 772
  6.5 4.0 %copy-start = (bf16[14,8,128,128]{3,2,1,0:T(8,128)(2,1)S(1)}, bf16[14,8,128,128]{3,2,1,0:T(8,128)(2,1)}, u32[]{:S(2)}) copy-start(bf16[14,8,128,128]{3,2,1,0:T(8,128)(2,1)} %refs_2_.11) | copy-start | bytes 11010052
  6.5 4.1 %copy-start.3 = (f32[2,1792]{1,0:T(2,128)S(1)}, f32[2,1792]{1,0:T(2,128)}, u32[]{:S(2)}) copy-start(f32[2,1792]{1,0:T(2,128)} %refs_4_.5) | copy-start | bytes 43012
  6.5 4.1 %copy-start.4 = (s32[2,1792]{1,0:T(2,128)S(1)}, s32[2,1792]{1,0:T(2,128)}, u32[]{:S(2)}) copy-start(s32[2,1792]{1,0:T(2,128)} %refs_5_.5) | copy-start | bytes 43012
  6.5 4.1 %copy-start.5 = (s32[14,8]{0,1:T(8,128)S(1)}, s32[14,8]{0,1:T(8,128)}, u32[]{:S(2)}) copy-start(s32[14,8]{0,1:T(8,128)} %param.8) | copy-start | bytes 1348
  6.5 4.1 %copy-start.6 = (f32[1792]{0:T(1024)S(1)}, f32[1792]{0:T(1024)}, u32[]{:S(2)}) copy-start(f32[1792]{0:T(1024)} %refs_6_.5) | copy-start | bytes 21508
  6.7 5.2 %collective-permute-start.2 = (f32[8,1792]{1,0:T(8,128)S(1)}, f32[8,1792]{1,0:T(8,128)S(1)}, u32[]{:S(2)}, u32[]{:S(2)}) collective-permute-start(f32[8,1792]{1,0:T(8,128)S(1)} %get-tuple-element.19), channel_id=1, source_target_pairs={{0,4},{4,0},{1,5},{5,1},{2,6},{6,2},{3,7},{7,3},{8,12},{12,8},{9,1... | collective-permute-start | bytes 172040 | tf_op jit(solution)/shard_map/ppermute | solution.py:33
  8.3 4.2 %collective-permute-start.3 = (f32[8,1792]{1,0:T(8,128)S(1)}, f32[8,1792]{1,0:T(8,128)S(1)}, u32[]{:S(2)}, u32[]{:S(2)}) collective-permute-start(f32[8,1792]{1,0:T(8,128)S(1)} %get-tuple-element.20), channel_id=1, source_target_pairs={{0,1},{1,0},{2,3},{3,2},{4,5},{5,4},{6,7},{7,6},{8,9},{9,8},{10,11... | collective-permute-start | bytes 172040 | tf_op jit(solution)/shard_map/ppermute | solution.py:33
  9.9 2.6 %collective-permute-start.4 = (f32[8,1792]{1,0:T(8,128)S(1)}, f32[8,1792]{1,0:T(8,128)S(1)}, u32[]{:S(2)}, u32[]{:S(2)}) collective-permute-start(f32[8,1792]{1,0:T(8,128)S(1)} %get-tuple-element.21), channel_id=1, source_target_pairs={{1,2},{2,1},{5,6},{6,5},{9,10},{10,9},{13,14},{14,13},{17,18},{18,... | collective-permute-start | bytes 172040 | tf_op jit(solution)/shard_map/ppermute | solution.py:33
  12.5 1.5 %collective-permute-start.5 = (bf16[64,1792]{1,0:T(8,128)(2,1)S(1)}, bf16[64,1792]{1,0:T(8,128)(2,1)S(1)}, u32[]{:S(2)}, u32[]{:S(2)}) collective-permute-start(bf16[64,1792]{1,0:T(8,128)(2,1)S(1)} %hand_on.3.refs_1_), channel_id=1, source_target_pairs={{0,8},{8,0},{16,24},{24,16},{1,9},{9,1},{17,25},{25,17},{2,10},{10... | collective-permute-start | bytes 688136 | tf_op jit(solution)/shard_map/ppermute | solution.py:40
  15.1 6.5 %collective-permute-start.7 = (bf16[64,1792]{1,0:T(8,128)(2,1)S(1)}, bf16[64,1792]{1,0:T(8,128)(2,1)S(1)}, u32[]{:S(2)}, u32[]{:S(2)}) collective-permute-start(bf16[64,1792]{1,0:T(8,128)(2,1)S(1)} %get-tuple-element.22.refs_1_), channel_id=1, source_target_pairs={{0,8},{8,0},{16,24},{24,16},{1,9},{9,1},{17,25},{25,17},{2,10},{10... | collective-permute-start | bytes 688136 | tf_op jit(solution)/shard_map/ppermute | solution.py:40
  15.3 7.9 %collective-permute-start.6 = (bf16[64,1792]{1,0:T(8,128)(2,1)S(1)}, bf16[64,1792]{1,0:T(8,128)(2,1)S(1)}, u32[]{:S(2)}, u32[]{:S(2)}) collective-permute-start(bf16[64,1792]{1,0:T(8,128)(2,1)S(1)} %get-tuple-element.22.refs_1_), channel_id=1, source_target_pairs={{0,16},{8,24},{16,0},{24,8},{1,17},{9,25},{17,1},{25,9},{2,18},{10... | collective-permute-start | bytes 688136 | tf_op jit(solution)/shard_map/ppermute | solution.py:40
  15.8 7.1 %collective-permute-start.8 = (f32[8,1792]{1,0:T(8,128)S(1)}, f32[8,1792]{1,0:T(8,128)S(1)}, u32[]{:S(2)}, u32[]{:S(2)}) collective-permute-start(f32[8,1792]{1,0:T(8,128)S(1)} %get-tuple-element.24), channel_id=1, source_target_pairs={{0,4},{4,0},{1,5},{5,1},{2,6},{6,2},{3,7},{7,3},{8,12},{12,8},{9,1... | collective-permute-start | bytes 172040 | tf_op jit(solution)/shard_map/ppermute | solution.py:33
  17.0 6.0 %collective-permute-start.9 = (f32[8,1792]{1,0:T(8,128)S(1)}, f32[8,1792]{1,0:T(8,128)S(1)}, u32[]{:S(2)}, u32[]{:S(2)}) collective-permute-start(f32[8,1792]{1,0:T(8,128)S(1)} %get-tuple-element.25), channel_id=1, source_target_pairs={{0,1},{1,0},{2,3},{3,2},{4,5},{5,4},{6,7},{7,6},{8,9},{9,8},{10,11... | collective-permute-start | bytes 172040 | tf_op jit(solution)/shard_map/ppermute | solution.py:33
  20.9 2.2 %collective-permute-start.10 = (f32[8,1792]{1,0:T(8,128)S(1)}, f32[8,1792]{1,0:T(8,128)S(1)}, u32[]{:S(2)}, u32[]{:S(2)}) collective-permute-start(f32[8,1792]{1,0:T(8,128)S(1)} %get-tuple-element.26), channel_id=1, source_target_pairs={{1,2},{2,1},{5,6},{6,5},{9,10},{10,9},{13,14},{14,13},{17,18},{18,... | collective-permute-start | bytes 172040 | tf_op jit(solution)/shard_map/ppermute | solution.py:33
  23.2 1.5 %collective-permute-start.11 = (bf16[64,1792]{1,0:T(8,128)(2,1)S(1)}, bf16[64,1792]{1,0:T(8,128)(2,1)S(1)}, u32[]{:S(2)}, u32[]{:S(2)}) collective-permute-start(bf16[64,1792]{1,0:T(8,128)(2,1)S(1)} %hand_on.4.refs_1_), channel_id=1, source_target_pairs={{0,8},{8,0},{16,24},{24,16},{1,9},{9,1},{17,25},{25,17},{2,10},{10... | collective-permute-start | bytes 688136 | tf_op jit(solution)/shard_map/ppermute | solution.py:40
  25.8 7.7 %collective-permute-start.13 = (bf16[64,1792]{1,0:T(8,128)(2,1)S(1)}, bf16[64,1792]{1,0:T(8,128)(2,1)S(1)}, u32[]{:S(2)}, u32[]{:S(2)}) collective-permute-start(bf16[64,1792]{1,0:T(8,128)(2,1)S(1)} %get-tuple-element.27.refs_1_), channel_id=1, source_target_pairs={{0,8},{8,0},{16,24},{24,16},{1,9},{9,1},{17,25},{25,17},{2,10},{10... | collective-permute-start | bytes 688136 | tf_op jit(solution)/shard_map/ppermute | solution.py:40
  26.0 9.0 %collective-permute-start.12 = (bf16[64,1792]{1,0:T(8,128)(2,1)S(1)}, bf16[64,1792]{1,0:T(8,128)(2,1)S(1)}, u32[]{:S(2)}, u32[]{:S(2)}) collective-permute-start(bf16[64,1792]{1,0:T(8,128)(2,1)S(1)} %get-tuple-element.27.refs_1_), channel_id=1, source_target_pairs={{0,16},{8,24},{16,0},{24,8},{1,17},{9,25},{17,1},{25,9},{2,18},{10... | collective-permute-start | bytes 688136 | tf_op jit(solution)/shard_map/ppermute | solution.py:40
  27.4 7.4 %collective-permute-start.14 = (f32[8,1792]{1,0:T(8,128)S(1)}, f32[8,1792]{1,0:T(8,128)S(1)}, u32[]{:S(2)}, u32[]{:S(2)}) collective-permute-start(f32[8,1792]{1,0:T(8,128)S(1)} %get-tuple-element.29), channel_id=1, source_target_pairs={{0,4},{4,0},{1,5},{5,1},{2,6},{6,2},{3,7},{7,3},{8,12},{12,8},{9,1... | collective-permute-start | bytes 172040 | tf_op jit(solution)/shard_map/ppermute | solution.py:33
  28.9 6.0 %collective-permute-start.15 = (f32[8,1792]{1,0:T(8,128)S(1)}, f32[8,1792]{1,0:T(8,128)S(1)}, u32[]{:S(2)}, u32[]{:S(2)}) collective-permute-start(f32[8,1792]{1,0:T(8,128)S(1)} %get-tuple-element.30), channel_id=1, source_target_pairs={{0,1},{1,0},{2,3},{3,2},{4,5},{5,4},{6,7},{7,6},{8,9},{9,8},{10,11... | collective-permute-start | bytes 172040 | tf_op jit(solution)/shard_map/ppermute | solution.py:33
  32.8 2.2 %collective-permute-start.16 = (f32[8,1792]{1,0:T(8,128)S(1)}, f32[8,1792]{1,0:T(8,128)S(1)}, u32[]{:S(2)}, u32[]{:S(2)}) collective-permute-start(f32[8,1792]{1,0:T(8,128)S(1)} %get-tuple-element.31), channel_id=1, source_target_pairs={{1,2},{2,1},{5,6},{6,5},{9,10},{10,9},{13,14},{14,13},{17,18},{18,... | collective-permute-start | bytes 172040 | tf_op jit(solution)/shard_map/ppermute | solution.py:33
  34.8 1.6 %copy-start.2 = (f32[8,8,1792]{2,1,0:T(8,128)S(1)}, f32[8,8,1792]{2,1,0:T(8,128)}, u32[]{:S(2)}) copy-start(f32[8,8,1792]{2,1,0:T(8,128)} %param.7) | copy-start | bytes 1376260
  34.9 1.5 %collective-permute-start.17 = (bf16[64,1792]{1,0:T(8,128)(2,1)S(1)}, bf16[64,1792]{1,0:T(8,128)(2,1)S(1)}, u32[]{:S(2)}, u32[]{:S(2)}) collective-permute-start(bf16[64,1792]{1,0:T(8,128)(2,1)S(1)} %hand_on.5.refs_1_), channel_id=1, source_target_pairs={{0,8},{8,0},{16,24},{24,16},{1,9},{9,1},{17,25},{25,17},{2,10},{10... | collective-permute-start | bytes 688136 | tf_op jit(solution)/shard_map/ppermute | solution.py:40

commit v4 on v3

--- a/solution.py
+++ b/solution.py
@@ -14,24 +14,22 @@
 epsilon = 1e-12
 
 
-def pair_list(count, first):
-    pairs = []
-    for low in range(first, count - 1, 2):
-        pairs += [(low, low + 1), (low + 1, low)]
-    return pairs
-
-
-def swaps_of(count):
-    return [pairs for pairs in (pair_list(count, 0), pair_list(count, 1)) if pairs]
-
-
-def face_swaps(faces):
+def moves_of(count):
+    if count == 1:
+        return []
+    if count == 2:
+        return [[(0, 1), (1, 0)]]
+    return [
+        [(i, (i + 1) % count) for i in range(count)],
+        [(i, (i - 1) % count) for i in range(count)],
+    ]
+
+
+def move_faces(faces):
     received = []
-    for axis in ("gx", "gy"):
-        swaps = swaps_of(lax.axis_size(axis))
-        received.append(
-            [lax.ppermute(face, axis, pairs) for face, pairs in zip(faces[axis], swaps)]
-        )
+    for axis in ("gy", "gx"):
+        moves = moves_of(lax.axis_size(axis))
+        received.append([lax.ppermute(face, axis, pairs) for face, pairs in zip(faces[axis], moves)])
     return received
 
 
@@ -66,24 +64,26 @@
     )(*arrays, *after)
 
 
+def store_faces(refs, axis, lanes, low, high):
+    if len(refs) == 1:
+        refs[0][:, lanes] = jnp.where(lax.axis_index(axis) == 0, high, low)
+    elif refs:
+        refs[0][:, lanes] = high
+        refs[1][:, lanes] = low
+
+
 def write_faces(masked, lanes, first, second, x_refs, y_refs):
-    if x_refs:
-        even = lax.rem(lax.axis_index("gx"), 2) == 0
-        low, high = masked[0], masked[first - 1]
-        for ref, take_high in zip(x_refs, (even, jnp.logical_not(even))):
-            ref[:, lanes] = jnp.where(take_high, high, low)
-    if y_refs:
-        even = lax.rem(lax.axis_index("gy"), 2) == 0
-        low, high = masked[:, 0, :], masked[:, second - 1, :]
-        for ref, take_high in zip(y_refs, (even, jnp.logical_not(even))):
-            ref[:, lanes] = jnp.where(take_high, high, low)
+    store_faces(x_refs, "gx", lanes, masked[0], masked[first - 1])
+    store_faces(y_refs, "gy", lanes, masked[:, 0, :], masked[:, second - 1, :])
 
 
 def halos(refs, axis, lanes, shape):
     zero = jnp.zeros(shape, jnp.float32)
-    values = [ref[:, lanes] for ref in refs] + [zero, zero]
-    odd = lax.rem(lax.axis_index(axis), 2) == 1
-    return jnp.where(odd, values[0], values[1]), jnp.where(odd, values[1], values[0])
+    if not refs:
+        return zero, zero
+    at = lax.axis_index(axis)
+    low, high = refs[0][:, lanes], refs[-1][:, lanes]
+    return jnp.where(at == 0, zero, low), jnp.where(at == lax.axis_size(axis) - 1, zero, high)
 
 
 def prepare_kernel(sizes, rhs_ref, wall_ref, x_refs, y_refs, open_ref):
@@ -323,7 +323,6 @@
 
 
 VMEM = pl.BlockSpec(memory_space=pltpu.VMEM)
-SMEM = pl.BlockSpec(memory_space=pltpu.SMEM)
 ANY = pl.BlockSpec(memory_space=pl.ANY)
 SCOPED = 16 * 1024 * 1024
 
@@ -365,26 +364,25 @@
     devices = count * lax.axis_size("gx") * lax.axis_size("gy")
     per_owner = slots // count
     sizes = (first, second, local_blocks, block)
-    x_swaps, y_swaps = len(swaps_of(lax.axis_size("gx"))), len(swaps_of(lax.axis_size("gy")))
-    n_faces = x_swaps + y_swaps
+    x_moves, y_moves = len(moves_of(lax.axis_size("gx"))), len(moves_of(lax.axis_size("gy")))
+    n_faces = x_moves + y_moves
     f32 = jnp.float32
     shape_of = jax.ShapeDtypeStruct
-    face_shapes = [shape_of((second, local_modes), f32)] * x_swaps + [
+    face_shapes = [shape_of((second, local_modes), f32)] * x_moves + [
         shape_of((first, local_modes), f32)
-    ] * y_swaps
+    ] * y_moves
     packed_shape = shape_of((cells, local_modes), jnp.bfloat16)
     vector_shape = shape_of((cells, local_modes), f32)
-    near = [place for place in (0, 1) if place < count]
-    far = [place for place in range(count) if place not in near]
-    middle = [place for place in far if place % 2 == 0]
-    final = [place for place in far if place % 2 == 1]
+    near = [0]
+    final = [place for place in range(3, count) if place % 2 == 1]
+    middle = [place for place in range(1, count) if place not in final]
 
     start = right_side.reshape(cells, local_modes)
     packed = start.astype(jnp.bfloat16)
 
     def prepare(ins, outs, scratch):
         faces, (open_ref,) = outs[:n_faces], outs[n_faces:]
-        prepare_kernel(sizes, *ins, faces[:x_swaps], faces[x_swaps:], open_ref)
+        prepare_kernel(sizes, *ins, faces[:x_moves], faces[x_moves:], open_ref)
 
     *faces, open_cells = call(
         "prepare",
@@ -399,10 +397,8 @@
     vectors = [start]
     for section in range(KRYLOV):
         sources = {0: packed}
-        if count > 1:
-            sources[1] = exchange(packed, 1)
         held = gather_far(packed)
-        x_in, y_in = face_swaps({"gx": faces[:x_swaps], "gy": faces[x_swaps:]})
+        y_in, x_in = move_faces({"gx": faces[:x_moves], "gy": faces[x_moves:]})
 
         def near_step(cols, sources, rest, params, outs, scratch):
             blocks_ref, current_ref, open_ref = rest
@@ -415,7 +411,7 @@
             "near_%d" % section,
             near_step,
             [
-                [(SMEM, columns)],
+                in_vmem([columns]),
                 in_vmem([sources[place] for place in near]),
                 in_vmem([blocks, vectors[-1], open_cells]),
                 in_vmem([relax_rate, drift_speed, upwind_sign]),
@@ -424,7 +420,10 @@
             flops=work * len(near),
         )
 
-        held = dict(zip(held, hand_on(list(held.values()), [partial, *x_in, *y_in])))
+        if count > 1:
+            (own,) = hand_on([packed], [partial])
+            sources[1] = exchange(own, 1)
+        held = dict(zip(held, hand_on(list(held.values()), [partial, sources[1], *x_in, *y_in])))
         for place, array in held.items():
             sources[place] = array
             sources[place ^ 1] = exchange(array, 1)
@@ -438,7 +437,7 @@
             "middle_%d" % section,
             middle_step,
             [
-                [(SMEM, columns)],
+                in_vmem([columns]),
                 in_vmem([sources[place] for place in middle]),
                 in_vmem([blocks, partial, drift_speed, upwind_sign]),
                 in_vmem(x_in),
@@ -455,7 +454,7 @@
             if last:
                 named.gram = outs[0]
             else:
-                named.x, named.y = outs[:x_swaps], outs[x_swaps:n_faces]
+                named.x, named.y = outs[:x_moves], outs[x_moves:n_faces]
                 named.packed, named.value = outs[n_faces:]
             last_kernel(
                 sizes, per_owner, final, cols[0], sources, blocks_ref, partial_ref,
@@ -470,7 +469,7 @@
             "last_%d" % section,
             last_step,
             [
-                [(SMEM, columns)],
+                in_vmem([columns]),
                 in_vmem([sources[place] for place in final]),
                 in_vmem([blocks, partial, open_cells]),
                 in_vmem(vectors if last else []),

time: 52.4 us -> 68.2 us (1.30)
  waiting for transfers between devices: 2.01 us -> 22.5 us
  Pallas kernels: 12.1 us -> 7.12 us
  local copies, waits for them, and re-layouts: 1.73 us -> 3.59 us
  blocking collectives: 13.3 us -> 11.6 us
    ppermute x9, waiting for transfers between devices: 1.38 us -> 14.4 us  [exchange(): return lax.ppermute(array, 'mode', [(i, i ^ bit) for i in range(count)])]
    ppermute x9, waiting for transfers between devices: 0.63 us -> 8.08 us  [move_faces(): lax.ppermute(face, axis, pairs)]
    pallas_call x11, Pallas kernels: 12.1 us -> 7.11 us  [call(): pl.pallas_call(body, out_shape=list(shapes), in_specs=[spec for spec, ope...]
    unnamed x16, local copies, waits for them, and re-layouts: 1.73 us -> 3.59 us
    all_to_all x1, blocking collectives: 13.3 us -> 11.6 us  [per_device(): gram = lax.all_to_all(gram, AXES, 0, 0)]
  transfers between devices with their start and end apart: 18 -> 18, of which waited for: 7 -> 12; matrix products, arithmetic and copies ran while one was open for 0% -> 0% of each run, Pallas kernels for 15% -> 6%
where the time goes in v4:
time: 68.2 us; the launch traced here: 68 us
  waiting for transfers between devices  22.5 us (33%)
  starting transfers between devices  21.4 us (31%)
  blocking collectives  11.6 us (17%)
  Pallas kernels  7.12 us (10%)
  local copies, waits for them, and re-layouts  3.59 us (5%)
  other arithmetic  1.05 us (2%)
  between operations  0.73 us (1%)
    ppermute x9, starting transfers between devices, move_faces(): lax.ppermute(face, axis, pairs)  15.2 us
    ppermute x9, waiting for transfers between devices, exchange(): return lax.ppermute(array, 'mode', [(i, i ^ bit) for i in range(count)])  14.4 us
    all_to_all x1, blocking collectives, per_device(): gram = lax.all_to_all(gram, AXES, 0, 0)  11.6 us
    ppermute x9, waiting for transfers between devices, move_faces(): lax.ppermute(face, axis, pairs)  8.08 us
    pallas_call x11, Pallas kernels, call(): pl.pallas_call(body, out_shape=list(shapes), in_specs=[spec for spec, ope...  7.11 us
    ppermute x9, starting transfers between devices, exchange(): return lax.ppermute(array, 'mode', [(i, i ^ bit) for i in range(count)])  6.22 us
    unnamed x16, local copies, waits for them, and re-layouts  3.59 us
  transfers between devices with their start and end apart: 18, of which 12 were waited for; matrix products, arithmetic and copies ran while one was open for 0% of the time, Pallas kernels for 6%

profile of v4, /device:TPU:0, one launch (start us, length us, event | category | flops | bytes accessed | tf_op | source)
XLA Modules:
  0.0 68.0 jit_solution(18034311185153913329)
XLA Ops:
  0.6 1.0 %bitcast_convert_fusion.refs_1_.refs_0_ = bf16[64,1792]{1,0:T(8,128)(2,1)S(1)} fusion(f32[8,8,1792]{2,1,0:T(8,128)} %param.7), kind=kLoop, calls=%fused_computation | loop fusion | flops 114688 | bytes 688128 | tf_op jit(solution)/shard_map/convert_element_type | solution.py:381
  1.7 3.0 %collective-permute-start = (bf16[64,1792]{1,0:T(8,128)(2,1)S(1)}, bf16[64,1792]{1,0:T(8,128)(2,1)S(1)}, u32[]{:S(2)}, u32[]{:S(2)}) collective-permute-start(bf16[64,1792]{1,0:T(8,128)(2,1)S(1)} %bitcast_convert_fusion.refs_1_.refs_0_), channel_id=1, source_target_pairs={{0,16},{8,24},{16,0},{24,8},{1,17},{9,25},{17,1},{25,9},{2,18},{10... | collective-permute-start | bytes 688136 | tf_op jit(solution)/shard_map/ppermute | solution.py:38
  4.7 1.0 %copy-done.1 = f32[8,8,1792]{2,1,0:T(8,128)S(1)} copy-done((f32[8,8,1792]{2,1,0:T(8,128)S(1)}, f32[8,8,1792]{2,1,0:T(8,128)}, u32[]{:S(2)}) %copy-start.1) | copy-done | bytes 458776
  5.7 0.7 %copy-done.7 = s32[8,8]{1,0:T(8,128)S(1)} copy-done((s32[8,8]{1,0:T(8,128)S(1)}, s32[8,8]{1,0:T(8,128)}, u32[]{:S(2)}) %copy-start.7) | copy-done | bytes 280
  6.4 0.0 copy-start.6
  6.4 0.2 prepare.1
  6.6 1.9 %copy-done = bf16[14,8,128,128]{3,2,1,0:T(8,128)(2,1)S(1)} copy-done((bf16[14,8,128,128]{3,2,1,0:T(8,128)(2,1)S(1)}, bf16[14,8,128,128]{3,2,1,0:T(8,128)(2,1)}, u32[]{:S(2)}) %copy-start) | copy-done | bytes 3670040
  8.5 0.5 near_0.1.refs_1_.refs_4_
  9.0 1.3 %collective-permute-done.refs_0_ = bf16[64,1792]{1,0:T(8,128)(2,1)S(1)} collective-permute-done((bf16[64,1792]{1,0:T(8,128)(2,1)S(1)}, bf16[64,1792]{1,0:T(8,128)(2,1)S(1)}, u32[]{:S(2)}, u32[]{:S(2)}) %collective-permute-start) | collective-permute-done | bytes 229408 | tf_op jit(solution)/shard_map/ppermute | solution.py:38
  10.3 0.0 collective-permute-start.1
  10.3 1.7 %collective-permute-start.2 = (f32[8,1792]{1,0:T(8,128)S(1)}, f32[8,1792]{1,0:T(8,128)S(1)}, u32[]{:S(2)}, u32[]{:S(2)}) collective-permute-start(f32[8,1792]{1,0:T(8,128)S(1)} %get-tuple-element.19), channel_id=1, source_target_pairs={{0,4},{4,0},{1,5},{5,1},{2,6},{6,2},{3,7},{7,3},{8,12},{12,8},{9,1... | collective-permute-start | bytes 172040 | tf_op jit(solution)/shard_map/ppermute | solution.py:32
  12.0 1.6 %collective-permute-start.3 = (f32[8,1792]{1,0:T(8,128)S(1)}, f32[8,1792]{1,0:T(8,128)S(1)}, u32[]{:S(2)}, u32[]{:S(2)}) collective-permute-start(f32[8,1792]{1,0:T(8,128)S(1)} %get-tuple-element.20), channel_id=1, source_target_pairs={{0,1},{1,2},{2,3},{3,0},{4,5},{5,6},{6,7},{7,4},{8,9},{9,10},{10,1... | collective-permute-start | bytes 172040 | tf_op jit(solution)/shard_map/ppermute | solution.py:32
  13.6 2.2 %collective-permute-start.4 = (f32[8,1792]{1,0:T(8,128)S(1)}, f32[8,1792]{1,0:T(8,128)S(1)}, u32[]{:S(2)}, u32[]{:S(2)}) collective-permute-start(f32[8,1792]{1,0:T(8,128)S(1)} %get-tuple-element.21), channel_id=1, source_target_pairs={{0,3},{1,0},{2,1},{3,2},{4,7},{5,4},{6,5},{7,6},{8,11},{9,8},{10,9... | collective-permute-start | bytes 172040 | tf_op jit(solution)/shard_map/ppermute | solution.py:32
  15.9 0.0 collective-permute-done.2.refs_3_.refs_7_
  15.9 2.2 %collective-permute-done.3.refs_4_.refs_8_ = f32[8,1792]{1,0:T(8,128)S(1)} collective-permute-done((f32[8,1792]{1,0:T(8,128)S(1)}, f32[8,1792]{1,0:T(8,128)S(1)}, u32[]{:S(2)}, u32[]{:S(2)}) %collective-permute-start.3) | collective-permute-done | bytes 57376 | tf_op jit(solution)/shard_map/ppermute | solution.py:32
  18.1 0.5 collective-permute-done.4.refs_5_.refs_9_
  18.6 0.0 collective-permute-start.5
  18.6 0.8 %middle_0.1.refs_3_ = f32[64,1792]{1,0:T(8,128)S(1)} custom-call(s32[8,14]{1,0:T(8,128)S(1)} %bitcast.9, bf16[64,1792]{1,0:T(8,128)(2,1)S(1)} %collective-permute-done.1.refs_2_.refs_1_, bf16[64,1792]{1,0:T(8,128)(2,1)S(1)} %hand_on.7.refs_2_, bf16[14,8,128,128]{3,2,1,0:T(8,128)(2,1)S(1)} %copy-done, f32[64,1792]{1,0:T(8,128)S(1)} %near_0.1.refs_1_.refs_4_, ...), custom_call_target="tpu_custom_call" | custom-call | flops 117440512 | bytes 5247424 | tf_op jit(solution)/shard_map/middle_0/pallas_call | solution.py:343
  19.5 0.6 collective-permute-done.5.refs_1_
  20.1 0.5 last_0.1
  20.6 1.6 %collective-permute-start.6 = (bf16[64,1792]{1,0:T(8,128)(2,1)S(1)}, bf16[64,1792]{1,0:T(8,128)(2,1)S(1)}, u32[]{:S(2)}, u32[]{:S(2)}) collective-permute-start(bf16[64,1792]{1,0:T(8,128)(2,1)S(1)} %get-tuple-element.22.refs_1_.refs_0_), channel_id=1, source_target_pairs={{0,16},{8,24},{16,0},{24,8},{1,17},{9,25},{17,1},{25,9},{2,18},{10... | collective-permute-start | bytes 688136 | tf_op jit(solution)/shard_map/ppermute | solution.py:38
  22.2 0.5 near_1.1.refs_1_.refs_4_
  22.7 5.6 %collective-permute-done.6.refs_0_ = bf16[64,1792]{1,0:T(8,128)(2,1)S(1)} collective-permute-done((bf16[64,1792]{1,0:T(8,128)(2,1)S(1)}, bf16[64,1792]{1,0:T(8,128)(2,1)S(1)}, u32[]{:S(2)}, u32[]{:S(2)}) %collective-permute-start.6) | collective-permute-done | bytes 229408 | tf_op jit(solution)/shard_map/ppermute | solution.py:38
  28.3 0.5 collective-permute-start.8
  28.9 1.1 %collective-permute-start.9 = (f32[8,1792]{1,0:T(8,128)S(1)}, f32[8,1792]{1,0:T(8,128)S(1)}, u32[]{:S(2)}, u32[]{:S(2)}) collective-permute-start(f32[8,1792]{1,0:T(8,128)S(1)} %get-tuple-element.25), channel_id=1, source_target_pairs={{0,1},{1,2},{2,3},{3,0},{4,5},{5,6},{6,7},{7,4},{8,9},{9,10},{10,1... | collective-permute-start | bytes 172040 | tf_op jit(solution)/shard_map/ppermute | solution.py:32
  30.0 2.7 %collective-permute-start.10 = (f32[8,1792]{1,0:T(8,128)S(1)}, f32[8,1792]{1,0:T(8,128)S(1)}, u32[]{:S(2)}, u32[]{:S(2)}) collective-permute-start(f32[8,1792]{1,0:T(8,128)S(1)} %get-tuple-element.26), channel_id=1, source_target_pairs={{0,3},{1,0},{2,1},{3,2},{4,7},{5,4},{6,5},{7,6},{8,11},{9,8},{10,9... | collective-permute-start | bytes 172040 | tf_op jit(solution)/shard_map/ppermute | solution.py:32
  32.7 0.0 collective-permute-done.8.refs_3_.refs_7_
  32.7 2.6 %collective-permute-done.9.refs_4_.refs_8_ = f32[8,1792]{1,0:T(8,128)S(1)} collective-permute-done((f32[8,1792]{1,0:T(8,128)S(1)}, f32[8,1792]{1,0:T(8,128)S(1)}, u32[]{:S(2)}, u32[]{:S(2)}) %collective-permute-start.9) | collective-permute-done | bytes 57376 | tf_op jit(solution)/shard_map/ppermute | solution.py:32
  35.3 0.1 collective-permute-done.10.refs_5_.refs_9_
  35.4 0.0 collective-permute-done.7.refs_2_.refs_1_
  35.4 0.0 collective-permute-start.11
  35.4 0.8 %middle_1.1.refs_3_ = f32[64,1792]{1,0:T(8,128)S(1)} custom-call(s32[8,14]{1,0:T(8,128)S(1)} %bitcast.12, bf16[64,1792]{1,0:T(8,128)(2,1)S(1)} %collective-permute-done.7.refs_2_.refs_1_, bf16[64,1792]{1,0:T(8,128)(2,1)S(1)} %hand_on.9.refs_2_, bf16[14,8,128,128]{3,2,1,0:T(8,128)(2,1)S(1)} %copy-done, f32[64,1792]{1,0:T(8,128)S(1)} %near_1.1.refs_1_.refs_4_, ...), custom_call_target="tpu_custom_call" | custom-call | flops 117440512 | bytes 5247424 | tf_op jit(solution)/shard_map/middle_1/pallas_call | solution.py:343
  36.3 0.6 collective-permute-done.11.refs_1_
  36.9 0.5 last_1.1
  37.4 1.6 %collective-permute-start.12 = (bf16[64,1792]{1,0:T(8,128)(2,1)S(1)}, bf16[64,1792]{1,0:T(8,128)(2,1)S(1)}, u32[]{:S(2)}, u32[]{:S(2)}) collective-permute-start(bf16[64,1792]{1,0:T(8,128)(2,1)S(1)} %get-tuple-element.27.refs_1_.refs_0_), channel_id=1, source_target_pairs={{0,16},{8,24},{16,0},{24,8},{1,17},{9,25},{17,1},{25,9},{2,18},{10... | collective-permute-start | bytes 688136 | tf_op jit(solution)/shard_map/ppermute | solution.py:38
  39.0 0.5 near_2.1.refs_1_.refs_4_
  39.5 0.0 copy-start.2
  39.5 5.6 %collective-permute-done.12.refs_0_ = bf16[64,1792]{1,0:T(8,128)(2,1)S(1)} collective-permute-done((bf16[64,1792]{1,0:T(8,128)(2,1)S(1)}, bf16[64,1792]{1,0:T(8,128)(2,1)S(1)}, u32[]{:S(2)}, u32[]{:S(2)}) %collective-permute-start.12) | collective-permute-done | bytes 229408 | tf_op jit(solution)/shard_map/ppermute | solution.py:38
  45.1 1.5 %collective-permute-start.14 = (f32[8,1792]{1,0:T(8,128)S(1)}, f32[8,1792]{1,0:T(8,128)S(1)}, u32[]{:S(2)}, u32[]{:S(2)}) collective-permute-start(f32[8,1792]{1,0:T(8,128)S(1)} %get-tuple-element.29), channel_id=1, source_target_pairs={{0,4},{4,0},{1,5},{5,1},{2,6},{6,2},{3,7},{7,3},{8,12},{12,8},{9,1... | collective-permute-start | bytes 172040 | tf_op jit(solution)/shard_map/ppermute | solution.py:32
  46.6 1.1 %collective-permute-start.15 = (f32[8,1792]{1,0:T(8,128)S(1)}, f32[8,1792]{1,0:T(8,128)S(1)}, u32[]{:S(2)}, u32[]{:S(2)}) collective-permute-start(f32[8,1792]{1,0:T(8,128)S(1)} %get-tuple-element.30), channel_id=1, source_target_pairs={{0,1},{1,2},{2,3},{3,0},{4,5},{5,6},{6,7},{7,4},{8,9},{9,10},{10,1... | collective-permute-start | bytes 172040 | tf_op jit(solution)/shard_map/ppermute | solution.py:32
  47.7 2.7 %collective-permute-start.16 = (f32[8,1792]{1,0:T(8,128)S(1)}, f32[8,1792]{1,0:T(8,128)S(1)}, u32[]{:S(2)}, u32[]{:S(2)}) collective-permute-start(f32[8,1792]{1,0:T(8,128)S(1)} %get-tuple-element.31), channel_id=1, source_target_pairs={{0,3},{1,0},{2,1},{3,2},{4,7},{5,4},{6,5},{7,6},{8,11},{9,8},{10,9... | collective-permute-start | bytes 172040 | tf_op jit(solution)/shard_map/ppermute | solution.py:32
  50.5 2.4 %collective-permute-done.15.refs_4_.refs_8_ = f32[8,1792]{1,0:T(8,128)S(1)} collective-permute-done((f32[8,1792]{1,0:T(8,128)S(1)}, f32[8,1792]{1,0:T(8,128)S(1)}, u32[]{:S(2)}, u32[]{:S(2)}) %collective-permute-start.15) | collective-permute-done | bytes 57376 | tf_op jit(solution)/shard_map/ppermute | solution.py:32
  52.8 0.3 collective-permute-done.16.refs_5_.refs_9_
  53.1 0.8 %middle_2.1.refs_3_ = f32[64,1792]{1,0:T(8,128)S(1)} custom-call(s32[8,14]{1,0:T(8,128)S(1)} %bitcast.15, bf16[64,1792]{1,0:T(8,128)(2,1)S(1)} %collective-permute-done.13.refs_2_.refs_1_, bf16[64,1792]{1,0:T(8,128)(2,1)S(1)} %hand_on.11.refs_2_, bf16[14,8,128,128]{3,2,1,0:T(8,128)(2,1)S(1)} %copy-done, f32[64,1792]{1,0:T(8,128)S(1)} %near_2.1.refs_1_.refs_4_, ...), custom_call_target="tpu_custom_call" | custom-call | flops 117440512 | bytes 5247424 | tf_op jit(solution)/shard_map/middle_2/pallas_call | solution.py:343
  53.9 0.6 collective-permute-done.17.refs_1_
  54.6 0.7 %last_2.1 = f32[32,1,128]{2,1,0:T(1,128)S(1)} custom-call(s32[8,14]{1,0:T(8,128)S(1)} %bitcast.16, bf16[64,1792]{1,0:T(8,128)(2,1)S(1)} %collective-permute-done.17.refs_1_, bf16[14,8,128,128]{3,2,1,0:T(8,128)(2,1)S(1)} %copy-done, f32[64,1792]{1,0:T(8,128)S(1)} %middle_2.1.refs_3_, f32[64,128]{1,0:T(8,128)S(1)} %get-tuple-element.18.refs_4_, ...), custom_call_target="tpu_custom_call" | custom-call | flops 58720256 | bytes 5784000 | tf_op jit(solution)/shard_map/last_2/pallas_call | solution.py:343
  55.3 11.6 %all_to_all.5.refs_0_ = f32[32,1,128]{2,1,0:T(1,128)S(1)} all-to-all(f32[32,1,128]{2,1,0:T(1,128)S(1)} %last_2.1), channel_id=1, replica_groups=mesh['mode'=4,'gx'=2,'gy'=4] {'mode','gx','gy'}, dimensions={0} | all-to-all | bytes 32768 | tf_op jit(solution)/shard_map/all_to_all | solution.py:486
  66.9 1.1 %finish.1 = (f32[64,1792]{1,0:T(8,128)}, f32[4,3]{1,0:T(4,128)}) custom-call(f32[32,1,128]{2,1,0:T(1,128)S(1)} %all_to_all.5.refs_0_, f32[64,1792]{1,0:T(8,128)S(1)} %bitcast.7, f32[64,1792]{1,0:T(8,128)S(1)} %get-tuple-element.23.refs_3_.refs_6_.refs_2_, f32[64,1792]{1,0:T(8,128)S(1)} %get-tuple-element.28.refs_3_.refs_7_), custom_call_target="tpu_custom_call" | custom-call | bytes 1851440 | tf_op jit(solution)/shard_map/finish/pallas_call | solution.py:343
  (23 shorter events, 0.0 us)
Async XLA Ops:
  1.7 8.6 %collective-permute-start = (bf16[64,1792]{1,0:T(8,128)(2,1)S(1)}, bf16[64,1792]{1,0:T(8,128)(2,1)S(1)}, u32[]{:S(2)}, u32[]{:S(2)}) collective-permute-start(bf16[64,1792]{1,0:T(8,128)(2,1)S(1)} %bitcast_convert_fusion.refs_1_.refs_0_), channel_id=1, source_target_pairs={{0,16},{8,24},{16,0},{24,8},{1,17},{9,25},{17,1},{25,9},{2,18},{10... | collective-permute-start | bytes 688136 | tf_op jit(solution)/shard_map/ppermute | solution.py:38
  4.7 1.0 %copy-start.1 = (f32[8,8,1792]{2,1,0:T(8,128)S(1)}, f32[8,8,1792]{2,1,0:T(8,128)}, u32[]{:S(2)}) copy-start(f32[8,8,1792]{2,1,0:T(8,128)} %param.7) | copy-start | bytes 1376260
  5.7 0.7 %copy-start.7 = (s32[8,8]{1,0:T(8,128)S(1)}, s32[8,8]{1,0:T(8,128)}, u32[]{:S(2)}) copy-start(s32[8,8]{1,0:T(8,128)} %refs_1_.1) | copy-start | bytes 772
  6.4 2.0 %copy-start = (bf16[14,8,128,128]{3,2,1,0:T(8,128)(2,1)S(1)}, bf16[14,8,128,128]{3,2,1,0:T(8,128)(2,1)}, u32[]{:S(2)}) copy-start(bf16[14,8,128,128]{3,2,1,0:T(8,128)(2,1)} %refs_2_.11) | copy-start | bytes 11010052
  6.4 2.0 %copy-start.3 = (f32[2,1792]{1,0:T(2,128)S(1)}, f32[2,1792]{1,0:T(2,128)}, u32[]{:S(2)}) copy-start(f32[2,1792]{1,0:T(2,128)} %refs_5_.11) | copy-start | bytes 43012
  6.4 2.0 %copy-start.4 = (s32[2,1792]{1,0:T(2,128)S(1)}, s32[2,1792]{1,0:T(2,128)}, u32[]{:S(2)}) copy-start(s32[2,1792]{1,0:T(2,128)} %refs_6_.11) | copy-start | bytes 43012
  6.4 2.0 %copy-start.5 = (s32[14,8]{0,1:T(8,128)S(1)}, s32[14,8]{0,1:T(8,128)}, u32[]{:S(2)}) copy-start(s32[14,8]{0,1:T(8,128)} %param.8) | copy-start | bytes 1348
  6.4 2.0 %copy-start.6 = (f32[1792]{0:T(1024)S(1)}, f32[1792]{0:T(1024)}, u32[]{:S(2)}) copy-start(f32[1792]{0:T(1024)} %refs_5_.10) | copy-start | bytes 21508
  10.3 8.3 %collective-permute-start.1 = (bf16[64,1792]{1,0:T(8,128)(2,1)S(1)}, bf16[64,1792]{1,0:T(8,128)(2,1)S(1)}, u32[]{:S(2)}, u32[]{:S(2)}) collective-permute-start(bf16[64,1792]{1,0:T(8,128)(2,1)S(1)} %hand_on.6), channel_id=1, source_target_pairs={{0,8},{8,0},{16,24},{24,16},{1,9},{9,1},{17,25},{25,17},{2,10},{10... | collective-permute-start | bytes 688136 | tf_op jit(solution)/shard_map/ppermute | solution.py:38
  10.3 5.5 %collective-permute-start.2 = (f32[8,1792]{1,0:T(8,128)S(1)}, f32[8,1792]{1,0:T(8,128)S(1)}, u32[]{:S(2)}, u32[]{:S(2)}) collective-permute-start(f32[8,1792]{1,0:T(8,128)S(1)} %get-tuple-element.19), channel_id=1, source_target_pairs={{0,4},{4,0},{1,5},{5,1},{2,6},{6,2},{3,7},{7,3},{8,12},{12,8},{9,1... | collective-permute-start | bytes 172040 | tf_op jit(solution)/shard_map/ppermute | solution.py:32
  12.0 6.0 %collective-permute-start.3 = (f32[8,1792]{1,0:T(8,128)S(1)}, f32[8,1792]{1,0:T(8,128)S(1)}, u32[]{:S(2)}, u32[]{:S(2)}) collective-permute-start(f32[8,1792]{1,0:T(8,128)S(1)} %get-tuple-element.20), channel_id=1, source_target_pairs={{0,1},{1,2},{2,3},{3,0},{4,5},{5,6},{6,7},{7,4},{8,9},{9,10},{10,1... | collective-permute-start | bytes 172040 | tf_op jit(solution)/shard_map/ppermute | solution.py:32
  13.6 5.0 %collective-permute-start.4 = (f32[8,1792]{1,0:T(8,128)S(1)}, f32[8,1792]{1,0:T(8,128)S(1)}, u32[]{:S(2)}, u32[]{:S(2)}) collective-permute-start(f32[8,1792]{1,0:T(8,128)S(1)} %get-tuple-element.21), channel_id=1, source_target_pairs={{0,3},{1,0},{2,1},{3,2},{4,7},{5,4},{6,5},{7,6},{8,11},{9,8},{10,9... | collective-permute-start | bytes 172040 | tf_op jit(solution)/shard_map/ppermute | solution.py:32
  18.6 1.5 %collective-permute-start.5 = (bf16[64,1792]{1,0:T(8,128)(2,1)S(1)}, bf16[64,1792]{1,0:T(8,128)(2,1)S(1)}, u32[]{:S(2)}, u32[]{:S(2)}) collective-permute-start(bf16[64,1792]{1,0:T(8,128)(2,1)S(1)} %hand_on.7.refs_2_), channel_id=1, source_target_pairs={{0,8},{8,0},{16,24},{24,16},{1,9},{9,1},{17,25},{25,17},{2,10},{10... | collective-permute-start | bytes 688136 | tf_op jit(solution)/shard_map/ppermute | solution.py:38
  20.6 7.7 %collective-permute-start.6 = (bf16[64,1792]{1,0:T(8,128)(2,1)S(1)}, bf16[64,1792]{1,0:T(8,128)(2,1)S(1)}, u32[]{:S(2)}, u32[]{:S(2)}) collective-permute-start(bf16[64,1792]{1,0:T(8,128)(2,1)S(1)} %get-tuple-element.22.refs_1_.refs_0_), channel_id=1, source_target_pairs={{0,16},{8,24},{16,0},{24,8},{1,17},{9,25},{17,1},{25,9},{2,18},{10... | collective-permute-start | bytes 688136 | tf_op jit(solution)/shard_map/ppermute | solution.py:38
  28.3 7.1 %collective-permute-start.7 = (bf16[64,1792]{1,0:T(8,128)(2,1)S(1)}, bf16[64,1792]{1,0:T(8,128)(2,1)S(1)}, u32[]{:S(2)}, u32[]{:S(2)}) collective-permute-start(bf16[64,1792]{1,0:T(8,128)(2,1)S(1)} %hand_on.8), channel_id=1, source_target_pairs={{0,8},{8,0},{16,24},{24,16},{1,9},{9,1},{17,25},{25,17},{2,10},{10... | collective-permute-start | bytes 688136 | tf_op jit(solution)/shard_map/ppermute | solution.py:38
  28.3 4.4 %collective-permute-start.8 = (f32[8,1792]{1,0:T(8,128)S(1)}, f32[8,1792]{1,0:T(8,128)S(1)}, u32[]{:S(2)}, u32[]{:S(2)}) collective-permute-start(f32[8,1792]{1,0:T(8,128)S(1)} %get-tuple-element.24), channel_id=1, source_target_pairs={{0,4},{4,0},{1,5},{5,1},{2,6},{6,2},{3,7},{7,3},{8,12},{12,8},{9,1... | collective-permute-start | bytes 172040 | tf_op jit(solution)/shard_map/ppermute | solution.py:32
  28.9 6.4 %collective-permute-start.9 = (f32[8,1792]{1,0:T(8,128)S(1)}, f32[8,1792]{1,0:T(8,128)S(1)}, u32[]{:S(2)}, u32[]{:S(2)}) collective-permute-start(f32[8,1792]{1,0:T(8,128)S(1)} %get-tuple-element.25), channel_id=1, source_target_pairs={{0,1},{1,2},{2,3},{3,0},{4,5},{5,6},{6,7},{7,4},{8,9},{9,10},{10,1... | collective-permute-start | bytes 172040 | tf_op jit(solution)/shard_map/ppermute | solution.py:32
  30.0 5.4 %collective-permute-start.10 = (f32[8,1792]{1,0:T(8,128)S(1)}, f32[8,1792]{1,0:T(8,128)S(1)}, u32[]{:S(2)}, u32[]{:S(2)}) collective-permute-start(f32[8,1792]{1,0:T(8,128)S(1)} %get-tuple-element.26), channel_id=1, source_target_pairs={{0,3},{1,0},{2,1},{3,2},{4,7},{5,4},{6,5},{7,6},{8,11},{9,8},{10,9... | collective-permute-start | bytes 172040 | tf_op jit(solution)/shard_map/ppermute | solution.py:32
  35.4 1.5 %collective-permute-start.11 = (bf16[64,1792]{1,0:T(8,128)(2,1)S(1)}, bf16[64,1792]{1,0:T(8,128)(2,1)S(1)}, u32[]{:S(2)}, u32[]{:S(2)}) collective-permute-start(bf16[64,1792]{1,0:T(8,128)(2,1)S(1)} %hand_on.9.refs_2_), channel_id=1, source_target_pairs={{0,8},{8,0},{16,24},{24,16},{1,9},{9,1},{17,25},{25,17},{2,10},{10... | collective-permute-start | bytes 688136 | tf_op jit(solution)/shard_map/ppermute | solution.py:38
  37.4 7.7 %collective-permute-start.12 = (bf16[64,1792]{1,0:T(8,128)(2,1)S(1)}, bf16[64,1792]{1,0:T(8,128)(2,1)S(1)}, u32[]{:S(2)}, u32[]{:S(2)}) collective-permute-start(bf16[64,1792]{1,0:T(8,128)(2,1)S(1)} %get-tuple-element.27.refs_1_.refs_0_), channel_id=1, source_target_pairs={{0,16},{8,24},{16,0},{24,8},{1,17},{9,25},{17,1},{25,9},{2,18},{10... | collective-permute-start | bytes 688136 | tf_op jit(solution)/shard_map/ppermute | solution.py:38
  39.5 15.1 %copy-start.2 = (f32[8,8,1792]{2,1,0:T(8,128)S(1)}, f32[8,8,1792]{2,1,0:T(8,128)}, u32[]{:S(2)}) copy-start(f32[8,8,1792]{2,1,0:T(8,128)} %param.7) | copy-start | bytes 1376260
  45.1 8.0 %collective-permute-start.13 = (bf16[64,1792]{1,0:T(8,128)(2,1)S(1)}, bf16[64,1792]{1,0:T(8,128)(2,1)S(1)}, u32[]{:S(2)}, u32[]{:S(2)}) collective-permute-start(bf16[64,1792]{1,0:T(8,128)(2,1)S(1)} %hand_on.10), channel_id=1, source_target_pairs={{0,8},{8,0},{16,24},{24,16},{1,9},{9,1},{17,25},{25,17},{2,10},{10... | collective-permute-start | bytes 688136 | tf_op jit(solution)/shard_map/ppermute | solution.py:38
  45.1 5.3 %collective-permute-start.14 = (f32[8,1792]{1,0:T(8,128)S(1)}, f32[8,1792]{1,0:T(8,128)S(1)}, u32[]{:S(2)}, u32[]{:S(2)}) collective-permute-start(f32[8,1792]{1,0:T(8,128)S(1)} %get-tuple-element.29), channel_id=1, source_target_pairs={{0,4},{4,0},{1,5},{5,1},{2,6},{6,2},{3,7},{7,3},{8,12},{12,8},{9,1... | collective-permute-start | bytes 172040 | tf_op jit(solution)/shard_map/ppermute | solution.py:32
  46.6 6.2 %collective-permute-start.15 = (f32[8,1792]{1,0:T(8,128)S(1)}, f32[8,1792]{1,0:T(8,128)S(1)}, u32[]{:S(2)}, u32[]{:S(2)}) collective-permute-start(f32[8,1792]{1,0:T(8,128)S(1)} %get-tuple-element.30), channel_id=1, source_target_pairs={{0,1},{1,2},{2,3},{3,0},{4,5},{5,6},{6,7},{7,4},{8,9},{9,10},{10,1... | collective-permute-start | bytes 172040 | tf_op jit(solution)/shard_map/ppermute | solution.py:32
  47.7 5.4 %collective-permute-start.16 = (f32[8,1792]{1,0:T(8,128)S(1)}, f32[8,1792]{1,0:T(8,128)S(1)}, u32[]{:S(2)}, u32[]{:S(2)}) collective-permute-start(f32[8,1792]{1,0:T(8,128)S(1)} %get-tuple-element.31), channel_id=1, source_target_pairs={{0,3},{1,0},{2,1},{3,2},{4,7},{5,4},{6,5},{7,6},{8,11},{9,8},{10,9... | collective-permute-start | bytes 172040 | tf_op jit(solution)/shard_map/ppermute | solution.py:32
  53.1 1.5 %collective-permute-start.17 = (bf16[64,1792]{1,0:T(8,128)(2,1)S(1)}, bf16[64,1792]{1,0:T(8,128)(2,1)S(1)}, u32[]{:S(2)}, u32[]{:S(2)}) collective-permute-start(bf16[64,1792]{1,0:T(8,128)(2,1)S(1)} %hand_on.11.refs_2_), channel_id=1, source_target_pairs={{0,8},{8,0},{16,24},{24,16},{1,9},{9,1},{17,25},{25,17},{2,10},{10... | collective-permute-start | bytes 688136 | tf_op jit(solution)/shard_map/ppermute | solution.py:38

commit v5 on v4

--- a/solution.py
+++ b/solution.py
@@ -373,9 +373,9 @@
     ] * y_moves
     packed_shape = shape_of((cells, local_modes), jnp.bfloat16)
     vector_shape = shape_of((cells, local_modes), f32)
-    near = [0]
+    near = [place for place in (0, 1) if place < count]
     final = [place for place in range(3, count) if place % 2 == 1]
-    middle = [place for place in range(1, count) if place not in final]
+    middle = [place for place in range(2, count) if place not in final]
 
     start = right_side.reshape(cells, local_modes)
     packed = start.astype(jnp.bfloat16)
@@ -397,6 +397,8 @@
     vectors = [start]
     for section in range(KRYLOV):
         sources = {0: packed}
+        if count > 1:
+            sources[1] = exchange(packed, 1)
         held = gather_far(packed)
         y_in, x_in = move_faces({"gx": faces[:x_moves], "gy": faces[x_moves:]})
 
@@ -420,10 +422,7 @@
             flops=work * len(near),
         )
 
-        if count > 1:
-            (own,) = hand_on([packed], [partial])
-            sources[1] = exchange(own, 1)
-        held = dict(zip(held, hand_on(list(held.values()), [partial, sources[1], *x_in, *y_in])))
+        held = dict(zip(held, hand_on(list(held.values()), [partial, *x_in, *y_in])))
         for place, array in held.items():
             sources[place] = array
             sources[place ^ 1] = exchange(array, 1)

time: 68.2 us -> 50.5 us (0.74)
  waiting for transfers between devices: 22.5 us -> 8.46 us
  local copies, waits for them, and re-layouts: 3.59 us -> 1.73 us
  starting transfers between devices: 21.4 us -> 20.3 us
  blocking collectives: 11.6 us -> 10.8 us
    ppermute x9, waiting for transfers between devices: 14.4 us -> 3.02 us  [exchange(): return lax.ppermute(array, 'mode', [(i, i ^ bit) for i in range(count)])]
    ppermute x9, waiting for transfers between devices: 8.08 us -> 5.44 us  [move_faces(): lax.ppermute(face, axis, pairs)]
    unnamed x16, local copies, waits for them, and re-layouts: 3.59 us -> 1.73 us
    ppermute x9, starting transfers between devices: 6.22 us -> 5.29 us  [exchange(): return lax.ppermute(array, 'mode', [(i, i ^ bit) for i in range(count)])]
    all_to_all x1, blocking collectives: 11.6 us -> 10.8 us  [per_device(): gram = lax.all_to_all(gram, AXES, 0, 0)]
  transfers between devices with their start and end apart: 18 -> 18, of which waited for: 12 -> 8; matrix products, arithmetic and copies ran while one was open for 0% -> 0% of each run, Pallas kernels for 6% -> 9%
where the time goes in v5:
time: 50.5 us; the launch traced here: 50.2 us
  starting transfers between devices  20.3 us (40%)
  blocking collectives  10.8 us (21%)
  waiting for transfers between devices  8.46 us (17%)
  Pallas kernels  7.09 us (14%)
  local copies, waits for them, and re-layouts  1.73 us (3%)
  other arithmetic  1.05 us (2%)
  between operations  0.78 us (2%)
    ppermute x9, starting transfers between devices, move_faces(): lax.ppermute(face, axis, pairs)  15.1 us
    all_to_all x1, blocking collectives, per_device(): gram = lax.all_to_all(gram, AXES, 0, 0)  10.8 us
    pallas_call x11, Pallas kernels, call(): pl.pallas_call(body, out_shape=list(shapes), in_specs=[spec for spec, ope...  7.09 us
    ppermute x9, waiting for transfers between devices, move_faces(): lax.ppermute(face, axis, pairs)  5.44 us
    ppermute x9, starting transfers between devices, exchange(): return lax.ppermute(array, 'mode', [(i, i ^ bit) for i in range(count)])  5.29 us
    ppermute x9, waiting for transfers between devices, exchange(): return lax.ppermute(array, 'mode', [(i, i ^ bit) for i in range(count)])  3.02 us
    unnamed x16, local copies, waits for them, and re-layouts  1.73 us
    convert_element_type x1, other arithmetic, per_device(): packed = start.astype(jnp.bfloat16)  1.05 us
  transfers between devices with their start and end apart: 18, of which 8 were waited for; matrix products, arithmetic and copies ran while one was open for 0% of the time, Pallas kernels for 9%

profile of v5, /device:TPU:0, one launch (start us, length us, event | category | flops | bytes accessed | tf_op | source)
XLA Modules:
  0.0 50.2 jit_solution(199645567629206347)
XLA Ops:
  0.6 1.0 %bitcast_convert_fusion.refs_1_ = bf16[64,1792]{1,0:T(8,128)(2,1)S(1)} fusion(f32[8,8,1792]{2,1,0:T(8,128)} %param.7), kind=kLoop, calls=%fused_computation | loop fusion | flops 114688 | bytes 688128 | tf_op jit(solution)/shard_map/convert_element_type | solution.py:381
  1.7 0.5 %collective-permute-start.1 = (bf16[64,1792]{1,0:T(8,128)(2,1)S(1)}, bf16[64,1792]{1,0:T(8,128)(2,1)S(1)}, u32[]{:S(2)}, u32[]{:S(2)}) collective-permute-start(bf16[64,1792]{1,0:T(8,128)(2,1)S(1)} %bitcast_convert_fusion.refs_1_), channel_id=1, source_target_pairs={{0,8},{8,0},{16,24},{24,16},{1,9},{9,1},{17,25},{25,17},{2,10},{10... | collective-permute-start | bytes 688136 | tf_op jit(solution)/shard_map/ppermute | solution.py:38
  2.2 2.6 %collective-permute-start = (bf16[64,1792]{1,0:T(8,128)(2,1)S(1)}, bf16[64,1792]{1,0:T(8,128)(2,1)S(1)}, u32[]{:S(2)}, u32[]{:S(2)}) collective-permute-start(bf16[64,1792]{1,0:T(8,128)(2,1)S(1)} %bitcast_convert_fusion.refs_1_), channel_id=1, source_target_pairs={{0,16},{8,24},{16,0},{24,8},{1,17},{9,25},{17,1},{25,9},{2,18},{10... | collective-permute-start | bytes 688136 | tf_op jit(solution)/shard_map/ppermute | solution.py:38
  4.8 1.0 %copy-done.1 = f32[8,8,1792]{2,1,0:T(8,128)S(1)} copy-done((f32[8,8,1792]{2,1,0:T(8,128)S(1)}, f32[8,8,1792]{2,1,0:T(8,128)}, u32[]{:S(2)}) %copy-start.1) | copy-done | bytes 458776
  5.8 0.7 %copy-done.7 = s32[8,8]{1,0:T(8,128)S(1)} copy-done((s32[8,8]{1,0:T(8,128)S(1)}, s32[8,8]{1,0:T(8,128)}, u32[]{:S(2)}) %copy-start.7) | copy-done | bytes 280
  6.5 0.0 copy-start.6
  6.5 0.2 prepare.1
  6.7 1.6 %collective-permute-start.2 = (f32[8,1792]{1,0:T(8,128)S(1)}, f32[8,1792]{1,0:T(8,128)S(1)}, u32[]{:S(2)}, u32[]{:S(2)}) collective-permute-start(f32[8,1792]{1,0:T(8,128)S(1)} %get-tuple-element.19), channel_id=1, source_target_pairs={{0,4},{4,0},{1,5},{5,1},{2,6},{6,2},{3,7},{7,3},{8,12},{12,8},{9,1... | collective-permute-start | bytes 172040 | tf_op jit(solution)/shard_map/ppermute | solution.py:32
  8.2 1.6 %collective-permute-start.3 = (f32[8,1792]{1,0:T(8,128)S(1)}, f32[8,1792]{1,0:T(8,128)S(1)}, u32[]{:S(2)}, u32[]{:S(2)}) collective-permute-start(f32[8,1792]{1,0:T(8,128)S(1)} %get-tuple-element.20), channel_id=1, source_target_pairs={{0,1},{1,2},{2,3},{3,0},{4,5},{5,6},{6,7},{7,4},{8,9},{9,10},{10,1... | collective-permute-start | bytes 172040 | tf_op jit(solution)/shard_map/ppermute | solution.py:32
  9.8 2.2 %collective-permute-start.4 = (f32[8,1792]{1,0:T(8,128)S(1)}, f32[8,1792]{1,0:T(8,128)S(1)}, u32[]{:S(2)}, u32[]{:S(2)}) collective-permute-start(f32[8,1792]{1,0:T(8,128)S(1)} %get-tuple-element.21), channel_id=1, source_target_pairs={{0,3},{1,0},{2,1},{3,2},{4,7},{5,4},{6,5},{7,6},{8,11},{9,8},{10,9... | collective-permute-start | bytes 172040 | tf_op jit(solution)/shard_map/ppermute | solution.py:32
  12.1 0.0 collective-permute-done.1.refs_2_
  12.1 0.9 %near_0.1.refs_1_.refs_3_ = f32[64,1792]{1,0:T(8,128)S(1)} custom-call(s32[8,14]{1,0:T(8,128)S(1)} %bitcast.8, bf16[64,1792]{1,0:T(8,128)(2,1)S(1)} %bitcast_convert_fusion.refs_1_, bf16[64,1792]{1,0:T(8,128)(2,1)S(1)} %collective-permute-done.1.refs_2_, bf16[14,8,128,128]{3,2,1,0:T(8,128)(2,1)S(1)} %copy-done, f32[64,1792]{1,0:T(8,128)S(1)} %bitcast.5, ...), custom_call_target="tpu_custom_call" | custom-call | flops 117440512 | bytes 5115328 | tf_op jit(solution)/shard_map/near_0/pallas_call | solution.py:343
  13.0 0.0 collective-permute-done.2.refs_2_.refs_6_
  13.0 1.5 %collective-permute-done.3.refs_3_.refs_7_ = f32[8,1792]{1,0:T(8,128)S(1)} collective-permute-done((f32[8,1792]{1,0:T(8,128)S(1)}, f32[8,1792]{1,0:T(8,128)S(1)}, u32[]{:S(2)}, u32[]{:S(2)}) %collective-permute-start.3) | collective-permute-done | bytes 57376 | tf_op jit(solution)/shard_map/ppermute | solution.py:32
  14.5 0.1 collective-permute-done.4.refs_4_.refs_8_
  14.6 0.0 collective-permute-done.refs_0_
  14.6 0.0 collective-permute-start.5
  14.6 0.5 %middle_0.1.refs_3_ = f32[64,1792]{1,0:T(8,128)S(1)} custom-call(s32[8,14]{1,0:T(8,128)S(1)} %bitcast.9, bf16[64,1792]{1,0:T(8,128)(2,1)S(1)} %hand_on.3.refs_1_, bf16[14,8,128,128]{3,2,1,0:T(8,128)(2,1)S(1)} %copy-done, f32[64,1792]{1,0:T(8,128)S(1)} %near_0.1.refs_1_.refs_3_, f32[2,1792]{1,0:T(2,128)S(1)} %copy-done.3, s32[2,1792]{1,0:T(2,128)S(1)} %copy-done.4, ...), custom_call_target="tpu_custom_call" | custom-call | flops 58720256 | bytes 5018048 | tf_op jit(solution)/shard_map/middle_0/pallas_call | solution.py:343
  15.1 0.9 %collective-permute-done.5.refs_1_ = bf16[64,1792]{1,0:T(8,128)(2,1)S(1)} collective-permute-done((bf16[64,1792]{1,0:T(8,128)(2,1)S(1)}, bf16[64,1792]{1,0:T(8,128)(2,1)S(1)}, u32[]{:S(2)}, u32[]{:S(2)}) %collective-permute-start.5) | collective-permute-done | bytes 229408 | tf_op jit(solution)/shard_map/ppermute | solution.py:38
  16.1 0.5 %last_0.1 = (f32[8,1792]{1,0:T(8,128)S(1)}, f32[8,1792]{1,0:T(8,128)S(1)}, f32[8,1792]{1,0:T(8,128)S(1)}, bf16[64,1792]{1,0:T(8,128)(2,1)S(1)}, f32[64,1792]{1,0:T(8,128)S(1)}) custom-call(s32[8,14]{1,0:T(8,128)S(1)} %bitcast.10, bf16[64,1792]{1,0:T(8,128)(2,1)S(1)} %collective-permute-done.5.refs_1_, bf16[14,8,128,128]{3,2,1,0:T(8,128)(2,1)S(1)} %copy-done, ...), custom_call_target="tpu_custom_call" | custom-call | flops 58720256 | bytes 5251520 | tf_op jit(solution)/shard_map/last_0/pallas_call | solution.py:343
  16.6 0.2 collective-permute-start.7
  16.8 0.5 %collective-permute-start.6 = (bf16[64,1792]{1,0:T(8,128)(2,1)S(1)}, bf16[64,1792]{1,0:T(8,128)(2,1)S(1)}, u32[]{:S(2)}, u32[]{:S(2)}) collective-permute-start(bf16[64,1792]{1,0:T(8,128)(2,1)S(1)} %get-tuple-element.22.refs_1_), channel_id=1, source_target_pairs={{0,16},{8,24},{16,0},{24,8},{1,17},{9,25},{17,1},{25,9},{2,18},{10... | collective-permute-start | bytes 688136 | tf_op jit(solution)/shard_map/ppermute | solution.py:38
  17.4 0.5 %collective-permute-start.8 = (f32[8,1792]{1,0:T(8,128)S(1)}, f32[8,1792]{1,0:T(8,128)S(1)}, u32[]{:S(2)}, u32[]{:S(2)}) collective-permute-start(f32[8,1792]{1,0:T(8,128)S(1)} %get-tuple-element.24), channel_id=1, source_target_pairs={{0,4},{4,0},{1,5},{5,1},{2,6},{6,2},{3,7},{7,3},{8,12},{12,8},{9,1... | collective-permute-start | bytes 172040 | tf_op jit(solution)/shard_map/ppermute | solution.py:32
  17.9 1.0 %collective-permute-start.9 = (f32[8,1792]{1,0:T(8,128)S(1)}, f32[8,1792]{1,0:T(8,128)S(1)}, u32[]{:S(2)}, u32[]{:S(2)}) collective-permute-start(f32[8,1792]{1,0:T(8,128)S(1)} %get-tuple-element.25), channel_id=1, source_target_pairs={{0,1},{1,2},{2,3},{3,0},{4,5},{5,6},{6,7},{7,4},{8,9},{9,10},{10,1... | collective-permute-start | bytes 172040 | tf_op jit(solution)/shard_map/ppermute | solution.py:32
  18.9 2.8 %collective-permute-start.10 = (f32[8,1792]{1,0:T(8,128)S(1)}, f32[8,1792]{1,0:T(8,128)S(1)}, u32[]{:S(2)}, u32[]{:S(2)}) collective-permute-start(f32[8,1792]{1,0:T(8,128)S(1)} %get-tuple-element.26), channel_id=1, source_target_pairs={{0,3},{1,0},{2,1},{3,2},{4,7},{5,4},{6,5},{7,6},{8,11},{9,8},{10,9... | collective-permute-start | bytes 172040 | tf_op jit(solution)/shard_map/ppermute | solution.py:32
  21.7 0.0 collective-permute-done.7.refs_2_
  21.7 0.8 %near_1.1.refs_1_.refs_3_ = f32[64,1792]{1,0:T(8,128)S(1)} custom-call(s32[8,14]{1,0:T(8,128)S(1)} %bitcast.11, bf16[64,1792]{1,0:T(8,128)(2,1)S(1)} %get-tuple-element.22.refs_1_, bf16[64,1792]{1,0:T(8,128)(2,1)S(1)} %collective-permute-done.7.refs_2_, bf16[14,8,128,128]{3,2,1,0:T(8,128)(2,1)S(1)} %copy-done, ...), custom_call_target="tpu_custom_call" | custom-call | flops 117440512 | bytes 5115328 | tf_op jit(solution)/shard_map/near_1/pallas_call | solution.py:343
  22.6 0.0 collective-permute-done.8.refs_2_.refs_6_
  22.6 2.0 %collective-permute-done.9.refs_3_.refs_7_ = f32[8,1792]{1,0:T(8,128)S(1)} collective-permute-done((f32[8,1792]{1,0:T(8,128)S(1)}, f32[8,1792]{1,0:T(8,128)S(1)}, u32[]{:S(2)}, u32[]{:S(2)}) %collective-permute-start.9) | collective-permute-done | bytes 57376 | tf_op jit(solution)/shard_map/ppermute | solution.py:32
  24.5 0.2 collective-permute-done.6.refs_0_
  24.7 0.5 %middle_1.1.refs_3_ = f32[64,1792]{1,0:T(8,128)S(1)} custom-call(s32[8,14]{1,0:T(8,128)S(1)} %bitcast.12, bf16[64,1792]{1,0:T(8,128)(2,1)S(1)} %hand_on.4.refs_1_, bf16[14,8,128,128]{3,2,1,0:T(8,128)(2,1)S(1)} %copy-done, f32[64,1792]{1,0:T(8,128)S(1)} %near_1.1.refs_1_.refs_3_, f32[2,1792]{1,0:T(2,128)S(1)} %copy-done.3, s32[2,1792]{1,0:T(2,128)S(1)} %copy-done.4, ...), custom_call_target="tpu_custom_call" | custom-call | flops 58720256 | bytes 5018048 | tf_op jit(solution)/shard_map/middle_1/pallas_call | solution.py:343
  25.2 1.0 %collective-permute-done.11.refs_1_ = bf16[64,1792]{1,0:T(8,128)(2,1)S(1)} collective-permute-done((bf16[64,1792]{1,0:T(8,128)(2,1)S(1)}, bf16[64,1792]{1,0:T(8,128)(2,1)S(1)}, u32[]{:S(2)}, u32[]{:S(2)}) %collective-permute-start.11) | collective-permute-done | bytes 229408 | tf_op jit(solution)/shard_map/ppermute | solution.py:38
  26.2 0.5 %last_1.1 = (f32[8,1792]{1,0:T(8,128)S(1)}, f32[8,1792]{1,0:T(8,128)S(1)}, f32[8,1792]{1,0:T(8,128)S(1)}, bf16[64,1792]{1,0:T(8,128)(2,1)S(1)}, f32[64,1792]{1,0:T(8,128)S(1)}) custom-call(s32[8,14]{1,0:T(8,128)S(1)} %bitcast.13, bf16[64,1792]{1,0:T(8,128)(2,1)S(1)} %collective-permute-done.11.refs_1_, bf16[14,8,128,128]{3,2,1,0:T(8,128)(2,1)S(1)} %copy-done, ...), custom_call_target="tpu_custom_call" | custom-call | flops 58720256 | bytes 5251520 | tf_op jit(solution)/shard_map/last_1/pallas_call | solution.py:343
  26.7 0.2 collective-permute-start.13
  26.9 1.2 %collective-permute-start.12 = (bf16[64,1792]{1,0:T(8,128)(2,1)S(1)}, bf16[64,1792]{1,0:T(8,128)(2,1)S(1)}, u32[]{:S(2)}, u32[]{:S(2)}) collective-permute-start(bf16[64,1792]{1,0:T(8,128)(2,1)S(1)} %get-tuple-element.27.refs_1_), channel_id=1, source_target_pairs={{0,16},{8,24},{16,0},{24,8},{1,17},{9,25},{17,1},{25,9},{2,18},{10... | collective-permute-start | bytes 688136 | tf_op jit(solution)/shard_map/ppermute | solution.py:38
  28.1 1.5 %collective-permute-start.14 = (f32[8,1792]{1,0:T(8,128)S(1)}, f32[8,1792]{1,0:T(8,128)S(1)}, u32[]{:S(2)}, u32[]{:S(2)}) collective-permute-start(f32[8,1792]{1,0:T(8,128)S(1)} %get-tuple-element.29), channel_id=1, source_target_pairs={{0,4},{4,0},{1,5},{5,1},{2,6},{6,2},{3,7},{7,3},{8,12},{12,8},{9,1... | collective-permute-start | bytes 172040 | tf_op jit(solution)/shard_map/ppermute | solution.py:32
  29.6 0.7 %collective-permute-start.15 = (f32[8,1792]{1,0:T(8,128)S(1)}, f32[8,1792]{1,0:T(8,128)S(1)}, u32[]{:S(2)}, u32[]{:S(2)}) collective-permute-start(f32[8,1792]{1,0:T(8,128)S(1)} %get-tuple-element.30), channel_id=1, source_target_pairs={{0,1},{1,2},{2,3},{3,0},{4,5},{5,6},{6,7},{7,4},{8,9},{9,10},{10,1... | collective-permute-start | bytes 172040 | tf_op jit(solution)/shard_map/ppermute | solution.py:32
  30.3 3.1 %collective-permute-start.16 = (f32[8,1792]{1,0:T(8,128)S(1)}, f32[8,1792]{1,0:T(8,128)S(1)}, u32[]{:S(2)}, u32[]{:S(2)}) collective-permute-start(f32[8,1792]{1,0:T(8,128)S(1)} %get-tuple-element.31), channel_id=1, source_target_pairs={{0,3},{1,0},{2,1},{3,2},{4,7},{5,4},{6,5},{7,6},{8,11},{9,8},{10,9... | collective-permute-start | bytes 172040 | tf_op jit(solution)/shard_map/ppermute | solution.py:32
  33.4 0.8 %near_2.1.refs_1_.refs_3_ = f32[64,1792]{1,0:T(8,128)S(1)} custom-call(s32[8,14]{1,0:T(8,128)S(1)} %bitcast.14, bf16[64,1792]{1,0:T(8,128)(2,1)S(1)} %get-tuple-element.27.refs_1_, bf16[64,1792]{1,0:T(8,128)(2,1)S(1)} %collective-permute-done.13.refs_2_, bf16[14,8,128,128]{3,2,1,0:T(8,128)(2,1)S(1)} %copy-done, ...), custom_call_target="tpu_custom_call" | custom-call | flops 117440512 | bytes 5115328 | tf_op jit(solution)/shard_map/near_2/pallas_call | solution.py:343
  34.3 0.0 copy-start.2
  34.3 0.0 collective-permute-done.14.refs_2_.refs_6_
  34.3 1.8 %collective-permute-done.15.refs_3_.refs_7_ = f32[8,1792]{1,0:T(8,128)S(1)} collective-permute-done((f32[8,1792]{1,0:T(8,128)S(1)}, f32[8,1792]{1,0:T(8,128)S(1)}, u32[]{:S(2)}, u32[]{:S(2)}) %collective-permute-start.15) | collective-permute-done | bytes 57376 | tf_op jit(solution)/shard_map/ppermute | solution.py:32
  36.1 0.1 collective-permute-start.17
  36.2 0.5 %middle_2.1.refs_3_ = f32[64,1792]{1,0:T(8,128)S(1)} custom-call(s32[8,14]{1,0:T(8,128)S(1)} %bitcast.15, bf16[64,1792]{1,0:T(8,128)(2,1)S(1)} %hand_on.5.refs_1_, bf16[14,8,128,128]{3,2,1,0:T(8,128)(2,1)S(1)} %copy-done, f32[64,1792]{1,0:T(8,128)S(1)} %near_2.1.refs_1_.refs_3_, f32[2,1792]{1,0:T(2,128)S(1)} %copy-done.3, s32[2,1792]{1,0:T(2,128)S(1)} %copy-done.4, ...), custom_call_target="tpu_custom_call" | custom-call | flops 58720256 | bytes 5018048 | tf_op jit(solution)/shard_map/middle_2/pallas_call | solution.py:343
  36.7 0.9 %collective-permute-done.17.refs_1_ = bf16[64,1792]{1,0:T(8,128)(2,1)S(1)} collective-permute-done((bf16[64,1792]{1,0:T(8,128)(2,1)S(1)}, bf16[64,1792]{1,0:T(8,128)(2,1)S(1)}, u32[]{:S(2)}, u32[]{:S(2)}) %collective-permute-start.17) | collective-permute-done | bytes 229408 | tf_op jit(solution)/shard_map/ppermute | solution.py:38
  37.7 0.7 %last_2.1 = f32[32,1,128]{2,1,0:T(1,128)S(1)} custom-call(s32[8,14]{1,0:T(8,128)S(1)} %bitcast.16, bf16[64,1792]{1,0:T(8,128)(2,1)S(1)} %collective-permute-done.17.refs_1_, bf16[14,8,128,128]{3,2,1,0:T(8,128)(2,1)S(1)} %copy-done, f32[64,1792]{1,0:T(8,128)S(1)} %middle_2.1.refs_3_, f32[64,128]{1,0:T(8,128)S(1)} %get-tuple-element.18.refs_5_.refs_4_, ...), custom_call_target="tpu_custom_call" | custom-call | flops 58720256 | bytes 5784000 | tf_op jit(solution)/shard_map/last_2/pallas_call | solution.py:343
  38.3 10.8 %all_to_all.5.refs_0_ = f32[32,1,128]{2,1,0:T(1,128)S(1)} all-to-all(f32[32,1,128]{2,1,0:T(1,128)S(1)} %last_2.1), channel_id=1, replica_groups=mesh['mode'=4,'gx'=2,'gy'=4] {'mode','gx','gy'}, dimensions={0} | all-to-all | bytes 32768 | tf_op jit(solution)/shard_map/all_to_all | solution.py:485
  49.1 1.1 %finish.1 = (f32[64,1792]{1,0:T(8,128)}, f32[4,3]{1,0:T(4,128)}) custom-call(f32[32,1,128]{2,1,0:T(1,128)S(1)} %all_to_all.5.refs_0_, f32[64,1792]{1,0:T(8,128)S(1)} %bitcast.7, f32[64,1792]{1,0:T(8,128)S(1)} %get-tuple-element.23.refs_4_.refs_6_.refs_2_, f32[64,1792]{1,0:T(8,128)S(1)} %get-tuple-element.28.refs_4_.refs_7_.refs_3_), custom_call_target="tpu_custom_call" | custom-call | bytes 1851440 | tf_op jit(solution)/shard_map/finish/pallas_call | solution.py:343
  (20 shorter events, 0.0 us)
Async XLA Ops:
  1.7 10.4 %collective-permute-start.1 = (bf16[64,1792]{1,0:T(8,128)(2,1)S(1)}, bf16[64,1792]{1,0:T(8,128)(2,1)S(1)}, u32[]{:S(2)}, u32[]{:S(2)}) collective-permute-start(bf16[64,1792]{1,0:T(8,128)(2,1)S(1)} %bitcast_convert_fusion.refs_1_), channel_id=1, source_target_pairs={{0,8},{8,0},{16,24},{24,16},{1,9},{9,1},{17,25},{25,17},{2,10},{10... | collective-permute-start | bytes 688136 | tf_op jit(solution)/shard_map/ppermute | solution.py:38
  2.2 12.4 %collective-permute-start = (bf16[64,1792]{1,0:T(8,128)(2,1)S(1)}, bf16[64,1792]{1,0:T(8,128)(2,1)S(1)}, u32[]{:S(2)}, u32[]{:S(2)}) collective-permute-start(bf16[64,1792]{1,0:T(8,128)(2,1)S(1)} %bitcast_convert_fusion.refs_1_), channel_id=1, source_target_pairs={{0,16},{8,24},{16,0},{24,8},{1,17},{9,25},{17,1},{25,9},{2,18},{10... | collective-permute-start | bytes 688136 | tf_op jit(solution)/shard_map/ppermute | solution.py:38
  4.8 1.0 %copy-start.1 = (f32[8,8,1792]{2,1,0:T(8,128)S(1)}, f32[8,8,1792]{2,1,0:T(8,128)}, u32[]{:S(2)}) copy-start(f32[8,8,1792]{2,1,0:T(8,128)} %param.7) | copy-start | bytes 1376260
  5.8 0.7 %copy-start.7 = (s32[8,8]{1,0:T(8,128)S(1)}, s32[8,8]{1,0:T(8,128)}, u32[]{:S(2)}) copy-start(s32[8,8]{1,0:T(8,128)} %refs_1_.1) | copy-start | bytes 772
  6.5 5.6 %copy-start = (bf16[14,8,128,128]{3,2,1,0:T(8,128)(2,1)S(1)}, bf16[14,8,128,128]{3,2,1,0:T(8,128)(2,1)}, u32[]{:S(2)}) copy-start(bf16[14,8,128,128]{3,2,1,0:T(8,128)(2,1)} %refs_2_.11) | copy-start | bytes 11010052
  6.5 5.6 %copy-start.3 = (f32[2,1792]{1,0:T(2,128)S(1)}, f32[2,1792]{1,0:T(2,128)}, u32[]{:S(2)}) copy-start(f32[2,1792]{1,0:T(2,128)} %refs_4_.5) | copy-start | bytes 43012
  6.5 5.6 %copy-start.4 = (s32[2,1792]{1,0:T(2,128)S(1)}, s32[2,1792]{1,0:T(2,128)}, u32[]{:S(2)}) copy-start(s32[2,1792]{1,0:T(2,128)} %refs_5_.5) | copy-start | bytes 43012
  6.5 5.6 %copy-start.5 = (s32[14,8]{0,1:T(8,128)S(1)}, s32[14,8]{0,1:T(8,128)}, u32[]{:S(2)}) copy-start(s32[14,8]{0,1:T(8,128)} %param.8) | copy-start | bytes 1348
  6.5 5.6 %copy-start.6 = (f32[1792]{0:T(1024)S(1)}, f32[1792]{0:T(1024)}, u32[]{:S(2)}) copy-start(f32[1792]{0:T(1024)} %refs_6_.5) | copy-start | bytes 21508
  6.7 6.3 %collective-permute-start.2 = (f32[8,1792]{1,0:T(8,128)S(1)}, f32[8,1792]{1,0:T(8,128)S(1)}, u32[]{:S(2)}, u32[]{:S(2)}) collective-permute-start(f32[8,1792]{1,0:T(8,128)S(1)} %get-tuple-element.19), channel_id=1, source_target_pairs={{0,4},{4,0},{1,5},{5,1},{2,6},{6,2},{3,7},{7,3},{8,12},{12,8},{9,1... | collective-permute-start | bytes 172040 | tf_op jit(solution)/shard_map/ppermute | solution.py:32
  8.2 6.2 %collective-permute-start.3 = (f32[8,1792]{1,0:T(8,128)S(1)}, f32[8,1792]{1,0:T(8,128)S(1)}, u32[]{:S(2)}, u32[]{:S(2)}) collective-permute-start(f32[8,1792]{1,0:T(8,128)S(1)} %get-tuple-element.20), channel_id=1, source_target_pairs={{0,1},{1,2},{2,3},{3,0},{4,5},{5,6},{6,7},{7,4},{8,9},{9,10},{10,1... | collective-permute-start | bytes 172040 | tf_op jit(solution)/shard_map/ppermute | solution.py:32
  9.8 4.8 %collective-permute-start.4 = (f32[8,1792]{1,0:T(8,128)S(1)}, f32[8,1792]{1,0:T(8,128)S(1)}, u32[]{:S(2)}, u32[]{:S(2)}) collective-permute-start(f32[8,1792]{1,0:T(8,128)S(1)} %get-tuple-element.21), channel_id=1, source_target_pairs={{0,3},{1,0},{2,1},{3,2},{4,7},{5,4},{6,5},{7,6},{8,11},{9,8},{10,9... | collective-permute-start | bytes 172040 | tf_op jit(solution)/shard_map/ppermute | solution.py:32
  14.6 1.5 %collective-permute-start.5 = (bf16[64,1792]{1,0:T(8,128)(2,1)S(1)}, bf16[64,1792]{1,0:T(8,128)(2,1)S(1)}, u32[]{:S(2)}, u32[]{:S(2)}) collective-permute-start(bf16[64,1792]{1,0:T(8,128)(2,1)S(1)} %hand_on.3.refs_1_), channel_id=1, source_target_pairs={{0,8},{8,0},{16,24},{24,16},{1,9},{9,1},{17,25},{25,17},{2,10},{10... | collective-permute-start | bytes 688136 | tf_op jit(solution)/shard_map/ppermute | solution.py:38
  16.6 5.1 %collective-permute-start.7 = (bf16[64,1792]{1,0:T(8,128)(2,1)S(1)}, bf16[64,1792]{1,0:T(8,128)(2,1)S(1)}, u32[]{:S(2)}, u32[]{:S(2)}) collective-permute-start(bf16[64,1792]{1,0:T(8,128)(2,1)S(1)} %get-tuple-element.22.refs_1_), channel_id=1, source_target_pairs={{0,8},{8,0},{16,24},{24,16},{1,9},{9,1},{17,25},{25,17},{2,10},{10... | collective-permute-start | bytes 688136 | tf_op jit(solution)/shard_map/ppermute | solution.py:38
  16.8 7.9 %collective-permute-start.6 = (bf16[64,1792]{1,0:T(8,128)(2,1)S(1)}, bf16[64,1792]{1,0:T(8,128)(2,1)S(1)}, u32[]{:S(2)}, u32[]{:S(2)}) collective-permute-start(bf16[64,1792]{1,0:T(8,128)(2,1)S(1)} %get-tuple-element.22.refs_1_), channel_id=1, source_target_pairs={{0,16},{8,24},{16,0},{24,8},{1,17},{9,25},{17,1},{25,9},{2,18},{10... | collective-permute-start | bytes 688136 | tf_op jit(solution)/shard_map/ppermute | solution.py:38
  17.4 5.2 %collective-permute-start.8 = (f32[8,1792]{1,0:T(8,128)S(1)}, f32[8,1792]{1,0:T(8,128)S(1)}, u32[]{:S(2)}, u32[]{:S(2)}) collective-permute-start(f32[8,1792]{1,0:T(8,128)S(1)} %get-tuple-element.24), channel_id=1, source_target_pairs={{0,4},{4,0},{1,5},{5,1},{2,6},{6,2},{3,7},{7,3},{8,12},{12,8},{9,1... | collective-permute-start | bytes 172040 | tf_op jit(solution)/shard_map/ppermute | solution.py:32
  17.9 6.7 %collective-permute-start.9 = (f32[8,1792]{1,0:T(8,128)S(1)}, f32[8,1792]{1,0:T(8,128)S(1)}, u32[]{:S(2)}, u32[]{:S(2)}) collective-permute-start(f32[8,1792]{1,0:T(8,128)S(1)} %get-tuple-element.25), channel_id=1, source_target_pairs={{0,1},{1,2},{2,3},{3,0},{4,5},{5,6},{6,7},{7,4},{8,9},{9,10},{10,1... | collective-permute-start | bytes 172040 | tf_op jit(solution)/shard_map/ppermute | solution.py:32
  18.9 5.7 %collective-permute-start.10 = (f32[8,1792]{1,0:T(8,128)S(1)}, f32[8,1792]{1,0:T(8,128)S(1)}, u32[]{:S(2)}, u32[]{:S(2)}) collective-permute-start(f32[8,1792]{1,0:T(8,128)S(1)} %get-tuple-element.26), channel_id=1, source_target_pairs={{0,3},{1,0},{2,1},{3,2},{4,7},{5,4},{6,5},{7,6},{8,11},{9,8},{10,9... | collective-permute-start | bytes 172040 | tf_op jit(solution)/shard_map/ppermute | solution.py:32
  24.7 1.5 %collective-permute-start.11 = (bf16[64,1792]{1,0:T(8,128)(2,1)S(1)}, bf16[64,1792]{1,0:T(8,128)(2,1)S(1)}, u32[]{:S(2)}, u32[]{:S(2)}) collective-permute-start(bf16[64,1792]{1,0:T(8,128)(2,1)S(1)} %hand_on.4.refs_1_), channel_id=1, source_target_pairs={{0,8},{8,0},{16,24},{24,16},{1,9},{9,1},{17,25},{25,17},{2,10},{10... | collective-permute-start | bytes 688136 | tf_op jit(solution)/shard_map/ppermute | solution.py:38
  26.7 6.7 %collective-permute-start.13 = (bf16[64,1792]{1,0:T(8,128)(2,1)S(1)}, bf16[64,1792]{1,0:T(8,128)(2,1)S(1)}, u32[]{:S(2)}, u32[]{:S(2)}) collective-permute-start(bf16[64,1792]{1,0:T(8,128)(2,1)S(1)} %get-tuple-element.27.refs_1_), channel_id=1, source_target_pairs={{0,8},{8,0},{16,24},{24,16},{1,9},{9,1},{17,25},{25,17},{2,10},{10... | collective-permute-start | bytes 688136 | tf_op jit(solution)/shard_map/ppermute | solution.py:38
  26.9 9.2 %collective-permute-start.12 = (bf16[64,1792]{1,0:T(8,128)(2,1)S(1)}, bf16[64,1792]{1,0:T(8,128)(2,1)S(1)}, u32[]{:S(2)}, u32[]{:S(2)}) collective-permute-start(bf16[64,1792]{1,0:T(8,128)(2,1)S(1)} %get-tuple-element.27.refs_1_), channel_id=1, source_target_pairs={{0,16},{8,24},{16,0},{24,8},{1,17},{9,25},{17,1},{25,9},{2,18},{10... | collective-permute-start | bytes 688136 | tf_op jit(solution)/shard_map/ppermute | solution.py:38
  28.1 6.2 %collective-permute-start.14 = (f32[8,1792]{1,0:T(8,128)S(1)}, f32[8,1792]{1,0:T(8,128)S(1)}, u32[]{:S(2)}, u32[]{:S(2)}) collective-permute-start(f32[8,1792]{1,0:T(8,128)S(1)} %get-tuple-element.29), channel_id=1, source_target_pairs={{0,4},{4,0},{1,5},{5,1},{2,6},{6,2},{3,7},{7,3},{8,12},{12,8},{9,1... | collective-permute-start | bytes 172040 | tf_op jit(solution)/shard_map/ppermute | solution.py:32
  29.6 6.5 %collective-permute-start.15 = (f32[8,1792]{1,0:T(8,128)S(1)}, f32[8,1792]{1,0:T(8,128)S(1)}, u32[]{:S(2)}, u32[]{:S(2)}) collective-permute-start(f32[8,1792]{1,0:T(8,128)S(1)} %get-tuple-element.30), channel_id=1, source_target_pairs={{0,1},{1,2},{2,3},{3,0},{4,5},{5,6},{6,7},{7,4},{8,9},{9,10},{10,1... | collective-permute-start | bytes 172040 | tf_op jit(solution)/shard_map/ppermute | solution.py:32
  30.3 5.8 %collective-permute-start.16 = (f32[8,1792]{1,0:T(8,128)S(1)}, f32[8,1792]{1,0:T(8,128)S(1)}, u32[]{:S(2)}, u32[]{:S(2)}) collective-permute-start(f32[8,1792]{1,0:T(8,128)S(1)} %get-tuple-element.31), channel_id=1, source_target_pairs={{0,3},{1,0},{2,1},{3,2},{4,7},{5,4},{6,5},{7,6},{8,11},{9,8},{10,9... | collective-permute-start | bytes 172040 | tf_op jit(solution)/shard_map/ppermute | solution.py:32
  34.3 3.4 %copy-start.2 = (f32[8,8,1792]{2,1,0:T(8,128)S(1)}, f32[8,8,1792]{2,1,0:T(8,128)}, u32[]{:S(2)}) copy-start(f32[8,8,1792]{2,1,0:T(8,128)} %param.7) | copy-start | bytes 1376260
  36.1 1.5 %collective-permute-start.17 = (bf16[64,1792]{1,0:T(8,128)(2,1)S(1)}, bf16[64,1792]{1,0:T(8,128)(2,1)S(1)}, u32[]{:S(2)}, u32[]{:S(2)}) collective-permute-start(bf16[64,1792]{1,0:T(8,128)(2,1)S(1)} %hand_on.5.refs_1_), channel_id=1, source_target_pairs={{0,8},{8,0},{16,24},{24,16},{1,9},{9,1},{17,25},{25,17},{2,10},{10... | collective-permute-start | bytes 688136 | tf_op jit(solution)/shard_map/ppermute | solution.py:38

commit v6 on v5

--- a/solution.py
+++ b/solution.py
@@ -378,7 +378,11 @@
     middle = [place for place in range(2, count) if place not in final]
 
     start = right_side.reshape(cells, local_modes)
-    packed = start.astype(jnp.bfloat16)
+
+    def pack(ins, outs, scratch):
+        outs[0][...] = ins[0][...].astype(jnp.bfloat16)
+
+    (packed,) = call("pack", pack, [in_vmem([start])], [packed_shape], flops=4 * 10**9)
 
     def prepare(ins, outs, scratch):
         faces, (open_ref,) = outs[:n_faces], outs[n_faces:]
@@ -422,12 +426,12 @@
             flops=work * len(near),
         )
 
-        held = dict(zip(held, hand_on(list(held.values()), [partial, *x_in, *y_in])))
+        held = dict(zip(held, hand_on(list(held.values()), [partial, *y_in, *x_in])))
         for place, array in held.items():
             sources[place] = array
             sources[place ^ 1] = exchange(array, 1)
 
-        def middle_step(cols, sources, rest, x_in, y_in, outs, scratch):
+        def middle_step(cols, sources, rest, y_in, x_in, outs, scratch):
             middle_kernel(
                 sizes, per_owner, middle, cols[0], sources, *rest, x_in, y_in, outs[0]
             )
@@ -439,8 +443,8 @@
                 in_vmem([columns]),
                 in_vmem([sources[place] for place in middle]),
                 in_vmem([blocks, partial, drift_speed, upwind_sign]),
+                in_vmem(y_in),
                 in_vmem(x_in),
-                in_vmem(y_in),
             ],
             [vector_shape],
             flops=work * len(middle),

time: 50.5 us -> 49.2 us (0.974)
  starting transfers between devices: 20.3 us -> 21.6 us
  other arithmetic: 1.05 us -> 0 us
  blocking collectives: 10.8 us -> 10.1 us
  local copies, waits for them, and re-layouts: 1.73 us -> 1.06 us
    convert_element_type x1 -> x0, other arithmetic: 1.05 us -> none  [per_device(): packed = start.astype(jnp.bfloat16)]
    ppermute x9, starting transfers between devices: 15.1 us -> 16.1 us  [move_faces(): lax.ppermute(face, axis, pairs)]
    all_to_all x1, blocking collectives: 10.8 us -> 10.1 us  [per_device(): gram = lax.all_to_all(gram, AXES, 0, 0)]
    unnamed x16, local copies, waits for them, and re-layouts: 1.73 us -> 1.06 us
    pallas_call x11 -> x12, Pallas kernels: 7.09 us -> 7.15 us  [call(): pl.pallas_call(body, out_shape=list(shapes), in_specs=[spec for spec, ope...]
  transfers between devices with their start and end apart: 18 -> 18, of which waited for: 8 -> 9; matrix products, arithmetic and copies ran while one was open for 0% -> 0% of each run, Pallas kernels for 9% -> 9%
where the time goes in v6:
time: 49.2 us; the launch traced here: 49 us
  starting transfers between devices  21.6 us (44%)
  blocking collectives  10.1 us (21%)
  waiting for transfers between devices  8.27 us (17%)
  Pallas kernels  7.15 us (15%)
  local copies, waits for them, and re-layouts  1.06 us (2%)
  between operations  0.8 us (2%)
    ppermute x9, starting transfers between devices, move_faces(): lax.ppermute(face, axis, pairs)  16.1 us
    all_to_all x1, blocking collectives, per_device(): gram = lax.all_to_all(gram, AXES, 0, 0)  10.1 us
    pallas_call x12, Pallas kernels, call(): pl.pallas_call(body, out_shape=list(shapes), in_specs=[spec for spec, ope...  7.15 us
    ppermute x9, starting transfers between devices, exchange(): return lax.ppermute(array, 'mode', [(i, i ^ bit) for i in range(count)])  5.57 us
    ppermute x9, waiting for transfers between devices, move_faces(): lax.ppermute(face, axis, pairs)  5.41 us
    ppermute x9, waiting for transfers between devices, exchange(): return lax.ppermute(array, 'mode', [(i, i ^ bit) for i in range(count)])  2.86 us
    unnamed x16, local copies, waits for them, and re-layouts  1.06 us
  transfers between devices with their start and end apart: 18, of which 9 were waited for; matrix products, arithmetic and copies ran while one was open for 0% of the time, Pallas kernels for 9%

profile of v6, /device:TPU:0, one launch (start us, length us, event | category | flops | bytes accessed | tf_op | source)
XLA Modules:
  0.0 49.0 jit_solution(8326471093898280448)
XLA Ops:
  0.6 0.0 copy-start.1
  0.6 1.0 %copy-done.1 = f32[8,8,1792]{2,1,0:T(8,128)S(1)} copy-done((f32[8,8,1792]{2,1,0:T(8,128)S(1)}, f32[8,8,1792]{2,1,0:T(8,128)}, u32[]{:S(2)}) %copy-start.1) | copy-done | bytes 458776
  1.7 0.0 copy-start
  1.7 0.0 copy-start.3
  1.7 0.0 copy-start.4
  1.7 0.0 copy-start.5
  1.7 0.0 copy-start.6
  1.7 0.5 %collective-permute-start.1 = (bf16[64,1792]{1,0:T(8,128)(2,1)S(1)}, bf16[64,1792]{1,0:T(8,128)(2,1)S(1)}, u32[]{:S(2)}, u32[]{:S(2)}) collective-permute-start(bf16[64,1792]{1,0:T(8,128)(2,1)S(1)} %pack.1.refs_1_), channel_id=1, source_target_pairs={{0,8},{8,0},{16,24},{24,16},{1,9},{9,1},{17,25},{25,17},{2,10},{10... | collective-permute-start | bytes 688136 | tf_op jit(solution)/shard_map/ppermute | solution.py:38
  2.3 2.6 %collective-permute-start = (bf16[64,1792]{1,0:T(8,128)(2,1)S(1)}, bf16[64,1792]{1,0:T(8,128)(2,1)S(1)}, u32[]{:S(2)}, u32[]{:S(2)}) collective-permute-start(bf16[64,1792]{1,0:T(8,128)(2,1)S(1)} %pack.1.refs_1_), channel_id=1, source_target_pairs={{0,16},{8,24},{16,0},{24,8},{1,17},{9,25},{17,1},{25,9},{2,18},{10... | collective-permute-start | bytes 688136 | tf_op jit(solution)/shard_map/ppermute | solution.py:38
  4.9 0.1 prepare.1
  5.0 1.6 %collective-permute-start.2 = (f32[8,1792]{1,0:T(8,128)S(1)}, f32[8,1792]{1,0:T(8,128)S(1)}, u32[]{:S(2)}, u32[]{:S(2)}) collective-permute-start(f32[8,1792]{1,0:T(8,128)S(1)} %get-tuple-element.19), channel_id=1, source_target_pairs={{0,1},{1,2},{2,3},{3,0},{4,5},{5,6},{6,7},{7,4},{8,9},{9,10},{10,1... | collective-permute-start | bytes 172040 | tf_op jit(solution)/shard_map/ppermute | solution.py:32
  6.6 2.2 %collective-permute-start.3 = (f32[8,1792]{1,0:T(8,128)S(1)}, f32[8,1792]{1,0:T(8,128)S(1)}, u32[]{:S(2)}, u32[]{:S(2)}) collective-permute-start(f32[8,1792]{1,0:T(8,128)S(1)} %get-tuple-element.20), channel_id=1, source_target_pairs={{0,3},{1,0},{2,1},{3,2},{4,7},{5,4},{6,5},{7,6},{8,11},{9,8},{10,9... | collective-permute-start | bytes 172040 | tf_op jit(solution)/shard_map/ppermute | solution.py:32
  8.9 1.5 %collective-permute-start.4 = (f32[8,1792]{1,0:T(8,128)S(1)}, f32[8,1792]{1,0:T(8,128)S(1)}, u32[]{:S(2)}, u32[]{:S(2)}) collective-permute-start(f32[8,1792]{1,0:T(8,128)S(1)} %get-tuple-element.21), channel_id=1, source_target_pairs={{0,4},{4,0},{1,5},{5,1},{2,6},{6,2},{3,7},{7,3},{8,12},{12,8},{9,1... | collective-permute-start | bytes 172040 | tf_op jit(solution)/shard_map/ppermute | solution.py:32
  10.4 0.8 %near_0.1.refs_1_.refs_3_ = f32[64,1792]{1,0:T(8,128)S(1)} custom-call(s32[8,14]{1,0:T(8,128)S(1)} %bitcast.8, bf16[64,1792]{1,0:T(8,128)(2,1)S(1)} %pack.1.refs_1_, bf16[64,1792]{1,0:T(8,128)(2,1)S(1)} %collective-permute-done.1.refs_2_, bf16[14,8,128,128]{3,2,1,0:T(8,128)(2,1)S(1)} %copy-done, f32[64,1792]{1,0:T(8,128)S(1)} %bitcast.5, ...), custom_call_target="tpu_custom_call" | custom-call | flops 117440512 | bytes 5115328 | tf_op jit(solution)/shard_map/near_0/pallas_call | solution.py:343
  11.3 0.0 collective-permute-done.2.refs_2_.refs_6_
  11.3 0.3 collective-permute-done.3.refs_3_.refs_7_
  11.6 1.5 %collective-permute-done.4.refs_4_.refs_8_ = f32[8,1792]{1,0:T(8,128)S(1)} collective-permute-done((f32[8,1792]{1,0:T(8,128)S(1)}, f32[8,1792]{1,0:T(8,128)S(1)}, u32[]{:S(2)}, u32[]{:S(2)}) %collective-permute-start.4) | collective-permute-done | bytes 57376 | tf_op jit(solution)/shard_map/ppermute | solution.py:32
  13.1 0.0 collective-permute-done.refs_0_
  13.1 0.0 collective-permute-start.5
  13.1 0.5 %middle_0.1.refs_3_ = f32[64,1792]{1,0:T(8,128)S(1)} custom-call(s32[8,14]{1,0:T(8,128)S(1)} %bitcast.9, bf16[64,1792]{1,0:T(8,128)(2,1)S(1)} %hand_on.3.refs_1_, bf16[14,8,128,128]{3,2,1,0:T(8,128)(2,1)S(1)} %copy-done, f32[64,1792]{1,0:T(8,128)S(1)} %near_0.1.refs_1_.refs_3_, f32[2,1792]{1,0:T(2,128)S(1)} %copy-done.3, s32[2,1792]{1,0:T(2,128)S(1)} %copy-done.4, ...), custom_call_target="tpu_custom_call" | custom-call | flops 58720256 | bytes 5018048 | tf_op jit(solution)/shard_map/middle_0/pallas_call | solution.py:343
  13.6 0.9 %collective-permute-done.5.refs_1_ = bf16[64,1792]{1,0:T(8,128)(2,1)S(1)} collective-permute-done((bf16[64,1792]{1,0:T(8,128)(2,1)S(1)}, bf16[64,1792]{1,0:T(8,128)(2,1)S(1)}, u32[]{:S(2)}, u32[]{:S(2)}) %collective-permute-start.5) | collective-permute-done | bytes 229408 | tf_op jit(solution)/shard_map/ppermute | solution.py:38
  14.6 0.5 %last_0.1 = (f32[8,1792]{1,0:T(8,128)S(1)}, f32[8,1792]{1,0:T(8,128)S(1)}, f32[8,1792]{1,0:T(8,128)S(1)}, bf16[64,1792]{1,0:T(8,128)(2,1)S(1)}, f32[64,1792]{1,0:T(8,128)S(1)}) custom-call(s32[8,14]{1,0:T(8,128)S(1)} %bitcast.10, bf16[64,1792]{1,0:T(8,128)(2,1)S(1)} %collective-permute-done.5.refs_1_, bf16[14,8,128,128]{3,2,1,0:T(8,128)(2,1)S(1)} %copy-done, ...), custom_call_target="tpu_custom_call" | custom-call | flops 58720256 | bytes 5251520 | tf_op jit(solution)/shard_map/last_0/pallas_call | solution.py:343
  15.1 0.2 collective-permute-start.7
  15.3 0.5 collective-permute-start.6
  15.8 0.9 %collective-permute-start.8 = (f32[8,1792]{1,0:T(8,128)S(1)}, f32[8,1792]{1,0:T(8,128)S(1)}, u32[]{:S(2)}, u32[]{:S(2)}) collective-permute-start(f32[8,1792]{1,0:T(8,128)S(1)} %get-tuple-element.24), channel_id=1, source_target_pairs={{0,1},{1,2},{2,3},{3,0},{4,5},{5,6},{6,7},{7,4},{8,9},{9,10},{10,1... | collective-permute-start | bytes 172040 | tf_op jit(solution)/shard_map/ppermute | solution.py:32
  16.6 3.0 %collective-permute-start.9 = (f32[8,1792]{1,0:T(8,128)S(1)}, f32[8,1792]{1,0:T(8,128)S(1)}, u32[]{:S(2)}, u32[]{:S(2)}) collective-permute-start(f32[8,1792]{1,0:T(8,128)S(1)} %get-tuple-element.25), channel_id=1, source_target_pairs={{0,3},{1,0},{2,1},{3,2},{4,7},{5,4},{6,5},{7,6},{8,11},{9,8},{10,9... | collective-permute-start | bytes 172040 | tf_op jit(solution)/shard_map/ppermute | solution.py:32
  19.6 1.5 %collective-permute-start.10 = (f32[8,1792]{1,0:T(8,128)S(1)}, f32[8,1792]{1,0:T(8,128)S(1)}, u32[]{:S(2)}, u32[]{:S(2)}) collective-permute-start(f32[8,1792]{1,0:T(8,128)S(1)} %get-tuple-element.26), channel_id=1, source_target_pairs={{0,4},{4,0},{1,5},{5,1},{2,6},{6,2},{3,7},{7,3},{8,12},{12,8},{9,1... | collective-permute-start | bytes 172040 | tf_op jit(solution)/shard_map/ppermute | solution.py:32
  21.1 0.0 collective-permute-done.7.refs_2_
  21.1 0.8 %near_1.1.refs_1_.refs_3_ = f32[64,1792]{1,0:T(8,128)S(1)} custom-call(s32[8,14]{1,0:T(8,128)S(1)} %bitcast.11, bf16[64,1792]{1,0:T(8,128)(2,1)S(1)} %get-tuple-element.22.refs_1_, bf16[64,1792]{1,0:T(8,128)(2,1)S(1)} %collective-permute-done.7.refs_2_, bf16[14,8,128,128]{3,2,1,0:T(8,128)(2,1)S(1)} %copy-done, ...), custom_call_target="tpu_custom_call" | custom-call | flops 117440512 | bytes 5115328 | tf_op jit(solution)/shard_map/near_1/pallas_call | solution.py:343
  22.0 0.3 collective-permute-done.8.refs_2_.refs_6_
  22.3 1.5 %collective-permute-done.10.refs_4_.refs_8_ = f32[8,1792]{1,0:T(8,128)S(1)} collective-permute-done((f32[8,1792]{1,0:T(8,128)S(1)}, f32[8,1792]{1,0:T(8,128)S(1)}, u32[]{:S(2)}, u32[]{:S(2)}) %collective-permute-start.10) | collective-permute-done | bytes 57376 | tf_op jit(solution)/shard_map/ppermute | solution.py:32
  23.8 0.0 collective-permute-done.6.refs_0_
  23.8 0.5 %middle_1.1.refs_3_ = f32[64,1792]{1,0:T(8,128)S(1)} custom-call(s32[8,14]{1,0:T(8,128)S(1)} %bitcast.12, bf16[64,1792]{1,0:T(8,128)(2,1)S(1)} %hand_on.4.refs_1_, bf16[14,8,128,128]{3,2,1,0:T(8,128)(2,1)S(1)} %copy-done, f32[64,1792]{1,0:T(8,128)S(1)} %near_1.1.refs_1_.refs_3_, f32[2,1792]{1,0:T(2,128)S(1)} %copy-done.3, s32[2,1792]{1,0:T(2,128)S(1)} %copy-done.4, ...), custom_call_target="tpu_custom_call" | custom-call | flops 58720256 | bytes 5018048 | tf_op jit(solution)/shard_map/middle_1/pallas_call | solution.py:343
  24.3 0.9 %collective-permute-done.11.refs_1_ = bf16[64,1792]{1,0:T(8,128)(2,1)S(1)} collective-permute-done((bf16[64,1792]{1,0:T(8,128)(2,1)S(1)}, bf16[64,1792]{1,0:T(8,128)(2,1)S(1)}, u32[]{:S(2)}, u32[]{:S(2)}) %collective-permute-start.11) | collective-permute-done | bytes 229408 | tf_op jit(solution)/shard_map/ppermute | solution.py:38
  25.3 0.5 %last_1.1 = (f32[8,1792]{1,0:T(8,128)S(1)}, f32[8,1792]{1,0:T(8,128)S(1)}, f32[8,1792]{1,0:T(8,128)S(1)}, bf16[64,1792]{1,0:T(8,128)(2,1)S(1)}, f32[64,1792]{1,0:T(8,128)S(1)}) custom-call(s32[8,14]{1,0:T(8,128)S(1)} %bitcast.13, bf16[64,1792]{1,0:T(8,128)(2,1)S(1)} %collective-permute-done.11.refs_1_, bf16[14,8,128,128]{3,2,1,0:T(8,128)(2,1)S(1)} %copy-done, ...), custom_call_target="tpu_custom_call" | custom-call | flops 58720256 | bytes 5251520 | tf_op jit(solution)/shard_map/last_1/pallas_call | solution.py:343
  25.8 0.2 collective-permute-start.13
  26.0 1.6 %collective-permute-start.12 = (bf16[64,1792]{1,0:T(8,128)(2,1)S(1)}, bf16[64,1792]{1,0:T(8,128)(2,1)S(1)}, u32[]{:S(2)}, u32[]{:S(2)}) collective-permute-start(bf16[64,1792]{1,0:T(8,128)(2,1)S(1)} %get-tuple-element.27.refs_1_), channel_id=1, source_target_pairs={{0,16},{8,24},{16,0},{24,8},{1,17},{9,25},{17,1},{25,9},{2,18},{10... | collective-permute-start | bytes 688136 | tf_op jit(solution)/shard_map/ppermute | solution.py:38
  27.6 3.8 %collective-permute-start.15 = (f32[8,1792]{1,0:T(8,128)S(1)}, f32[8,1792]{1,0:T(8,128)S(1)}, u32[]{:S(2)}, u32[]{:S(2)}) collective-permute-start(f32[8,1792]{1,0:T(8,128)S(1)} %get-tuple-element.30), channel_id=1, source_target_pairs={{0,3},{1,0},{2,1},{3,2},{4,7},{5,4},{6,5},{7,6},{8,11},{9,8},{10,9... | collective-permute-start | bytes 172040 | tf_op jit(solution)/shard_map/ppermute | solution.py:32
  31.4 1.5 %collective-permute-start.16 = (f32[8,1792]{1,0:T(8,128)S(1)}, f32[8,1792]{1,0:T(8,128)S(1)}, u32[]{:S(2)}, u32[]{:S(2)}) collective-permute-start(f32[8,1792]{1,0:T(8,128)S(1)} %get-tuple-element.31), channel_id=1, source_target_pairs={{0,4},{4,0},{1,5},{5,1},{2,6},{6,2},{3,7},{7,3},{8,12},{12,8},{9,1... | collective-permute-start | bytes 172040 | tf_op jit(solution)/shard_map/ppermute | solution.py:32
  32.9 0.8 %near_2.1.refs_1_.refs_3_ = f32[64,1792]{1,0:T(8,128)S(1)} custom-call(s32[8,14]{1,0:T(8,128)S(1)} %bitcast.14, bf16[64,1792]{1,0:T(8,128)(2,1)S(1)} %get-tuple-element.27.refs_1_, bf16[64,1792]{1,0:T(8,128)(2,1)S(1)} %collective-permute-done.13.refs_2_, bf16[14,8,128,128]{3,2,1,0:T(8,128)(2,1)S(1)} %copy-done, ...), custom_call_target="tpu_custom_call" | custom-call | flops 117440512 | bytes 5115328 | tf_op jit(solution)/shard_map/near_2/pallas_call | solution.py:343
  33.7 0.0 copy-start.2
  33.7 0.1 collective-permute-done.14.refs_2_.refs_6_
  33.9 1.7 %collective-permute-done.16.refs_4_.refs_8_ = f32[8,1792]{1,0:T(8,128)S(1)} collective-permute-done((f32[8,1792]{1,0:T(8,128)S(1)}, f32[8,1792]{1,0:T(8,128)S(1)}, u32[]{:S(2)}, u32[]{:S(2)}) %collective-permute-start.16) | collective-permute-done | bytes 57376 | tf_op jit(solution)/shard_map/ppermute | solution.py:32
  35.6 0.5 %middle_2.1.refs_3_ = f32[64,1792]{1,0:T(8,128)S(1)} custom-call(s32[8,14]{1,0:T(8,128)S(1)} %bitcast.15, bf16[64,1792]{1,0:T(8,128)(2,1)S(1)} %hand_on.5.refs_1_, bf16[14,8,128,128]{3,2,1,0:T(8,128)(2,1)S(1)} %copy-done, f32[64,1792]{1,0:T(8,128)S(1)} %near_2.1.refs_1_.refs_3_, f32[2,1792]{1,0:T(2,128)S(1)} %copy-done.3, s32[2,1792]{1,0:T(2,128)S(1)} %copy-done.4, ...), custom_call_target="tpu_custom_call" | custom-call | flops 58720256 | bytes 5018048 | tf_op jit(solution)/shard_map/middle_2/pallas_call | solution.py:343
  36.1 0.9 %collective-permute-done.17.refs_1_ = bf16[64,1792]{1,0:T(8,128)(2,1)S(1)} collective-permute-done((bf16[64,1792]{1,0:T(8,128)(2,1)S(1)}, bf16[64,1792]{1,0:T(8,128)(2,1)S(1)}, u32[]{:S(2)}, u32[]{:S(2)}) %collective-permute-start.17) | collective-permute-done | bytes 229408 | tf_op jit(solution)/shard_map/ppermute | solution.py:38
  37.1 0.7 %last_2.1 = f32[32,1,128]{2,1,0:T(1,128)S(1)} custom-call(s32[8,14]{1,0:T(8,128)S(1)} %bitcast.16, bf16[64,1792]{1,0:T(8,128)(2,1)S(1)} %collective-permute-done.17.refs_1_, bf16[14,8,128,128]{3,2,1,0:T(8,128)(2,1)S(1)} %copy-done, f32[64,1792]{1,0:T(8,128)S(1)} %middle_2.1.refs_3_, f32[64,128]{1,0:T(8,128)S(1)} %get-tuple-element.18.refs_5_.refs_4_, ...), custom_call_target="tpu_custom_call" | custom-call | flops 58720256 | bytes 5784000 | tf_op jit(solution)/shard_map/last_2/pallas_call | solution.py:343
  37.8 10.1 %all_to_all.5.refs_0_ = f32[32,1,128]{2,1,0:T(1,128)S(1)} all-to-all(f32[32,1,128]{2,1,0:T(1,128)S(1)} %last_2.1), channel_id=1, replica_groups=mesh['mode'=4,'gx'=2,'gy'=4] {'mode','gx','gy'}, dimensions={0} | all-to-all | bytes 32768 | tf_op jit(solution)/shard_map/all_to_all | solution.py:489
  47.8 1.1 %finish.1 = (f32[64,1792]{1,0:T(8,128)}, f32[4,3]{1,0:T(4,128)}) custom-call(f32[32,1,128]{2,1,0:T(1,128)S(1)} %all_to_all.5.refs_0_, f32[64,1792]{1,0:T(8,128)S(1)} %bitcast.7, f32[64,1792]{1,0:T(8,128)S(1)} %get-tuple-element.23.refs_4_.refs_6_.refs_2_, f32[64,1792]{1,0:T(8,128)S(1)} %get-tuple-element.28.refs_4_.refs_7_.refs_3_), custom_call_target="tpu_custom_call" | custom-call | bytes 1851440 | tf_op jit(solution)/shard_map/finish/pallas_call | solution.py:343
  (20 shorter events, 0.1 us)
Async XLA Ops:
  0.6 1.0 %copy-start.1 = (f32[8,8,1792]{2,1,0:T(8,128)S(1)}, f32[8,8,1792]{2,1,0:T(8,128)}, u32[]{:S(2)}) copy-start(f32[8,8,1792]{2,1,0:T(8,128)} %param.7) | copy-start | bytes 1376260
  1.7 3.2 %copy-start.7 = (s32[8,8]{1,0:T(8,128)S(1)}, s32[8,8]{1,0:T(8,128)}, u32[]{:S(2)}) copy-start(s32[8,8]{1,0:T(8,128)} %refs_1_.1) | copy-start | bytes 772
  1.7 8.7 %copy-start = (bf16[14,8,128,128]{3,2,1,0:T(8,128)(2,1)S(1)}, bf16[14,8,128,128]{3,2,1,0:T(8,128)(2,1)}, u32[]{:S(2)}) copy-start(bf16[14,8,128,128]{3,2,1,0:T(8,128)(2,1)} %refs_2_.11) | copy-start | bytes 11010052
  1.7 8.7 %copy-start.3 = (f32[2,1792]{1,0:T(2,128)S(1)}, f32[2,1792]{1,0:T(2,128)}, u32[]{:S(2)}) copy-start(f32[2,1792]{1,0:T(2,128)} %refs_4_.5) | copy-start | bytes 43012
  1.7 8.7 %copy-start.4 = (s32[2,1792]{1,0:T(2,128)S(1)}, s32[2,1792]{1,0:T(2,128)}, u32[]{:S(2)}) copy-start(s32[2,1792]{1,0:T(2,128)} %refs_5_.5) | copy-start | bytes 43012
  1.7 8.7 %copy-start.5 = (s32[14,8]{0,1:T(8,128)S(1)}, s32[14,8]{0,1:T(8,128)}, u32[]{:S(2)}) copy-start(s32[14,8]{0,1:T(8,128)} %param.8) | copy-start | bytes 1348
  1.7 8.7 %copy-start.6 = (f32[1792]{0:T(1024)S(1)}, f32[1792]{0:T(1024)}, u32[]{:S(2)}) copy-start(f32[1792]{0:T(1024)} %refs_6_.5) | copy-start | bytes 21508
  1.7 8.6 %collective-permute-start.1 = (bf16[64,1792]{1,0:T(8,128)(2,1)S(1)}, bf16[64,1792]{1,0:T(8,128)(2,1)S(1)}, u32[]{:S(2)}, u32[]{:S(2)}) collective-permute-start(bf16[64,1792]{1,0:T(8,128)(2,1)S(1)} %pack.1.refs_1_), channel_id=1, source_target_pairs={{0,8},{8,0},{16,24},{24,16},{1,9},{9,1},{17,25},{25,17},{2,10},{10... | collective-permute-start | bytes 688136 | tf_op jit(solution)/shard_map/ppermute | solution.py:38
  2.3 10.8 %collective-permute-start = (bf16[64,1792]{1,0:T(8,128)(2,1)S(1)}, bf16[64,1792]{1,0:T(8,128)(2,1)S(1)}, u32[]{:S(2)}, u32[]{:S(2)}) collective-permute-start(bf16[64,1792]{1,0:T(8,128)(2,1)S(1)} %pack.1.refs_1_), channel_id=1, source_target_pairs={{0,16},{8,24},{16,0},{24,8},{1,17},{9,25},{17,1},{25,9},{2,18},{10... | collective-permute-start | bytes 688136 | tf_op jit(solution)/shard_map/ppermute | solution.py:38
  5.0 6.3 %collective-permute-start.2 = (f32[8,1792]{1,0:T(8,128)S(1)}, f32[8,1792]{1,0:T(8,128)S(1)}, u32[]{:S(2)}, u32[]{:S(2)}) collective-permute-start(f32[8,1792]{1,0:T(8,128)S(1)} %get-tuple-element.19), channel_id=1, source_target_pairs={{0,1},{1,2},{2,3},{3,0},{4,5},{5,6},{6,7},{7,4},{8,9},{9,10},{10,1... | collective-permute-start | bytes 172040 | tf_op jit(solution)/shard_map/ppermute | solution.py:32
  6.6 4.9 %collective-permute-start.3 = (f32[8,1792]{1,0:T(8,128)S(1)}, f32[8,1792]{1,0:T(8,128)S(1)}, u32[]{:S(2)}, u32[]{:S(2)}) collective-permute-start(f32[8,1792]{1,0:T(8,128)S(1)} %get-tuple-element.20), channel_id=1, source_target_pairs={{0,3},{1,0},{2,1},{3,2},{4,7},{5,4},{6,5},{7,6},{8,11},{9,8},{10,9... | collective-permute-start | bytes 172040 | tf_op jit(solution)/shard_map/ppermute | solution.py:32
  8.9 4.2 %collective-permute-start.4 = (f32[8,1792]{1,0:T(8,128)S(1)}, f32[8,1792]{1,0:T(8,128)S(1)}, u32[]{:S(2)}, u32[]{:S(2)}) collective-permute-start(f32[8,1792]{1,0:T(8,128)S(1)} %get-tuple-element.21), channel_id=1, source_target_pairs={{0,4},{4,0},{1,5},{5,1},{2,6},{6,2},{3,7},{7,3},{8,12},{12,8},{9,1... | collective-permute-start | bytes 172040 | tf_op jit(solution)/shard_map/ppermute | solution.py:32
  13.1 1.5 %collective-permute-start.5 = (bf16[64,1792]{1,0:T(8,128)(2,1)S(1)}, bf16[64,1792]{1,0:T(8,128)(2,1)S(1)}, u32[]{:S(2)}, u32[]{:S(2)}) collective-permute-start(bf16[64,1792]{1,0:T(8,128)(2,1)S(1)} %hand_on.3.refs_1_), channel_id=1, source_target_pairs={{0,8},{8,0},{16,24},{24,16},{1,9},{9,1},{17,25},{25,17},{2,10},{10... | collective-permute-start | bytes 688136 | tf_op jit(solution)/shard_map/ppermute | solution.py:38
  15.1 6.0 %collective-permute-start.7 = (bf16[64,1792]{1,0:T(8,128)(2,1)S(1)}, bf16[64,1792]{1,0:T(8,128)(2,1)S(1)}, u32[]{:S(2)}, u32[]{:S(2)}) collective-permute-start(bf16[64,1792]{1,0:T(8,128)(2,1)S(1)} %get-tuple-element.22.refs_1_), channel_id=1, source_target_pairs={{0,8},{8,0},{16,24},{24,16},{1,9},{9,1},{17,25},{25,17},{2,10},{10... | collective-permute-start | bytes 688136 | tf_op jit(solution)/shard_map/ppermute | solution.py:38
  15.3 8.5 %collective-permute-start.6 = (bf16[64,1792]{1,0:T(8,128)(2,1)S(1)}, bf16[64,1792]{1,0:T(8,128)(2,1)S(1)}, u32[]{:S(2)}, u32[]{:S(2)}) collective-permute-start(bf16[64,1792]{1,0:T(8,128)(2,1)S(1)} %get-tuple-element.22.refs_1_), channel_id=1, source_target_pairs={{0,16},{8,24},{16,0},{24,8},{1,17},{9,25},{17,1},{25,9},{2,18},{10... | collective-permute-start | bytes 688136 | tf_op jit(solution)/shard_map/ppermute | solution.py:38
  15.8 6.5 %collective-permute-start.8 = (f32[8,1792]{1,0:T(8,128)S(1)}, f32[8,1792]{1,0:T(8,128)S(1)}, u32[]{:S(2)}, u32[]{:S(2)}) collective-permute-start(f32[8,1792]{1,0:T(8,128)S(1)} %get-tuple-element.24), channel_id=1, source_target_pairs={{0,1},{1,2},{2,3},{3,0},{4,5},{5,6},{6,7},{7,4},{8,9},{9,10},{10,1... | collective-permute-start | bytes 172040 | tf_op jit(solution)/shard_map/ppermute | solution.py:32
  16.6 5.7 %collective-permute-start.9 = (f32[8,1792]{1,0:T(8,128)S(1)}, f32[8,1792]{1,0:T(8,128)S(1)}, u32[]{:S(2)}, u32[]{:S(2)}) collective-permute-start(f32[8,1792]{1,0:T(8,128)S(1)} %get-tuple-element.25), channel_id=1, source_target_pairs={{0,3},{1,0},{2,1},{3,2},{4,7},{5,4},{6,5},{7,6},{8,11},{9,8},{10,9... | collective-permute-start | bytes 172040 | tf_op jit(solution)/shard_map/ppermute | solution.py:32
  19.6 4.2 %collective-permute-start.10 = (f32[8,1792]{1,0:T(8,128)S(1)}, f32[8,1792]{1,0:T(8,128)S(1)}, u32[]{:S(2)}, u32[]{:S(2)}) collective-permute-start(f32[8,1792]{1,0:T(8,128)S(1)} %get-tuple-element.26), channel_id=1, source_target_pairs={{0,4},{4,0},{1,5},{5,1},{2,6},{6,2},{3,7},{7,3},{8,12},{12,8},{9,1... | collective-permute-start | bytes 172040 | tf_op jit(solution)/shard_map/ppermute | solution.py:32
  23.8 1.5 %collective-permute-start.11 = (bf16[64,1792]{1,0:T(8,128)(2,1)S(1)}, bf16[64,1792]{1,0:T(8,128)(2,1)S(1)}, u32[]{:S(2)}, u32[]{:S(2)}) collective-permute-start(bf16[64,1792]{1,0:T(8,128)(2,1)S(1)} %hand_on.4.refs_1_), channel_id=1, source_target_pairs={{0,8},{8,0},{16,24},{24,16},{1,9},{9,1},{17,25},{25,17},{2,10},{10... | collective-permute-start | bytes 688136 | tf_op jit(solution)/shard_map/ppermute | solution.py:38
  25.8 7.1 %collective-permute-start.13 = (bf16[64,1792]{1,0:T(8,128)(2,1)S(1)}, bf16[64,1792]{1,0:T(8,128)(2,1)S(1)}, u32[]{:S(2)}, u32[]{:S(2)}) collective-permute-start(bf16[64,1792]{1,0:T(8,128)(2,1)S(1)} %get-tuple-element.27.refs_1_), channel_id=1, source_target_pairs={{0,8},{8,0},{16,24},{24,16},{1,9},{9,1},{17,25},{25,17},{2,10},{10... | collective-permute-start | bytes 688136 | tf_op jit(solution)/shard_map/ppermute | solution.py:38
  26.0 9.6 %collective-permute-start.12 = (bf16[64,1792]{1,0:T(8,128)(2,1)S(1)}, bf16[64,1792]{1,0:T(8,128)(2,1)S(1)}, u32[]{:S(2)}, u32[]{:S(2)}) collective-permute-start(bf16[64,1792]{1,0:T(8,128)(2,1)S(1)} %get-tuple-element.27.refs_1_), channel_id=1, source_target_pairs={{0,16},{8,24},{16,0},{24,8},{1,17},{9,25},{17,1},{25,9},{2,18},{10... | collective-permute-start | bytes 688136 | tf_op jit(solution)/shard_map/ppermute | solution.py:38
  27.6 6.3 %collective-permute-start.14 = (f32[8,1792]{1,0:T(8,128)S(1)}, f32[8,1792]{1,0:T(8,128)S(1)}, u32[]{:S(2)}, u32[]{:S(2)}) collective-permute-start(f32[8,1792]{1,0:T(8,128)S(1)} %get-tuple-element.29), channel_id=1, source_target_pairs={{0,1},{1,2},{2,3},{3,0},{4,5},{5,6},{6,7},{7,4},{8,9},{9,10},{10,1... | collective-permute-start | bytes 172040 | tf_op jit(solution)/shard_map/ppermute | solution.py:32
  27.6 6.3 %collective-permute-start.15 = (f32[8,1792]{1,0:T(8,128)S(1)}, f32[8,1792]{1,0:T(8,128)S(1)}, u32[]{:S(2)}, u32[]{:S(2)}) collective-permute-start(f32[8,1792]{1,0:T(8,128)S(1)} %get-tuple-element.30), channel_id=1, source_target_pairs={{0,3},{1,0},{2,1},{3,2},{4,7},{5,4},{6,5},{7,6},{8,11},{9,8},{10,9... | collective-permute-start | bytes 172040 | tf_op jit(solution)/shard_map/ppermute | solution.py:32
  31.4 4.2 %collective-permute-start.16 = (f32[8,1792]{1,0:T(8,128)S(1)}, f32[8,1792]{1,0:T(8,128)S(1)}, u32[]{:S(2)}, u32[]{:S(2)}) collective-permute-start(f32[8,1792]{1,0:T(8,128)S(1)} %get-tuple-element.31), channel_id=1, source_target_pairs={{0,4},{4,0},{1,5},{5,1},{2,6},{6,2},{3,7},{7,3},{8,12},{12,8},{9,1... | collective-permute-start | bytes 172040 | tf_op jit(solution)/shard_map/ppermute | solution.py:32
  33.7 3.3 %copy-start.2 = (f32[8,8,1792]{2,1,0:T(8,128)S(1)}, f32[8,8,1792]{2,1,0:T(8,128)}, u32[]{:S(2)}) copy-start(f32[8,8,1792]{2,1,0:T(8,128)} %param.7) | copy-start | bytes 1376260
  35.6 1.5 %collective-permute-start.17 = (bf16[64,1792]{1,0:T(8,128)(2,1)S(1)}, bf16[64,1792]{1,0:T(8,128)(2,1)S(1)}, u32[]{:S(2)}, u32[]{:S(2)}) collective-permute-start(bf16[64,1792]{1,0:T(8,128)(2,1)S(1)} %hand_on.5.refs_1_), channel_id=1, source_target_pairs={{0,8},{8,0},{16,24},{24,16},{1,9},{9,1},{17,25},{25,17},{2,10},{10... | collective-permute-start | bytes 688136 | tf_op jit(solution)/shard_map/ppermute | solution.py:38

commit v7 on v6

--- a/solution.py
+++ b/solution.py
@@ -15,21 +15,30 @@
 
 
 def moves_of(count):
-    if count == 1:
-        return []
-    if count == 2:
-        return [[(0, 1), (1, 0)]]
-    return [
-        [(i, (i + 1) % count) for i in range(count)],
-        [(i, (i - 1) % count) for i in range(count)],
-    ]
+    moves = []
+    for first in (0, 1)[: count - 1]:
+        partner = list(range(count))
+        for low in range(first, count - 1, 2):
+            partner[low], partner[low + 1] = low + 1, low
+        moves.append(partner)
+    return moves
 
 
 def move_faces(faces):
     received = []
+    shards = lax.axis_size("mode")
     for axis in ("gy", "gx"):
-        moves = moves_of(lax.axis_size(axis))
-        received.append([lax.ppermute(face, axis, pairs) for face, pairs in zip(faces[axis], moves)])
+        count = lax.axis_size(axis)
+        arrived = []
+        for face, partner in zip(faces[axis], moves_of(count)):
+            pairs = []
+            for shard in range(shards):
+                for at in range(count):
+                    alone = partner[at] == at
+                    other = (shard ^ 1 if alone and shards > 1 else shard) * count + partner[at]
+                    pairs.append((shard * count + at, other))
+            arrived.append(lax.ppermute(face, ("mode", axis), pairs))
+        received.append(arrived)
     return received
 
 
@@ -65,11 +74,9 @@
 
 
 def store_faces(refs, axis, lanes, low, high):
-    if len(refs) == 1:
-        refs[0][:, lanes] = jnp.where(lax.axis_index(axis) == 0, high, low)
-    elif refs:
-        refs[0][:, lanes] = high
-        refs[1][:, lanes] = low
+    even = lax.rem(lax.axis_index(axis), 2) == 0
+    for ref, take_high in zip(refs, (even, jnp.logical_not(even))):
+        ref[:, lanes] = jnp.where(take_high, high, low)
 
 
 def write_faces(masked, lanes, first, second, x_refs, y_refs):
@@ -82,7 +89,9 @@
     if not refs:
         return zero, zero
     at = lax.axis_index(axis)
-    low, high = refs[0][:, lanes], refs[-1][:, lanes]
+    odd = lax.rem(at, 2) == 1
+    one, two = refs[0][:, lanes], refs[-1][:, lanes]
+    low, high = jnp.where(odd, one, two), jnp.where(odd, two, one)
     return jnp.where(at == 0, zero, low), jnp.where(at == lax.axis_size(axis) - 1, zero, high)
 
 

time: 49.2 us -> 47.8 us (0.972)
  starting transfers between devices: 21.6 us -> 16.7 us
  blocking collectives: 10.1 us -> 13 us
  waiting for transfers between devices: 8.27 us -> 8.88 us
    ppermute x9, starting transfers between devices: 16.1 us -> 9.62 us  [move_faces(): arrived.append(lax.ppermute(face, ('mode', axis), pairs))]
    all_to_all x1, blocking collectives: 10.1 us -> 13 us  [per_device(): gram = lax.all_to_all(gram, AXES, 0, 0)]
    ppermute x9, starting transfers between devices: 5.57 us -> 7.05 us  [exchange(): return lax.ppermute(array, 'mode', [(i, i ^ bit) for i in range(count)])]
    ppermute x9, waiting for transfers between devices: 5.41 us -> 5.93 us  [move_faces(): arrived.append(lax.ppermute(face, ('mode', axis), pairs))]
where the time goes in v7:
time: 47.8 us; the launch traced here: 47.6 us
  starting transfers between devices  16.7 us (35%)
  blocking collectives  13 us (27%)
  waiting for transfers between devices  8.88 us (19%)
  Pallas kernels  7.21 us (15%)
  local copies, waits for them, and re-layouts  1.06 us (2%)
  between operations  0.79 us (2%)
    all_to_all x1, blocking collectives, per_device(): gram = lax.all_to_all(gram, AXES, 0, 0)  13 us
    ppermute x9, starting transfers between devices, move_faces(): arrived.append(lax.ppermute(face, ('mode', axis), pairs))  9.62 us
    pallas_call x12, Pallas kernels, call(): pl.pallas_call(body, out_shape=list(shapes), in_specs=[spec for spec, ope...  7.2 us
    ppermute x9, starting transfers between devices, exchange(): return lax.ppermute(array, 'mode', [(i, i ^ bit) for i in range(count)])  7.05 us
    ppermute x9, waiting for transfers between devices, move_faces(): arrived.append(lax.ppermute(face, ('mode', axis), pairs))  5.93 us
    ppermute x9, waiting for transfers between devices, exchange(): return lax.ppermute(array, 'mode', [(i, i ^ bit) for i in range(count)])  2.96 us
    unnamed x16, local copies, waits for them, and re-layouts  1.06 us
  transfers between devices with their start and end apart: 18, of which 9 were waited for; matrix products, arithmetic and copies ran while one was open for 0% of the time, Pallas kernels for 9%

profile of v7, /device:TPU:0, one launch (start us, length us, event | category | flops | bytes accessed | tf_op | source)
XLA Modules:
  0.0 47.6 jit_solution(2516379125626027384)
XLA Ops:
  0.6 0.0 copy-start.1
  0.6 1.0 %copy-done.1 = f32[8,8,1792]{2,1,0:T(8,128)S(1)} copy-done((f32[8,8,1792]{2,1,0:T(8,128)S(1)}, f32[8,8,1792]{2,1,0:T(8,128)}, u32[]{:S(2)}) %copy-start.1) | copy-done | bytes 458776
  1.7 0.0 copy-start
  1.7 0.0 copy-start.3
  1.7 0.0 copy-start.4
  1.7 0.0 copy-start.5
  1.7 0.0 copy-start.6
  1.7 0.5 %collective-permute-start.1 = (bf16[64,1792]{1,0:T(8,128)(2,1)S(1)}, bf16[64,1792]{1,0:T(8,128)(2,1)S(1)}, u32[]{:S(2)}, u32[]{:S(2)}) collective-permute-start(bf16[64,1792]{1,0:T(8,128)(2,1)S(1)} %pack.1.refs_1_), channel_id=1, source_target_pairs={{0,8},{8,0},{16,24},{24,16},{1,9},{9,1},{17,25},{25,17},{2,10},{10... | collective-permute-start | bytes 688136 | tf_op jit(solution)/shard_map/ppermute | solution.py:47
  2.3 2.6 %collective-permute-start = (bf16[64,1792]{1,0:T(8,128)(2,1)S(1)}, bf16[64,1792]{1,0:T(8,128)(2,1)S(1)}, u32[]{:S(2)}, u32[]{:S(2)}) collective-permute-start(bf16[64,1792]{1,0:T(8,128)(2,1)S(1)} %pack.1.refs_1_), channel_id=1, source_target_pairs={{0,16},{8,24},{16,0},{24,8},{1,17},{9,25},{17,1},{25,9},{2,18},{10... | collective-permute-start | bytes 688136 | tf_op jit(solution)/shard_map/ppermute | solution.py:47
  4.9 0.2 prepare.1
  5.1 1.6 %collective-permute-start.2 = (f32[8,1792]{1,0:T(8,128)S(1)}, f32[8,1792]{1,0:T(8,128)S(1)}, u32[]{:S(2)}, u32[]{:S(2)}) collective-permute-start(f32[8,1792]{1,0:T(8,128)S(1)} %get-tuple-element.19), channel_id=1, source_target_pairs={{0,1},{1,0},{2,3},{3,2},{8,9},{9,8},{10,11},{11,10},{16,17},{17,16... | collective-permute-start | bytes 172040 | tf_op jit(solution)/shard_map/ppermute | solution.py:40
  6.7 0.0 collective-permute-start.3
  6.7 1.5 %collective-permute-start.4 = (f32[8,1792]{1,0:T(8,128)S(1)}, f32[8,1792]{1,0:T(8,128)S(1)}, u32[]{:S(2)}, u32[]{:S(2)}) collective-permute-start(f32[8,1792]{1,0:T(8,128)S(1)} %get-tuple-element.21), channel_id=1, source_target_pairs={{0,4},{4,0},{8,12},{12,8},{16,20},{20,16},{24,28},{28,24},{1,5},{5... | collective-permute-start | bytes 172040 | tf_op jit(solution)/shard_map/ppermute | solution.py:40
  8.2 0.8 %near_0.1.refs_1_.refs_3_ = f32[64,1792]{1,0:T(8,128)S(1)} custom-call(s32[8,14]{1,0:T(8,128)S(1)} %bitcast.8, bf16[64,1792]{1,0:T(8,128)(2,1)S(1)} %pack.1.refs_1_, bf16[64,1792]{1,0:T(8,128)(2,1)S(1)} %collective-permute-done.1.refs_2_, bf16[14,8,128,128]{3,2,1,0:T(8,128)(2,1)S(1)} %copy-done, f32[64,1792]{1,0:T(8,128)S(1)} %bitcast.5, ...), custom_call_target="tpu_custom_call" | custom-call | flops 117440512 | bytes 5115328 | tf_op jit(solution)/shard_map/near_0/pallas_call | solution.py:352
  9.1 0.2 collective-permute-done.2.refs_2_.refs_6_
  9.3 1.7 %collective-permute-done.4.refs_4_.refs_8_ = f32[8,1792]{1,0:T(8,128)S(1)} collective-permute-done((f32[8,1792]{1,0:T(8,128)S(1)}, f32[8,1792]{1,0:T(8,128)S(1)}, u32[]{:S(2)}, u32[]{:S(2)}) %collective-permute-start.4) | collective-permute-done | bytes 57376 | tf_op jit(solution)/shard_map/ppermute | solution.py:40
  11.1 0.0 collective-permute-start.5
  11.1 0.5 %middle_0.1.refs_3_ = f32[64,1792]{1,0:T(8,128)S(1)} custom-call(s32[8,14]{1,0:T(8,128)S(1)} %bitcast.9, bf16[64,1792]{1,0:T(8,128)(2,1)S(1)} %hand_on.3.refs_1_, bf16[14,8,128,128]{3,2,1,0:T(8,128)(2,1)S(1)} %copy-done, f32[64,1792]{1,0:T(8,128)S(1)} %near_0.1.refs_1_.refs_3_, f32[2,1792]{1,0:T(2,128)S(1)} %copy-done.3, s32[2,1792]{1,0:T(2,128)S(1)} %copy-done.4, ...), custom_call_target="tpu_custom_call" | custom-call | flops 58720256 | bytes 5018048 | tf_op jit(solution)/shard_map/middle_0/pallas_call | solution.py:352
  11.6 0.9 %collective-permute-done.5.refs_1_ = bf16[64,1792]{1,0:T(8,128)(2,1)S(1)} collective-permute-done((bf16[64,1792]{1,0:T(8,128)(2,1)S(1)}, bf16[64,1792]{1,0:T(8,128)(2,1)S(1)}, u32[]{:S(2)}, u32[]{:S(2)}) %collective-permute-start.5) | collective-permute-done | bytes 229408 | tf_op jit(solution)/shard_map/ppermute | solution.py:47
  12.5 0.5 %last_0.1 = (f32[8,1792]{1,0:T(8,128)S(1)}, f32[8,1792]{1,0:T(8,128)S(1)}, f32[8,1792]{1,0:T(8,128)S(1)}, bf16[64,1792]{1,0:T(8,128)(2,1)S(1)}, f32[64,1792]{1,0:T(8,128)S(1)}) custom-call(s32[8,14]{1,0:T(8,128)S(1)} %bitcast.10, bf16[64,1792]{1,0:T(8,128)(2,1)S(1)} %collective-permute-done.5.refs_1_, bf16[14,8,128,128]{3,2,1,0:T(8,128)(2,1)S(1)} %copy-done, ...), custom_call_target="tpu_custom_call" | custom-call | flops 58720256 | bytes 5251520 | tf_op jit(solution)/shard_map/last_0/pallas_call | solution.py:352
  13.1 0.2 collective-permute-start.7
  13.3 1.8 %collective-permute-start.6 = (bf16[64,1792]{1,0:T(8,128)(2,1)S(1)}, bf16[64,1792]{1,0:T(8,128)(2,1)S(1)}, u32[]{:S(2)}, u32[]{:S(2)}) collective-permute-start(bf16[64,1792]{1,0:T(8,128)(2,1)S(1)} %get-tuple-element.22.refs_1_), channel_id=1, source_target_pairs={{0,16},{8,24},{16,0},{24,8},{1,17},{9,25},{17,1},{25,9},{2,18},{10... | collective-permute-start | bytes 688136 | tf_op jit(solution)/shard_map/ppermute | solution.py:47
  15.1 1.7 %collective-permute-start.8 = (f32[8,1792]{1,0:T(8,128)S(1)}, f32[8,1792]{1,0:T(8,128)S(1)}, u32[]{:S(2)}, u32[]{:S(2)}) collective-permute-start(f32[8,1792]{1,0:T(8,128)S(1)} %get-tuple-element.24), channel_id=1, source_target_pairs={{0,1},{1,0},{2,3},{3,2},{8,9},{9,8},{10,11},{11,10},{16,17},{17,16... | collective-permute-start | bytes 172040 | tf_op jit(solution)/shard_map/ppermute | solution.py:40
  16.8 0.0 collective-permute-start.9
  16.8 1.5 %collective-permute-start.10 = (f32[8,1792]{1,0:T(8,128)S(1)}, f32[8,1792]{1,0:T(8,128)S(1)}, u32[]{:S(2)}, u32[]{:S(2)}) collective-permute-start(f32[8,1792]{1,0:T(8,128)S(1)} %get-tuple-element.26), channel_id=1, source_target_pairs={{0,4},{4,0},{8,12},{12,8},{16,20},{20,16},{24,28},{28,24},{1,5},{5... | collective-permute-start | bytes 172040 | tf_op jit(solution)/shard_map/ppermute | solution.py:40
  18.3 0.8 %near_1.1.refs_1_.refs_3_ = f32[64,1792]{1,0:T(8,128)S(1)} custom-call(s32[8,14]{1,0:T(8,128)S(1)} %bitcast.11, bf16[64,1792]{1,0:T(8,128)(2,1)S(1)} %get-tuple-element.22.refs_1_, bf16[64,1792]{1,0:T(8,128)(2,1)S(1)} %collective-permute-done.7.refs_2_, bf16[14,8,128,128]{3,2,1,0:T(8,128)(2,1)S(1)} %copy-done, ...), custom_call_target="tpu_custom_call" | custom-call | flops 117440512 | bytes 5115328 | tf_op jit(solution)/shard_map/near_1/pallas_call | solution.py:352
  19.1 0.1 collective-permute-done.8.refs_2_.refs_6_
  19.2 0.0 collective-permute-done.9.refs_3_.refs_7_
  19.2 1.9 %collective-permute-done.10.refs_4_.refs_8_ = f32[8,1792]{1,0:T(8,128)S(1)} collective-permute-done((f32[8,1792]{1,0:T(8,128)S(1)}, f32[8,1792]{1,0:T(8,128)S(1)}, u32[]{:S(2)}, u32[]{:S(2)}) %collective-permute-start.10) | collective-permute-done | bytes 57376 | tf_op jit(solution)/shard_map/ppermute | solution.py:40
  21.1 0.0 collective-permute-done.6.refs_0_
  21.2 0.5 %middle_1.1.refs_3_ = f32[64,1792]{1,0:T(8,128)S(1)} custom-call(s32[8,14]{1,0:T(8,128)S(1)} %bitcast.12, bf16[64,1792]{1,0:T(8,128)(2,1)S(1)} %hand_on.4.refs_1_, bf16[14,8,128,128]{3,2,1,0:T(8,128)(2,1)S(1)} %copy-done, f32[64,1792]{1,0:T(8,128)S(1)} %near_1.1.refs_1_.refs_3_, f32[2,1792]{1,0:T(2,128)S(1)} %copy-done.3, s32[2,1792]{1,0:T(2,128)S(1)} %copy-done.4, ...), custom_call_target="tpu_custom_call" | custom-call | flops 58720256 | bytes 5018048 | tf_op jit(solution)/shard_map/middle_1/pallas_call | solution.py:352
  21.7 1.0 %collective-permute-done.11.refs_1_ = bf16[64,1792]{1,0:T(8,128)(2,1)S(1)} collective-permute-done((bf16[64,1792]{1,0:T(8,128)(2,1)S(1)}, bf16[64,1792]{1,0:T(8,128)(2,1)S(1)}, u32[]{:S(2)}, u32[]{:S(2)}) %collective-permute-start.11) | collective-permute-done | bytes 229408 | tf_op jit(solution)/shard_map/ppermute | solution.py:47
  22.7 0.5 %last_1.1 = (f32[8,1792]{1,0:T(8,128)S(1)}, f32[8,1792]{1,0:T(8,128)S(1)}, f32[8,1792]{1,0:T(8,128)S(1)}, bf16[64,1792]{1,0:T(8,128)(2,1)S(1)}, f32[64,1792]{1,0:T(8,128)S(1)}) custom-call(s32[8,14]{1,0:T(8,128)S(1)} %bitcast.13, bf16[64,1792]{1,0:T(8,128)(2,1)S(1)} %collective-permute-done.11.refs_1_, bf16[14,8,128,128]{3,2,1,0:T(8,128)(2,1)S(1)} %copy-done, ...), custom_call_target="tpu_custom_call" | custom-call | flops 58720256 | bytes 5251520 | tf_op jit(solution)/shard_map/last_1/pallas_call | solution.py:352
  23.2 0.2 collective-permute-start.13
  23.4 1.8 %collective-permute-start.12 = (bf16[64,1792]{1,0:T(8,128)(2,1)S(1)}, bf16[64,1792]{1,0:T(8,128)(2,1)S(1)}, u32[]{:S(2)}, u32[]{:S(2)}) collective-permute-start(bf16[64,1792]{1,0:T(8,128)(2,1)S(1)} %get-tuple-element.27.refs_1_), channel_id=1, source_target_pairs={{0,16},{8,24},{16,0},{24,8},{1,17},{9,25},{17,1},{25,9},{2,18},{10... | collective-permute-start | bytes 688136 | tf_op jit(solution)/shard_map/ppermute | solution.py:47
  25.2 1.7 %collective-permute-start.14 = (f32[8,1792]{1,0:T(8,128)S(1)}, f32[8,1792]{1,0:T(8,128)S(1)}, u32[]{:S(2)}, u32[]{:S(2)}) collective-permute-start(f32[8,1792]{1,0:T(8,128)S(1)} %get-tuple-element.29), channel_id=1, source_target_pairs={{0,1},{1,0},{2,3},{3,2},{8,9},{9,8},{10,11},{11,10},{16,17},{17,16... | collective-permute-start | bytes 172040 | tf_op jit(solution)/shard_map/ppermute | solution.py:40
  26.9 1.5 %collective-permute-start.16 = (f32[8,1792]{1,0:T(8,128)S(1)}, f32[8,1792]{1,0:T(8,128)S(1)}, u32[]{:S(2)}, u32[]{:S(2)}) collective-permute-start(f32[8,1792]{1,0:T(8,128)S(1)} %get-tuple-element.31), channel_id=1, source_target_pairs={{0,4},{4,0},{8,12},{12,8},{16,20},{20,16},{24,28},{28,24},{1,5},{5... | collective-permute-start | bytes 172040 | tf_op jit(solution)/shard_map/ppermute | solution.py:40
  28.4 0.0 collective-permute-done.13.refs_2_
  28.4 0.8 %near_2.1.refs_1_.refs_3_ = f32[64,1792]{1,0:T(8,128)S(1)} custom-call(s32[8,14]{1,0:T(8,128)S(1)} %bitcast.14, bf16[64,1792]{1,0:T(8,128)(2,1)S(1)} %get-tuple-element.27.refs_1_, bf16[64,1792]{1,0:T(8,128)(2,1)S(1)} %collective-permute-done.13.refs_2_, bf16[14,8,128,128]{3,2,1,0:T(8,128)(2,1)S(1)} %copy-done, ...), custom_call_target="tpu_custom_call" | custom-call | flops 117440512 | bytes 5115328 | tf_op jit(solution)/shard_map/near_2/pallas_call | solution.py:352
  29.2 0.0 copy-start.2
  29.3 0.1 collective-permute-done.14.refs_2_.refs_6_
  29.3 1.9 %collective-permute-done.16.refs_4_.refs_8_ = f32[8,1792]{1,0:T(8,128)S(1)} collective-permute-done((f32[8,1792]{1,0:T(8,128)S(1)}, f32[8,1792]{1,0:T(8,128)S(1)}, u32[]{:S(2)}, u32[]{:S(2)}) %collective-permute-start.16) | collective-permute-done | bytes 57376 | tf_op jit(solution)/shard_map/ppermute | solution.py:40
  31.2 0.0 collective-permute-done.12.refs_0_
  31.3 0.5 %middle_2.1.refs_3_ = f32[64,1792]{1,0:T(8,128)S(1)} custom-call(s32[8,14]{1,0:T(8,128)S(1)} %bitcast.15, bf16[64,1792]{1,0:T(8,128)(2,1)S(1)} %hand_on.5.refs_1_, bf16[14,8,128,128]{3,2,1,0:T(8,128)(2,1)S(1)} %copy-done, f32[64,1792]{1,0:T(8,128)S(1)} %near_2.1.refs_1_.refs_3_, f32[2,1792]{1,0:T(2,128)S(1)} %copy-done.3, s32[2,1792]{1,0:T(2,128)S(1)} %copy-done.4, ...), custom_call_target="tpu_custom_call" | custom-call | flops 58720256 | bytes 5018048 | tf_op jit(solution)/shard_map/middle_2/pallas_call | solution.py:352
  31.8 1.0 %collective-permute-done.17.refs_1_ = bf16[64,1792]{1,0:T(8,128)(2,1)S(1)} collective-permute-done((bf16[64,1792]{1,0:T(8,128)(2,1)S(1)}, bf16[64,1792]{1,0:T(8,128)(2,1)S(1)}, u32[]{:S(2)}, u32[]{:S(2)}) %collective-permute-start.17) | collective-permute-done | bytes 229408 | tf_op jit(solution)/shard_map/ppermute | solution.py:47
  32.8 0.7 %last_2.1 = f32[32,1,128]{2,1,0:T(1,128)S(1)} custom-call(s32[8,14]{1,0:T(8,128)S(1)} %bitcast.16, bf16[64,1792]{1,0:T(8,128)(2,1)S(1)} %collective-permute-done.17.refs_1_, bf16[14,8,128,128]{3,2,1,0:T(8,128)(2,1)S(1)} %copy-done, f32[64,1792]{1,0:T(8,128)S(1)} %middle_2.1.refs_3_, f32[64,128]{1,0:T(8,128)S(1)} %get-tuple-element.18.refs_5_.refs_4_, ...), custom_call_target="tpu_custom_call" | custom-call | flops 58720256 | bytes 5784000 | tf_op jit(solution)/shard_map/last_2/pallas_call | solution.py:352
  33.5 13.0 %all_to_all.5.refs_0_ = f32[32,1,128]{2,1,0:T(1,128)S(1)} all-to-all(f32[32,1,128]{2,1,0:T(1,128)S(1)} %last_2.1), channel_id=1, replica_groups=mesh['mode'=4,'gx'=2,'gy'=4] {'mode','gx','gy'}, dimensions={0} | all-to-all | bytes 32768 | tf_op jit(solution)/shard_map/all_to_all | solution.py:498
  46.5 1.1 %finish.1 = (f32[64,1792]{1,0:T(8,128)}, f32[4,3]{1,0:T(4,128)}) custom-call(f32[32,1,128]{2,1,0:T(1,128)S(1)} %all_to_all.5.refs_0_, f32[64,1792]{1,0:T(8,128)S(1)} %bitcast.7, f32[64,1792]{1,0:T(8,128)S(1)} %get-tuple-element.23.refs_4_.refs_6_.refs_2_, f32[64,1792]{1,0:T(8,128)S(1)} %get-tuple-element.28.refs_4_.refs_7_.refs_3_), custom_call_target="tpu_custom_call" | custom-call | bytes 1851440 | tf_op jit(solution)/shard_map/finish/pallas_call | solution.py:352
  (20 shorter events, 0.1 us)
Async XLA Ops:
  0.6 1.0 %copy-start.1 = (f32[8,8,1792]{2,1,0:T(8,128)S(1)}, f32[8,8,1792]{2,1,0:T(8,128)}, u32[]{:S(2)}) copy-start(f32[8,8,1792]{2,1,0:T(8,128)} %param.7) | copy-start | bytes 1376260
  1.7 3.2 %copy-start.7 = (s32[8,8]{1,0:T(8,128)S(1)}, s32[8,8]{1,0:T(8,128)}, u32[]{:S(2)}) copy-start(s32[8,8]{1,0:T(8,128)} %refs_1_.1) | copy-start | bytes 772
  1.7 6.5 %copy-start = (bf16[14,8,128,128]{3,2,1,0:T(8,128)(2,1)S(1)}, bf16[14,8,128,128]{3,2,1,0:T(8,128)(2,1)}, u32[]{:S(2)}) copy-start(bf16[14,8,128,128]{3,2,1,0:T(8,128)(2,1)} %refs_2_.11) | copy-start | bytes 11010052
  1.7 6.5 %copy-start.3 = (f32[2,1792]{1,0:T(2,128)S(1)}, f32[2,1792]{1,0:T(2,128)}, u32[]{:S(2)}) copy-start(f32[2,1792]{1,0:T(2,128)} %refs_4_.5) | copy-start | bytes 43012
  1.7 6.5 %copy-start.4 = (s32[2,1792]{1,0:T(2,128)S(1)}, s32[2,1792]{1,0:T(2,128)}, u32[]{:S(2)}) copy-start(s32[2,1792]{1,0:T(2,128)} %refs_5_.5) | copy-start | bytes 43012
  1.7 6.5 %copy-start.5 = (s32[14,8]{0,1:T(8,128)S(1)}, s32[14,8]{0,1:T(8,128)}, u32[]{:S(2)}) copy-start(s32[14,8]{0,1:T(8,128)} %param.8) | copy-start | bytes 1348
  1.7 6.5 %copy-start.6 = (f32[1792]{0:T(1024)S(1)}, f32[1792]{0:T(1024)}, u32[]{:S(2)}) copy-start(f32[1792]{0:T(1024)} %refs_6_.5) | copy-start | bytes 21508
  1.7 6.5 %collective-permute-start.1 = (bf16[64,1792]{1,0:T(8,128)(2,1)S(1)}, bf16[64,1792]{1,0:T(8,128)(2,1)S(1)}, u32[]{:S(2)}, u32[]{:S(2)}) collective-permute-start(bf16[64,1792]{1,0:T(8,128)(2,1)S(1)} %pack.1.refs_1_), channel_id=1, source_target_pairs={{0,8},{8,0},{16,24},{24,16},{1,9},{9,1},{17,25},{25,17},{2,10},{10... | collective-permute-start | bytes 688136 | tf_op jit(solution)/shard_map/ppermute | solution.py:47
  2.3 8.8 %collective-permute-start = (bf16[64,1792]{1,0:T(8,128)(2,1)S(1)}, bf16[64,1792]{1,0:T(8,128)(2,1)S(1)}, u32[]{:S(2)}, u32[]{:S(2)}) collective-permute-start(bf16[64,1792]{1,0:T(8,128)(2,1)S(1)} %pack.1.refs_1_), channel_id=1, source_target_pairs={{0,16},{8,24},{16,0},{24,8},{1,17},{9,25},{17,1},{25,9},{2,18},{10... | collective-permute-start | bytes 688136 | tf_op jit(solution)/shard_map/ppermute | solution.py:47
  5.1 4.2 %collective-permute-start.2 = (f32[8,1792]{1,0:T(8,128)S(1)}, f32[8,1792]{1,0:T(8,128)S(1)}, u32[]{:S(2)}, u32[]{:S(2)}) collective-permute-start(f32[8,1792]{1,0:T(8,128)S(1)} %get-tuple-element.19), channel_id=1, source_target_pairs={{0,1},{1,0},{2,3},{3,2},{8,9},{9,8},{10,11},{11,10},{16,17},{17,16... | collective-permute-start | bytes 172040 | tf_op jit(solution)/shard_map/ppermute | solution.py:40
  6.7 2.6 %collective-permute-start.3 = (f32[8,1792]{1,0:T(8,128)S(1)}, f32[8,1792]{1,0:T(8,128)S(1)}, u32[]{:S(2)}, u32[]{:S(2)}) collective-permute-start(f32[8,1792]{1,0:T(8,128)S(1)} %get-tuple-element.20), channel_id=1, source_target_pairs={{0,8},{1,2},{2,1},{3,11},{8,0},{9,10},{10,9},{11,3},{16,24},{17,18... | collective-permute-start | bytes 172040 | tf_op jit(solution)/shard_map/ppermute | solution.py:40
  6.7 4.3 %collective-permute-start.4 = (f32[8,1792]{1,0:T(8,128)S(1)}, f32[8,1792]{1,0:T(8,128)S(1)}, u32[]{:S(2)}, u32[]{:S(2)}) collective-permute-start(f32[8,1792]{1,0:T(8,128)S(1)} %get-tuple-element.21), channel_id=1, source_target_pairs={{0,4},{4,0},{8,12},{12,8},{16,20},{20,16},{24,28},{28,24},{1,5},{5... | collective-permute-start | bytes 172040 | tf_op jit(solution)/shard_map/ppermute | solution.py:40
  11.1 1.5 %collective-permute-start.5 = (bf16[64,1792]{1,0:T(8,128)(2,1)S(1)}, bf16[64,1792]{1,0:T(8,128)(2,1)S(1)}, u32[]{:S(2)}, u32[]{:S(2)}) collective-permute-start(bf16[64,1792]{1,0:T(8,128)(2,1)S(1)} %hand_on.3.refs_1_), channel_id=1, source_target_pairs={{0,8},{8,0},{16,24},{24,16},{1,9},{9,1},{17,25},{25,17},{2,10},{10... | collective-permute-start | bytes 688136 | tf_op jit(solution)/shard_map/ppermute | solution.py:47
  13.1 5.2 %collective-permute-start.7 = (bf16[64,1792]{1,0:T(8,128)(2,1)S(1)}, bf16[64,1792]{1,0:T(8,128)(2,1)S(1)}, u32[]{:S(2)}, u32[]{:S(2)}) collective-permute-start(bf16[64,1792]{1,0:T(8,128)(2,1)S(1)} %get-tuple-element.22.refs_1_), channel_id=1, source_target_pairs={{0,8},{8,0},{16,24},{24,16},{1,9},{9,1},{17,25},{25,17},{2,10},{10... | collective-permute-start | bytes 688136 | tf_op jit(solution)/shard_map/ppermute | solution.py:47
  13.3 7.9 %collective-permute-start.6 = (bf16[64,1792]{1,0:T(8,128)(2,1)S(1)}, bf16[64,1792]{1,0:T(8,128)(2,1)S(1)}, u32[]{:S(2)}, u32[]{:S(2)}) collective-permute-start(bf16[64,1792]{1,0:T(8,128)(2,1)S(1)} %get-tuple-element.22.refs_1_), channel_id=1, source_target_pairs={{0,16},{8,24},{16,0},{24,8},{1,17},{9,25},{17,1},{25,9},{2,18},{10... | collective-permute-start | bytes 688136 | tf_op jit(solution)/shard_map/ppermute | solution.py:47
  15.1 4.2 %collective-permute-start.8 = (f32[8,1792]{1,0:T(8,128)S(1)}, f32[8,1792]{1,0:T(8,128)S(1)}, u32[]{:S(2)}, u32[]{:S(2)}) collective-permute-start(f32[8,1792]{1,0:T(8,128)S(1)} %get-tuple-element.24), channel_id=1, source_target_pairs={{0,1},{1,0},{2,3},{3,2},{8,9},{9,8},{10,11},{11,10},{16,17},{17,16... | collective-permute-start | bytes 172040 | tf_op jit(solution)/shard_map/ppermute | solution.py:40
  16.8 2.4 %collective-permute-start.9 = (f32[8,1792]{1,0:T(8,128)S(1)}, f32[8,1792]{1,0:T(8,128)S(1)}, u32[]{:S(2)}, u32[]{:S(2)}) collective-permute-start(f32[8,1792]{1,0:T(8,128)S(1)} %get-tuple-element.25), channel_id=1, source_target_pairs={{0,8},{1,2},{2,1},{3,11},{8,0},{9,10},{10,9},{11,3},{16,24},{17,18... | collective-permute-start | bytes 172040 | tf_op jit(solution)/shard_map/ppermute | solution.py:40
  16.8 4.3 %collective-permute-start.10 = (f32[8,1792]{1,0:T(8,128)S(1)}, f32[8,1792]{1,0:T(8,128)S(1)}, u32[]{:S(2)}, u32[]{:S(2)}) collective-permute-start(f32[8,1792]{1,0:T(8,128)S(1)} %get-tuple-element.26), channel_id=1, source_target_pairs={{0,4},{4,0},{8,12},{12,8},{16,20},{20,16},{24,28},{28,24},{1,5},{5... | collective-permute-start | bytes 172040 | tf_op jit(solution)/shard_map/ppermute | solution.py:40
  21.2 1.5 %collective-permute-start.11 = (bf16[64,1792]{1,0:T(8,128)(2,1)S(1)}, bf16[64,1792]{1,0:T(8,128)(2,1)S(1)}, u32[]{:S(2)}, u32[]{:S(2)}) collective-permute-start(bf16[64,1792]{1,0:T(8,128)(2,1)S(1)} %hand_on.4.refs_1_), channel_id=1, source_target_pairs={{0,8},{8,0},{16,24},{24,16},{1,9},{9,1},{17,25},{25,17},{2,10},{10... | collective-permute-start | bytes 688136 | tf_op jit(solution)/shard_map/ppermute | solution.py:47
  23.2 5.2 %collective-permute-start.13 = (bf16[64,1792]{1,0:T(8,128)(2,1)S(1)}, bf16[64,1792]{1,0:T(8,128)(2,1)S(1)}, u32[]{:S(2)}, u32[]{:S(2)}) collective-permute-start(bf16[64,1792]{1,0:T(8,128)(2,1)S(1)} %get-tuple-element.27.refs_1_), channel_id=1, source_target_pairs={{0,8},{8,0},{16,24},{24,16},{1,9},{9,1},{17,25},{25,17},{2,10},{10... | collective-permute-start | bytes 688136 | tf_op jit(solution)/shard_map/ppermute | solution.py:47
  23.4 7.9 %collective-permute-start.12 = (bf16[64,1792]{1,0:T(8,128)(2,1)S(1)}, bf16[64,1792]{1,0:T(8,128)(2,1)S(1)}, u32[]{:S(2)}, u32[]{:S(2)}) collective-permute-start(bf16[64,1792]{1,0:T(8,128)(2,1)S(1)} %get-tuple-element.27.refs_1_), channel_id=1, source_target_pairs={{0,16},{8,24},{16,0},{24,8},{1,17},{9,25},{17,1},{25,9},{2,18},{10... | collective-permute-start | bytes 688136 | tf_op jit(solution)/shard_map/ppermute | solution.py:47
  25.2 4.2 %collective-permute-start.14 = (f32[8,1792]{1,0:T(8,128)S(1)}, f32[8,1792]{1,0:T(8,128)S(1)}, u32[]{:S(2)}, u32[]{:S(2)}) collective-permute-start(f32[8,1792]{1,0:T(8,128)S(1)} %get-tuple-element.29), channel_id=1, source_target_pairs={{0,1},{1,0},{2,3},{3,2},{8,9},{9,8},{10,11},{11,10},{16,17},{17,16... | collective-permute-start | bytes 172040 | tf_op jit(solution)/shard_map/ppermute | solution.py:40
  26.9 2.4 %collective-permute-start.15 = (f32[8,1792]{1,0:T(8,128)S(1)}, f32[8,1792]{1,0:T(8,128)S(1)}, u32[]{:S(2)}, u32[]{:S(2)}) collective-permute-start(f32[8,1792]{1,0:T(8,128)S(1)} %get-tuple-element.30), channel_id=1, source_target_pairs={{0,8},{1,2},{2,1},{3,11},{8,0},{9,10},{10,9},{11,3},{16,24},{17,18... | collective-permute-start | bytes 172040 | tf_op jit(solution)/shard_map/ppermute | solution.py:40
  26.9 4.3 %collective-permute-start.16 = (f32[8,1792]{1,0:T(8,128)S(1)}, f32[8,1792]{1,0:T(8,128)S(1)}, u32[]{:S(2)}, u32[]{:S(2)}) collective-permute-start(f32[8,1792]{1,0:T(8,128)S(1)} %get-tuple-element.31), channel_id=1, source_target_pairs={{0,4},{4,0},{8,12},{12,8},{16,20},{20,16},{24,28},{28,24},{1,5},{5... | collective-permute-start | bytes 172040 | tf_op jit(solution)/shard_map/ppermute | solution.py:40
  29.2 3.5 %copy-start.2 = (f32[8,8,1792]{2,1,0:T(8,128)S(1)}, f32[8,8,1792]{2,1,0:T(8,128)}, u32[]{:S(2)}) copy-start(f32[8,8,1792]{2,1,0:T(8,128)} %param.7) | copy-start | bytes 1376260
  31.3 1.5 %collective-permute-start.17 = (bf16[64,1792]{1,0:T(8,128)(2,1)S(1)}, bf16[64,1792]{1,0:T(8,128)(2,1)S(1)}, u32[]{:S(2)}, u32[]{:S(2)}) collective-permute-start(bf16[64,1792]{1,0:T(8,128)(2,1)S(1)} %hand_on.5.refs_1_), channel_id=1, source_target_pairs={{0,8},{8,0},{16,24},{24,16},{1,9},{9,1},{17,25},{25,17},{2,10},{10... | collective-permute-start | bytes 688136 | tf_op jit(solution)/shard_map/ppermute | solution.py:47

commit v8 on v7

--- a/solution.py
+++ b/solution.py
@@ -305,7 +305,7 @@
 
 
 def finish_kernel(gram_ref, *refs):
-    vectors, (solution_ref, hessenberg_ref) = refs[:KRYLOV], refs[KRYLOV:]
+    vectors, (solution_ref, hessenberg_ref, held_ref, sems) = refs[:KRYLOV], refs[KRYLOV:]
     block = gram_ref.shape[2]
     total = jnp.sum(gram_ref[...], axis=0)
     lane = lax.broadcasted_iota(jnp.int32, (1, block), 1)
@@ -324,11 +324,21 @@
         for j in range(KRYLOV):
             table = jnp.where((rows == i) & (cols == j), hessenberg[i][j][:, :KRYLOV], table)
     hessenberg_ref[...] = table
-    for b in range(solution_ref.shape[1] // block):
-        lanes = slice(b * block, (b + 1) * block)
-        solution_ref[:, lanes] = sum(
-            weight * ref[:, lanes] for weight, ref in zip(weights, vectors)
+    rows = held_ref.shape[0] // sems.shape[0]
+    copies = []
+    for part in range(sems.shape[0]):
+        cells = slice(part * rows, (part + 1) * rows)
+        for b in range(held_ref.shape[1] // block):
+            lanes = slice(b * block, (b + 1) * block)
+            held_ref[cells, lanes] = sum(
+                weight * ref[cells, lanes] for weight, ref in zip(weights, vectors)
+            )
+        copies.append(
+            pltpu.make_async_copy(held_ref.at[cells, :], solution_ref.at[cells, :], sems.at[part])
         )
+        copies[-1].start()
+    for copy in copies:
+        copy.wait()
 
 
 VMEM = pl.BlockSpec(memory_space=pltpu.VMEM)
@@ -336,7 +346,7 @@
 SCOPED = 16 * 1024 * 1024
 
 
-def call(name, kernel, groups, shapes, scratch=(), flops=0):
+def call(name, kernel, groups, shapes, scratch=(), flops=0, out_specs=None):
     flat = [pair for group in groups for pair in group]
 
     def body(*refs):
@@ -353,7 +363,7 @@
         body,
         out_shape=list(shapes),
         in_specs=[spec for spec, operand in flat],
-        out_specs=[VMEM] * len(shapes),
+        out_specs=out_specs or [VMEM] * len(shapes),
         scratch_shapes=list(scratch),
         compiler_params=pltpu.CompilerParams(vmem_limit_bytes=SCOPED),
         cost_estimate=pl.CostEstimate(flops=flops, bytes_accessed=size, transcendentals=0),
@@ -435,12 +445,12 @@
             flops=work * len(near),
         )
 
-        held = dict(zip(held, hand_on(list(held.values()), [partial, *y_in, *x_in])))
+        held = dict(zip(held, hand_on(list(held.values()), [partial, *x_in, *y_in])))
         for place, array in held.items():
             sources[place] = array
             sources[place ^ 1] = exchange(array, 1)
 
-        def middle_step(cols, sources, rest, y_in, x_in, outs, scratch):
+        def middle_step(cols, sources, rest, x_in, y_in, outs, scratch):
             middle_kernel(
                 sizes, per_owner, middle, cols[0], sources, *rest, x_in, y_in, outs[0]
             )
@@ -452,8 +462,8 @@
                 in_vmem([columns]),
                 in_vmem([sources[place] for place in middle]),
                 in_vmem([blocks, partial, drift_speed, upwind_sign]),
+                in_vmem(x_in),
                 in_vmem(y_in),
-                in_vmem(x_in),
             ],
             [vector_shape],
             flops=work * len(middle),
@@ -498,13 +508,15 @@
     gram = lax.all_to_all(gram, AXES, 0, 0)
 
     def finish(ins, outs, scratch):
-        finish_kernel(*ins, *outs)
+        finish_kernel(*ins, *outs, *scratch)
 
     solution, hessenberg = call(
         "finish",
         finish,
         [in_vmem([gram, *vectors])],
         [vector_shape, shape_of((KRYLOV + 1, KRYLOV), f32)],
+        [pltpu.VMEM((cells, local_modes), f32), pltpu.SemaphoreType.DMA((cells // 16,))],
+        out_specs=[ANY, VMEM],
     )
     return solution.reshape(first, second, local_modes), hessenberg
 

time: 47.8 us -> 48.3 us (1.010)
  Pallas kernels: 7.21 us -> 7.74 us
    ppermute x9, waiting for transfers between devices: 2.96 us -> 4 us  [exchange(): return lax.ppermute(array, 'mode', [(i, i ^ bit) for i in range(count)])]
    ppermute x9, waiting for transfers between devices: 5.93 us -> 5.2 us  [move_faces(): arrived.append(lax.ppermute(face, ('mode', axis), pairs))]
    pallas_call x12, Pallas kernels: 7.2 us -> 7.74 us  [call(): pl.pallas_call(body, out_shape=list(shapes), in_specs=[spec for spec, ope...]
  transfers between devices with their start and end apart: 18 -> 18, of which waited for: 9 -> 12; matrix products, arithmetic and copies ran while one was open for 0% -> 0% of each run, Pallas kernels for 9% -> 9%
where the time goes in v8:
time: 48.3 us; the launch traced here: 48.1 us
  starting transfers between devices  16.3 us (34%)
  blocking collectives  13 us (27%)
  waiting for transfers between devices  9.2 us (19%)
  Pallas kernels  7.74 us (16%)
  local copies, waits for them, and re-layouts  1.06 us (2%)
  between operations  0.8 us (2%)
    all_to_all x1, blocking collectives, per_device(): gram = lax.all_to_all(gram, AXES, 0, 0)  13 us
    ppermute x9, starting transfers between devices, move_faces(): arrived.append(lax.ppermute(face, ('mode', axis), pairs))  9.28 us
    pallas_call x12, Pallas kernels, call(): pl.pallas_call(body, out_shape=list(shapes), in_specs=[spec for spec, ope...  7.74 us
    ppermute x9, starting transfers between devices, exchange(): return lax.ppermute(array, 'mode', [(i, i ^ bit) for i in range(count)])  7.05 us
    ppermute x9, waiting for transfers between devices, move_faces(): arrived.append(lax.ppermute(face, ('mode', axis), pairs))  5.2 us
    ppermute x9, waiting for transfers between devices, exchange(): return lax.ppermute(array, 'mode', [(i, i ^ bit) for i in range(count)])  4 us
    unnamed x16, local copies, waits for them, and re-layouts  1.06 us
  transfers between devices with their start and end apart: 18, of which 12 were waited for; matrix products, arithmetic and copies ran while one was open for 0% of the time, Pallas kernels for 9%

profile of v8, /device:TPU:0, one launch (start us, length us, event | category | flops | bytes accessed | tf_op | source)
XLA Modules:
  0.0 48.1 jit_solution(4913494066106884092)
XLA Ops:
  0.6 0.0 copy-start.1
  0.6 1.0 %copy-done.1 = f32[8,8,1792]{2,1,0:T(8,128)S(1)} copy-done((f32[8,8,1792]{2,1,0:T(8,128)S(1)}, f32[8,8,1792]{2,1,0:T(8,128)}, u32[]{:S(2)}) %copy-start.1) | copy-done | bytes 458776
  1.7 0.0 copy-start
  1.7 0.0 copy-start.3
  1.7 0.0 copy-start.4
  1.7 0.0 copy-start.5
  1.7 0.0 copy-start.6
  1.7 0.5 %collective-permute-start.1 = (bf16[64,1792]{1,0:T(8,128)(2,1)S(1)}, bf16[64,1792]{1,0:T(8,128)(2,1)S(1)}, u32[]{:S(2)}, u32[]{:S(2)}) collective-permute-start(bf16[64,1792]{1,0:T(8,128)(2,1)S(1)} %pack.1.refs_1_), channel_id=1, source_target_pairs={{0,8},{8,0},{16,24},{24,16},{1,9},{9,1},{17,25},{25,17},{2,10},{10... | collective-permute-start | bytes 688136 | tf_op jit(solution)/shard_map/ppermute | solution.py:47
  2.3 2.6 %collective-permute-start = (bf16[64,1792]{1,0:T(8,128)(2,1)S(1)}, bf16[64,1792]{1,0:T(8,128)(2,1)S(1)}, u32[]{:S(2)}, u32[]{:S(2)}) collective-permute-start(bf16[64,1792]{1,0:T(8,128)(2,1)S(1)} %pack.1.refs_1_), channel_id=1, source_target_pairs={{0,16},{8,24},{16,0},{24,8},{1,17},{9,25},{17,1},{25,9},{2,18},{10... | collective-permute-start | bytes 688136 | tf_op jit(solution)/shard_map/ppermute | solution.py:47
  4.9 0.2 prepare.1
  5.1 1.6 %collective-permute-start.2 = (f32[8,1792]{1,0:T(8,128)S(1)}, f32[8,1792]{1,0:T(8,128)S(1)}, u32[]{:S(2)}, u32[]{:S(2)}) collective-permute-start(f32[8,1792]{1,0:T(8,128)S(1)} %get-tuple-element.19), channel_id=1, source_target_pairs={{0,4},{4,0},{8,12},{12,8},{16,20},{20,16},{24,28},{28,24},{1,5},{5... | collective-permute-start | bytes 172040 | tf_op jit(solution)/shard_map/ppermute | solution.py:40
  6.6 1.6 %collective-permute-start.3 = (f32[8,1792]{1,0:T(8,128)S(1)}, f32[8,1792]{1,0:T(8,128)S(1)}, u32[]{:S(2)}, u32[]{:S(2)}) collective-permute-start(f32[8,1792]{1,0:T(8,128)S(1)} %get-tuple-element.20), channel_id=1, source_target_pairs={{0,1},{1,0},{2,3},{3,2},{8,9},{9,8},{10,11},{11,10},{16,17},{17,16... | collective-permute-start | bytes 172040 | tf_op jit(solution)/shard_map/ppermute | solution.py:40
  8.2 0.0 collective-permute-start.4
  8.3 0.8 %near_0.1.refs_1_.refs_3_ = f32[64,1792]{1,0:T(8,128)S(1)} custom-call(s32[8,14]{1,0:T(8,128)S(1)} %bitcast.8, bf16[64,1792]{1,0:T(8,128)(2,1)S(1)} %pack.1.refs_1_, bf16[64,1792]{1,0:T(8,128)(2,1)S(1)} %collective-permute-done.1.refs_2_, bf16[14,8,128,128]{3,2,1,0:T(8,128)(2,1)S(1)} %copy-done, f32[64,1792]{1,0:T(8,128)S(1)} %bitcast.5, ...), custom_call_target="tpu_custom_call" | custom-call | flops 117440512 | bytes 5115328 | tf_op jit(solution)/shard_map/near_0/pallas_call | solution.py:362
  9.1 0.2 collective-permute-done.2.refs_2_.refs_6_
  9.3 1.5 %collective-permute-done.3.refs_3_.refs_7_ = f32[8,1792]{1,0:T(8,128)S(1)} collective-permute-done((f32[8,1792]{1,0:T(8,128)S(1)}, f32[8,1792]{1,0:T(8,128)S(1)}, u32[]{:S(2)}, u32[]{:S(2)}) %collective-permute-start.3) | collective-permute-done | bytes 57376 | tf_op jit(solution)/shard_map/ppermute | solution.py:40
  10.8 0.0 collective-permute-done.4.refs_4_.refs_8_
  10.8 0.2 collective-permute-done.refs_0_
  11.1 0.0 collective-permute-start.5
  11.1 0.5 %middle_0.1.refs_3_ = f32[64,1792]{1,0:T(8,128)S(1)} custom-call(s32[8,14]{1,0:T(8,128)S(1)} %bitcast.9, bf16[64,1792]{1,0:T(8,128)(2,1)S(1)} %hand_on.3.refs_1_, bf16[14,8,128,128]{3,2,1,0:T(8,128)(2,1)S(1)} %copy-done, f32[64,1792]{1,0:T(8,128)S(1)} %near_0.1.refs_1_.refs_3_, f32[2,1792]{1,0:T(2,128)S(1)} %copy-done.3, s32[2,1792]{1,0:T(2,128)S(1)} %copy-done.4, ...), custom_call_target="tpu_custom_call" | custom-call | flops 58720256 | bytes 5018048 | tf_op jit(solution)/shard_map/middle_0/pallas_call | solution.py:362
  11.6 1.0 %collective-permute-done.5.refs_1_ = bf16[64,1792]{1,0:T(8,128)(2,1)S(1)} collective-permute-done((bf16[64,1792]{1,0:T(8,128)(2,1)S(1)}, bf16[64,1792]{1,0:T(8,128)(2,1)S(1)}, u32[]{:S(2)}, u32[]{:S(2)}) %collective-permute-start.5) | collective-permute-done | bytes 229408 | tf_op jit(solution)/shard_map/ppermute | solution.py:47
  12.5 0.5 %last_0.1 = (f32[8,1792]{1,0:T(8,128)S(1)}, f32[8,1792]{1,0:T(8,128)S(1)}, f32[8,1792]{1,0:T(8,128)S(1)}, bf16[64,1792]{1,0:T(8,128)(2,1)S(1)}, f32[64,1792]{1,0:T(8,128)S(1)}) custom-call(s32[8,14]{1,0:T(8,128)S(1)} %bitcast.10, bf16[64,1792]{1,0:T(8,128)(2,1)S(1)} %collective-permute-done.5.refs_1_, bf16[14,8,128,128]{3,2,1,0:T(8,128)(2,1)S(1)} %copy-done, ...), custom_call_target="tpu_custom_call" | custom-call | flops 58720256 | bytes 5251520 | tf_op jit(solution)/shard_map/last_0/pallas_call | solution.py:362
  13.1 0.2 collective-permute-start.7
  13.3 1.8 %collective-permute-start.6 = (bf16[64,1792]{1,0:T(8,128)(2,1)S(1)}, bf16[64,1792]{1,0:T(8,128)(2,1)S(1)}, u32[]{:S(2)}, u32[]{:S(2)}) collective-permute-start(bf16[64,1792]{1,0:T(8,128)(2,1)S(1)} %get-tuple-element.22.refs_1_), channel_id=1, source_target_pairs={{0,16},{8,24},{16,0},{24,8},{1,17},{9,25},{17,1},{25,9},{2,18},{10... | collective-permute-start | bytes 688136 | tf_op jit(solution)/shard_map/ppermute | solution.py:47
  15.1 1.5 %collective-permute-start.8 = (f32[8,1792]{1,0:T(8,128)S(1)}, f32[8,1792]{1,0:T(8,128)S(1)}, u32[]{:S(2)}, u32[]{:S(2)}) collective-permute-start(f32[8,1792]{1,0:T(8,128)S(1)} %get-tuple-element.24), channel_id=1, source_target_pairs={{0,4},{4,0},{8,12},{12,8},{16,20},{20,16},{24,28},{28,24},{1,5},{5... | collective-permute-start | bytes 172040 | tf_op jit(solution)/shard_map/ppermute | solution.py:40
  16.5 1.6 %collective-permute-start.9 = (f32[8,1792]{1,0:T(8,128)S(1)}, f32[8,1792]{1,0:T(8,128)S(1)}, u32[]{:S(2)}, u32[]{:S(2)}) collective-permute-start(f32[8,1792]{1,0:T(8,128)S(1)} %get-tuple-element.25), channel_id=1, source_target_pairs={{0,1},{1,0},{2,3},{3,2},{8,9},{9,8},{10,11},{11,10},{16,17},{17,16... | collective-permute-start | bytes 172040 | tf_op jit(solution)/shard_map/ppermute | solution.py:40
  18.1 0.0 collective-permute-start.10
  18.1 0.8 %near_1.1.refs_1_.refs_3_ = f32[64,1792]{1,0:T(8,128)S(1)} custom-call(s32[8,14]{1,0:T(8,128)S(1)} %bitcast.11, bf16[64,1792]{1,0:T(8,128)(2,1)S(1)} %get-tuple-element.22.refs_1_, bf16[64,1792]{1,0:T(8,128)(2,1)S(1)} %collective-permute-done.7.refs_2_, bf16[14,8,128,128]{3,2,1,0:T(8,128)(2,1)S(1)} %copy-done, ...), custom_call_target="tpu_custom_call" | custom-call | flops 117440512 | bytes 5115328 | tf_op jit(solution)/shard_map/near_1/pallas_call | solution.py:362
  19.0 0.3 collective-permute-done.8.refs_2_.refs_6_
  19.2 1.5 %collective-permute-done.9.refs_3_.refs_7_ = f32[8,1792]{1,0:T(8,128)S(1)} collective-permute-done((f32[8,1792]{1,0:T(8,128)S(1)}, f32[8,1792]{1,0:T(8,128)S(1)}, u32[]{:S(2)}, u32[]{:S(2)}) %collective-permute-start.9) | collective-permute-done | bytes 57376 | tf_op jit(solution)/shard_map/ppermute | solution.py:40
  20.7 0.4 collective-permute-done.6.refs_0_
  21.2 0.5 %middle_1.1.refs_3_ = f32[64,1792]{1,0:T(8,128)S(1)} custom-call(s32[8,14]{1,0:T(8,128)S(1)} %bitcast.12, bf16[64,1792]{1,0:T(8,128)(2,1)S(1)} %hand_on.4.refs_1_, bf16[14,8,128,128]{3,2,1,0:T(8,128)(2,1)S(1)} %copy-done, f32[64,1792]{1,0:T(8,128)S(1)} %near_1.1.refs_1_.refs_3_, f32[2,1792]{1,0:T(2,128)S(1)} %copy-done.3, s32[2,1792]{1,0:T(2,128)S(1)} %copy-done.4, ...), custom_call_target="tpu_custom_call" | custom-call | flops 58720256 | bytes 5018048 | tf_op jit(solution)/shard_map/middle_1/pallas_call | solution.py:362
  21.7 1.0 %collective-permute-done.11.refs_1_ = bf16[64,1792]{1,0:T(8,128)(2,1)S(1)} collective-permute-done((bf16[64,1792]{1,0:T(8,128)(2,1)S(1)}, bf16[64,1792]{1,0:T(8,128)(2,1)S(1)}, u32[]{:S(2)}, u32[]{:S(2)}) %collective-permute-start.11) | collective-permute-done | bytes 229408 | tf_op jit(solution)/shard_map/ppermute | solution.py:47
  22.7 0.5 %last_1.1 = (f32[8,1792]{1,0:T(8,128)S(1)}, f32[8,1792]{1,0:T(8,128)S(1)}, f32[8,1792]{1,0:T(8,128)S(1)}, bf16[64,1792]{1,0:T(8,128)(2,1)S(1)}, f32[64,1792]{1,0:T(8,128)S(1)}) custom-call(s32[8,14]{1,0:T(8,128)S(1)} %bitcast.13, bf16[64,1792]{1,0:T(8,128)(2,1)S(1)} %collective-permute-done.11.refs_1_, bf16[14,8,128,128]{3,2,1,0:T(8,128)(2,1)S(1)} %copy-done, ...), custom_call_target="tpu_custom_call" | custom-call | flops 58720256 | bytes 5251520 | tf_op jit(solution)/shard_map/last_1/pallas_call | solution.py:362
  23.2 0.2 collective-permute-start.13
  23.4 1.8 %collective-permute-start.12 = (bf16[64,1792]{1,0:T(8,128)(2,1)S(1)}, bf16[64,1792]{1,0:T(8,128)(2,1)S(1)}, u32[]{:S(2)}, u32[]{:S(2)}) collective-permute-start(bf16[64,1792]{1,0:T(8,128)(2,1)S(1)} %get-tuple-element.27.refs_1_), channel_id=1, source_target_pairs={{0,16},{8,24},{16,0},{24,8},{1,17},{9,25},{17,1},{25,9},{2,18},{10... | collective-permute-start | bytes 688136 | tf_op jit(solution)/shard_map/ppermute | solution.py:47
  25.2 1.5 %collective-permute-start.14 = (f32[8,1792]{1,0:T(8,128)S(1)}, f32[8,1792]{1,0:T(8,128)S(1)}, u32[]{:S(2)}, u32[]{:S(2)}) collective-permute-start(f32[8,1792]{1,0:T(8,128)S(1)} %get-tuple-element.29), channel_id=1, source_target_pairs={{0,4},{4,0},{8,12},{12,8},{16,20},{20,16},{24,28},{28,24},{1,5},{5... | collective-permute-start | bytes 172040 | tf_op jit(solution)/shard_map/ppermute | solution.py:40
  26.7 1.6 %collective-permute-start.15 = (f32[8,1792]{1,0:T(8,128)S(1)}, f32[8,1792]{1,0:T(8,128)S(1)}, u32[]{:S(2)}, u32[]{:S(2)}) collective-permute-start(f32[8,1792]{1,0:T(8,128)S(1)} %get-tuple-element.30), channel_id=1, source_target_pairs={{0,1},{1,0},{2,3},{3,2},{8,9},{9,8},{10,11},{11,10},{16,17},{17,16... | collective-permute-start | bytes 172040 | tf_op jit(solution)/shard_map/ppermute | solution.py:40
  28.2 0.8 %near_2.1.refs_1_.refs_3_ = f32[64,1792]{1,0:T(8,128)S(1)} custom-call(s32[8,14]{1,0:T(8,128)S(1)} %bitcast.14, bf16[64,1792]{1,0:T(8,128)(2,1)S(1)} %get-tuple-element.27.refs_1_, bf16[64,1792]{1,0:T(8,128)(2,1)S(1)} %collective-permute-done.13.refs_2_, bf16[14,8,128,128]{3,2,1,0:T(8,128)(2,1)S(1)} %copy-done, ...), custom_call_target="tpu_custom_call" | custom-call | flops 117440512 | bytes 5115328 | tf_op jit(solution)/shard_map/near_2/pallas_call | solution.py:362
  29.1 0.0 copy-start.2
  29.1 0.3 collective-permute-done.14.refs_2_.refs_6_
  29.3 1.5 %collective-permute-done.15.refs_3_.refs_7_ = f32[8,1792]{1,0:T(8,128)S(1)} collective-permute-done((f32[8,1792]{1,0:T(8,128)S(1)}, f32[8,1792]{1,0:T(8,128)S(1)}, u32[]{:S(2)}, u32[]{:S(2)}) %collective-permute-start.15) | collective-permute-done | bytes 57376 | tf_op jit(solution)/shard_map/ppermute | solution.py:40
  30.8 0.5 collective-permute-done.12.refs_0_
  31.3 0.5 %middle_2.1.refs_3_ = f32[64,1792]{1,0:T(8,128)S(1)} custom-call(s32[8,14]{1,0:T(8,128)S(1)} %bitcast.15, bf16[64,1792]{1,0:T(8,128)(2,1)S(1)} %hand_on.5.refs_1_, bf16[14,8,128,128]{3,2,1,0:T(8,128)(2,1)S(1)} %copy-done, f32[64,1792]{1,0:T(8,128)S(1)} %near_2.1.refs_1_.refs_3_, f32[2,1792]{1,0:T(2,128)S(1)} %copy-done.3, s32[2,1792]{1,0:T(2,128)S(1)} %copy-done.4, ...), custom_call_target="tpu_custom_call" | custom-call | flops 58720256 | bytes 5018048 | tf_op jit(solution)/shard_map/middle_2/pallas_call | solution.py:362
  31.8 0.9 %collective-permute-done.17.refs_1_ = bf16[64,1792]{1,0:T(8,128)(2,1)S(1)} collective-permute-done((bf16[64,1792]{1,0:T(8,128)(2,1)S(1)}, bf16[64,1792]{1,0:T(8,128)(2,1)S(1)}, u32[]{:S(2)}, u32[]{:S(2)}) %collective-permute-start.17) | collective-permute-done | bytes 229408 | tf_op jit(solution)/shard_map/ppermute | solution.py:47
  32.8 0.7 %last_2.1 = f32[32,1,128]{2,1,0:T(1,128)S(1)} custom-call(s32[8,14]{1,0:T(8,128)S(1)} %bitcast.16, bf16[64,1792]{1,0:T(8,128)(2,1)S(1)} %collective-permute-done.17.refs_1_, bf16[14,8,128,128]{3,2,1,0:T(8,128)(2,1)S(1)} %copy-done, f32[64,1792]{1,0:T(8,128)S(1)} %middle_2.1.refs_3_, f32[64,128]{1,0:T(8,128)S(1)} %get-tuple-element.18.refs_5_.refs_4_, ...), custom_call_target="tpu_custom_call" | custom-call | flops 58720256 | bytes 5784000 | tf_op jit(solution)/shard_map/last_2/pallas_call | solution.py:362
  33.5 13.0 %all_to_all.5.refs_0_ = f32[32,1,128]{2,1,0:T(1,128)S(1)} all-to-all(f32[32,1,128]{2,1,0:T(1,128)S(1)} %last_2.1), channel_id=1, replica_groups=mesh['mode'=4,'gx'=2,'gy'=4] {'mode','gx','gy'}, dimensions={0} | all-to-all | bytes 32768 | tf_op jit(solution)/shard_map/all_to_all | solution.py:508
  46.5 1.7 %finish.1 = (f32[64,1792]{1,0:T(8,128)}, f32[4,3]{1,0:T(4,128)}) custom-call(f32[32,1,128]{2,1,0:T(1,128)S(1)} %all_to_all.5.refs_0_, f32[64,1792]{1,0:T(8,128)S(1)} %bitcast.7, f32[64,1792]{1,0:T(8,128)S(1)} %get-tuple-element.23.refs_4_.refs_6_.refs_2_, f32[64,1792]{1,0:T(8,128)S(1)} %get-tuple-element.28.refs_4_.refs_7_.refs_3_), custom_call_target="tpu_custom_call" | custom-call | bytes 1851440 | tf_op jit(solution)/shard_map/finish/pallas_call | solution.py:362
  (20 shorter events, 0.1 us)
Async XLA Ops:
  0.6 1.0 %copy-start.1 = (f32[8,8,1792]{2,1,0:T(8,128)S(1)}, f32[8,8,1792]{2,1,0:T(8,128)}, u32[]{:S(2)}) copy-start(f32[8,8,1792]{2,1,0:T(8,128)} %param.7) | copy-start | bytes 1376260
  1.7 3.2 %copy-start.7 = (s32[8,8]{1,0:T(8,128)S(1)}, s32[8,8]{1,0:T(8,128)}, u32[]{:S(2)}) copy-start(s32[8,8]{1,0:T(8,128)} %refs_1_.1) | copy-start | bytes 772
  1.7 6.5 %copy-start = (bf16[14,8,128,128]{3,2,1,0:T(8,128)(2,1)S(1)}, bf16[14,8,128,128]{3,2,1,0:T(8,128)(2,1)}, u32[]{:S(2)}) copy-start(bf16[14,8,128,128]{3,2,1,0:T(8,128)(2,1)} %refs_2_.11) | copy-start | bytes 11010052
  1.7 6.5 %copy-start.3 = (f32[2,1792]{1,0:T(2,128)S(1)}, f32[2,1792]{1,0:T(2,128)}, u32[]{:S(2)}) copy-start(f32[2,1792]{1,0:T(2,128)} %refs_4_.5) | copy-start | bytes 43012
  1.7 6.5 %copy-start.4 = (s32[2,1792]{1,0:T(2,128)S(1)}, s32[2,1792]{1,0:T(2,128)}, u32[]{:S(2)}) copy-start(s32[2,1792]{1,0:T(2,128)} %refs_5_.5) | copy-start | bytes 43012
  1.7 6.5 %copy-start.5 = (s32[14,8]{0,1:T(8,128)S(1)}, s32[14,8]{0,1:T(8,128)}, u32[]{:S(2)}) copy-start(s32[14,8]{0,1:T(8,128)} %param.8) | copy-start | bytes 1348
  1.7 6.5 %copy-start.6 = (f32[1792]{0:T(1024)S(1)}, f32[1792]{0:T(1024)}, u32[]{:S(2)}) copy-start(f32[1792]{0:T(1024)} %refs_6_.5) | copy-start | bytes 21508
  1.7 6.5 %collective-permute-start.1 = (bf16[64,1792]{1,0:T(8,128)(2,1)S(1)}, bf16[64,1792]{1,0:T(8,128)(2,1)S(1)}, u32[]{:S(2)}, u32[]{:S(2)}) collective-permute-start(bf16[64,1792]{1,0:T(8,128)(2,1)S(1)} %pack.1.refs_1_), channel_id=1, source_target_pairs={{0,8},{8,0},{16,24},{24,16},{1,9},{9,1},{17,25},{25,17},{2,10},{10... | collective-permute-start | bytes 688136 | tf_op jit(solution)/shard_map/ppermute | solution.py:47
  2.3 8.8 %collective-permute-start = (bf16[64,1792]{1,0:T(8,128)(2,1)S(1)}, bf16[64,1792]{1,0:T(8,128)(2,1)S(1)}, u32[]{:S(2)}, u32[]{:S(2)}) collective-permute-start(bf16[64,1792]{1,0:T(8,128)(2,1)S(1)} %pack.1.refs_1_), channel_id=1, source_target_pairs={{0,16},{8,24},{16,0},{24,8},{1,17},{9,25},{17,1},{25,9},{2,18},{10... | collective-permute-start | bytes 688136 | tf_op jit(solution)/shard_map/ppermute | solution.py:47
  5.1 4.2 %collective-permute-start.2 = (f32[8,1792]{1,0:T(8,128)S(1)}, f32[8,1792]{1,0:T(8,128)S(1)}, u32[]{:S(2)}, u32[]{:S(2)}) collective-permute-start(f32[8,1792]{1,0:T(8,128)S(1)} %get-tuple-element.19), channel_id=1, source_target_pairs={{0,4},{4,0},{8,12},{12,8},{16,20},{20,16},{24,28},{28,24},{1,5},{5... | collective-permute-start | bytes 172040 | tf_op jit(solution)/shard_map/ppermute | solution.py:40
  6.6 4.2 %collective-permute-start.3 = (f32[8,1792]{1,0:T(8,128)S(1)}, f32[8,1792]{1,0:T(8,128)S(1)}, u32[]{:S(2)}, u32[]{:S(2)}) collective-permute-start(f32[8,1792]{1,0:T(8,128)S(1)} %get-tuple-element.20), channel_id=1, source_target_pairs={{0,1},{1,0},{2,3},{3,2},{8,9},{9,8},{10,11},{11,10},{16,17},{17,16... | collective-permute-start | bytes 172040 | tf_op jit(solution)/shard_map/ppermute | solution.py:40
  8.2 2.6 %collective-permute-start.4 = (f32[8,1792]{1,0:T(8,128)S(1)}, f32[8,1792]{1,0:T(8,128)S(1)}, u32[]{:S(2)}, u32[]{:S(2)}) collective-permute-start(f32[8,1792]{1,0:T(8,128)S(1)} %get-tuple-element.21), channel_id=1, source_target_pairs={{0,8},{1,2},{2,1},{3,11},{8,0},{9,10},{10,9},{11,3},{16,24},{17,18... | collective-permute-start | bytes 172040 | tf_op jit(solution)/shard_map/ppermute | solution.py:40
  11.1 1.5 %collective-permute-start.5 = (bf16[64,1792]{1,0:T(8,128)(2,1)S(1)}, bf16[64,1792]{1,0:T(8,128)(2,1)S(1)}, u32[]{:S(2)}, u32[]{:S(2)}) collective-permute-start(bf16[64,1792]{1,0:T(8,128)(2,1)S(1)} %hand_on.3.refs_1_), channel_id=1, source_target_pairs={{0,8},{8,0},{16,24},{24,16},{1,9},{9,1},{17,25},{25,17},{2,10},{10... | collective-permute-start | bytes 688136 | tf_op jit(solution)/shard_map/ppermute | solution.py:47
  13.1 5.0 %collective-permute-start.7 = (bf16[64,1792]{1,0:T(8,128)(2,1)S(1)}, bf16[64,1792]{1,0:T(8,128)(2,1)S(1)}, u32[]{:S(2)}, u32[]{:S(2)}) collective-permute-start(bf16[64,1792]{1,0:T(8,128)(2,1)S(1)} %get-tuple-element.22.refs_1_), channel_id=1, source_target_pairs={{0,8},{8,0},{16,24},{24,16},{1,9},{9,1},{17,25},{25,17},{2,10},{10... | collective-permute-start | bytes 688136 | tf_op jit(solution)/shard_map/ppermute | solution.py:47
  13.3 7.9 %collective-permute-start.6 = (bf16[64,1792]{1,0:T(8,128)(2,1)S(1)}, bf16[64,1792]{1,0:T(8,128)(2,1)S(1)}, u32[]{:S(2)}, u32[]{:S(2)}) collective-permute-start(bf16[64,1792]{1,0:T(8,128)(2,1)S(1)} %get-tuple-element.22.refs_1_), channel_id=1, source_target_pairs={{0,16},{8,24},{16,0},{24,8},{1,17},{9,25},{17,1},{25,9},{2,18},{10... | collective-permute-start | bytes 688136 | tf_op jit(solution)/shard_map/ppermute | solution.py:47
  15.1 4.2 %collective-permute-start.8 = (f32[8,1792]{1,0:T(8,128)S(1)}, f32[8,1792]{1,0:T(8,128)S(1)}, u32[]{:S(2)}, u32[]{:S(2)}) collective-permute-start(f32[8,1792]{1,0:T(8,128)S(1)} %get-tuple-element.24), channel_id=1, source_target_pairs={{0,4},{4,0},{8,12},{12,8},{16,20},{20,16},{24,28},{28,24},{1,5},{5... | collective-permute-start | bytes 172040 | tf_op jit(solution)/shard_map/ppermute | solution.py:40
  16.5 4.2 %collective-permute-start.9 = (f32[8,1792]{1,0:T(8,128)S(1)}, f32[8,1792]{1,0:T(8,128)S(1)}, u32[]{:S(2)}, u32[]{:S(2)}) collective-permute-start(f32[8,1792]{1,0:T(8,128)S(1)} %get-tuple-element.25), channel_id=1, source_target_pairs={{0,1},{1,0},{2,3},{3,2},{8,9},{9,8},{10,11},{11,10},{16,17},{17,16... | collective-permute-start | bytes 172040 | tf_op jit(solution)/shard_map/ppermute | solution.py:40
  18.1 2.6 %collective-permute-start.10 = (f32[8,1792]{1,0:T(8,128)S(1)}, f32[8,1792]{1,0:T(8,128)S(1)}, u32[]{:S(2)}, u32[]{:S(2)}) collective-permute-start(f32[8,1792]{1,0:T(8,128)S(1)} %get-tuple-element.26), channel_id=1, source_target_pairs={{0,8},{1,2},{2,1},{3,11},{8,0},{9,10},{10,9},{11,3},{16,24},{17,18... | collective-permute-start | bytes 172040 | tf_op jit(solution)/shard_map/ppermute | solution.py:40
  21.2 1.5 %collective-permute-start.11 = (bf16[64,1792]{1,0:T(8,128)(2,1)S(1)}, bf16[64,1792]{1,0:T(8,128)(2,1)S(1)}, u32[]{:S(2)}, u32[]{:S(2)}) collective-permute-start(bf16[64,1792]{1,0:T(8,128)(2,1)S(1)} %hand_on.4.refs_1_), channel_id=1, source_target_pairs={{0,8},{8,0},{16,24},{24,16},{1,9},{9,1},{17,25},{25,17},{2,10},{10... | collective-permute-start | bytes 688136 | tf_op jit(solution)/shard_map/ppermute | solution.py:47
  23.2 5.0 %collective-permute-start.13 = (bf16[64,1792]{1,0:T(8,128)(2,1)S(1)}, bf16[64,1792]{1,0:T(8,128)(2,1)S(1)}, u32[]{:S(2)}, u32[]{:S(2)}) collective-permute-start(bf16[64,1792]{1,0:T(8,128)(2,1)S(1)} %get-tuple-element.27.refs_1_), channel_id=1, source_target_pairs={{0,8},{8,0},{16,24},{24,16},{1,9},{9,1},{17,25},{25,17},{2,10},{10... | collective-permute-start | bytes 688136 | tf_op jit(solution)/shard_map/ppermute | solution.py:47
  23.4 7.9 %collective-permute-start.12 = (bf16[64,1792]{1,0:T(8,128)(2,1)S(1)}, bf16[64,1792]{1,0:T(8,128)(2,1)S(1)}, u32[]{:S(2)}, u32[]{:S(2)}) collective-permute-start(bf16[64,1792]{1,0:T(8,128)(2,1)S(1)} %get-tuple-element.27.refs_1_), channel_id=1, source_target_pairs={{0,16},{8,24},{16,0},{24,8},{1,17},{9,25},{17,1},{25,9},{2,18},{10... | collective-permute-start | bytes 688136 | tf_op jit(solution)/shard_map/ppermute | solution.py:47
  25.2 4.2 %collective-permute-start.14 = (f32[8,1792]{1,0:T(8,128)S(1)}, f32[8,1792]{1,0:T(8,128)S(1)}, u32[]{:S(2)}, u32[]{:S(2)}) collective-permute-start(f32[8,1792]{1,0:T(8,128)S(1)} %get-tuple-element.29), channel_id=1, source_target_pairs={{0,4},{4,0},{8,12},{12,8},{16,20},{20,16},{24,28},{28,24},{1,5},{5... | collective-permute-start | bytes 172040 | tf_op jit(solution)/shard_map/ppermute | solution.py:40
  26.7 4.2 %collective-permute-start.15 = (f32[8,1792]{1,0:T(8,128)S(1)}, f32[8,1792]{1,0:T(8,128)S(1)}, u32[]{:S(2)}, u32[]{:S(2)}) collective-permute-start(f32[8,1792]{1,0:T(8,128)S(1)} %get-tuple-element.30), channel_id=1, source_target_pairs={{0,1},{1,0},{2,3},{3,2},{8,9},{9,8},{10,11},{11,10},{16,17},{17,16... | collective-permute-start | bytes 172040 | tf_op jit(solution)/shard_map/ppermute | solution.py:40
  28.2 2.6 %collective-permute-start.16 = (f32[8,1792]{1,0:T(8,128)S(1)}, f32[8,1792]{1,0:T(8,128)S(1)}, u32[]{:S(2)}, u32[]{:S(2)}) collective-permute-start(f32[8,1792]{1,0:T(8,128)S(1)} %get-tuple-element.31), channel_id=1, source_target_pairs={{0,8},{1,2},{2,1},{3,11},{8,0},{9,10},{10,9},{11,3},{16,24},{17,18... | collective-permute-start | bytes 172040 | tf_op jit(solution)/shard_map/ppermute | solution.py:40
  29.1 3.7 %copy-start.2 = (f32[8,8,1792]{2,1,0:T(8,128)S(1)}, f32[8,8,1792]{2,1,0:T(8,128)}, u32[]{:S(2)}) copy-start(f32[8,8,1792]{2,1,0:T(8,128)} %param.7) | copy-start | bytes 1376260
  31.3 1.5 %collective-permute-start.17 = (bf16[64,1792]{1,0:T(8,128)(2,1)S(1)}, bf16[64,1792]{1,0:T(8,128)(2,1)S(1)}, u32[]{:S(2)}, u32[]{:S(2)}) collective-permute-start(bf16[64,1792]{1,0:T(8,128)(2,1)S(1)} %hand_on.5.refs_1_), channel_id=1, source_target_pairs={{0,8},{8,0},{16,24},{24,16},{1,9},{9,1},{17,25},{25,17},{2,10},{10... | collective-permute-start | bytes 688136 | tf_op jit(solution)/shard_map/ppermute | solution.py:47

commit v9 on v7

--- a/solution.py
+++ b/solution.py
@@ -58,6 +58,15 @@
     return held
 
 
+def store_packed(refs, lanes, value):
+    refs[0][:, lanes] = value.astype(jnp.bfloat16)
+    at = 0
+    for ref in refs[1:]:
+        rows = ref.shape[0]
+        ref[:, lanes] = value[at : at + rows].astype(jnp.bfloat16)
+        at += rows
+
+
 def hand_on(arrays, after):
     count = len(arrays)
     if not count:
@@ -120,7 +129,8 @@
         for p in range(per_owner):
             slot = owner * per_owner + p
             column = cols_ref[slot, b] - owner * local_blocks
-            picks.append(source[:, pl.ds(pl.multiple_of(column * block, block), block)])
+            lanes = pl.ds(pl.multiple_of(column * block, block), block)
+            picks.append(jnp.concatenate([part[:, lanes] for part in source], axis=0))
             weights.append(blocks_ref[b, slot])
     return lax.dot_general(
         jnp.concatenate(picks, axis=1),
@@ -200,7 +210,7 @@
         result = partial_ref[:, lanes] - scattered
         if outs.gram is None:
             outs.value[:, lanes] = result
-            outs.packed[:, lanes] = result.astype(jnp.bfloat16)
+            store_packed(outs.packed, lanes, result)
             write_faces(
                 (result * open_ref[...]).reshape(first, second, block),
                 lanes, first, second, outs.x, outs.y,
@@ -224,8 +234,8 @@
 
 
 class Outs:
-    value = packed = gram = None
-    x = y = ()
+    value = gram = None
+    x = y = packed = ()
 
 
 def least_squares(hessenberg, initial):
@@ -380,7 +390,9 @@
     face_shapes = [shape_of((second, local_modes), f32)] * x_moves + [
         shape_of((first, local_modes), f32)
     ] * y_moves
-    packed_shape = shape_of((cells, local_modes), jnp.bfloat16)
+    parts = 2 if cells % 32 == 0 else 1
+    packed_shapes = [shape_of((cells, local_modes), jnp.bfloat16)]
+    packed_shapes += [shape_of((cells // parts, local_modes), jnp.bfloat16)] * parts
     vector_shape = shape_of((cells, local_modes), f32)
     near = [place for place in (0, 1) if place < count]
     final = [place for place in range(3, count) if place % 2 == 1]
@@ -389,9 +401,9 @@
     start = right_side.reshape(cells, local_modes)
 
     def pack(ins, outs, scratch):
-        outs[0][...] = ins[0][...].astype(jnp.bfloat16)
-
-    (packed,) = call("pack", pack, [in_vmem([start])], [packed_shape], flops=4 * 10**9)
+        store_packed(outs, slice(None), ins[0][...])
+
+    packed = call("pack", pack, [in_vmem([start])], packed_shapes, flops=4 * 10**9)
 
     def prepare(ins, outs, scratch):
         faces, (open_ref,) = outs[:n_faces], outs[n_faces:]
@@ -409,13 +421,13 @@
     work = 2 * cells * local_modes * per_owner * block
     vectors = [start]
     for section in range(KRYLOV):
-        sources = {0: packed}
-        if count > 1:
-            sources[1] = exchange(packed, 1)
-        held = gather_far(packed)
+        sources = {0: packed[0]}
+        held = gather_far(packed[0])
+        neighbour = [exchange(part, 1) for part in packed[1:]] if count > 1 else []
         y_in, x_in = move_faces({"gx": faces[:x_moves], "gy": faces[x_moves:]})
 
         def near_step(cols, sources, rest, params, outs, scratch):
+            sources = [sources[:1], sources[1:]]
             blocks_ref, current_ref, open_ref = rest
             near_kernel(
                 sizes, per_owner, near, cols[0], sources, blocks_ref, current_ref, params,
@@ -427,7 +439,7 @@
             near_step,
             [
                 in_vmem([columns]),
-                in_vmem([sources[place] for place in near]),
+                in_vmem([packed[0], *neighbour]),
                 in_vmem([blocks, vectors[-1], open_cells]),
                 in_vmem([relax_rate, drift_speed, upwind_sign]),
             ],
@@ -435,14 +447,14 @@
             flops=work * len(near),
         )
 
-        held = dict(zip(held, hand_on(list(held.values()), [partial, *y_in, *x_in])))
+        held = dict(zip(held, hand_on(list(held.values()), [partial, *x_in, *y_in])))
         for place, array in held.items():
             sources[place] = array
             sources[place ^ 1] = exchange(array, 1)
 
-        def middle_step(cols, sources, rest, y_in, x_in, outs, scratch):
+        def middle_step(cols, sources, rest, x_in, y_in, outs, scratch):
             middle_kernel(
-                sizes, per_owner, middle, cols[0], sources, *rest, x_in, y_in, outs[0]
+                sizes, per_owner, middle, cols[0], [[ref] for ref in sources], *rest, x_in, y_in, outs[0]
             )
 
         (partial,) = call(
@@ -452,8 +464,8 @@
                 in_vmem([columns]),
                 in_vmem([sources[place] for place in middle]),
                 in_vmem([blocks, partial, drift_speed, upwind_sign]),
+                in_vmem(x_in),
                 in_vmem(y_in),
-                in_vmem(x_in),
             ],
             [vector_shape],
             flops=work * len(middle),
@@ -467,16 +479,16 @@
                 named.gram = outs[0]
             else:
                 named.x, named.y = outs[:x_moves], outs[x_moves:n_faces]
-                named.packed, named.value = outs[n_faces:]
+                *named.packed, named.value = outs[n_faces:]
             last_kernel(
-                sizes, per_owner, final, cols[0], sources, blocks_ref, partial_ref,
+                sizes, per_owner, final, cols[0], [[ref] for ref in sources], blocks_ref, partial_ref,
                 earlier, open_ref, named,
             )
 
         if last:
             shapes = [shape_of((devices, 1, block), f32)]
         else:
-            shapes = face_shapes + [packed_shape, vector_shape]
+            shapes = face_shapes + packed_shapes + [vector_shape]
         results = call(
             "last_%d" % section,
             last_step,
@@ -492,7 +504,7 @@
         if last:
             (gram,) = results
         else:
-            *faces, packed, value = results
+            faces, packed, value = results[:n_faces], results[n_faces:-1], results[-1]
             vectors.append(value)
 
     gram = lax.all_to_all(gram, AXES, 0, 0)

time: 47.8 us -> 47.1 us (0.985)
  waiting for transfers between devices: 8.88 us -> 8.03 us
    ppermute x9 -> x12, starting transfers between devices: 7.05 us -> 7.87 us  [exchange(): return lax.ppermute(array, 'mode', [(i, i ^ bit) for i in range(count)])]
    ppermute x9, waiting for transfers between devices: 5.93 us -> 5.17 us  [move_faces(): arrived.append(lax.ppermute(face, ('mode', axis), pairs))]
    ppermute x9 -> x12, waiting for transfers between devices: 2.96 us -> 2.86 us  [exchange(): return lax.ppermute(array, 'mode', [(i, i ^ bit) for i in range(count)])]
  transfers between devices with their start and end apart: 18 -> 21, of which waited for: 9 -> 10; matrix products, arithmetic and copies ran while one was open for 0% -> 0% of each run, Pallas kernels for 9% -> 9%
where the time goes in v9:
time: 47.1 us; the launch traced here: 47 us
  starting transfers between devices  17.1 us (36%)
  blocking collectives  12.7 us (27%)
  waiting for transfers between devices  8.03 us (17%)
  Pallas kernels  7.26 us (15%)
  local copies, waits for them, and re-layouts  1.04 us (2%)
  between operations  0.81 us (2%)
    all_to_all x1, blocking collectives, per_device(): gram = lax.all_to_all(gram, AXES, 0, 0)  12.7 us
    ppermute x9, starting transfers between devices, move_faces(): arrived.append(lax.ppermute(face, ('mode', axis), pairs))  9.28 us
    ppermute x12, starting transfers between devices, exchange(): return lax.ppermute(array, 'mode', [(i, i ^ bit) for i in range(count)])  7.87 us
    pallas_call x12, Pallas kernels, call(): pl.pallas_call(body, out_shape=list(shapes), in_specs=[spec for spec, ope...  7.26 us
    ppermute x9, waiting for transfers between devices, move_faces(): arrived.append(lax.ppermute(face, ('mode', axis), pairs))  5.17 us
    ppermute x12, waiting for transfers between devices, exchange(): return lax.ppermute(array, 'mode', [(i, i ^ bit) for i in range(count)])  2.86 us
    unnamed x16, local copies, waits for them, and re-layouts  1.04 us
  transfers between devices with their start and end apart: 21, of which 10 were waited for; matrix products, arithmetic and copies ran while one was open for 0% of the time, Pallas kernels for 9%

profile of v9, /device:TPU:0, one launch (start us, length us, event | category | flops | bytes accessed | tf_op | source)
XLA Modules:
  0.0 47.0 jit_solution(17727411836095564022)
XLA Ops:
  0.6 0.0 copy-start.1
  0.6 1.0 %copy-done.1 = f32[8,8,1792]{2,1,0:T(8,128)S(1)} copy-done((f32[8,8,1792]{2,1,0:T(8,128)S(1)}, f32[8,8,1792]{2,1,0:T(8,128)}, u32[]{:S(2)}) %copy-start.1) | copy-done | bytes 458776
  1.7 0.5 %collective-permute-start.1 = (bf16[32,1792]{1,0:T(8,128)(2,1)S(1)}, bf16[32,1792]{1,0:T(8,128)(2,1)S(1)}, u32[]{:S(2)}, u32[]{:S(2)}) collective-permute-start(bf16[32,1792]{1,0:T(8,128)(2,1)S(1)} %get-tuple-element.26), channel_id=1, source_target_pairs={{0,8},{8,0},{16,24},{24,16},{1,9},{9,1},{17,25},{25,17},{2,10},{10... | collective-permute-start | bytes 344072 | tf_op jit(solution)/shard_map/ppermute | solution.py:47
  2.2 0.1 collective-permute-start.2
  2.3 0.0 copy-start.6
  2.3 3.0 %collective-permute-start = (bf16[64,1792]{1,0:T(8,128)(2,1)S(1)}, bf16[64,1792]{1,0:T(8,128)(2,1)S(1)}, u32[]{:S(2)}, u32[]{:S(2)}) collective-permute-start(bf16[64,1792]{1,0:T(8,128)(2,1)S(1)} %get-tuple-element.25.refs_1_), channel_id=1, source_target_pairs={{0,16},{8,24},{16,0},{24,8},{1,17},{9,25},{17,1},{25,9},{2,18},{10... | collective-permute-start | bytes 688136 | tf_op jit(solution)/shard_map/ppermute | solution.py:47
  5.3 0.2 prepare.1
  5.5 1.6 %collective-permute-start.3 = (f32[8,1792]{1,0:T(8,128)S(1)}, f32[8,1792]{1,0:T(8,128)S(1)}, u32[]{:S(2)}, u32[]{:S(2)}) collective-permute-start(f32[8,1792]{1,0:T(8,128)S(1)} %get-tuple-element.29), channel_id=1, source_target_pairs={{0,4},{4,0},{8,12},{12,8},{16,20},{20,16},{24,28},{28,24},{1,5},{5... | collective-permute-start | bytes 172040 | tf_op jit(solution)/shard_map/ppermute | solution.py:40
  7.1 1.6 %collective-permute-start.4 = (f32[8,1792]{1,0:T(8,128)S(1)}, f32[8,1792]{1,0:T(8,128)S(1)}, u32[]{:S(2)}, u32[]{:S(2)}) collective-permute-start(f32[8,1792]{1,0:T(8,128)S(1)} %get-tuple-element.30), channel_id=1, source_target_pairs={{0,1},{1,0},{2,3},{3,2},{8,9},{9,8},{10,11},{11,10},{16,17},{17,16... | collective-permute-start | bytes 172040 | tf_op jit(solution)/shard_map/ppermute | solution.py:40
  8.7 0.0 collective-permute-done.1.refs_2_
  8.7 0.0 collective-permute-start.5
  8.7 0.0 collective-permute-done.2.refs_3_
  8.7 0.8 %near_0.1.refs_1_.refs_3_ = f32[64,1792]{1,0:T(8,128)S(1)} custom-call(s32[8,14]{1,0:T(8,128)S(1)} %bitcast.8, bf16[64,1792]{1,0:T(8,128)(2,1)S(1)} %get-tuple-element.25.refs_1_, bf16[32,1792]{1,0:T(8,128)(2,1)S(1)} %collective-permute-done.1.refs_2_, bf16[32,1792]{1,0:T(8,128)(2,1)S(1)} %collective-permute-done.2.refs_3_, ...), custom_call_target="tpu_custom_call" | custom-call | flops 117440512 | bytes 5115328 | tf_op jit(solution)/shard_map/near_0/pallas_call | solution.py:362
  9.6 0.2 collective-permute-done.3.refs_2_.refs_6_
  9.8 1.5 %collective-permute-done.4.refs_3_.refs_7_ = f32[8,1792]{1,0:T(8,128)S(1)} collective-permute-done((f32[8,1792]{1,0:T(8,128)S(1)}, f32[8,1792]{1,0:T(8,128)S(1)}, u32[]{:S(2)}, u32[]{:S(2)}) %collective-permute-start.4) | collective-permute-done | bytes 57376 | tf_op jit(solution)/shard_map/ppermute | solution.py:40
  11.3 0.0 collective-permute-done.5.refs_4_.refs_8_
  11.3 0.0 collective-permute-done.refs_0_
  11.3 0.1 collective-permute-start.6
  11.4 0.5 %middle_0.1.refs_3_ = f32[64,1792]{1,0:T(8,128)S(1)} custom-call(s32[8,14]{1,0:T(8,128)S(1)} %bitcast.9, bf16[64,1792]{1,0:T(8,128)(2,1)S(1)} %hand_on.3.refs_1_, bf16[14,8,128,128]{3,2,1,0:T(8,128)(2,1)S(1)} %copy-done, f32[64,1792]{1,0:T(8,128)S(1)} %near_0.1.refs_1_.refs_3_, f32[2,1792]{1,0:T(2,128)S(1)} %copy-done.3, s32[2,1792]{1,0:T(2,128)S(1)} %copy-done.4, ...), custom_call_target="tpu_custom_call" | custom-call | flops 58720256 | bytes 5018048 | tf_op jit(solution)/shard_map/middle_0/pallas_call | solution.py:362
  11.9 0.9 %collective-permute-done.6.refs_1_ = bf16[64,1792]{1,0:T(8,128)(2,1)S(1)} collective-permute-done((bf16[64,1792]{1,0:T(8,128)(2,1)S(1)}, bf16[64,1792]{1,0:T(8,128)(2,1)S(1)}, u32[]{:S(2)}, u32[]{:S(2)}) %collective-permute-start.6) | collective-permute-done | bytes 229408 | tf_op jit(solution)/shard_map/ppermute | solution.py:47
  12.8 0.5 %last_0.1 = (f32[8,1792]{1,0:T(8,128)S(1)}, f32[8,1792]{1,0:T(8,128)S(1)}, f32[8,1792]{1,0:T(8,128)S(1)}, bf16[64,1792]{1,0:T(8,128)(2,1)S(1)}, bf16[32,1792]{1,...) custom-call(s32[8,14]{1,0:T(8,128)S(1)} %bitcast.10, ...), custom_call_target="tpu_custom_call" | custom-call | flops 58720256 | bytes 5480896 | tf_op jit(solution)/shard_map/last_0/pallas_call | solution.py:362
  13.4 1.6 %collective-permute-start.7 = (bf16[64,1792]{1,0:T(8,128)(2,1)S(1)}, bf16[64,1792]{1,0:T(8,128)(2,1)S(1)}, u32[]{:S(2)}, u32[]{:S(2)}) collective-permute-start(bf16[64,1792]{1,0:T(8,128)(2,1)S(1)} %get-tuple-element.32.refs_1_), channel_id=1, source_target_pairs={{0,16},{8,24},{16,0},{24,8},{1,17},{9,25},{17,1},{25,9},{2,18},{10... | collective-permute-start | bytes 688136 | tf_op jit(solution)/shard_map/ppermute | solution.py:47
  15.0 0.5 %collective-permute-start.9 = (bf16[32,1792]{1,0:T(8,128)(2,1)S(1)}, bf16[32,1792]{1,0:T(8,128)(2,1)S(1)}, u32[]{:S(2)}, u32[]{:S(2)}) collective-permute-start(bf16[32,1792]{1,0:T(8,128)(2,1)S(1)} %get-tuple-element.34), channel_id=1, source_target_pairs={{0,8},{8,0},{16,24},{24,16},{1,9},{9,1},{17,25},{25,17},{2,10},{10... | collective-permute-start | bytes 344072 | tf_op jit(solution)/shard_map/ppermute | solution.py:47
  15.5 1.5 %collective-permute-start.10 = (f32[8,1792]{1,0:T(8,128)S(1)}, f32[8,1792]{1,0:T(8,128)S(1)}, u32[]{:S(2)}, u32[]{:S(2)}) collective-permute-start(f32[8,1792]{1,0:T(8,128)S(1)} %get-tuple-element.36), channel_id=1, source_target_pairs={{0,4},{4,0},{8,12},{12,8},{16,20},{20,16},{24,28},{28,24},{1,5},{5... | collective-permute-start | bytes 172040 | tf_op jit(solution)/shard_map/ppermute | solution.py:40
  17.0 1.6 %collective-permute-start.11 = (f32[8,1792]{1,0:T(8,128)S(1)}, f32[8,1792]{1,0:T(8,128)S(1)}, u32[]{:S(2)}, u32[]{:S(2)}) collective-permute-start(f32[8,1792]{1,0:T(8,128)S(1)} %get-tuple-element.37), channel_id=1, source_target_pairs={{0,1},{1,0},{2,3},{3,2},{8,9},{9,8},{10,11},{11,10},{16,17},{17,16... | collective-permute-start | bytes 172040 | tf_op jit(solution)/shard_map/ppermute | solution.py:40
  18.6 0.0 collective-permute-start.12
  18.6 0.8 %near_1.1.refs_1_.refs_3_ = f32[64,1792]{1,0:T(8,128)S(1)} custom-call(s32[8,14]{1,0:T(8,128)S(1)} %bitcast.11, bf16[64,1792]{1,0:T(8,128)(2,1)S(1)} %get-tuple-element.32.refs_1_, bf16[32,1792]{1,0:T(8,128)(2,1)S(1)} %collective-permute-done.8.refs_2_, bf16[32,1792]{1,0:T(8,128)(2,1)S(1)} %collective-permute-done.9.refs_3_, ...), custom_call_target="tpu_custom_call" | custom-call | flops 117440512 | bytes 5115328 | tf_op jit(solution)/shard_map/near_1/pallas_call | solution.py:362
  19.4 0.2 collective-permute-done.10.refs_2_.refs_6_
  19.7 1.5 %collective-permute-done.11.refs_3_.refs_7_ = f32[8,1792]{1,0:T(8,128)S(1)} collective-permute-done((f32[8,1792]{1,0:T(8,128)S(1)}, f32[8,1792]{1,0:T(8,128)S(1)}, u32[]{:S(2)}, u32[]{:S(2)}) %collective-permute-start.11) | collective-permute-done | bytes 57376 | tf_op jit(solution)/shard_map/ppermute | solution.py:40
  21.2 0.1 collective-permute-start.13
  21.3 0.5 %middle_1.1.refs_3_ = f32[64,1792]{1,0:T(8,128)S(1)} custom-call(s32[8,14]{1,0:T(8,128)S(1)} %bitcast.12, bf16[64,1792]{1,0:T(8,128)(2,1)S(1)} %hand_on.4.refs_1_, bf16[14,8,128,128]{3,2,1,0:T(8,128)(2,1)S(1)} %copy-done, f32[64,1792]{1,0:T(8,128)S(1)} %near_1.1.refs_1_.refs_3_, f32[2,1792]{1,0:T(2,128)S(1)} %copy-done.3, s32[2,1792]{1,0:T(2,128)S(1)} %copy-done.4, ...), custom_call_target="tpu_custom_call" | custom-call | flops 58720256 | bytes 5018048 | tf_op jit(solution)/shard_map/middle_1/pallas_call | solution.py:362
  21.8 0.9 %collective-permute-done.13.refs_1_ = bf16[64,1792]{1,0:T(8,128)(2,1)S(1)} collective-permute-done((bf16[64,1792]{1,0:T(8,128)(2,1)S(1)}, bf16[64,1792]{1,0:T(8,128)(2,1)S(1)}, u32[]{:S(2)}, u32[]{:S(2)}) %collective-permute-start.13) | collective-permute-done | bytes 229408 | tf_op jit(solution)/shard_map/ppermute | solution.py:47
  22.7 0.5 %last_1.1 = (f32[8,1792]{1,0:T(8,128)S(1)}, f32[8,1792]{1,0:T(8,128)S(1)}, f32[8,1792]{1,0:T(8,128)S(1)}, bf16[64,1792]{1,0:T(8,128)(2,1)S(1)}, bf16[32,1792]{1,...) custom-call(s32[8,14]{1,0:T(8,128)S(1)} %bitcast.13, ...), custom_call_target="tpu_custom_call" | custom-call | flops 58720256 | bytes 5480896 | tf_op jit(solution)/shard_map/last_1/pallas_call | solution.py:362
  23.3 1.5 %collective-permute-start.14 = (bf16[64,1792]{1,0:T(8,128)(2,1)S(1)}, bf16[64,1792]{1,0:T(8,128)(2,1)S(1)}, u32[]{:S(2)}, u32[]{:S(2)}) collective-permute-start(bf16[64,1792]{1,0:T(8,128)(2,1)S(1)} %get-tuple-element.39.refs_1_), channel_id=1, source_target_pairs={{0,16},{8,24},{16,0},{24,8},{1,17},{9,25},{17,1},{25,9},{2,18},{10... | collective-permute-start | bytes 688136 | tf_op jit(solution)/shard_map/ppermute | solution.py:47
  24.7 0.5 %collective-permute-start.16 = (bf16[32,1792]{1,0:T(8,128)(2,1)S(1)}, bf16[32,1792]{1,0:T(8,128)(2,1)S(1)}, u32[]{:S(2)}, u32[]{:S(2)}) collective-permute-start(bf16[32,1792]{1,0:T(8,128)(2,1)S(1)} %get-tuple-element.41), channel_id=1, source_target_pairs={{0,8},{8,0},{16,24},{24,16},{1,9},{9,1},{17,25},{25,17},{2,10},{10... | collective-permute-start | bytes 344072 | tf_op jit(solution)/shard_map/ppermute | solution.py:47
  25.2 1.5 %collective-permute-start.17 = (f32[8,1792]{1,0:T(8,128)S(1)}, f32[8,1792]{1,0:T(8,128)S(1)}, u32[]{:S(2)}, u32[]{:S(2)}) collective-permute-start(f32[8,1792]{1,0:T(8,128)S(1)} %get-tuple-element.43), channel_id=1, source_target_pairs={{0,4},{4,0},{8,12},{12,8},{16,20},{20,16},{24,28},{28,24},{1,5},{5... | collective-permute-start | bytes 172040 | tf_op jit(solution)/shard_map/ppermute | solution.py:40
  26.7 1.6 %collective-permute-start.18 = (f32[8,1792]{1,0:T(8,128)S(1)}, f32[8,1792]{1,0:T(8,128)S(1)}, u32[]{:S(2)}, u32[]{:S(2)}) collective-permute-start(f32[8,1792]{1,0:T(8,128)S(1)} %get-tuple-element.44), channel_id=1, source_target_pairs={{0,1},{1,0},{2,3},{3,2},{8,9},{9,8},{10,11},{11,10},{16,17},{17,16... | collective-permute-start | bytes 172040 | tf_op jit(solution)/shard_map/ppermute | solution.py:40
  28.3 0.8 %near_2.1.refs_1_.refs_3_ = f32[64,1792]{1,0:T(8,128)S(1)} custom-call(s32[8,14]{1,0:T(8,128)S(1)} %bitcast.14, bf16[64,1792]{1,0:T(8,128)(2,1)S(1)} %get-tuple-element.39.refs_1_, bf16[32,1792]{1,0:T(8,128)(2,1)S(1)} %collective-permute-done.15.refs_2_, bf16[32,1792]{1,0:T(8,128)(2,1)S(1)} %collective-permute-done.16.refs_3_, ...), custom_call_target="tpu_custom_call" | custom-call | flops 117440512 | bytes 5115328 | tf_op jit(solution)/shard_map/near_2/pallas_call | solution.py:362
  29.2 0.0 copy-start.2
  29.2 0.2 collective-permute-done.17.refs_2_.refs_6_
  29.4 1.5 %collective-permute-done.18.refs_3_.refs_7_ = f32[8,1792]{1,0:T(8,128)S(1)} collective-permute-done((f32[8,1792]{1,0:T(8,128)S(1)}, f32[8,1792]{1,0:T(8,128)S(1)}, u32[]{:S(2)}, u32[]{:S(2)}) %collective-permute-start.18) | collective-permute-done | bytes 57376 | tf_op jit(solution)/shard_map/ppermute | solution.py:40
  30.9 0.1 collective-permute-done.14.refs_0_
  31.0 0.0 collective-permute-start.20
  31.0 0.5 %middle_2.1.refs_3_ = f32[64,1792]{1,0:T(8,128)S(1)} custom-call(s32[8,14]{1,0:T(8,128)S(1)} %bitcast.15, bf16[64,1792]{1,0:T(8,128)(2,1)S(1)} %hand_on.5.refs_1_, bf16[14,8,128,128]{3,2,1,0:T(8,128)(2,1)S(1)} %copy-done, f32[64,1792]{1,0:T(8,128)S(1)} %near_2.1.refs_1_.refs_3_, f32[2,1792]{1,0:T(2,128)S(1)} %copy-done.3, s32[2,1792]{1,0:T(2,128)S(1)} %copy-done.4, ...), custom_call_target="tpu_custom_call" | custom-call | flops 58720256 | bytes 5018048 | tf_op jit(solution)/shard_map/middle_2/pallas_call | solution.py:362
  31.5 0.9 %collective-permute-done.20.refs_1_ = bf16[64,1792]{1,0:T(8,128)(2,1)S(1)} collective-permute-done((bf16[64,1792]{1,0:T(8,128)(2,1)S(1)}, bf16[64,1792]{1,0:T(8,128)(2,1)S(1)}, u32[]{:S(2)}, u32[]{:S(2)}) %collective-permute-start.20) | collective-permute-done | bytes 229408 | tf_op jit(solution)/shard_map/ppermute | solution.py:47
  32.5 0.7 %last_2.1 = f32[32,1,128]{2,1,0:T(1,128)S(1)} custom-call(s32[8,14]{1,0:T(8,128)S(1)} %bitcast.16, bf16[64,1792]{1,0:T(8,128)(2,1)S(1)} %collective-permute-done.20.refs_1_, bf16[14,8,128,128]{3,2,1,0:T(8,128)(2,1)S(1)} %copy-done, f32[64,1792]{1,0:T(8,128)S(1)} %middle_2.1.refs_3_, f32[64,128]{1,0:T(8,128)S(1)} %get-tuple-element.28.refs_6_.refs_4_, ...), custom_call_target="tpu_custom_call" | custom-call | flops 58720256 | bytes 5784000 | tf_op jit(solution)/shard_map/last_2/pallas_call | solution.py:362
  33.2 12.7 %all_to_all.5.refs_0_ = f32[32,1,128]{2,1,0:T(1,128)S(1)} all-to-all(f32[32,1,128]{2,1,0:T(1,128)S(1)} %last_2.1), channel_id=1, replica_groups=mesh['mode'=4,'gx'=2,'gy'=4] {'mode','gx','gy'}, dimensions={0} | all-to-all | bytes 32768 | tf_op jit(solution)/shard_map/all_to_all | solution.py:510
  45.8 1.1 %finish.1 = (f32[64,1792]{1,0:T(8,128)}, f32[4,3]{1,0:T(4,128)}) custom-call(f32[32,1,128]{2,1,0:T(1,128)S(1)} %all_to_all.5.refs_0_, f32[64,1792]{1,0:T(8,128)S(1)} %bitcast.7, f32[64,1792]{1,0:T(8,128)S(1)} %get-tuple-element.35.refs_5_.refs_6_.refs_2_, f32[64,1792]{1,0:T(8,128)S(1)} %get-tuple-element.42.refs_5_.refs_7_.refs_3_), custom_call_target="tpu_custom_call" | custom-call | bytes 1851440 | tf_op jit(solution)/shard_map/finish/pallas_call | solution.py:362
  (26 shorter events, 0.1 us)
Async XLA Ops:
  0.6 1.0 %copy-start.1 = (f32[8,8,1792]{2,1,0:T(8,128)S(1)}, f32[8,8,1792]{2,1,0:T(8,128)}, u32[]{:S(2)}) copy-start(f32[8,8,1792]{2,1,0:T(8,128)} %param.7) | copy-start | bytes 1376260
  1.7 3.7 %copy-start.7 = (s32[8,8]{1,0:T(8,128)S(1)}, s32[8,8]{1,0:T(8,128)}, u32[]{:S(2)}) copy-start(s32[8,8]{1,0:T(8,128)} %refs_1_.1) | copy-start | bytes 772
  1.7 7.0 %collective-permute-start.1 = (bf16[32,1792]{1,0:T(8,128)(2,1)S(1)}, bf16[32,1792]{1,0:T(8,128)(2,1)S(1)}, u32[]{:S(2)}, u32[]{:S(2)}) collective-permute-start(bf16[32,1792]{1,0:T(8,128)(2,1)S(1)} %get-tuple-element.26), channel_id=1, source_target_pairs={{0,8},{8,0},{16,24},{24,16},{1,9},{9,1},{17,25},{25,17},{2,10},{10... | collective-permute-start | bytes 344072 | tf_op jit(solution)/shard_map/ppermute | solution.py:47
  2.2 6.5 %collective-permute-start.2 = (bf16[32,1792]{1,0:T(8,128)(2,1)S(1)}, bf16[32,1792]{1,0:T(8,128)(2,1)S(1)}, u32[]{:S(2)}, u32[]{:S(2)}) collective-permute-start(bf16[32,1792]{1,0:T(8,128)(2,1)S(1)} %get-tuple-element.27), channel_id=1, source_target_pairs={{0,8},{8,0},{16,24},{24,16},{1,9},{9,1},{17,25},{25,17},{2,10},{10... | collective-permute-start | bytes 344072 | tf_op jit(solution)/shard_map/ppermute | solution.py:47
  2.3 6.4 %copy-start = (bf16[14,8,128,128]{3,2,1,0:T(8,128)(2,1)S(1)}, bf16[14,8,128,128]{3,2,1,0:T(8,128)(2,1)}, u32[]{:S(2)}) copy-start(bf16[14,8,128,128]{3,2,1,0:T(8,128)(2,1)} %refs_2_.11) | copy-start | bytes 11010052
  2.3 6.4 %copy-start.3 = (f32[2,1792]{1,0:T(2,128)S(1)}, f32[2,1792]{1,0:T(2,128)}, u32[]{:S(2)}) copy-start(f32[2,1792]{1,0:T(2,128)} %refs_4_.11) | copy-start | bytes 43012
  2.3 6.4 %copy-start.4 = (s32[2,1792]{1,0:T(2,128)S(1)}, s32[2,1792]{1,0:T(2,128)}, u32[]{:S(2)}) copy-start(s32[2,1792]{1,0:T(2,128)} %refs_5_.5) | copy-start | bytes 43012
  2.3 6.4 %copy-start.5 = (s32[14,8]{0,1:T(8,128)S(1)}, s32[14,8]{0,1:T(8,128)}, u32[]{:S(2)}) copy-start(s32[14,8]{0,1:T(8,128)} %param.8) | copy-start | bytes 1348
  2.3 6.4 %copy-start.6 = (f32[1792]{0:T(1024)S(1)}, f32[1792]{0:T(1024)}, u32[]{:S(2)}) copy-start(f32[1792]{0:T(1024)} %refs_7_.5) | copy-start | bytes 21508
  2.3 9.0 %collective-permute-start = (bf16[64,1792]{1,0:T(8,128)(2,1)S(1)}, bf16[64,1792]{1,0:T(8,128)(2,1)S(1)}, u32[]{:S(2)}, u32[]{:S(2)}) collective-permute-start(bf16[64,1792]{1,0:T(8,128)(2,1)S(1)} %get-tuple-element.25.refs_1_), channel_id=1, source_target_pairs={{0,16},{8,24},{16,0},{24,8},{1,17},{9,25},{17,1},{25,9},{2,18},{10... | collective-permute-start | bytes 688136 | tf_op jit(solution)/shard_map/ppermute | solution.py:47
  5.5 4.2 %collective-permute-start.3 = (f32[8,1792]{1,0:T(8,128)S(1)}, f32[8,1792]{1,0:T(8,128)S(1)}, u32[]{:S(2)}, u32[]{:S(2)}) collective-permute-start(f32[8,1792]{1,0:T(8,128)S(1)} %get-tuple-element.29), channel_id=1, source_target_pairs={{0,4},{4,0},{8,12},{12,8},{16,20},{20,16},{24,28},{28,24},{1,5},{5... | collective-permute-start | bytes 172040 | tf_op jit(solution)/shard_map/ppermute | solution.py:40
  7.1 4.2 %collective-permute-start.4 = (f32[8,1792]{1,0:T(8,128)S(1)}, f32[8,1792]{1,0:T(8,128)S(1)}, u32[]{:S(2)}, u32[]{:S(2)}) collective-permute-start(f32[8,1792]{1,0:T(8,128)S(1)} %get-tuple-element.30), channel_id=1, source_target_pairs={{0,1},{1,0},{2,3},{3,2},{8,9},{9,8},{10,11},{11,10},{16,17},{17,16... | collective-permute-start | bytes 172040 | tf_op jit(solution)/shard_map/ppermute | solution.py:40
  8.7 2.6 %collective-permute-start.5 = (f32[8,1792]{1,0:T(8,128)S(1)}, f32[8,1792]{1,0:T(8,128)S(1)}, u32[]{:S(2)}, u32[]{:S(2)}) collective-permute-start(f32[8,1792]{1,0:T(8,128)S(1)} %get-tuple-element.31), channel_id=1, source_target_pairs={{0,8},{1,2},{2,1},{3,11},{8,0},{9,10},{10,9},{11,3},{16,24},{17,18... | collective-permute-start | bytes 172040 | tf_op jit(solution)/shard_map/ppermute | solution.py:40
  11.3 1.5 %collective-permute-start.6 = (bf16[64,1792]{1,0:T(8,128)(2,1)S(1)}, bf16[64,1792]{1,0:T(8,128)(2,1)S(1)}, u32[]{:S(2)}, u32[]{:S(2)}) collective-permute-start(bf16[64,1792]{1,0:T(8,128)(2,1)S(1)} %hand_on.3.refs_1_), channel_id=1, source_target_pairs={{0,8},{8,0},{16,24},{24,16},{1,9},{9,1},{17,25},{25,17},{2,10},{10... | collective-permute-start | bytes 688136 | tf_op jit(solution)/shard_map/ppermute | solution.py:47
  13.4 7.8 %collective-permute-start.7 = (bf16[64,1792]{1,0:T(8,128)(2,1)S(1)}, bf16[64,1792]{1,0:T(8,128)(2,1)S(1)}, u32[]{:S(2)}, u32[]{:S(2)}) collective-permute-start(bf16[64,1792]{1,0:T(8,128)(2,1)S(1)} %get-tuple-element.32.refs_1_), channel_id=1, source_target_pairs={{0,16},{8,24},{16,0},{24,8},{1,17},{9,25},{17,1},{25,9},{2,18},{10... | collective-permute-start | bytes 688136 | tf_op jit(solution)/shard_map/ppermute | solution.py:47
  15.0 3.6 %collective-permute-start.8 = (bf16[32,1792]{1,0:T(8,128)(2,1)S(1)}, bf16[32,1792]{1,0:T(8,128)(2,1)S(1)}, u32[]{:S(2)}, u32[]{:S(2)}) collective-permute-start(bf16[32,1792]{1,0:T(8,128)(2,1)S(1)} %get-tuple-element.33), channel_id=1, source_target_pairs={{0,8},{8,0},{16,24},{24,16},{1,9},{9,1},{17,25},{25,17},{2,10},{10... | collective-permute-start | bytes 344072 | tf_op jit(solution)/shard_map/ppermute | solution.py:47
  15.0 3.6 %collective-permute-start.9 = (bf16[32,1792]{1,0:T(8,128)(2,1)S(1)}, bf16[32,1792]{1,0:T(8,128)(2,1)S(1)}, u32[]{:S(2)}, u32[]{:S(2)}) collective-permute-start(bf16[32,1792]{1,0:T(8,128)(2,1)S(1)} %get-tuple-element.34), channel_id=1, source_target_pairs={{0,8},{8,0},{16,24},{24,16},{1,9},{9,1},{17,25},{25,17},{2,10},{10... | collective-permute-start | bytes 344072 | tf_op jit(solution)/shard_map/ppermute | solution.py:47
  15.5 4.2 %collective-permute-start.10 = (f32[8,1792]{1,0:T(8,128)S(1)}, f32[8,1792]{1,0:T(8,128)S(1)}, u32[]{:S(2)}, u32[]{:S(2)}) collective-permute-start(f32[8,1792]{1,0:T(8,128)S(1)} %get-tuple-element.36), channel_id=1, source_target_pairs={{0,4},{4,0},{8,12},{12,8},{16,20},{20,16},{24,28},{28,24},{1,5},{5... | collective-permute-start | bytes 172040 | tf_op jit(solution)/shard_map/ppermute | solution.py:40
  17.0 4.2 %collective-permute-start.11 = (f32[8,1792]{1,0:T(8,128)S(1)}, f32[8,1792]{1,0:T(8,128)S(1)}, u32[]{:S(2)}, u32[]{:S(2)}) collective-permute-start(f32[8,1792]{1,0:T(8,128)S(1)} %get-tuple-element.37), channel_id=1, source_target_pairs={{0,1},{1,0},{2,3},{3,2},{8,9},{9,8},{10,11},{11,10},{16,17},{17,16... | collective-permute-start | bytes 172040 | tf_op jit(solution)/shard_map/ppermute | solution.py:40
  18.6 2.6 %collective-permute-start.12 = (f32[8,1792]{1,0:T(8,128)S(1)}, f32[8,1792]{1,0:T(8,128)S(1)}, u32[]{:S(2)}, u32[]{:S(2)}) collective-permute-start(f32[8,1792]{1,0:T(8,128)S(1)} %get-tuple-element.38), channel_id=1, source_target_pairs={{0,8},{1,2},{2,1},{3,11},{8,0},{9,10},{10,9},{11,3},{16,24},{17,18... | collective-permute-start | bytes 172040 | tf_op jit(solution)/shard_map/ppermute | solution.py:40
  21.2 1.5 %collective-permute-start.13 = (bf16[64,1792]{1,0:T(8,128)(2,1)S(1)}, bf16[64,1792]{1,0:T(8,128)(2,1)S(1)}, u32[]{:S(2)}, u32[]{:S(2)}) collective-permute-start(bf16[64,1792]{1,0:T(8,128)(2,1)S(1)} %hand_on.4.refs_1_), channel_id=1, source_target_pairs={{0,8},{8,0},{16,24},{24,16},{1,9},{9,1},{17,25},{25,17},{2,10},{10... | collective-permute-start | bytes 688136 | tf_op jit(solution)/shard_map/ppermute | solution.py:47
  23.3 7.7 %collective-permute-start.14 = (bf16[64,1792]{1,0:T(8,128)(2,1)S(1)}, bf16[64,1792]{1,0:T(8,128)(2,1)S(1)}, u32[]{:S(2)}, u32[]{:S(2)}) collective-permute-start(bf16[64,1792]{1,0:T(8,128)(2,1)S(1)} %get-tuple-element.39.refs_1_), channel_id=1, source_target_pairs={{0,16},{8,24},{16,0},{24,8},{1,17},{9,25},{17,1},{25,9},{2,18},{10... | collective-permute-start | bytes 688136 | tf_op jit(solution)/shard_map/ppermute | solution.py:47
  24.7 3.6 %collective-permute-start.15 = (bf16[32,1792]{1,0:T(8,128)(2,1)S(1)}, bf16[32,1792]{1,0:T(8,128)(2,1)S(1)}, u32[]{:S(2)}, u32[]{:S(2)}) collective-permute-start(bf16[32,1792]{1,0:T(8,128)(2,1)S(1)} %get-tuple-element.40), channel_id=1, source_target_pairs={{0,8},{8,0},{16,24},{24,16},{1,9},{9,1},{17,25},{25,17},{2,10},{10... | collective-permute-start | bytes 344072 | tf_op jit(solution)/shard_map/ppermute | solution.py:47
  24.7 3.6 %collective-permute-start.16 = (bf16[32,1792]{1,0:T(8,128)(2,1)S(1)}, bf16[32,1792]{1,0:T(8,128)(2,1)S(1)}, u32[]{:S(2)}, u32[]{:S(2)}) collective-permute-start(bf16[32,1792]{1,0:T(8,128)(2,1)S(1)} %get-tuple-element.41), channel_id=1, source_target_pairs={{0,8},{8,0},{16,24},{24,16},{1,9},{9,1},{17,25},{25,17},{2,10},{10... | collective-permute-start | bytes 344072 | tf_op jit(solution)/shard_map/ppermute | solution.py:47
  25.2 4.2 %collective-permute-start.17 = (f32[8,1792]{1,0:T(8,128)S(1)}, f32[8,1792]{1,0:T(8,128)S(1)}, u32[]{:S(2)}, u32[]{:S(2)}) collective-permute-start(f32[8,1792]{1,0:T(8,128)S(1)} %get-tuple-element.43), channel_id=1, source_target_pairs={{0,4},{4,0},{8,12},{12,8},{16,20},{20,16},{24,28},{28,24},{1,5},{5... | collective-permute-start | bytes 172040 | tf_op jit(solution)/shard_map/ppermute | solution.py:40
  26.7 4.2 %collective-permute-start.18 = (f32[8,1792]{1,0:T(8,128)S(1)}, f32[8,1792]{1,0:T(8,128)S(1)}, u32[]{:S(2)}, u32[]{:S(2)}) collective-permute-start(f32[8,1792]{1,0:T(8,128)S(1)} %get-tuple-element.44), channel_id=1, source_target_pairs={{0,1},{1,0},{2,3},{3,2},{8,9},{9,8},{10,11},{11,10},{16,17},{17,16... | collective-permute-start | bytes 172040 | tf_op jit(solution)/shard_map/ppermute | solution.py:40
  28.3 2.6 %collective-permute-start.19 = (f32[8,1792]{1,0:T(8,128)S(1)}, f32[8,1792]{1,0:T(8,128)S(1)}, u32[]{:S(2)}, u32[]{:S(2)}) collective-permute-start(f32[8,1792]{1,0:T(8,128)S(1)} %get-tuple-element.45), channel_id=1, source_target_pairs={{0,8},{1,2},{2,1},{3,11},{8,0},{9,10},{10,9},{11,3},{16,24},{17,18... | collective-permute-start | bytes 172040 | tf_op jit(solution)/shard_map/ppermute | solution.py:40
  29.2 3.3 %copy-start.2 = (f32[8,8,1792]{2,1,0:T(8,128)S(1)}, f32[8,8,1792]{2,1,0:T(8,128)}, u32[]{:S(2)}) copy-start(f32[8,8,1792]{2,1,0:T(8,128)} %param.7) | copy-start | bytes 1376260
  31.0 1.5 %collective-permute-start.20 = (bf16[64,1792]{1,0:T(8,128)(2,1)S(1)}, bf16[64,1792]{1,0:T(8,128)(2,1)S(1)}, u32[]{:S(2)}, u32[]{:S(2)}) collective-permute-start(bf16[64,1792]{1,0:T(8,128)(2,1)S(1)} %hand_on.5.refs_1_), channel_id=1, source_target_pairs={{0,8},{8,0},{16,24},{24,16},{1,9},{9,1},{17,25},{25,17},{2,10},{10... | collective-permute-start | bytes 688136 | tf_op jit(solution)/shard_map/ppermute | solution.py:47

commit v10 on v9

--- a/solution.py
+++ b/solution.py
@@ -403,7 +403,7 @@
     def pack(ins, outs, scratch):
         store_packed(outs, slice(None), ins[0][...])
 
-    packed = call("pack", pack, [in_vmem([start])], packed_shapes, flops=4 * 10**9)
+    packed = call("pack", pack, [in_vmem([start])], packed_shapes, flops=8 * 10**9)
 
     def prepare(ins, outs, scratch):
         faces, (open_ref,) = outs[:n_faces], outs[n_faces:]
@@ -414,7 +414,7 @@
         prepare,
         [in_vmem([start, wall_mask])],
         face_shapes + [shape_of((cells, block), f32)],
-        flops=8 * 10**9,
+        flops=1 * 10**9,
     )
     columns = col_block.T
 

time: 47.1 us -> 46.3 us (0.983)
  starting transfers between devices: 17.1 us -> 15.7 us
  waiting for transfers between devices: 8.03 us -> 9.33 us
  blocking collectives: 12.7 us -> 12.1 us
    ppermute x12, starting transfers between devices: 7.87 us -> 6.38 us  [exchange(): return lax.ppermute(array, 'mode', [(i, i ^ bit) for i in range(count)])]
    ppermute x12, waiting for transfers between devices: 2.86 us -> 4.16 us  [exchange(): return lax.ppermute(array, 'mode', [(i, i ^ bit) for i in range(count)])]
    all_to_all x1, blocking collectives: 12.7 us -> 12.1 us  [per_device(): gram = lax.all_to_all(gram, AXES, 0, 0)]
  transfers between devices with their start and end apart: 21 -> 21, of which waited for: 10 -> 11; matrix products, arithmetic and copies ran while one was open for 0% -> 0% of each run, Pallas kernels for 9% -> 9%
where the time goes in v10:
time: 46.3 us; the launch traced here: 46.2 us
  starting transfers between devices  15.7 us (34%)
  blocking collectives  12.1 us (26%)
  waiting for transfers between devices  9.33 us (20%)
  Pallas kernels  7.22 us (16%)
  local copies, waits for them, and re-layouts  1.06 us (2%)
  between operations  0.82 us (2%)
    all_to_all x1, blocking collectives, per_device(): gram = lax.all_to_all(gram, AXES, 0, 0)  12.1 us
    ppermute x9, starting transfers between devices, move_faces(): arrived.append(lax.ppermute(face, ('mode', axis), pairs))  9.28 us
    pallas_call x12, Pallas kernels, call(): pl.pallas_call(body, out_shape=list(shapes), in_specs=[spec for spec, ope...  7.22 us
    ppermute x12, starting transfers between devices, exchange(): return lax.ppermute(array, 'mode', [(i, i ^ bit) for i in range(count)])  6.38 us
    ppermute x9, waiting for transfers between devices, move_faces(): arrived.append(lax.ppermute(face, ('mode', axis), pairs))  5.18 us
    ppermute x12, waiting for transfers between devices, exchange(): return lax.ppermute(array, 'mode', [(i, i ^ bit) for i in range(count)])  4.16 us
    unnamed x16, local copies, waits for them, and re-layouts  1.06 us
  transfers between devices with their start and end apart: 21, of which 11 were waited for; matrix products, arithmetic and copies ran while one was open for 0% of the time, Pallas kernels for 9%

profile of v10, /device:TPU:0, one launch (start us, length us, event | category | flops | bytes accessed | tf_op | source)
XLA Modules:
  0.0 46.2 jit_solution(15847757133048938365)
XLA Ops:
  0.6 0.0 copy-start.1
  0.6 1.0 %copy-done.1 = f32[8,8,1792]{2,1,0:T(8,128)S(1)} copy-done((f32[8,8,1792]{2,1,0:T(8,128)S(1)}, f32[8,8,1792]{2,1,0:T(8,128)}, u32[]{:S(2)}) %copy-start.1) | copy-done | bytes 458776
  1.7 0.0 copy-start
  1.7 0.0 copy-start.3
  1.7 0.0 copy-start.4
  1.7 0.0 copy-start.5
  1.7 0.0 copy-start.6
  1.7 3.0 %collective-permute-start = (bf16[64,1792]{1,0:T(8,128)(2,1)S(1)}, bf16[64,1792]{1,0:T(8,128)(2,1)S(1)}, u32[]{:S(2)}, u32[]{:S(2)}) collective-permute-start(bf16[64,1792]{1,0:T(8,128)(2,1)S(1)} %get-tuple-element.25.refs_1_), channel_id=1, source_target_pairs={{0,16},{8,24},{16,0},{24,8},{1,17},{9,25},{17,1},{25,9},{2,18},{10... | collective-permute-start | bytes 688136 | tf_op jit(solution)/shard_map/ppermute | solution.py:47
  4.8 0.0 collective-permute-start.1
  4.8 0.5 %collective-permute-start.2 = (bf16[32,1792]{1,0:T(8,128)(2,1)S(1)}, bf16[32,1792]{1,0:T(8,128)(2,1)S(1)}, u32[]{:S(2)}, u32[]{:S(2)}) collective-permute-start(bf16[32,1792]{1,0:T(8,128)(2,1)S(1)} %get-tuple-element.27), channel_id=1, source_target_pairs={{0,8},{8,0},{16,24},{24,16},{1,9},{9,1},{17,25},{25,17},{2,10},{10... | collective-permute-start | bytes 344072 | tf_op jit(solution)/shard_map/ppermute | solution.py:47
  5.3 0.2 prepare.1
  5.5 1.6 %collective-permute-start.3 = (f32[8,1792]{1,0:T(8,128)S(1)}, f32[8,1792]{1,0:T(8,128)S(1)}, u32[]{:S(2)}, u32[]{:S(2)}) collective-permute-start(f32[8,1792]{1,0:T(8,128)S(1)} %get-tuple-element.29), channel_id=1, source_target_pairs={{0,4},{4,0},{8,12},{12,8},{16,20},{20,16},{24,28},{28,24},{1,5},{5... | collective-permute-start | bytes 172040 | tf_op jit(solution)/shard_map/ppermute | solution.py:40
  7.1 1.6 %collective-permute-start.4 = (f32[8,1792]{1,0:T(8,128)S(1)}, f32[8,1792]{1,0:T(8,128)S(1)}, u32[]{:S(2)}, u32[]{:S(2)}) collective-permute-start(f32[8,1792]{1,0:T(8,128)S(1)} %get-tuple-element.30), channel_id=1, source_target_pairs={{0,1},{1,0},{2,3},{3,2},{8,9},{9,8},{10,11},{11,10},{16,17},{17,16... | collective-permute-start | bytes 172040 | tf_op jit(solution)/shard_map/ppermute | solution.py:40
  8.7 0.0 collective-permute-done.2.refs_3_
  8.7 0.8 %near_0.1.refs_1_.refs_3_ = f32[64,1792]{1,0:T(8,128)S(1)} custom-call(s32[8,14]{1,0:T(8,128)S(1)} %bitcast.8, bf16[64,1792]{1,0:T(8,128)(2,1)S(1)} %get-tuple-element.25.refs_1_, bf16[32,1792]{1,0:T(8,128)(2,1)S(1)} %collective-permute-done.1.refs_2_, bf16[32,1792]{1,0:T(8,128)(2,1)S(1)} %collective-permute-done.2.refs_3_, ...), custom_call_target="tpu_custom_call" | custom-call | flops 117440512 | bytes 5115328 | tf_op jit(solution)/shard_map/near_0/pallas_call | solution.py:362
  9.6 0.2 collective-permute-done.3.refs_2_.refs_6_
  9.8 1.5 %collective-permute-done.4.refs_3_.refs_7_ = f32[8,1792]{1,0:T(8,128)S(1)} collective-permute-done((f32[8,1792]{1,0:T(8,128)S(1)}, f32[8,1792]{1,0:T(8,128)S(1)}, u32[]{:S(2)}, u32[]{:S(2)}) %collective-permute-start.4) | collective-permute-done | bytes 57376 | tf_op jit(solution)/shard_map/ppermute | solution.py:40
  11.3 0.1 collective-permute-start.6
  11.3 0.5 %middle_0.1.refs_3_ = f32[64,1792]{1,0:T(8,128)S(1)} custom-call(s32[8,14]{1,0:T(8,128)S(1)} %bitcast.9, bf16[64,1792]{1,0:T(8,128)(2,1)S(1)} %hand_on.3.refs_1_, bf16[14,8,128,128]{3,2,1,0:T(8,128)(2,1)S(1)} %copy-done, f32[64,1792]{1,0:T(8,128)S(1)} %near_0.1.refs_1_.refs_3_, f32[2,1792]{1,0:T(2,128)S(1)} %copy-done.3, s32[2,1792]{1,0:T(2,128)S(1)} %copy-done.4, ...), custom_call_target="tpu_custom_call" | custom-call | flops 58720256 | bytes 5018048 | tf_op jit(solution)/shard_map/middle_0/pallas_call | solution.py:362
  11.9 0.9 %collective-permute-done.6.refs_1_ = bf16[64,1792]{1,0:T(8,128)(2,1)S(1)} collective-permute-done((bf16[64,1792]{1,0:T(8,128)(2,1)S(1)}, bf16[64,1792]{1,0:T(8,128)(2,1)S(1)}, u32[]{:S(2)}, u32[]{:S(2)}) %collective-permute-start.6) | collective-permute-done | bytes 229408 | tf_op jit(solution)/shard_map/ppermute | solution.py:47
  12.8 0.5 %last_0.1 = (f32[8,1792]{1,0:T(8,128)S(1)}, f32[8,1792]{1,0:T(8,128)S(1)}, f32[8,1792]{1,0:T(8,128)S(1)}, bf16[64,1792]{1,0:T(8,128)(2,1)S(1)}, bf16[32,1792]{1,...) custom-call(s32[8,14]{1,0:T(8,128)S(1)} %bitcast.10, ...), custom_call_target="tpu_custom_call" | custom-call | flops 58720256 | bytes 5480896 | tf_op jit(solution)/shard_map/last_0/pallas_call | solution.py:362
  13.3 0.9 %collective-permute-start.7 = (bf16[64,1792]{1,0:T(8,128)(2,1)S(1)}, bf16[64,1792]{1,0:T(8,128)(2,1)S(1)}, u32[]{:S(2)}, u32[]{:S(2)}) collective-permute-start(bf16[64,1792]{1,0:T(8,128)(2,1)S(1)} %get-tuple-element.32.refs_1_), channel_id=1, source_target_pairs={{0,16},{8,24},{16,0},{24,8},{1,17},{9,25},{17,1},{25,9},{2,18},{10... | collective-permute-start | bytes 688136 | tf_op jit(solution)/shard_map/ppermute | solution.py:47
  14.2 0.5 %collective-permute-start.9 = (bf16[32,1792]{1,0:T(8,128)(2,1)S(1)}, bf16[32,1792]{1,0:T(8,128)(2,1)S(1)}, u32[]{:S(2)}, u32[]{:S(2)}) collective-permute-start(bf16[32,1792]{1,0:T(8,128)(2,1)S(1)} %get-tuple-element.34), channel_id=1, source_target_pairs={{0,8},{8,0},{16,24},{24,16},{1,9},{9,1},{17,25},{25,17},{2,10},{10... | collective-permute-start | bytes 344072 | tf_op jit(solution)/shard_map/ppermute | solution.py:47
  14.7 1.5 %collective-permute-start.10 = (f32[8,1792]{1,0:T(8,128)S(1)}, f32[8,1792]{1,0:T(8,128)S(1)}, u32[]{:S(2)}, u32[]{:S(2)}) collective-permute-start(f32[8,1792]{1,0:T(8,128)S(1)} %get-tuple-element.36), channel_id=1, source_target_pairs={{0,4},{4,0},{8,12},{12,8},{16,20},{20,16},{24,28},{28,24},{1,5},{5... | collective-permute-start | bytes 172040 | tf_op jit(solution)/shard_map/ppermute | solution.py:40
  16.2 1.6 %collective-permute-start.11 = (f32[8,1792]{1,0:T(8,128)S(1)}, f32[8,1792]{1,0:T(8,128)S(1)}, u32[]{:S(2)}, u32[]{:S(2)}) collective-permute-start(f32[8,1792]{1,0:T(8,128)S(1)} %get-tuple-element.37), channel_id=1, source_target_pairs={{0,1},{1,0},{2,3},{3,2},{8,9},{9,8},{10,11},{11,10},{16,17},{17,16... | collective-permute-start | bytes 172040 | tf_op jit(solution)/shard_map/ppermute | solution.py:40
  17.8 0.0 collective-permute-done.9.refs_3_
  17.8 0.8 %near_1.1.refs_1_.refs_3_ = f32[64,1792]{1,0:T(8,128)S(1)} custom-call(s32[8,14]{1,0:T(8,128)S(1)} %bitcast.11, bf16[64,1792]{1,0:T(8,128)(2,1)S(1)} %get-tuple-element.32.refs_1_, bf16[32,1792]{1,0:T(8,128)(2,1)S(1)} %collective-permute-done.8.refs_2_, bf16[32,1792]{1,0:T(8,128)(2,1)S(1)} %collective-permute-done.9.refs_3_, ...), custom_call_target="tpu_custom_call" | custom-call | flops 117440512 | bytes 5115328 | tf_op jit(solution)/shard_map/near_1/pallas_call | solution.py:362
  18.7 0.3 collective-permute-done.10.refs_2_.refs_6_
  18.9 1.5 %collective-permute-done.11.refs_3_.refs_7_ = f32[8,1792]{1,0:T(8,128)S(1)} collective-permute-done((f32[8,1792]{1,0:T(8,128)S(1)}, f32[8,1792]{1,0:T(8,128)S(1)}, u32[]{:S(2)}, u32[]{:S(2)}) %collective-permute-start.11) | collective-permute-done | bytes 57376 | tf_op jit(solution)/shard_map/ppermute | solution.py:40
  20.4 0.7 %collective-permute-done.7.refs_0_ = bf16[64,1792]{1,0:T(8,128)(2,1)S(1)} collective-permute-done((bf16[64,1792]{1,0:T(8,128)(2,1)S(1)}, bf16[64,1792]{1,0:T(8,128)(2,1)S(1)}, u32[]{:S(2)}, u32[]{:S(2)}) %collective-permute-start.7) | collective-permute-done | bytes 229408 | tf_op jit(solution)/shard_map/ppermute | solution.py:47
  21.1 0.0 collective-permute-start.13
  21.1 0.5 %middle_1.1.refs_3_ = f32[64,1792]{1,0:T(8,128)S(1)} custom-call(s32[8,14]{1,0:T(8,128)S(1)} %bitcast.12, bf16[64,1792]{1,0:T(8,128)(2,1)S(1)} %hand_on.4.refs_1_, bf16[14,8,128,128]{3,2,1,0:T(8,128)(2,1)S(1)} %copy-done, f32[64,1792]{1,0:T(8,128)S(1)} %near_1.1.refs_1_.refs_3_, f32[2,1792]{1,0:T(2,128)S(1)} %copy-done.3, s32[2,1792]{1,0:T(2,128)S(1)} %copy-done.4, ...), custom_call_target="tpu_custom_call" | custom-call | flops 58720256 | bytes 5018048 | tf_op jit(solution)/shard_map/middle_1/pallas_call | solution.py:362
  21.6 1.0 %collective-permute-done.13.refs_1_ = bf16[64,1792]{1,0:T(8,128)(2,1)S(1)} collective-permute-done((bf16[64,1792]{1,0:T(8,128)(2,1)S(1)}, bf16[64,1792]{1,0:T(8,128)(2,1)S(1)}, u32[]{:S(2)}, u32[]{:S(2)}) %collective-permute-start.13) | collective-permute-done | bytes 229408 | tf_op jit(solution)/shard_map/ppermute | solution.py:47
  22.5 0.5 %last_1.1 = (f32[8,1792]{1,0:T(8,128)S(1)}, f32[8,1792]{1,0:T(8,128)S(1)}, f32[8,1792]{1,0:T(8,128)S(1)}, bf16[64,1792]{1,0:T(8,128)(2,1)S(1)}, bf16[32,1792]{1,...) custom-call(s32[8,14]{1,0:T(8,128)S(1)} %bitcast.13, ...), custom_call_target="tpu_custom_call" | custom-call | flops 58720256 | bytes 5480896 | tf_op jit(solution)/shard_map/last_1/pallas_call | solution.py:362
  23.1 0.9 %collective-permute-start.14 = (bf16[64,1792]{1,0:T(8,128)(2,1)S(1)}, bf16[64,1792]{1,0:T(8,128)(2,1)S(1)}, u32[]{:S(2)}, u32[]{:S(2)}) collective-permute-start(bf16[64,1792]{1,0:T(8,128)(2,1)S(1)} %get-tuple-element.39.refs_1_), channel_id=1, source_target_pairs={{0,16},{8,24},{16,0},{24,8},{1,17},{9,25},{17,1},{25,9},{2,18},{10... | collective-permute-start | bytes 688136 | tf_op jit(solution)/shard_map/ppermute | solution.py:47
  24.0 0.5 %collective-permute-start.16 = (bf16[32,1792]{1,0:T(8,128)(2,1)S(1)}, bf16[32,1792]{1,0:T(8,128)(2,1)S(1)}, u32[]{:S(2)}, u32[]{:S(2)}) collective-permute-start(bf16[32,1792]{1,0:T(8,128)(2,1)S(1)} %get-tuple-element.41), channel_id=1, source_target_pairs={{0,8},{8,0},{16,24},{24,16},{1,9},{9,1},{17,25},{25,17},{2,10},{10... | collective-permute-start | bytes 344072 | tf_op jit(solution)/shard_map/ppermute | solution.py:47
  24.5 1.5 %collective-permute-start.17 = (f32[8,1792]{1,0:T(8,128)S(1)}, f32[8,1792]{1,0:T(8,128)S(1)}, u32[]{:S(2)}, u32[]{:S(2)}) collective-permute-start(f32[8,1792]{1,0:T(8,128)S(1)} %get-tuple-element.43), channel_id=1, source_target_pairs={{0,4},{4,0},{8,12},{12,8},{16,20},{20,16},{24,28},{28,24},{1,5},{5... | collective-permute-start | bytes 172040 | tf_op jit(solution)/shard_map/ppermute | solution.py:40
  26.0 1.6 %collective-permute-start.18 = (f32[8,1792]{1,0:T(8,128)S(1)}, f32[8,1792]{1,0:T(8,128)S(1)}, u32[]{:S(2)}, u32[]{:S(2)}) collective-permute-start(f32[8,1792]{1,0:T(8,128)S(1)} %get-tuple-element.44), channel_id=1, source_target_pairs={{0,1},{1,0},{2,3},{3,2},{8,9},{9,8},{10,11},{11,10},{16,17},{17,16... | collective-permute-start | bytes 172040 | tf_op jit(solution)/shard_map/ppermute | solution.py:40
  27.6 0.8 %near_2.1.refs_1_.refs_3_ = f32[64,1792]{1,0:T(8,128)S(1)} custom-call(s32[8,14]{1,0:T(8,128)S(1)} %bitcast.14, bf16[64,1792]{1,0:T(8,128)(2,1)S(1)} %get-tuple-element.39.refs_1_, bf16[32,1792]{1,0:T(8,128)(2,1)S(1)} %collective-permute-done.15.refs_2_, bf16[32,1792]{1,0:T(8,128)(2,1)S(1)} %collective-permute-done.16.refs_3_, ...), custom_call_target="tpu_custom_call" | custom-call | flops 117440512 | bytes 5115328 | tf_op jit(solution)/shard_map/near_2/pallas_call | solution.py:362
  28.4 0.0 copy-start.2
  28.4 0.2 collective-permute-done.17.refs_2_.refs_6_
  28.6 1.5 %collective-permute-done.18.refs_3_.refs_7_ = f32[8,1792]{1,0:T(8,128)S(1)} collective-permute-done((f32[8,1792]{1,0:T(8,128)S(1)}, f32[8,1792]{1,0:T(8,128)S(1)}, u32[]{:S(2)}, u32[]{:S(2)}) %collective-permute-start.18) | collective-permute-done | bytes 57376 | tf_op jit(solution)/shard_map/ppermute | solution.py:40
  30.1 0.6 %collective-permute-done.14.refs_0_ = bf16[64,1792]{1,0:T(8,128)(2,1)S(1)} collective-permute-done((bf16[64,1792]{1,0:T(8,128)(2,1)S(1)}, bf16[64,1792]{1,0:T(8,128)(2,1)S(1)}, u32[]{:S(2)}, u32[]{:S(2)}) %collective-permute-start.14) | collective-permute-done | bytes 229408 | tf_op jit(solution)/shard_map/ppermute | solution.py:47
  30.8 0.5 %middle_2.1.refs_3_ = f32[64,1792]{1,0:T(8,128)S(1)} custom-call(s32[8,14]{1,0:T(8,128)S(1)} %bitcast.15, bf16[64,1792]{1,0:T(8,128)(2,1)S(1)} %hand_on.5.refs_1_, bf16[14,8,128,128]{3,2,1,0:T(8,128)(2,1)S(1)} %copy-done, f32[64,1792]{1,0:T(8,128)S(1)} %near_2.1.refs_1_.refs_3_, f32[2,1792]{1,0:T(2,128)S(1)} %copy-done.3, s32[2,1792]{1,0:T(2,128)S(1)} %copy-done.4, ...), custom_call_target="tpu_custom_call" | custom-call | flops 58720256 | bytes 5018048 | tf_op jit(solution)/shard_map/middle_2/pallas_call | solution.py:362
  31.3 1.0 %collective-permute-done.20.refs_1_ = bf16[64,1792]{1,0:T(8,128)(2,1)S(1)} collective-permute-done((bf16[64,1792]{1,0:T(8,128)(2,1)S(1)}, bf16[64,1792]{1,0:T(8,128)(2,1)S(1)}, u32[]{:S(2)}, u32[]{:S(2)}) %collective-permute-start.20) | collective-permute-done | bytes 229408 | tf_op jit(solution)/shard_map/ppermute | solution.py:47
  32.3 0.7 %last_2.1 = f32[32,1,128]{2,1,0:T(1,128)S(1)} custom-call(s32[8,14]{1,0:T(8,128)S(1)} %bitcast.16, bf16[64,1792]{1,0:T(8,128)(2,1)S(1)} %collective-permute-done.20.refs_1_, bf16[14,8,128,128]{3,2,1,0:T(8,128)(2,1)S(1)} %copy-done, f32[64,1792]{1,0:T(8,128)S(1)} %middle_2.1.refs_3_, f32[64,128]{1,0:T(8,128)S(1)} %get-tuple-element.28.refs_6_.refs_4_, ...), custom_call_target="tpu_custom_call" | custom-call | flops 58720256 | bytes 5784000 | tf_op jit(solution)/shard_map/last_2/pallas_call | solution.py:362
  33.0 12.1 %all_to_all.5.refs_0_ = f32[32,1,128]{2,1,0:T(1,128)S(1)} all-to-all(f32[32,1,128]{2,1,0:T(1,128)S(1)} %last_2.1), channel_id=1, replica_groups=mesh['mode'=4,'gx'=2,'gy'=4] {'mode','gx','gy'}, dimensions={0} | all-to-all | bytes 32768 | tf_op jit(solution)/shard_map/all_to_all | solution.py:510
  45.0 1.1 %finish.1 = (f32[64,1792]{1,0:T(8,128)}, f32[4,3]{1,0:T(4,128)}) custom-call(f32[32,1,128]{2,1,0:T(1,128)S(1)} %all_to_all.5.refs_0_, f32[64,1792]{1,0:T(8,128)S(1)} %bitcast.7, f32[64,1792]{1,0:T(8,128)S(1)} %get-tuple-element.35.refs_5_.refs_6_.refs_2_, f32[64,1792]{1,0:T(8,128)S(1)} %get-tuple-element.42.refs_5_.refs_7_.refs_3_), custom_call_target="tpu_custom_call" | custom-call | bytes 1851440 | tf_op jit(solution)/shard_map/finish/pallas_call | solution.py:362
  (26 shorter events, 0.1 us)
Async XLA Ops:
  0.6 1.0 %copy-start.1 = (f32[8,8,1792]{2,1,0:T(8,128)S(1)}, f32[8,8,1792]{2,1,0:T(8,128)}, u32[]{:S(2)}) copy-start(f32[8,8,1792]{2,1,0:T(8,128)} %param.7) | copy-start | bytes 1376260
  1.7 3.6 %copy-start.7 = (s32[8,8]{1,0:T(8,128)S(1)}, s32[8,8]{1,0:T(8,128)}, u32[]{:S(2)}) copy-start(s32[8,8]{1,0:T(8,128)} %refs_1_.1) | copy-start | bytes 772
  1.7 7.0 %copy-start = (bf16[14,8,128,128]{3,2,1,0:T(8,128)(2,1)S(1)}, bf16[14,8,128,128]{3,2,1,0:T(8,128)(2,1)}, u32[]{:S(2)}) copy-start(bf16[14,8,128,128]{3,2,1,0:T(8,128)(2,1)} %refs_2_.11) | copy-start | bytes 11010052
  1.7 7.0 %copy-start.3 = (f32[2,1792]{1,0:T(2,128)S(1)}, f32[2,1792]{1,0:T(2,128)}, u32[]{:S(2)}) copy-start(f32[2,1792]{1,0:T(2,128)} %refs_4_.11) | copy-start | bytes 43012
  1.7 7.0 %copy-start.4 = (s32[2,1792]{1,0:T(2,128)S(1)}, s32[2,1792]{1,0:T(2,128)}, u32[]{:S(2)}) copy-start(s32[2,1792]{1,0:T(2,128)} %refs_5_.5) | copy-start | bytes 43012
  1.7 7.0 %copy-start.5 = (s32[14,8]{0,1:T(8,128)S(1)}, s32[14,8]{0,1:T(8,128)}, u32[]{:S(2)}) copy-start(s32[14,8]{0,1:T(8,128)} %param.8) | copy-start | bytes 1348
  1.7 7.0 %copy-start.6 = (f32[1792]{0:T(1024)S(1)}, f32[1792]{0:T(1024)}, u32[]{:S(2)}) copy-start(f32[1792]{0:T(1024)} %refs_7_.5) | copy-start | bytes 21508
  1.7 9.5 %collective-permute-start = (bf16[64,1792]{1,0:T(8,128)(2,1)S(1)}, bf16[64,1792]{1,0:T(8,128)(2,1)S(1)}, u32[]{:S(2)}, u32[]{:S(2)}) collective-permute-start(bf16[64,1792]{1,0:T(8,128)(2,1)S(1)} %get-tuple-element.25.refs_1_), channel_id=1, source_target_pairs={{0,16},{8,24},{16,0},{24,8},{1,17},{9,25},{17,1},{25,9},{2,18},{10... | collective-permute-start | bytes 688136 | tf_op jit(solution)/shard_map/ppermute | solution.py:47
  4.8 3.9 %collective-permute-start.1 = (bf16[32,1792]{1,0:T(8,128)(2,1)S(1)}, bf16[32,1792]{1,0:T(8,128)(2,1)S(1)}, u32[]{:S(2)}, u32[]{:S(2)}) collective-permute-start(bf16[32,1792]{1,0:T(8,128)(2,1)S(1)} %get-tuple-element.26), channel_id=1, source_target_pairs={{0,8},{8,0},{16,24},{24,16},{1,9},{9,1},{17,25},{25,17},{2,10},{10... | collective-permute-start | bytes 344072 | tf_op jit(solution)/shard_map/ppermute | solution.py:47
  4.8 3.9 %collective-permute-start.2 = (bf16[32,1792]{1,0:T(8,128)(2,1)S(1)}, bf16[32,1792]{1,0:T(8,128)(2,1)S(1)}, u32[]{:S(2)}, u32[]{:S(2)}) collective-permute-start(bf16[32,1792]{1,0:T(8,128)(2,1)S(1)} %get-tuple-element.27), channel_id=1, source_target_pairs={{0,8},{8,0},{16,24},{24,16},{1,9},{9,1},{17,25},{25,17},{2,10},{10... | collective-permute-start | bytes 344072 | tf_op jit(solution)/shard_map/ppermute | solution.py:47
  5.5 4.2 %collective-permute-start.3 = (f32[8,1792]{1,0:T(8,128)S(1)}, f32[8,1792]{1,0:T(8,128)S(1)}, u32[]{:S(2)}, u32[]{:S(2)}) collective-permute-start(f32[8,1792]{1,0:T(8,128)S(1)} %get-tuple-element.29), channel_id=1, source_target_pairs={{0,4},{4,0},{8,12},{12,8},{16,20},{20,16},{24,28},{28,24},{1,5},{5... | collective-permute-start | bytes 172040 | tf_op jit(solution)/shard_map/ppermute | solution.py:40
  7.1 4.2 %collective-permute-start.4 = (f32[8,1792]{1,0:T(8,128)S(1)}, f32[8,1792]{1,0:T(8,128)S(1)}, u32[]{:S(2)}, u32[]{:S(2)}) collective-permute-start(f32[8,1792]{1,0:T(8,128)S(1)} %get-tuple-element.30), channel_id=1, source_target_pairs={{0,1},{1,0},{2,3},{3,2},{8,9},{9,8},{10,11},{11,10},{16,17},{17,16... | collective-permute-start | bytes 172040 | tf_op jit(solution)/shard_map/ppermute | solution.py:40
  8.6 2.6 %collective-permute-start.5 = (f32[8,1792]{1,0:T(8,128)S(1)}, f32[8,1792]{1,0:T(8,128)S(1)}, u32[]{:S(2)}, u32[]{:S(2)}) collective-permute-start(f32[8,1792]{1,0:T(8,128)S(1)} %get-tuple-element.31), channel_id=1, source_target_pairs={{0,8},{1,2},{2,1},{3,11},{8,0},{9,10},{10,9},{11,3},{16,24},{17,18... | collective-permute-start | bytes 172040 | tf_op jit(solution)/shard_map/ppermute | solution.py:40
  11.3 1.5 %collective-permute-start.6 = (bf16[64,1792]{1,0:T(8,128)(2,1)S(1)}, bf16[64,1792]{1,0:T(8,128)(2,1)S(1)}, u32[]{:S(2)}, u32[]{:S(2)}) collective-permute-start(bf16[64,1792]{1,0:T(8,128)(2,1)S(1)} %hand_on.3.refs_1_), channel_id=1, source_target_pairs={{0,8},{8,0},{16,24},{24,16},{1,9},{9,1},{17,25},{25,17},{2,10},{10... | collective-permute-start | bytes 688136 | tf_op jit(solution)/shard_map/ppermute | solution.py:47
  13.3 7.7 %collective-permute-start.7 = (bf16[64,1792]{1,0:T(8,128)(2,1)S(1)}, bf16[64,1792]{1,0:T(8,128)(2,1)S(1)}, u32[]{:S(2)}, u32[]{:S(2)}) collective-permute-start(bf16[64,1792]{1,0:T(8,128)(2,1)S(1)} %get-tuple-element.32.refs_1_), channel_id=1, source_target_pairs={{0,16},{8,24},{16,0},{24,8},{1,17},{9,25},{17,1},{25,9},{2,18},{10... | collective-permute-start | bytes 688136 | tf_op jit(solution)/shard_map/ppermute | solution.py:47
  14.2 3.6 %collective-permute-start.8 = (bf16[32,1792]{1,0:T(8,128)(2,1)S(1)}, bf16[32,1792]{1,0:T(8,128)(2,1)S(1)}, u32[]{:S(2)}, u32[]{:S(2)}) collective-permute-start(bf16[32,1792]{1,0:T(8,128)(2,1)S(1)} %get-tuple-element.33), channel_id=1, source_target_pairs={{0,8},{8,0},{16,24},{24,16},{1,9},{9,1},{17,25},{25,17},{2,10},{10... | collective-permute-start | bytes 344072 | tf_op jit(solution)/shard_map/ppermute | solution.py:47
  14.2 3.6 %collective-permute-start.9 = (bf16[32,1792]{1,0:T(8,128)(2,1)S(1)}, bf16[32,1792]{1,0:T(8,128)(2,1)S(1)}, u32[]{:S(2)}, u32[]{:S(2)}) collective-permute-start(bf16[32,1792]{1,0:T(8,128)(2,1)S(1)} %get-tuple-element.34), channel_id=1, source_target_pairs={{0,8},{8,0},{16,24},{24,16},{1,9},{9,1},{17,25},{25,17},{2,10},{10... | collective-permute-start | bytes 344072 | tf_op jit(solution)/shard_map/ppermute | solution.py:47
  14.7 4.2 %collective-permute-start.10 = (f32[8,1792]{1,0:T(8,128)S(1)}, f32[8,1792]{1,0:T(8,128)S(1)}, u32[]{:S(2)}, u32[]{:S(2)}) collective-permute-start(f32[8,1792]{1,0:T(8,128)S(1)} %get-tuple-element.36), channel_id=1, source_target_pairs={{0,4},{4,0},{8,12},{12,8},{16,20},{20,16},{24,28},{28,24},{1,5},{5... | collective-permute-start | bytes 172040 | tf_op jit(solution)/shard_map/ppermute | solution.py:40
  16.2 4.2 %collective-permute-start.11 = (f32[8,1792]{1,0:T(8,128)S(1)}, f32[8,1792]{1,0:T(8,128)S(1)}, u32[]{:S(2)}, u32[]{:S(2)}) collective-permute-start(f32[8,1792]{1,0:T(8,128)S(1)} %get-tuple-element.37), channel_id=1, source_target_pairs={{0,1},{1,0},{2,3},{3,2},{8,9},{9,8},{10,11},{11,10},{16,17},{17,16... | collective-permute-start | bytes 172040 | tf_op jit(solution)/shard_map/ppermute | solution.py:40
  17.8 2.6 %collective-permute-start.12 = (f32[8,1792]{1,0:T(8,128)S(1)}, f32[8,1792]{1,0:T(8,128)S(1)}, u32[]{:S(2)}, u32[]{:S(2)}) collective-permute-start(f32[8,1792]{1,0:T(8,128)S(1)} %get-tuple-element.38), channel_id=1, source_target_pairs={{0,8},{1,2},{2,1},{3,11},{8,0},{9,10},{10,9},{11,3},{16,24},{17,18... | collective-permute-start | bytes 172040 | tf_op jit(solution)/shard_map/ppermute | solution.py:40
  21.1 1.5 %collective-permute-start.13 = (bf16[64,1792]{1,0:T(8,128)(2,1)S(1)}, bf16[64,1792]{1,0:T(8,128)(2,1)S(1)}, u32[]{:S(2)}, u32[]{:S(2)}) collective-permute-start(bf16[64,1792]{1,0:T(8,128)(2,1)S(1)} %hand_on.4.refs_1_), channel_id=1, source_target_pairs={{0,8},{8,0},{16,24},{24,16},{1,9},{9,1},{17,25},{25,17},{2,10},{10... | collective-permute-start | bytes 688136 | tf_op jit(solution)/shard_map/ppermute | solution.py:47
  23.1 7.7 %collective-permute-start.14 = (bf16[64,1792]{1,0:T(8,128)(2,1)S(1)}, bf16[64,1792]{1,0:T(8,128)(2,1)S(1)}, u32[]{:S(2)}, u32[]{:S(2)}) collective-permute-start(bf16[64,1792]{1,0:T(8,128)(2,1)S(1)} %get-tuple-element.39.refs_1_), channel_id=1, source_target_pairs={{0,16},{8,24},{16,0},{24,8},{1,17},{9,25},{17,1},{25,9},{2,18},{10... | collective-permute-start | bytes 688136 | tf_op jit(solution)/shard_map/ppermute | solution.py:47
  24.0 3.6 %collective-permute-start.15 = (bf16[32,1792]{1,0:T(8,128)(2,1)S(1)}, bf16[32,1792]{1,0:T(8,128)(2,1)S(1)}, u32[]{:S(2)}, u32[]{:S(2)}) collective-permute-start(bf16[32,1792]{1,0:T(8,128)(2,1)S(1)} %get-tuple-element.40), channel_id=1, source_target_pairs={{0,8},{8,0},{16,24},{24,16},{1,9},{9,1},{17,25},{25,17},{2,10},{10... | collective-permute-start | bytes 344072 | tf_op jit(solution)/shard_map/ppermute | solution.py:47
  24.0 3.6 %collective-permute-start.16 = (bf16[32,1792]{1,0:T(8,128)(2,1)S(1)}, bf16[32,1792]{1,0:T(8,128)(2,1)S(1)}, u32[]{:S(2)}, u32[]{:S(2)}) collective-permute-start(bf16[32,1792]{1,0:T(8,128)(2,1)S(1)} %get-tuple-element.41), channel_id=1, source_target_pairs={{0,8},{8,0},{16,24},{24,16},{1,9},{9,1},{17,25},{25,17},{2,10},{10... | collective-permute-start | bytes 344072 | tf_op jit(solution)/shard_map/ppermute | solution.py:47
  24.5 4.2 %collective-permute-start.17 = (f32[8,1792]{1,0:T(8,128)S(1)}, f32[8,1792]{1,0:T(8,128)S(1)}, u32[]{:S(2)}, u32[]{:S(2)}) collective-permute-start(f32[8,1792]{1,0:T(8,128)S(1)} %get-tuple-element.43), channel_id=1, source_target_pairs={{0,4},{4,0},{8,12},{12,8},{16,20},{20,16},{24,28},{28,24},{1,5},{5... | collective-permute-start | bytes 172040 | tf_op jit(solution)/shard_map/ppermute | solution.py:40
  26.0 4.2 %collective-permute-start.18 = (f32[8,1792]{1,0:T(8,128)S(1)}, f32[8,1792]{1,0:T(8,128)S(1)}, u32[]{:S(2)}, u32[]{:S(2)}) collective-permute-start(f32[8,1792]{1,0:T(8,128)S(1)} %get-tuple-element.44), channel_id=1, source_target_pairs={{0,1},{1,0},{2,3},{3,2},{8,9},{9,8},{10,11},{11,10},{16,17},{17,16... | collective-permute-start | bytes 172040 | tf_op jit(solution)/shard_map/ppermute | solution.py:40
  27.5 2.6 %collective-permute-start.19 = (f32[8,1792]{1,0:T(8,128)S(1)}, f32[8,1792]{1,0:T(8,128)S(1)}, u32[]{:S(2)}, u32[]{:S(2)}) collective-permute-start(f32[8,1792]{1,0:T(8,128)S(1)} %get-tuple-element.45), channel_id=1, source_target_pairs={{0,8},{1,2},{2,1},{3,11},{8,0},{9,10},{10,9},{11,3},{16,24},{17,18... | collective-permute-start | bytes 172040 | tf_op jit(solution)/shard_map/ppermute | solution.py:40
  28.4 3.9 %copy-start.2 = (f32[8,8,1792]{2,1,0:T(8,128)S(1)}, f32[8,8,1792]{2,1,0:T(8,128)}, u32[]{:S(2)}) copy-start(f32[8,8,1792]{2,1,0:T(8,128)} %param.7) | copy-start | bytes 1376260
  30.8 1.5 %collective-permute-start.20 = (bf16[64,1792]{1,0:T(8,128)(2,1)S(1)}, bf16[64,1792]{1,0:T(8,128)(2,1)S(1)}, u32[]{:S(2)}, u32[]{:S(2)}) collective-permute-start(bf16[64,1792]{1,0:T(8,128)(2,1)S(1)} %hand_on.5.refs_1_), channel_id=1, source_target_pairs={{0,8},{8,0},{16,24},{24,16},{1,9},{9,1},{17,25},{25,17},{2,10},{10... | collective-permute-start | bytes 688136 | tf_op jit(solution)/shard_map/ppermute | solution.py:47

commit v11 on v10

--- a/solution.py
+++ b/solution.py
@@ -140,6 +140,33 @@
     )
 
 
+def add_product(sums, key, left, right):
+    cells, block = left.shape
+    term = jnp.sum((left * right).reshape(cells // 8, 8, block), axis=0)
+    sums[key] = sums[key] + term if key in sums else term
+
+
+def lane_sum(value):
+    return jnp.sum(jnp.sum(value, axis=0, keepdims=True), axis=1, keepdims=True)
+
+
+def early_products(sizes, vectors, early_ref):
+    first, second, local_blocks, block = sizes
+    sums = {}
+    for b in range(local_blocks):
+        lanes = slice(b * block, (b + 1) * block)
+        values = [ref[:, lanes] for ref in vectors]
+        for i in range(len(values)):
+            for j in range(i, len(values)):
+                add_product(sums, (i, j), values[i], values[j])
+    at = 0
+    for i in range(len(vectors) + 1):
+        for j in range(i, len(vectors) + 1):
+            if j < len(vectors):
+                early_ref[at : at + 1, :] = jnp.broadcast_to(lane_sum(sums[i, j]), (1, block))
+            at += 1
+
+
 def split_speeds(speed_ref, sign_ref, lanes):
     parts = []
     for axis in range(2):
@@ -148,12 +175,18 @@
     return parts
 
 
-def near_kernel(sizes, per_owner, places, cols_ref, sources, blocks_ref, current_ref, params, open_ref, out_ref):
+def near_kernel(sizes, per_owner, places, cols_ref, sources, blocks_ref, current_ref, params, open_ref, out_ref, finer_ref=None):
     first, second, local_blocks, block = sizes
     cells = first * second
     open_cells = open_ref[...]
     row_at = lax.broadcasted_iota(jnp.int32, (first, second, block), 1)
     zero = jnp.zeros((1, second, block), jnp.float32)
+    if finer_ref is not None:
+        for b in range(local_blocks):
+            lanes = slice(b * block, (b + 1) * block)
+            rounded = sources[0][0][:, lanes].astype(jnp.float32)
+            finer_ref[:, lanes] = (current_ref[:, lanes] - rounded).astype(jnp.bfloat16)
+        places, sources = places + [0], sources + [[finer_ref]]
     for b in range(local_blocks):
         lanes = slice(b * block, (b + 1) * block)
         scattered = scatter(sizes, per_owner, b, places, cols_ref, sources, blocks_ref)
@@ -200,7 +233,7 @@
         out_ref[:, lanes] = value.reshape(cells, block)
 
 
-def last_kernel(sizes, per_owner, places, cols_ref, sources, blocks_ref, partial_ref, earlier, open_ref, outs):
+def last_kernel(sizes, per_owner, places, cols_ref, sources, blocks_ref, partial_ref, earlier, open_ref, outs, early_ref=None):
     first, second, local_blocks, block = sizes
     cells = first * second
     sums = {}
@@ -217,19 +250,22 @@
             )
         else:
             vectors = [ref[:, lanes] for ref in earlier] + [result]
-            at = 0
-            for i in range(len(vectors)):
-                for j in range(i, len(vectors)):
-                    term = jnp.sum((vectors[i] * vectors[j]).reshape(cells // 8, 8, block), axis=0)
-                    sums[at] = term if b == 0 else sums[at] + term
-                    at += 1
+            for i, vector in enumerate(vectors):
+                add_product(sums, (i, len(earlier)), vector, result)
     if outs.gram is not None:
         devices = outs.gram.shape[0]
         lane = lax.broadcasted_iota(jnp.int32, (1, block), 1)
         row = jnp.zeros((1, block), jnp.float32)
-        for at, value in sums.items():
-            total = jnp.sum(jnp.sum(value, axis=0, keepdims=True), axis=1, keepdims=True)
-            row = jnp.where(lane == at, total, row)
+        size = len(earlier) + 1
+        at = 0
+        for i in range(size):
+            for j in range(i, size):
+                if j < size - 1:
+                    total = early_ref[at : at + 1, :]
+                else:
+                    total = lane_sum(sums[i, j])
+                row = jnp.where(lane == at, total, row)
+                at += 1
         outs.gram[...] = jnp.broadcast_to(row[None], (devices, 1, block))
 
 
@@ -426,15 +462,19 @@
         neighbour = [exchange(part, 1) for part in packed[1:]] if count > 1 else []
         y_in, x_in = move_faces({"gx": faces[:x_moves], "gy": faces[x_moves:]})
 
-        def near_step(cols, sources, rest, params, outs, scratch):
-            sources = [sources[:1], sources[1:]]
+        last = section == KRYLOV - 1
+
+        def near_step(cols, sources, rest, params, known, outs, scratch, section=section, last=last):
+            sources = [sources[:1], sources[1:]][: len(near)]
             blocks_ref, current_ref, open_ref = rest
             near_kernel(
                 sizes, per_owner, near, cols[0], sources, blocks_ref, current_ref, params,
-                open_ref, outs[0],
+                open_ref, outs[0], scratch[0] if section == 0 else None,
             )
-
-        (partial,) = call(
+            if last:
+                early_products(sizes, known, outs[1])
+
+        partial, *early = call(
             "near_%d" % section,
             near_step,
             [
@@ -442,8 +482,10 @@
                 in_vmem([packed[0], *neighbour]),
                 in_vmem([blocks, vectors[-1], open_cells]),
                 in_vmem([relax_rate, drift_speed, upwind_sign]),
+                in_vmem(vectors if last else []),
             ],
-            [vector_shape],
+            [vector_shape] + [shape_of((16, block), f32)] * last,
+            [pltpu.VMEM((cells, local_modes), jnp.bfloat16)] * (section == 0),
             flops=work * len(near),
         )
 
@@ -471,8 +513,7 @@
             flops=work * len(middle),
         )
 
-        last = section == KRYLOV - 1
-        def last_step(cols, sources, rest, earlier, outs, scratch, last=last):
+        def last_step(cols, sources, rest, earlier, early, outs, scratch, last=last):
             blocks_ref, partial_ref, open_ref = rest
             named = Outs()
             if last:
@@ -482,7 +523,7 @@
                 *named.packed, named.value = outs[n_faces:]
             last_kernel(
                 sizes, per_owner, final, cols[0], [[ref] for ref in sources], blocks_ref, partial_ref,
-                earlier, open_ref, named,
+                earlier, open_ref, named, early[0] if last else None,
             )
 
         if last:
@@ -497,6 +538,7 @@
                 in_vmem([sources[place] for place in final]),
                 in_vmem([blocks, partial, open_cells]),
                 in_vmem(vectors if last else []),
+                in_vmem(early),
             ],
             shapes,
             flops=work * len(final),

time: 46.3 us -> 46.3 us (level)
  waiting for transfers between devices: 9.33 us -> 8.83 us
    ppermute x9, waiting for transfers between devices: 5.18 us -> 4.67 us  [move_faces(): arrived.append(lax.ppermute(face, ('mode', axis), pairs))]
  transfers between devices with their start and end apart: 21 -> 21, of which waited for: 11 -> 10; matrix products, arithmetic and copies ran while one was open for 0% -> 0% of each run, Pallas kernels for 9% -> 10%
where the time goes in v11:
time: 46.3 us; the launch traced here: 46.1 us
  starting transfers between devices  15.7 us (34%)
  blocking collectives  12.1 us (26%)
  waiting for transfers between devices  8.83 us (19%)
  Pallas kernels  7.66 us (17%)
  local copies, waits for them, and re-layouts  1.05 us (2%)
  between operations  0.83 us (2%)
    all_to_all x1, blocking collectives, per_device(): gram = lax.all_to_all(gram, AXES, 0, 0)  12.1 us
    ppermute x9, starting transfers between devices, move_faces(): arrived.append(lax.ppermute(face, ('mode', axis), pairs))  9.27 us
    pallas_call x12, Pallas kernels, call(): pl.pallas_call(body, out_shape=list(shapes), in_specs=[spec for spec, ope...  7.66 us
    ppermute x12, starting transfers between devices, exchange(): return lax.ppermute(array, 'mode', [(i, i ^ bit) for i in range(count)])  6.39 us
    ppermute x9, waiting for transfers between devices, move_faces(): arrived.append(lax.ppermute(face, ('mode', axis), pairs))  4.67 us
    ppermute x12, waiting for transfers between devices, exchange(): return lax.ppermute(array, 'mode', [(i, i ^ bit) for i in range(count)])  4.16 us
    unnamed x16, local copies, waits for them, and re-layouts  1.05 us
  transfers between devices with their start and end apart: 21, of which 10 were waited for; matrix products, arithmetic and copies ran while one was open for 0% of the time, Pallas kernels for 10%

profile of v11, /device:TPU:0, one launch (start us, length us, event | category | flops | bytes accessed | tf_op | source)
XLA Modules:
  0.0 46.1 jit_solution(7572877309047108748)
XLA Ops:
  0.6 0.0 copy-start.1
  0.6 1.0 %copy-done.1 = f32[8,8,1792]{2,1,0:T(8,128)S(1)} copy-done((f32[8,8,1792]{2,1,0:T(8,128)S(1)}, f32[8,8,1792]{2,1,0:T(8,128)}, u32[]{:S(2)}) %copy-start.1) | copy-done | bytes 458776
  1.7 0.0 copy-start
  1.7 0.0 copy-start.3
  1.7 0.0 copy-start.4
  1.7 0.0 copy-start.5
  1.7 0.0 copy-start.6
  1.7 3.0 %collective-permute-start = (bf16[64,1792]{1,0:T(8,128)(2,1)S(1)}, bf16[64,1792]{1,0:T(8,128)(2,1)S(1)}, u32[]{:S(2)}, u32[]{:S(2)}) collective-permute-start(bf16[64,1792]{1,0:T(8,128)(2,1)S(1)} %get-tuple-element.27.refs_1_), channel_id=1, source_target_pairs={{0,16},{8,24},{16,0},{24,8},{1,17},{9,25},{17,1},{25,9},{2,18},{10... | collective-permute-start | bytes 688136 | tf_op jit(solution)/shard_map/ppermute | solution.py:47
  4.8 0.0 collective-permute-start.1
  4.8 0.5 %collective-permute-start.2 = (bf16[32,1792]{1,0:T(8,128)(2,1)S(1)}, bf16[32,1792]{1,0:T(8,128)(2,1)S(1)}, u32[]{:S(2)}, u32[]{:S(2)}) collective-permute-start(bf16[32,1792]{1,0:T(8,128)(2,1)S(1)} %get-tuple-element.29), channel_id=1, source_target_pairs={{0,8},{8,0},{16,24},{24,16},{1,9},{9,1},{17,25},{25,17},{2,10},{10... | collective-permute-start | bytes 344072 | tf_op jit(solution)/shard_map/ppermute | solution.py:47
  5.3 0.2 prepare.1
  5.5 1.6 %collective-permute-start.3 = (f32[8,1792]{1,0:T(8,128)S(1)}, f32[8,1792]{1,0:T(8,128)S(1)}, u32[]{:S(2)}, u32[]{:S(2)}) collective-permute-start(f32[8,1792]{1,0:T(8,128)S(1)} %get-tuple-element.31), channel_id=1, source_target_pairs={{0,4},{4,0},{8,12},{12,8},{16,20},{20,16},{24,28},{28,24},{1,5},{5... | collective-permute-start | bytes 172040 | tf_op jit(solution)/shard_map/ppermute | solution.py:40
  7.1 1.6 %collective-permute-start.4 = (f32[8,1792]{1,0:T(8,128)S(1)}, f32[8,1792]{1,0:T(8,128)S(1)}, u32[]{:S(2)}, u32[]{:S(2)}) collective-permute-start(f32[8,1792]{1,0:T(8,128)S(1)} %get-tuple-element.32), channel_id=1, source_target_pairs={{0,1},{1,0},{2,3},{3,2},{8,9},{9,8},{10,11},{11,10},{16,17},{17,16... | collective-permute-start | bytes 172040 | tf_op jit(solution)/shard_map/ppermute | solution.py:40
  8.6 0.0 collective-permute-done.1.refs_2_
  8.6 0.0 collective-permute-start.5
  8.7 1.2 %near_0.1.refs_1_.refs_3_ = f32[64,1792]{1,0:T(8,128)S(1)} custom-call(s32[8,14]{1,0:T(8,128)S(1)} %bitcast.9, bf16[64,1792]{1,0:T(8,128)(2,1)S(1)} %get-tuple-element.27.refs_1_, bf16[32,1792]{1,0:T(8,128)(2,1)S(1)} %collective-permute-done.1.refs_2_, bf16[32,1792]{1,0:T(8,128)(2,1)S(1)} %collective-permute-done.2.refs_3_, ...), custom_call_target="tpu_custom_call" | custom-call | flops 117440512 | bytes 5115328 | tf_op jit(solution)/shard_map/near_0/pallas_call | solution.py:398
  9.9 0.0 collective-permute-done.3.refs_2_.refs_6_
  9.9 1.3 %collective-permute-done.4.refs_3_.refs_7_ = f32[8,1792]{1,0:T(8,128)S(1)} collective-permute-done((f32[8,1792]{1,0:T(8,128)S(1)}, f32[8,1792]{1,0:T(8,128)S(1)}, u32[]{:S(2)}, u32[]{:S(2)}) %collective-permute-start.4) | collective-permute-done | bytes 57376 | tf_op jit(solution)/shard_map/ppermute | solution.py:40
  11.2 0.0 collective-permute-done.5.refs_4_.refs_8_
  11.3 0.1 collective-permute-start.6
  11.3 0.5 %middle_0.1.refs_3_ = f32[64,1792]{1,0:T(8,128)S(1)} custom-call(s32[8,14]{1,0:T(8,128)S(1)} %bitcast.10, bf16[64,1792]{1,0:T(8,128)(2,1)S(1)} %hand_on.3.refs_1_, bf16[14,8,128,128]{3,2,1,0:T(8,128)(2,1)S(1)} %copy-done, f32[64,1792]{1,0:T(8,128)S(1)} %near_0.1.refs_1_.refs_3_, f32[2,1792]{1,0:T(2,128)S(1)} %copy-done.3, s32[2,1792]{1,0:T(2,128)S(1)} %copy-done.4, ...), custom_call_target="tpu_custom_call" | custom-call | flops 58720256 | bytes 5018048 | tf_op jit(solution)/shard_map/middle_0/pallas_call | solution.py:398
  11.9 0.9 %collective-permute-done.6.refs_1_ = bf16[64,1792]{1,0:T(8,128)(2,1)S(1)} collective-permute-done((bf16[64,1792]{1,0:T(8,128)(2,1)S(1)}, bf16[64,1792]{1,0:T(8,128)(2,1)S(1)}, u32[]{:S(2)}, u32[]{:S(2)}) %collective-permute-start.6) | collective-permute-done | bytes 229408 | tf_op jit(solution)/shard_map/ppermute | solution.py:47
  12.8 0.5 %last_0.1 = (f32[8,1792]{1,0:T(8,128)S(1)}, f32[8,1792]{1,0:T(8,128)S(1)}, f32[8,1792]{1,0:T(8,128)S(1)}, bf16[64,1792]{1,0:T(8,128)(2,1)S(1)}, bf16[32,1792]{1,...) custom-call(s32[8,14]{1,0:T(8,128)S(1)} %bitcast.11, ...), custom_call_target="tpu_custom_call" | custom-call | flops 58720256 | bytes 5480896 | tf_op jit(solution)/shard_map/last_0/pallas_call | solution.py:398
  13.3 0.9 %collective-permute-start.7 = (bf16[64,1792]{1,0:T(8,128)(2,1)S(1)}, bf16[64,1792]{1,0:T(8,128)(2,1)S(1)}, u32[]{:S(2)}, u32[]{:S(2)}) collective-permute-start(bf16[64,1792]{1,0:T(8,128)(2,1)S(1)} %get-tuple-element.34.refs_1_), channel_id=1, source_target_pairs={{0,16},{8,24},{16,0},{24,8},{1,17},{9,25},{17,1},{25,9},{2,18},{10... | collective-permute-start | bytes 688136 | tf_op jit(solution)/shard_map/ppermute | solution.py:47
  14.2 0.5 %collective-permute-start.9 = (bf16[32,1792]{1,0:T(8,128)(2,1)S(1)}, bf16[32,1792]{1,0:T(8,128)(2,1)S(1)}, u32[]{:S(2)}, u32[]{:S(2)}) collective-permute-start(bf16[32,1792]{1,0:T(8,128)(2,1)S(1)} %get-tuple-element.36), channel_id=1, source_target_pairs={{0,8},{8,0},{16,24},{24,16},{1,9},{9,1},{17,25},{25,17},{2,10},{10... | collective-permute-start | bytes 344072 | tf_op jit(solution)/shard_map/ppermute | solution.py:47
  14.7 1.5 %collective-permute-start.10 = (f32[8,1792]{1,0:T(8,128)S(1)}, f32[8,1792]{1,0:T(8,128)S(1)}, u32[]{:S(2)}, u32[]{:S(2)}) collective-permute-start(f32[8,1792]{1,0:T(8,128)S(1)} %get-tuple-element.38), channel_id=1, source_target_pairs={{0,4},{4,0},{8,12},{12,8},{16,20},{20,16},{24,28},{28,24},{1,5},{5... | collective-permute-start | bytes 172040 | tf_op jit(solution)/shard_map/ppermute | solution.py:40
  16.2 1.6 %collective-permute-start.11 = (f32[8,1792]{1,0:T(8,128)S(1)}, f32[8,1792]{1,0:T(8,128)S(1)}, u32[]{:S(2)}, u32[]{:S(2)}) collective-permute-start(f32[8,1792]{1,0:T(8,128)S(1)} %get-tuple-element.39), channel_id=1, source_target_pairs={{0,1},{1,0},{2,3},{3,2},{8,9},{9,8},{10,11},{11,10},{16,17},{17,16... | collective-permute-start | bytes 172040 | tf_op jit(solution)/shard_map/ppermute | solution.py:40
  17.8 0.0 collective-permute-done.8.refs_2_
  17.8 0.8 %near_1.1.refs_1_.refs_3_ = f32[64,1792]{1,0:T(8,128)S(1)} custom-call(s32[8,14]{1,0:T(8,128)S(1)} %bitcast.12, bf16[64,1792]{1,0:T(8,128)(2,1)S(1)} %get-tuple-element.34.refs_1_, bf16[32,1792]{1,0:T(8,128)(2,1)S(1)} %collective-permute-done.8.refs_2_, bf16[32,1792]{1,0:T(8,128)(2,1)S(1)} %collective-permute-done.9.refs_3_, ...), custom_call_target="tpu_custom_call" | custom-call | flops 117440512 | bytes 5115328 | tf_op jit(solution)/shard_map/near_1/pallas_call | solution.py:398
  18.7 0.2 collective-permute-done.10.refs_2_.refs_6_
  18.9 1.5 %collective-permute-done.11.refs_3_.refs_7_ = f32[8,1792]{1,0:T(8,128)S(1)} collective-permute-done((f32[8,1792]{1,0:T(8,128)S(1)}, f32[8,1792]{1,0:T(8,128)S(1)}, u32[]{:S(2)}, u32[]{:S(2)}) %collective-permute-start.11) | collective-permute-done | bytes 57376 | tf_op jit(solution)/shard_map/ppermute | solution.py:40
  20.4 0.6 %collective-permute-done.7.refs_0_ = bf16[64,1792]{1,0:T(8,128)(2,1)S(1)} collective-permute-done((bf16[64,1792]{1,0:T(8,128)(2,1)S(1)}, bf16[64,1792]{1,0:T(8,128)(2,1)S(1)}, u32[]{:S(2)}, u32[]{:S(2)}) %collective-permute-start.7) | collective-permute-done | bytes 229408 | tf_op jit(solution)/shard_map/ppermute | solution.py:47
  21.1 0.5 %middle_1.1.refs_3_ = f32[64,1792]{1,0:T(8,128)S(1)} custom-call(s32[8,14]{1,0:T(8,128)S(1)} %bitcast.13, bf16[64,1792]{1,0:T(8,128)(2,1)S(1)} %hand_on.4.refs_1_, bf16[14,8,128,128]{3,2,1,0:T(8,128)(2,1)S(1)} %copy-done, f32[64,1792]{1,0:T(8,128)S(1)} %near_1.1.refs_1_.refs_3_, f32[2,1792]{1,0:T(2,128)S(1)} %copy-done.3, s32[2,1792]{1,0:T(2,128)S(1)} %copy-done.4, ...), custom_call_target="tpu_custom_call" | custom-call | flops 58720256 | bytes 5018048 | tf_op jit(solution)/shard_map/middle_1/pallas_call | solution.py:398
  21.6 1.0 %collective-permute-done.13.refs_1_ = bf16[64,1792]{1,0:T(8,128)(2,1)S(1)} collective-permute-done((bf16[64,1792]{1,0:T(8,128)(2,1)S(1)}, bf16[64,1792]{1,0:T(8,128)(2,1)S(1)}, u32[]{:S(2)}, u32[]{:S(2)}) %collective-permute-start.13) | collective-permute-done | bytes 229408 | tf_op jit(solution)/shard_map/ppermute | solution.py:47
  22.5 0.5 %last_1.1 = (f32[8,1792]{1,0:T(8,128)S(1)}, f32[8,1792]{1,0:T(8,128)S(1)}, f32[8,1792]{1,0:T(8,128)S(1)}, bf16[64,1792]{1,0:T(8,128)(2,1)S(1)}, bf16[32,1792]{1,...) custom-call(s32[8,14]{1,0:T(8,128)S(1)} %bitcast.14, ...), custom_call_target="tpu_custom_call" | custom-call | flops 58720256 | bytes 5480896 | tf_op jit(solution)/shard_map/last_1/pallas_call | solution.py:398
  23.1 0.9 %collective-permute-start.14 = (bf16[64,1792]{1,0:T(8,128)(2,1)S(1)}, bf16[64,1792]{1,0:T(8,128)(2,1)S(1)}, u32[]{:S(2)}, u32[]{:S(2)}) collective-permute-start(bf16[64,1792]{1,0:T(8,128)(2,1)S(1)} %get-tuple-element.41.refs_1_), channel_id=1, source_target_pairs={{0,16},{8,24},{16,0},{24,8},{1,17},{9,25},{17,1},{25,9},{2,18},{10... | collective-permute-start | bytes 688136 | tf_op jit(solution)/shard_map/ppermute | solution.py:47
  24.0 0.5 %collective-permute-start.16 = (bf16[32,1792]{1,0:T(8,128)(2,1)S(1)}, bf16[32,1792]{1,0:T(8,128)(2,1)S(1)}, u32[]{:S(2)}, u32[]{:S(2)}) collective-permute-start(bf16[32,1792]{1,0:T(8,128)(2,1)S(1)} %get-tuple-element.43), channel_id=1, source_target_pairs={{0,8},{8,0},{16,24},{24,16},{1,9},{9,1},{17,25},{25,17},{2,10},{10... | collective-permute-start | bytes 344072 | tf_op jit(solution)/shard_map/ppermute | solution.py:47
  24.5 1.5 %collective-permute-start.17 = (f32[8,1792]{1,0:T(8,128)S(1)}, f32[8,1792]{1,0:T(8,128)S(1)}, u32[]{:S(2)}, u32[]{:S(2)}) collective-permute-start(f32[8,1792]{1,0:T(8,128)S(1)} %get-tuple-element.46), channel_id=1, source_target_pairs={{0,4},{4,0},{8,12},{12,8},{16,20},{20,16},{24,28},{28,24},{1,5},{5... | collective-permute-start | bytes 172040 | tf_op jit(solution)/shard_map/ppermute | solution.py:40
  26.0 1.6 %collective-permute-start.18 = (f32[8,1792]{1,0:T(8,128)S(1)}, f32[8,1792]{1,0:T(8,128)S(1)}, u32[]{:S(2)}, u32[]{:S(2)}) collective-permute-start(f32[8,1792]{1,0:T(8,128)S(1)} %get-tuple-element.47), channel_id=1, source_target_pairs={{0,1},{1,0},{2,3},{3,2},{8,9},{9,8},{10,11},{11,10},{16,17},{17,16... | collective-permute-start | bytes 172040 | tf_op jit(solution)/shard_map/ppermute | solution.py:40
  27.6 1.0 %near_2.1 = (f32[64,1792]{1,0:T(8,128)S(1)}, f32[16,128]{1,0:T(8,128)S(1)}) custom-call(s32[8,14]{1,0:T(8,128)S(1)} %bitcast.15, bf16[64,1792]{1,0:T(8,128)(2,1)S(1)} %get-tuple-element.41.refs_1_, bf16[32,1792]{1,0:T(8,128)(2,1)S(1)} %collective-permute-done.15.refs_2_, bf16[32,1792]{1,0:T(8,128)(2,1)S(1)} %collective-permute-done.16.refs_3_, ...), custom_call_target="tpu_custom_call" | custom-call | flops 117440512 | bytes 6499776 | tf_op jit(solution)/shard_map/near_2/pallas_call | solution.py:398
  28.6 0.1 collective-permute-done.17.refs_2_.refs_6_
  28.6 1.5 %collective-permute-done.18.refs_3_.refs_7_ = f32[8,1792]{1,0:T(8,128)S(1)} collective-permute-done((f32[8,1792]{1,0:T(8,128)S(1)}, f32[8,1792]{1,0:T(8,128)S(1)}, u32[]{:S(2)}, u32[]{:S(2)}) %collective-permute-start.18) | collective-permute-done | bytes 57376 | tf_op jit(solution)/shard_map/ppermute | solution.py:40
  30.1 0.6 %collective-permute-done.14.refs_0_ = bf16[64,1792]{1,0:T(8,128)(2,1)S(1)} collective-permute-done((bf16[64,1792]{1,0:T(8,128)(2,1)S(1)}, bf16[64,1792]{1,0:T(8,128)(2,1)S(1)}, u32[]{:S(2)}, u32[]{:S(2)}) %collective-permute-start.14) | collective-permute-done | bytes 229408 | tf_op jit(solution)/shard_map/ppermute | solution.py:47
  30.8 0.5 %middle_2.1.refs_3_ = f32[64,1792]{1,0:T(8,128)S(1)} custom-call(s32[8,14]{1,0:T(8,128)S(1)} %bitcast.16, bf16[64,1792]{1,0:T(8,128)(2,1)S(1)} %hand_on.5.refs_1_, bf16[14,8,128,128]{3,2,1,0:T(8,128)(2,1)S(1)} %copy-done, f32[64,1792]{1,0:T(8,128)S(1)} %get-tuple-element.45.refs_1_.refs_3_, f32[2,1792]{1,0:T(2,128)S(1)} %copy-done.3, ...), custom_call_target="tpu_custom_call" | custom-call | flops 58720256 | bytes 5018048 | tf_op jit(solution)/shard_map/middle_2/pallas_call | solution.py:398
  31.3 1.0 %collective-permute-done.20.refs_1_ = bf16[64,1792]{1,0:T(8,128)(2,1)S(1)} collective-permute-done((bf16[64,1792]{1,0:T(8,128)(2,1)S(1)}, bf16[64,1792]{1,0:T(8,128)(2,1)S(1)}, u32[]{:S(2)}, u32[]{:S(2)}) %collective-permute-start.20) | collective-permute-done | bytes 229408 | tf_op jit(solution)/shard_map/ppermute | solution.py:47
  32.3 0.6 %last_2.1 = f32[32,1,128]{2,1,0:T(1,128)S(1)} custom-call(s32[8,14]{1,0:T(8,128)S(1)} %bitcast.17, bf16[64,1792]{1,0:T(8,128)(2,1)S(1)} %collective-permute-done.20.refs_1_, bf16[14,8,128,128]{3,2,1,0:T(8,128)(2,1)S(1)} %copy-done, f32[64,1792]{1,0:T(8,128)S(1)} %middle_2.1.refs_3_, f32[64,128]{1,0:T(8,128)S(1)} %get-tuple-element.30.refs_6_.refs_4_, ...), custom_call_target="tpu_custom_call" | custom-call | flops 58720256 | bytes 5792192 | tf_op jit(solution)/shard_map/last_2/pallas_call | solution.py:398
  32.9 12.1 %all_to_all.5.refs_0_ = f32[32,1,128]{2,1,0:T(1,128)S(1)} all-to-all(f32[32,1,128]{2,1,0:T(1,128)S(1)} %last_2.1), channel_id=1, replica_groups=mesh['mode'=4,'gx'=2,'gy'=4] {'mode','gx','gy'}, dimensions={0} | all-to-all | bytes 32768 | tf_op jit(solution)/shard_map/all_to_all | solution.py:552
  45.0 1.1 %finish.1 = (f32[64,1792]{1,0:T(8,128)}, f32[4,3]{1,0:T(4,128)}) custom-call(f32[32,1,128]{2,1,0:T(1,128)S(1)} %all_to_all.5.refs_0_, f32[64,1792]{1,0:T(8,128)S(1)} %bitcast.8, f32[64,1792]{1,0:T(8,128)S(1)} %get-tuple-element.37.refs_5_.refs_11_.refs_6_.refs_2_, f32[64,1792]{1,0:T(8,128)S(1)} %get-tuple-element.44.refs_5_.refs_12_.refs_7_.refs_3_), custom_call_target="tpu_custom_call" | custom-call | bytes 1851440 | tf_op jit(solution)/shard_map/finish/pallas_call | solution.py:398
  (26 shorter events, 0.1 us)
Async XLA Ops:
  0.6 1.0 %copy-start.1 = (f32[8,8,1792]{2,1,0:T(8,128)S(1)}, f32[8,8,1792]{2,1,0:T(8,128)}, u32[]{:S(2)}) copy-start(f32[8,8,1792]{2,1,0:T(8,128)} %param.7) | copy-start | bytes 1376260
  1.7 3.6 %copy-start.7 = (s32[8,8]{1,0:T(8,128)S(1)}, s32[8,8]{1,0:T(8,128)}, u32[]{:S(2)}) copy-start(s32[8,8]{1,0:T(8,128)} %refs_1_.1) | copy-start | bytes 772
  1.7 7.0 %copy-start = (bf16[14,8,128,128]{3,2,1,0:T(8,128)(2,1)S(1)}, bf16[14,8,128,128]{3,2,1,0:T(8,128)(2,1)}, u32[]{:S(2)}) copy-start(bf16[14,8,128,128]{3,2,1,0:T(8,128)(2,1)} %refs_2_.11) | copy-start | bytes 11010052
  1.7 7.0 %copy-start.3 = (f32[2,1792]{1,0:T(2,128)S(1)}, f32[2,1792]{1,0:T(2,128)}, u32[]{:S(2)}) copy-start(f32[2,1792]{1,0:T(2,128)} %refs_4_.11) | copy-start | bytes 43012
  1.7 7.0 %copy-start.4 = (s32[2,1792]{1,0:T(2,128)S(1)}, s32[2,1792]{1,0:T(2,128)}, u32[]{:S(2)}) copy-start(s32[2,1792]{1,0:T(2,128)} %refs_5_.5) | copy-start | bytes 43012
  1.7 7.0 %copy-start.5 = (s32[14,8]{0,1:T(8,128)S(1)}, s32[14,8]{0,1:T(8,128)}, u32[]{:S(2)}) copy-start(s32[14,8]{0,1:T(8,128)} %param.8) | copy-start | bytes 1348
  1.7 7.0 %copy-start.6 = (f32[1792]{0:T(1024)S(1)}, f32[1792]{0:T(1024)}, u32[]{:S(2)}) copy-start(f32[1792]{0:T(1024)} %refs_7_.5) | copy-start | bytes 21508
  1.7 9.5 %collective-permute-start = (bf16[64,1792]{1,0:T(8,128)(2,1)S(1)}, bf16[64,1792]{1,0:T(8,128)(2,1)S(1)}, u32[]{:S(2)}, u32[]{:S(2)}) collective-permute-start(bf16[64,1792]{1,0:T(8,128)(2,1)S(1)} %get-tuple-element.27.refs_1_), channel_id=1, source_target_pairs={{0,16},{8,24},{16,0},{24,8},{1,17},{9,25},{17,1},{25,9},{2,18},{10... | collective-permute-start | bytes 688136 | tf_op jit(solution)/shard_map/ppermute | solution.py:47
  4.8 3.9 %collective-permute-start.1 = (bf16[32,1792]{1,0:T(8,128)(2,1)S(1)}, bf16[32,1792]{1,0:T(8,128)(2,1)S(1)}, u32[]{:S(2)}, u32[]{:S(2)}) collective-permute-start(bf16[32,1792]{1,0:T(8,128)(2,1)S(1)} %get-tuple-element.28), channel_id=1, source_target_pairs={{0,8},{8,0},{16,24},{24,16},{1,9},{9,1},{17,25},{25,17},{2,10},{10... | collective-permute-start | bytes 344072 | tf_op jit(solution)/shard_map/ppermute | solution.py:47
  4.8 3.9 %collective-permute-start.2 = (bf16[32,1792]{1,0:T(8,128)(2,1)S(1)}, bf16[32,1792]{1,0:T(8,128)(2,1)S(1)}, u32[]{:S(2)}, u32[]{:S(2)}) collective-permute-start(bf16[32,1792]{1,0:T(8,128)(2,1)S(1)} %get-tuple-element.29), channel_id=1, source_target_pairs={{0,8},{8,0},{16,24},{24,16},{1,9},{9,1},{17,25},{25,17},{2,10},{10... | collective-permute-start | bytes 344072 | tf_op jit(solution)/shard_map/ppermute | solution.py:47
  5.5 4.4 %collective-permute-start.3 = (f32[8,1792]{1,0:T(8,128)S(1)}, f32[8,1792]{1,0:T(8,128)S(1)}, u32[]{:S(2)}, u32[]{:S(2)}) collective-permute-start(f32[8,1792]{1,0:T(8,128)S(1)} %get-tuple-element.31), channel_id=1, source_target_pairs={{0,4},{4,0},{8,12},{12,8},{16,20},{20,16},{24,28},{28,24},{1,5},{5... | collective-permute-start | bytes 172040 | tf_op jit(solution)/shard_map/ppermute | solution.py:40
  7.1 4.2 %collective-permute-start.4 = (f32[8,1792]{1,0:T(8,128)S(1)}, f32[8,1792]{1,0:T(8,128)S(1)}, u32[]{:S(2)}, u32[]{:S(2)}) collective-permute-start(f32[8,1792]{1,0:T(8,128)S(1)} %get-tuple-element.32), channel_id=1, source_target_pairs={{0,1},{1,0},{2,3},{3,2},{8,9},{9,8},{10,11},{11,10},{16,17},{17,16... | collective-permute-start | bytes 172040 | tf_op jit(solution)/shard_map/ppermute | solution.py:40
  8.6 2.6 %collective-permute-start.5 = (f32[8,1792]{1,0:T(8,128)S(1)}, f32[8,1792]{1,0:T(8,128)S(1)}, u32[]{:S(2)}, u32[]{:S(2)}) collective-permute-start(f32[8,1792]{1,0:T(8,128)S(1)} %get-tuple-element.33), channel_id=1, source_target_pairs={{0,8},{1,2},{2,1},{3,11},{8,0},{9,10},{10,9},{11,3},{16,24},{17,18... | collective-permute-start | bytes 172040 | tf_op jit(solution)/shard_map/ppermute | solution.py:40
  11.3 1.5 %collective-permute-start.6 = (bf16[64,1792]{1,0:T(8,128)(2,1)S(1)}, bf16[64,1792]{1,0:T(8,128)(2,1)S(1)}, u32[]{:S(2)}, u32[]{:S(2)}) collective-permute-start(bf16[64,1792]{1,0:T(8,128)(2,1)S(1)} %hand_on.3.refs_1_), channel_id=1, source_target_pairs={{0,8},{8,0},{16,24},{24,16},{1,9},{9,1},{17,25},{25,17},{2,10},{10... | collective-permute-start | bytes 688136 | tf_op jit(solution)/shard_map/ppermute | solution.py:47
  13.3 7.7 %collective-permute-start.7 = (bf16[64,1792]{1,0:T(8,128)(2,1)S(1)}, bf16[64,1792]{1,0:T(8,128)(2,1)S(1)}, u32[]{:S(2)}, u32[]{:S(2)}) collective-permute-start(bf16[64,1792]{1,0:T(8,128)(2,1)S(1)} %get-tuple-element.34.refs_1_), channel_id=1, source_target_pairs={{0,16},{8,24},{16,0},{24,8},{1,17},{9,25},{17,1},{25,9},{2,18},{10... | collective-permute-start | bytes 688136 | tf_op jit(solution)/shard_map/ppermute | solution.py:47
  14.2 3.6 %collective-permute-start.8 = (bf16[32,1792]{1,0:T(8,128)(2,1)S(1)}, bf16[32,1792]{1,0:T(8,128)(2,1)S(1)}, u32[]{:S(2)}, u32[]{:S(2)}) collective-permute-start(bf16[32,1792]{1,0:T(8,128)(2,1)S(1)} %get-tuple-element.35), channel_id=1, source_target_pairs={{0,8},{8,0},{16,24},{24,16},{1,9},{9,1},{17,25},{25,17},{2,10},{10... | collective-permute-start | bytes 344072 | tf_op jit(solution)/shard_map/ppermute | solution.py:47
  14.2 3.6 %collective-permute-start.9 = (bf16[32,1792]{1,0:T(8,128)(2,1)S(1)}, bf16[32,1792]{1,0:T(8,128)(2,1)S(1)}, u32[]{:S(2)}, u32[]{:S(2)}) collective-permute-start(bf16[32,1792]{1,0:T(8,128)(2,1)S(1)} %get-tuple-element.36), channel_id=1, source_target_pairs={{0,8},{8,0},{16,24},{24,16},{1,9},{9,1},{17,25},{25,17},{2,10},{10... | collective-permute-start | bytes 344072 | tf_op jit(solution)/shard_map/ppermute | solution.py:47
  14.7 4.2 %collective-permute-start.10 = (f32[8,1792]{1,0:T(8,128)S(1)}, f32[8,1792]{1,0:T(8,128)S(1)}, u32[]{:S(2)}, u32[]{:S(2)}) collective-permute-start(f32[8,1792]{1,0:T(8,128)S(1)} %get-tuple-element.38), channel_id=1, source_target_pairs={{0,4},{4,0},{8,12},{12,8},{16,20},{20,16},{24,28},{28,24},{1,5},{5... | collective-permute-start | bytes 172040 | tf_op jit(solution)/shard_map/ppermute | solution.py:40
  16.2 4.2 %collective-permute-start.11 = (f32[8,1792]{1,0:T(8,128)S(1)}, f32[8,1792]{1,0:T(8,128)S(1)}, u32[]{:S(2)}, u32[]{:S(2)}) collective-permute-start(f32[8,1792]{1,0:T(8,128)S(1)} %get-tuple-element.39), channel_id=1, source_target_pairs={{0,1},{1,0},{2,3},{3,2},{8,9},{9,8},{10,11},{11,10},{16,17},{17,16... | collective-permute-start | bytes 172040 | tf_op jit(solution)/shard_map/ppermute | solution.py:40
  17.8 2.6 %collective-permute-start.12 = (f32[8,1792]{1,0:T(8,128)S(1)}, f32[8,1792]{1,0:T(8,128)S(1)}, u32[]{:S(2)}, u32[]{:S(2)}) collective-permute-start(f32[8,1792]{1,0:T(8,128)S(1)} %get-tuple-element.40), channel_id=1, source_target_pairs={{0,8},{1,2},{2,1},{3,11},{8,0},{9,10},{10,9},{11,3},{16,24},{17,18... | collective-permute-start | bytes 172040 | tf_op jit(solution)/shard_map/ppermute | solution.py:40
  21.1 6.5 %copy-start.2 = (f32[8,8,1792]{2,1,0:T(8,128)S(1)}, f32[8,8,1792]{2,1,0:T(8,128)}, u32[]{:S(2)}) copy-start(f32[8,8,1792]{2,1,0:T(8,128)} %param.7) | copy-start | bytes 1376260
  21.1 1.5 %collective-permute-start.13 = (bf16[64,1792]{1,0:T(8,128)(2,1)S(1)}, bf16[64,1792]{1,0:T(8,128)(2,1)S(1)}, u32[]{:S(2)}, u32[]{:S(2)}) collective-permute-start(bf16[64,1792]{1,0:T(8,128)(2,1)S(1)} %hand_on.4.refs_1_), channel_id=1, source_target_pairs={{0,8},{8,0},{16,24},{24,16},{1,9},{9,1},{17,25},{25,17},{2,10},{10... | collective-permute-start | bytes 688136 | tf_op jit(solution)/shard_map/ppermute | solution.py:47
  23.1 7.7 %collective-permute-start.14 = (bf16[64,1792]{1,0:T(8,128)(2,1)S(1)}, bf16[64,1792]{1,0:T(8,128)(2,1)S(1)}, u32[]{:S(2)}, u32[]{:S(2)}) collective-permute-start(bf16[64,1792]{1,0:T(8,128)(2,1)S(1)} %get-tuple-element.41.refs_1_), channel_id=1, source_target_pairs={{0,16},{8,24},{16,0},{24,8},{1,17},{9,25},{17,1},{25,9},{2,18},{10... | collective-permute-start | bytes 688136 | tf_op jit(solution)/shard_map/ppermute | solution.py:47
  24.0 3.6 %collective-permute-start.15 = (bf16[32,1792]{1,0:T(8,128)(2,1)S(1)}, bf16[32,1792]{1,0:T(8,128)(2,1)S(1)}, u32[]{:S(2)}, u32[]{:S(2)}) collective-permute-start(bf16[32,1792]{1,0:T(8,128)(2,1)S(1)} %get-tuple-element.42), channel_id=1, source_target_pairs={{0,8},{8,0},{16,24},{24,16},{1,9},{9,1},{17,25},{25,17},{2,10},{10... | collective-permute-start | bytes 344072 | tf_op jit(solution)/shard_map/ppermute | solution.py:47
  24.0 3.6 %collective-permute-start.16 = (bf16[32,1792]{1,0:T(8,128)(2,1)S(1)}, bf16[32,1792]{1,0:T(8,128)(2,1)S(1)}, u32[]{:S(2)}, u32[]{:S(2)}) collective-permute-start(bf16[32,1792]{1,0:T(8,128)(2,1)S(1)} %get-tuple-element.43), channel_id=1, source_target_pairs={{0,8},{8,0},{16,24},{24,16},{1,9},{9,1},{17,25},{25,17},{2,10},{10... | collective-permute-start | bytes 344072 | tf_op jit(solution)/shard_map/ppermute | solution.py:47
  24.5 4.2 %collective-permute-start.17 = (f32[8,1792]{1,0:T(8,128)S(1)}, f32[8,1792]{1,0:T(8,128)S(1)}, u32[]{:S(2)}, u32[]{:S(2)}) collective-permute-start(f32[8,1792]{1,0:T(8,128)S(1)} %get-tuple-element.46), channel_id=1, source_target_pairs={{0,4},{4,0},{8,12},{12,8},{16,20},{20,16},{24,28},{28,24},{1,5},{5... | collective-permute-start | bytes 172040 | tf_op jit(solution)/shard_map/ppermute | solution.py:40
  26.0 4.2 %collective-permute-start.18 = (f32[8,1792]{1,0:T(8,128)S(1)}, f32[8,1792]{1,0:T(8,128)S(1)}, u32[]{:S(2)}, u32[]{:S(2)}) collective-permute-start(f32[8,1792]{1,0:T(8,128)S(1)} %get-tuple-element.47), channel_id=1, source_target_pairs={{0,1},{1,0},{2,3},{3,2},{8,9},{9,8},{10,11},{11,10},{16,17},{17,16... | collective-permute-start | bytes 172040 | tf_op jit(solution)/shard_map/ppermute | solution.py:40
  27.5 2.6 %collective-permute-start.19 = (f32[8,1792]{1,0:T(8,128)S(1)}, f32[8,1792]{1,0:T(8,128)S(1)}, u32[]{:S(2)}, u32[]{:S(2)}) collective-permute-start(f32[8,1792]{1,0:T(8,128)S(1)} %get-tuple-element.48), channel_id=1, source_target_pairs={{0,8},{1,2},{2,1},{3,11},{8,0},{9,10},{10,9},{11,3},{16,24},{17,18... | collective-permute-start | bytes 172040 | tf_op jit(solution)/shard_map/ppermute | solution.py:40
  30.8 1.5 %collective-permute-start.20 = (bf16[64,1792]{1,0:T(8,128)(2,1)S(1)}, bf16[64,1792]{1,0:T(8,128)(2,1)S(1)}, u32[]{:S(2)}, u32[]{:S(2)}) collective-permute-start(bf16[64,1792]{1,0:T(8,128)(2,1)S(1)} %hand_on.5.refs_1_), channel_id=1, source_target_pairs={{0,8},{8,0},{16,24},{24,16},{1,9},{9,1},{17,25},{25,17},{2,10},{10... | collective-permute-start | bytes 688136 | tf_op jit(solution)/shard_map/ppermute | solution.py:47

commit v12 on v11

--- a/solution.py
+++ b/solution.py
@@ -120,7 +120,7 @@
         write_faces(masked, lanes, first, second, x_refs, y_refs)
 
 
-def scatter(sizes, per_owner, b, places, cols_ref, sources, blocks_ref):
+def scatter(sizes, per_owner, b, places, cols_ref, sources, blocks_ref, turned=False):
     first, second, local_blocks, block = sizes
     mine = lax.axis_index("mode")
     picks, weights = [], []
@@ -131,13 +131,28 @@
             column = cols_ref[slot, b] - owner * local_blocks
             lanes = pl.ds(pl.multiple_of(column * block, block), block)
             picks.append(jnp.concatenate([part[:, lanes] for part in source], axis=0))
-            weights.append(blocks_ref[b, slot])
+            if not turned:
+                weights.append(blocks_ref[b, slot])
+    picks = jnp.concatenate(picks, axis=1)
+    if turned:
+        return jnp.dot(picks, blocks_ref[b], preferred_element_type=jnp.float32)
     return lax.dot_general(
-        jnp.concatenate(picks, axis=1),
+        picks,
         jnp.concatenate(weights, axis=1),
         (((1,), (1,)), ((), ())),
         preferred_element_type=jnp.float32,
     )
+
+
+def turn_blocks(per_owner, places, blocks_ref, turned_ref):
+    block = blocks_ref.shape[2]
+    mine = lax.axis_index("mode")
+    for b in range(blocks_ref.shape[0]):
+        at = 0
+        for place in places:
+            for p in range(per_owner):
+                turned_ref[b, at : at + block, :] = blocks_ref[b, (mine ^ place) * per_owner + p].T
+                at += block
 
 
 def add_product(sums, key, left, right):
@@ -239,7 +254,7 @@
     sums = {}
     for b in range(local_blocks):
         lanes = slice(b * block, (b + 1) * block)
-        scattered = scatter(sizes, per_owner, b, places, cols_ref, sources, blocks_ref)
+        scattered = scatter(sizes, per_owner, b, places, cols_ref, sources, blocks_ref, True)
         result = partial_ref[:, lanes] - scattered
         if outs.gram is None:
             outs.value[:, lanes] = result
@@ -454,6 +469,7 @@
     )
     columns = col_block.T
 
+    turned_shape = shape_of((local_blocks, len(final) * per_owner * block, block), blocks.dtype)
     work = 2 * cells * local_modes * per_owner * block
     vectors = [start]
     for section in range(KRYLOV):
@@ -471,6 +487,8 @@
                 sizes, per_owner, near, cols[0], sources, blocks_ref, current_ref, params,
                 open_ref, outs[0], scratch[0] if section == 0 else None,
             )
+            if section == 0:
+                turn_blocks(per_owner, final, blocks_ref, outs[1])
             if last:
                 early_products(sizes, known, outs[1])
 
@@ -484,11 +502,13 @@
                 in_vmem([relax_rate, drift_speed, upwind_sign]),
                 in_vmem(vectors if last else []),
             ],
-            [vector_shape] + [shape_of((16, block), f32)] * last,
+            [vector_shape] + [turned_shape] * (section == 0) + [shape_of((16, block), f32)] * last,
             [pltpu.VMEM((cells, local_modes), jnp.bfloat16)] * (section == 0),
             flops=work * len(near),
         )
 
+        if section == 0:
+            turned, *early = early
         held = dict(zip(held, hand_on(list(held.values()), [partial, *x_in, *y_in])))
         for place, array in held.items():
             sources[place] = array
@@ -536,7 +556,7 @@
             [
                 in_vmem([columns]),
                 in_vmem([sources[place] for place in final]),
-                in_vmem([blocks, partial, open_cells]),
+                in_vmem([turned, partial, open_cells]),
                 in_vmem(vectors if last else []),
                 in_vmem(early),
             ],

time: 46.3 us -> 46 us (level)
  transfers between devices with their start and end apart: 21 -> 21, of which waited for: 10 -> 10; matrix products, arithmetic and copies ran while one was open for 0% -> 0% of each run, Pallas kernels for 10% -> 11%
where the time goes in v12:
time: 46 us; the launch traced here: 45.8 us
  starting transfers between devices  15.7 us (34%)
  blocking collectives  12.1 us (26%)
  waiting for transfers between devices  8.8 us (19%)
  Pallas kernels  7.42 us (16%)
  local copies, waits for them, and re-layouts  1.06 us (2%)
  between operations  0.84 us (2%)
    all_to_all x1, blocking collectives, per_device(): gram = lax.all_to_all(gram, AXES, 0, 0)  12.1 us
    ppermute x9, starting transfers between devices, move_faces(): arrived.append(lax.ppermute(face, ('mode', axis), pairs))  9.28 us
    pallas_call x12, Pallas kernels, call(): pl.pallas_call(body, out_shape=list(shapes), in_specs=[spec for spec, ope...  7.41 us
    ppermute x12, starting transfers between devices, exchange(): return lax.ppermute(array, 'mode', [(i, i ^ bit) for i in range(count)])  6.38 us
    ppermute x9, waiting for transfers between devices, move_faces(): arrived.append(lax.ppermute(face, ('mode', axis), pairs))  4.63 us
    ppermute x12, waiting for transfers between devices, exchange(): return lax.ppermute(array, 'mode', [(i, i ^ bit) for i in range(count)])  4.17 us
    unnamed x16, local copies, waits for them, and re-layouts  1.06 us
  transfers between devices with their start and end apart: 21, of which 10 were waited for; matrix products, arithmetic and copies ran while one was open for 0% of the time, Pallas kernels for 11%

profile of v12, /device:TPU:0, one launch (start us, length us, event | category | flops | bytes accessed | tf_op | source)
XLA Modules:
  0.0 45.8 jit_solution(2977912732779890883)
XLA Ops:
  0.6 0.0 copy-start.1
  0.6 1.0 %copy-done.1 = f32[8,8,1792]{2,1,0:T(8,128)S(1)} copy-done((f32[8,8,1792]{2,1,0:T(8,128)S(1)}, f32[8,8,1792]{2,1,0:T(8,128)}, u32[]{:S(2)}) %copy-start.1) | copy-done | bytes 458776
  1.7 0.0 copy-start
  1.7 0.0 copy-start.3
  1.7 0.0 copy-start.4
  1.7 0.0 copy-start.5
  1.7 0.0 copy-start.6
  1.7 3.0 %collective-permute-start = (bf16[64,1792]{1,0:T(8,128)(2,1)S(1)}, bf16[64,1792]{1,0:T(8,128)(2,1)S(1)}, u32[]{:S(2)}, u32[]{:S(2)}) collective-permute-start(bf16[64,1792]{1,0:T(8,128)(2,1)S(1)} %get-tuple-element.29.refs_1_), channel_id=1, source_target_pairs={{0,16},{8,24},{16,0},{24,8},{1,17},{9,25},{17,1},{25,9},{2,18},{10... | collective-permute-start | bytes 688136 | tf_op jit(solution)/shard_map/ppermute | solution.py:47
  4.8 0.0 collective-permute-start.1
  4.8 0.5 %collective-permute-start.2 = (bf16[32,1792]{1,0:T(8,128)(2,1)S(1)}, bf16[32,1792]{1,0:T(8,128)(2,1)S(1)}, u32[]{:S(2)}, u32[]{:S(2)}) collective-permute-start(bf16[32,1792]{1,0:T(8,128)(2,1)S(1)} %get-tuple-element.31), channel_id=1, source_target_pairs={{0,8},{8,0},{16,24},{24,16},{1,9},{9,1},{17,25},{25,17},{2,10},{10... | collective-permute-start | bytes 344072 | tf_op jit(solution)/shard_map/ppermute | solution.py:47
  5.3 0.2 prepare.1
  5.5 1.6 %collective-permute-start.3 = (f32[8,1792]{1,0:T(8,128)S(1)}, f32[8,1792]{1,0:T(8,128)S(1)}, u32[]{:S(2)}, u32[]{:S(2)}) collective-permute-start(f32[8,1792]{1,0:T(8,128)S(1)} %get-tuple-element.34), channel_id=1, source_target_pairs={{0,4},{4,0},{8,12},{12,8},{16,20},{20,16},{24,28},{28,24},{1,5},{5... | collective-permute-start | bytes 172040 | tf_op jit(solution)/shard_map/ppermute | solution.py:40
  7.1 1.6 %collective-permute-start.4 = (f32[8,1792]{1,0:T(8,128)S(1)}, f32[8,1792]{1,0:T(8,128)S(1)}, u32[]{:S(2)}, u32[]{:S(2)}) collective-permute-start(f32[8,1792]{1,0:T(8,128)S(1)} %get-tuple-element.35), channel_id=1, source_target_pairs={{0,1},{1,0},{2,3},{3,2},{8,9},{9,8},{10,11},{11,10},{16,17},{17,16... | collective-permute-start | bytes 172040 | tf_op jit(solution)/shard_map/ppermute | solution.py:40
  8.7 0.0 collective-permute-done.2.refs_3_
  8.7 1.2 %near_0.1 = (f32[64,1792]{1,0:T(8,128)S(1)}, bf16[14,256,128]{2,1,0:T(8,128)(2,1)S(1)}) custom-call(s32[8,14]{1,0:T(8,128)S(1)} %bitcast.9, bf16[64,1792]{1,0:T(8,128)(2,1)S(1)} %get-tuple-element.29.refs_1_, bf16[32,1792]{1,0:T(8,128)(2,1)S(1)} %collective-permute-done.1.refs_2_, bf16[32,1792]{1,0:T(8,128)(2,1)S(1)} %collective-permute-done.2.refs_3_, ...), custom_call_target="tpu_custom_call" | custom-call | flops 117440512 | bytes 6032832 | tf_op jit(solution)/shard_map/near_0/pallas_call | solution.py:413
  9.9 0.0 collective-permute-done.3.refs_2_.refs_6_
  9.9 1.3 %collective-permute-done.4.refs_3_.refs_7_ = f32[8,1792]{1,0:T(8,128)S(1)} collective-permute-done((f32[8,1792]{1,0:T(8,128)S(1)}, f32[8,1792]{1,0:T(8,128)S(1)}, u32[]{:S(2)}, u32[]{:S(2)}) %collective-permute-start.4) | collective-permute-done | bytes 57376 | tf_op jit(solution)/shard_map/ppermute | solution.py:40
  11.3 0.1 collective-permute-start.6
  11.3 0.5 %middle_0.1.refs_3_ = f32[64,1792]{1,0:T(8,128)S(1)} custom-call(s32[8,14]{1,0:T(8,128)S(1)} %bitcast.10, bf16[64,1792]{1,0:T(8,128)(2,1)S(1)} %hand_on.3.refs_1_, bf16[14,8,128,128]{3,2,1,0:T(8,128)(2,1)S(1)} %copy-done, f32[64,1792]{1,0:T(8,128)S(1)} %get-tuple-element.33.refs_1_.refs_3_, f32[2,1792]{1,0:T(2,128)S(1)} %copy-done.3, ...), custom_call_target="tpu_custom_call" | custom-call | flops 58720256 | bytes 5018048 | tf_op jit(solution)/shard_map/middle_0/pallas_call | solution.py:413
  11.9 0.9 %collective-permute-done.6.refs_1_ = bf16[64,1792]{1,0:T(8,128)(2,1)S(1)} collective-permute-done((bf16[64,1792]{1,0:T(8,128)(2,1)S(1)}, bf16[64,1792]{1,0:T(8,128)(2,1)S(1)}, u32[]{:S(2)}, u32[]{:S(2)}) %collective-permute-start.6) | collective-permute-done | bytes 229408 | tf_op jit(solution)/shard_map/ppermute | solution.py:47
  12.8 0.4 last_0.1
  13.2 0.9 %collective-permute-start.7 = (bf16[64,1792]{1,0:T(8,128)(2,1)S(1)}, bf16[64,1792]{1,0:T(8,128)(2,1)S(1)}, u32[]{:S(2)}, u32[]{:S(2)}) collective-permute-start(bf16[64,1792]{1,0:T(8,128)(2,1)S(1)} %get-tuple-element.38.refs_1_), channel_id=1, source_target_pairs={{0,16},{8,24},{16,0},{24,8},{1,17},{9,25},{17,1},{25,9},{2,18},{10... | collective-permute-start | bytes 688136 | tf_op jit(solution)/shard_map/ppermute | solution.py:47
  14.1 0.0 collective-permute-start.8
  14.1 0.5 %collective-permute-start.9 = (bf16[32,1792]{1,0:T(8,128)(2,1)S(1)}, bf16[32,1792]{1,0:T(8,128)(2,1)S(1)}, u32[]{:S(2)}, u32[]{:S(2)}) collective-permute-start(bf16[32,1792]{1,0:T(8,128)(2,1)S(1)} %get-tuple-element.40), channel_id=1, source_target_pairs={{0,8},{8,0},{16,24},{24,16},{1,9},{9,1},{17,25},{25,17},{2,10},{10... | collective-permute-start | bytes 344072 | tf_op jit(solution)/shard_map/ppermute | solution.py:47
  14.6 1.5 %collective-permute-start.10 = (f32[8,1792]{1,0:T(8,128)S(1)}, f32[8,1792]{1,0:T(8,128)S(1)}, u32[]{:S(2)}, u32[]{:S(2)}) collective-permute-start(f32[8,1792]{1,0:T(8,128)S(1)} %get-tuple-element.42), channel_id=1, source_target_pairs={{0,4},{4,0},{8,12},{12,8},{16,20},{20,16},{24,28},{28,24},{1,5},{5... | collective-permute-start | bytes 172040 | tf_op jit(solution)/shard_map/ppermute | solution.py:40
  16.1 1.6 %collective-permute-start.11 = (f32[8,1792]{1,0:T(8,128)S(1)}, f32[8,1792]{1,0:T(8,128)S(1)}, u32[]{:S(2)}, u32[]{:S(2)}) collective-permute-start(f32[8,1792]{1,0:T(8,128)S(1)} %get-tuple-element.43), channel_id=1, source_target_pairs={{0,1},{1,0},{2,3},{3,2},{8,9},{9,8},{10,11},{11,10},{16,17},{17,16... | collective-permute-start | bytes 172040 | tf_op jit(solution)/shard_map/ppermute | solution.py:40
  17.7 0.0 collective-permute-done.8.refs_2_
  17.7 0.8 %near_1.1.refs_1_.refs_3_ = f32[64,1792]{1,0:T(8,128)S(1)} custom-call(s32[8,14]{1,0:T(8,128)S(1)} %bitcast.12, bf16[64,1792]{1,0:T(8,128)(2,1)S(1)} %get-tuple-element.38.refs_1_, bf16[32,1792]{1,0:T(8,128)(2,1)S(1)} %collective-permute-done.8.refs_2_, bf16[32,1792]{1,0:T(8,128)(2,1)S(1)} %collective-permute-done.9.refs_3_, ...), custom_call_target="tpu_custom_call" | custom-call | flops 117440512 | bytes 5115328 | tf_op jit(solution)/shard_map/near_1/pallas_call | solution.py:413
  18.6 0.0 copy-start.2
  18.6 0.2 collective-permute-done.10.refs_2_.refs_6_
  18.8 1.5 %collective-permute-done.11.refs_3_.refs_7_ = f32[8,1792]{1,0:T(8,128)S(1)} collective-permute-done((f32[8,1792]{1,0:T(8,128)S(1)}, f32[8,1792]{1,0:T(8,128)S(1)}, u32[]{:S(2)}, u32[]{:S(2)}) %collective-permute-start.11) | collective-permute-done | bytes 57376 | tf_op jit(solution)/shard_map/ppermute | solution.py:40
  20.3 0.7 %collective-permute-done.7.refs_0_ = bf16[64,1792]{1,0:T(8,128)(2,1)S(1)} collective-permute-done((bf16[64,1792]{1,0:T(8,128)(2,1)S(1)}, bf16[64,1792]{1,0:T(8,128)(2,1)S(1)}, u32[]{:S(2)}, u32[]{:S(2)}) %collective-permute-start.7) | collective-permute-done | bytes 229408 | tf_op jit(solution)/shard_map/ppermute | solution.py:47
  21.0 0.5 %middle_1.1.refs_3_ = f32[64,1792]{1,0:T(8,128)S(1)} custom-call(s32[8,14]{1,0:T(8,128)S(1)} %bitcast.13, bf16[64,1792]{1,0:T(8,128)(2,1)S(1)} %hand_on.4.refs_1_, bf16[14,8,128,128]{3,2,1,0:T(8,128)(2,1)S(1)} %copy-done, f32[64,1792]{1,0:T(8,128)S(1)} %near_1.1.refs_1_.refs_3_, f32[2,1792]{1,0:T(2,128)S(1)} %copy-done.3, s32[2,1792]{1,0:T(2,128)S(1)} %copy-done.4, ...), custom_call_target="tpu_custom_call" | custom-call | flops 58720256 | bytes 5018048 | tf_op jit(solution)/shard_map/middle_1/pallas_call | solution.py:413
  21.5 1.0 %collective-permute-done.13.refs_1_ = bf16[64,1792]{1,0:T(8,128)(2,1)S(1)} collective-permute-done((bf16[64,1792]{1,0:T(8,128)(2,1)S(1)}, bf16[64,1792]{1,0:T(8,128)(2,1)S(1)}, u32[]{:S(2)}, u32[]{:S(2)}) %collective-permute-start.13) | collective-permute-done | bytes 229408 | tf_op jit(solution)/shard_map/ppermute | solution.py:47
  22.5 0.4 last_1.1
  22.9 0.9 %collective-permute-start.14 = (bf16[64,1792]{1,0:T(8,128)(2,1)S(1)}, bf16[64,1792]{1,0:T(8,128)(2,1)S(1)}, u32[]{:S(2)}, u32[]{:S(2)}) collective-permute-start(bf16[64,1792]{1,0:T(8,128)(2,1)S(1)} %get-tuple-element.45.refs_1_), channel_id=1, source_target_pairs={{0,16},{8,24},{16,0},{24,8},{1,17},{9,25},{17,1},{25,9},{2,18},{10... | collective-permute-start | bytes 688136 | tf_op jit(solution)/shard_map/ppermute | solution.py:47
  23.8 0.5 %collective-permute-start.16 = (bf16[32,1792]{1,0:T(8,128)(2,1)S(1)}, bf16[32,1792]{1,0:T(8,128)(2,1)S(1)}, u32[]{:S(2)}, u32[]{:S(2)}) collective-permute-start(bf16[32,1792]{1,0:T(8,128)(2,1)S(1)} %get-tuple-element.47), channel_id=1, source_target_pairs={{0,8},{8,0},{16,24},{24,16},{1,9},{9,1},{17,25},{25,17},{2,10},{10... | collective-permute-start | bytes 344072 | tf_op jit(solution)/shard_map/ppermute | solution.py:47
  24.3 1.5 %collective-permute-start.17 = (f32[8,1792]{1,0:T(8,128)S(1)}, f32[8,1792]{1,0:T(8,128)S(1)}, u32[]{:S(2)}, u32[]{:S(2)}) collective-permute-start(f32[8,1792]{1,0:T(8,128)S(1)} %get-tuple-element.50), channel_id=1, source_target_pairs={{0,4},{4,0},{8,12},{12,8},{16,20},{20,16},{24,28},{28,24},{1,5},{5... | collective-permute-start | bytes 172040 | tf_op jit(solution)/shard_map/ppermute | solution.py:40
  25.8 1.6 %collective-permute-start.18 = (f32[8,1792]{1,0:T(8,128)S(1)}, f32[8,1792]{1,0:T(8,128)S(1)}, u32[]{:S(2)}, u32[]{:S(2)}) collective-permute-start(f32[8,1792]{1,0:T(8,128)S(1)} %get-tuple-element.51), channel_id=1, source_target_pairs={{0,1},{1,0},{2,3},{3,2},{8,9},{9,8},{10,11},{11,10},{16,17},{17,16... | collective-permute-start | bytes 172040 | tf_op jit(solution)/shard_map/ppermute | solution.py:40
  27.4 1.0 %near_2.1 = (f32[64,1792]{1,0:T(8,128)S(1)}, f32[16,128]{1,0:T(8,128)S(1)}) custom-call(s32[8,14]{1,0:T(8,128)S(1)} %bitcast.15, bf16[64,1792]{1,0:T(8,128)(2,1)S(1)} %get-tuple-element.45.refs_1_, bf16[32,1792]{1,0:T(8,128)(2,1)S(1)} %collective-permute-done.15.refs_2_, bf16[32,1792]{1,0:T(8,128)(2,1)S(1)} %collective-permute-done.16.refs_3_, ...), custom_call_target="tpu_custom_call" | custom-call | flops 117440512 | bytes 6499776 | tf_op jit(solution)/shard_map/near_2/pallas_call | solution.py:413
  28.4 0.1 collective-permute-done.17.refs_2_.refs_6_
  28.5 1.5 %collective-permute-done.18.refs_3_.refs_7_ = f32[8,1792]{1,0:T(8,128)S(1)} collective-permute-done((f32[8,1792]{1,0:T(8,128)S(1)}, f32[8,1792]{1,0:T(8,128)S(1)}, u32[]{:S(2)}, u32[]{:S(2)}) %collective-permute-start.18) | collective-permute-done | bytes 57376 | tf_op jit(solution)/shard_map/ppermute | solution.py:40
  30.0 0.7 %collective-permute-done.14.refs_0_ = bf16[64,1792]{1,0:T(8,128)(2,1)S(1)} collective-permute-done((bf16[64,1792]{1,0:T(8,128)(2,1)S(1)}, bf16[64,1792]{1,0:T(8,128)(2,1)S(1)}, u32[]{:S(2)}, u32[]{:S(2)}) %collective-permute-start.14) | collective-permute-done | bytes 229408 | tf_op jit(solution)/shard_map/ppermute | solution.py:47
  30.6 0.5 %middle_2.1.refs_3_ = f32[64,1792]{1,0:T(8,128)S(1)} custom-call(s32[8,14]{1,0:T(8,128)S(1)} %bitcast.16, bf16[64,1792]{1,0:T(8,128)(2,1)S(1)} %hand_on.5.refs_1_, bf16[14,8,128,128]{3,2,1,0:T(8,128)(2,1)S(1)} %copy-done, f32[64,1792]{1,0:T(8,128)S(1)} %get-tuple-element.49.refs_1_.refs_3_, f32[2,1792]{1,0:T(2,128)S(1)} %copy-done.3, ...), custom_call_target="tpu_custom_call" | custom-call | flops 58720256 | bytes 5018048 | tf_op jit(solution)/shard_map/middle_2/pallas_call | solution.py:413
  31.1 1.0 %collective-permute-done.20.refs_1_ = bf16[64,1792]{1,0:T(8,128)(2,1)S(1)} collective-permute-done((bf16[64,1792]{1,0:T(8,128)(2,1)S(1)}, bf16[64,1792]{1,0:T(8,128)(2,1)S(1)}, u32[]{:S(2)}, u32[]{:S(2)}) %collective-permute-start.20) | collective-permute-done | bytes 229408 | tf_op jit(solution)/shard_map/ppermute | solution.py:47
  32.1 0.5 %last_2.1 = f32[32,1,128]{2,1,0:T(1,128)S(1)} custom-call(s32[8,14]{1,0:T(8,128)S(1)} %bitcast.17, bf16[64,1792]{1,0:T(8,128)(2,1)S(1)} %collective-permute-done.20.refs_1_, bf16[14,256,128]{2,1,0:T(8,128)(2,1)S(1)} %get-tuple-element.37.refs_2_, f32[64,1792]{1,0:T(8,128)S(1)} %middle_2.1.refs_3_, f32[64,128]{1,0:T(8,128)S(1)} %get-tuple-element.32.refs_6_.refs_4_, ...), custom_call_target="tpu_custom_call" | custom-call | flops 58720256 | bytes 3039680 | tf_op jit(solution)/shard_map/last_2/pallas_call | solution.py:413
  32.6 12.1 %all_to_all.5.refs_0_ = f32[32,1,128]{2,1,0:T(1,128)S(1)} all-to-all(f32[32,1,128]{2,1,0:T(1,128)S(1)} %last_2.1), channel_id=1, replica_groups=mesh['mode'=4,'gx'=2,'gy'=4] {'mode','gx','gy'}, dimensions={0} | all-to-all | bytes 32768 | tf_op jit(solution)/shard_map/all_to_all | solution.py:572
  44.7 1.1 %finish.1 = (f32[64,1792]{1,0:T(8,128)}, f32[4,3]{1,0:T(4,128)}) custom-call(f32[32,1,128]{2,1,0:T(1,128)S(1)} %all_to_all.5.refs_0_, f32[64,1792]{1,0:T(8,128)S(1)} %bitcast.8, f32[64,1792]{1,0:T(8,128)S(1)} %get-tuple-element.41.refs_5_.refs_11_.refs_6_.refs_2_, f32[64,1792]{1,0:T(8,128)S(1)} %get-tuple-element.48.refs_5_.refs_12_.refs_7_.refs_3_), custom_call_target="tpu_custom_call" | custom-call | bytes 1851440 | tf_op jit(solution)/shard_map/finish/pallas_call | solution.py:413
  (26 shorter events, 0.1 us)
Async XLA Ops:
  0.6 1.0 %copy-start.1 = (f32[8,8,1792]{2,1,0:T(8,128)S(1)}, f32[8,8,1792]{2,1,0:T(8,128)}, u32[]{:S(2)}) copy-start(f32[8,8,1792]{2,1,0:T(8,128)} %param.7) | copy-start | bytes 1376260
  1.7 3.6 %copy-start.7 = (s32[8,8]{1,0:T(8,128)S(1)}, s32[8,8]{1,0:T(8,128)}, u32[]{:S(2)}) copy-start(s32[8,8]{1,0:T(8,128)} %refs_1_.1) | copy-start | bytes 772
  1.7 7.0 %copy-start = (bf16[14,8,128,128]{3,2,1,0:T(8,128)(2,1)S(1)}, bf16[14,8,128,128]{3,2,1,0:T(8,128)(2,1)}, u32[]{:S(2)}) copy-start(bf16[14,8,128,128]{3,2,1,0:T(8,128)(2,1)} %refs_2_.5) | copy-start | bytes 11010052
  1.7 7.0 %copy-start.3 = (f32[2,1792]{1,0:T(2,128)S(1)}, f32[2,1792]{1,0:T(2,128)}, u32[]{:S(2)}) copy-start(f32[2,1792]{1,0:T(2,128)} %refs_4_.11) | copy-start | bytes 43012
  1.7 7.0 %copy-start.4 = (s32[2,1792]{1,0:T(2,128)S(1)}, s32[2,1792]{1,0:T(2,128)}, u32[]{:S(2)}) copy-start(s32[2,1792]{1,0:T(2,128)} %refs_5_.5) | copy-start | bytes 43012
  1.7 7.0 %copy-start.5 = (s32[14,8]{0,1:T(8,128)S(1)}, s32[14,8]{0,1:T(8,128)}, u32[]{:S(2)}) copy-start(s32[14,8]{0,1:T(8,128)} %param.8) | copy-start | bytes 1348
  1.7 7.0 %copy-start.6 = (f32[1792]{0:T(1024)S(1)}, f32[1792]{0:T(1024)}, u32[]{:S(2)}) copy-start(f32[1792]{0:T(1024)} %refs_7_.5) | copy-start | bytes 21508
  1.7 9.5 %collective-permute-start = (bf16[64,1792]{1,0:T(8,128)(2,1)S(1)}, bf16[64,1792]{1,0:T(8,128)(2,1)S(1)}, u32[]{:S(2)}, u32[]{:S(2)}) collective-permute-start(bf16[64,1792]{1,0:T(8,128)(2,1)S(1)} %get-tuple-element.29.refs_1_), channel_id=1, source_target_pairs={{0,16},{8,24},{16,0},{24,8},{1,17},{9,25},{17,1},{25,9},{2,18},{10... | collective-permute-start | bytes 688136 | tf_op jit(solution)/shard_map/ppermute | solution.py:47
  4.8 3.9 %collective-permute-start.1 = (bf16[32,1792]{1,0:T(8,128)(2,1)S(1)}, bf16[32,1792]{1,0:T(8,128)(2,1)S(1)}, u32[]{:S(2)}, u32[]{:S(2)}) collective-permute-start(bf16[32,1792]{1,0:T(8,128)(2,1)S(1)} %get-tuple-element.30), channel_id=1, source_target_pairs={{0,8},{8,0},{16,24},{24,16},{1,9},{9,1},{17,25},{25,17},{2,10},{10... | collective-permute-start | bytes 344072 | tf_op jit(solution)/shard_map/ppermute | solution.py:47
  4.8 3.9 %collective-permute-start.2 = (bf16[32,1792]{1,0:T(8,128)(2,1)S(1)}, bf16[32,1792]{1,0:T(8,128)(2,1)S(1)}, u32[]{:S(2)}, u32[]{:S(2)}) collective-permute-start(bf16[32,1792]{1,0:T(8,128)(2,1)S(1)} %get-tuple-element.31), channel_id=1, source_target_pairs={{0,8},{8,0},{16,24},{24,16},{1,9},{9,1},{17,25},{25,17},{2,10},{10... | collective-permute-start | bytes 344072 | tf_op jit(solution)/shard_map/ppermute | solution.py:47
  5.5 4.4 %collective-permute-start.3 = (f32[8,1792]{1,0:T(8,128)S(1)}, f32[8,1792]{1,0:T(8,128)S(1)}, u32[]{:S(2)}, u32[]{:S(2)}) collective-permute-start(f32[8,1792]{1,0:T(8,128)S(1)} %get-tuple-element.34), channel_id=1, source_target_pairs={{0,4},{4,0},{8,12},{12,8},{16,20},{20,16},{24,28},{28,24},{1,5},{5... | collective-permute-start | bytes 172040 | tf_op jit(solution)/shard_map/ppermute | solution.py:40
  7.1 4.2 %collective-permute-start.4 = (f32[8,1792]{1,0:T(8,128)S(1)}, f32[8,1792]{1,0:T(8,128)S(1)}, u32[]{:S(2)}, u32[]{:S(2)}) collective-permute-start(f32[8,1792]{1,0:T(8,128)S(1)} %get-tuple-element.35), channel_id=1, source_target_pairs={{0,1},{1,0},{2,3},{3,2},{8,9},{9,8},{10,11},{11,10},{16,17},{17,16... | collective-permute-start | bytes 172040 | tf_op jit(solution)/shard_map/ppermute | solution.py:40
  8.6 2.6 %collective-permute-start.5 = (f32[8,1792]{1,0:T(8,128)S(1)}, f32[8,1792]{1,0:T(8,128)S(1)}, u32[]{:S(2)}, u32[]{:S(2)}) collective-permute-start(f32[8,1792]{1,0:T(8,128)S(1)} %get-tuple-element.36), channel_id=1, source_target_pairs={{0,8},{1,2},{2,1},{3,11},{8,0},{9,10},{10,9},{11,3},{16,24},{17,18... | collective-permute-start | bytes 172040 | tf_op jit(solution)/shard_map/ppermute | solution.py:40
  11.3 1.5 %collective-permute-start.6 = (bf16[64,1792]{1,0:T(8,128)(2,1)S(1)}, bf16[64,1792]{1,0:T(8,128)(2,1)S(1)}, u32[]{:S(2)}, u32[]{:S(2)}) collective-permute-start(bf16[64,1792]{1,0:T(8,128)(2,1)S(1)} %hand_on.3.refs_1_), channel_id=1, source_target_pairs={{0,8},{8,0},{16,24},{24,16},{1,9},{9,1},{17,25},{25,17},{2,10},{10... | collective-permute-start | bytes 688136 | tf_op jit(solution)/shard_map/ppermute | solution.py:47
  13.2 7.7 %collective-permute-start.7 = (bf16[64,1792]{1,0:T(8,128)(2,1)S(1)}, bf16[64,1792]{1,0:T(8,128)(2,1)S(1)}, u32[]{:S(2)}, u32[]{:S(2)}) collective-permute-start(bf16[64,1792]{1,0:T(8,128)(2,1)S(1)} %get-tuple-element.38.refs_1_), channel_id=1, source_target_pairs={{0,16},{8,24},{16,0},{24,8},{1,17},{9,25},{17,1},{25,9},{2,18},{10... | collective-permute-start | bytes 688136 | tf_op jit(solution)/shard_map/ppermute | solution.py:47
  14.1 3.6 %collective-permute-start.8 = (bf16[32,1792]{1,0:T(8,128)(2,1)S(1)}, bf16[32,1792]{1,0:T(8,128)(2,1)S(1)}, u32[]{:S(2)}, u32[]{:S(2)}) collective-permute-start(bf16[32,1792]{1,0:T(8,128)(2,1)S(1)} %get-tuple-element.39), channel_id=1, source_target_pairs={{0,8},{8,0},{16,24},{24,16},{1,9},{9,1},{17,25},{25,17},{2,10},{10... | collective-permute-start | bytes 344072 | tf_op jit(solution)/shard_map/ppermute | solution.py:47
  14.1 3.6 %collective-permute-start.9 = (bf16[32,1792]{1,0:T(8,128)(2,1)S(1)}, bf16[32,1792]{1,0:T(8,128)(2,1)S(1)}, u32[]{:S(2)}, u32[]{:S(2)}) collective-permute-start(bf16[32,1792]{1,0:T(8,128)(2,1)S(1)} %get-tuple-element.40), channel_id=1, source_target_pairs={{0,8},{8,0},{16,24},{24,16},{1,9},{9,1},{17,25},{25,17},{2,10},{10... | collective-permute-start | bytes 344072 | tf_op jit(solution)/shard_map/ppermute | solution.py:47
  14.6 4.2 %collective-permute-start.10 = (f32[8,1792]{1,0:T(8,128)S(1)}, f32[8,1792]{1,0:T(8,128)S(1)}, u32[]{:S(2)}, u32[]{:S(2)}) collective-permute-start(f32[8,1792]{1,0:T(8,128)S(1)} %get-tuple-element.42), channel_id=1, source_target_pairs={{0,4},{4,0},{8,12},{12,8},{16,20},{20,16},{24,28},{28,24},{1,5},{5... | collective-permute-start | bytes 172040 | tf_op jit(solution)/shard_map/ppermute | solution.py:40
  16.1 4.2 %collective-permute-start.11 = (f32[8,1792]{1,0:T(8,128)S(1)}, f32[8,1792]{1,0:T(8,128)S(1)}, u32[]{:S(2)}, u32[]{:S(2)}) collective-permute-start(f32[8,1792]{1,0:T(8,128)S(1)} %get-tuple-element.43), channel_id=1, source_target_pairs={{0,1},{1,0},{2,3},{3,2},{8,9},{9,8},{10,11},{11,10},{16,17},{17,16... | collective-permute-start | bytes 172040 | tf_op jit(solution)/shard_map/ppermute | solution.py:40
  17.7 2.6 %collective-permute-start.12 = (f32[8,1792]{1,0:T(8,128)S(1)}, f32[8,1792]{1,0:T(8,128)S(1)}, u32[]{:S(2)}, u32[]{:S(2)}) collective-permute-start(f32[8,1792]{1,0:T(8,128)S(1)} %get-tuple-element.44), channel_id=1, source_target_pairs={{0,8},{1,2},{2,1},{3,11},{8,0},{9,10},{10,9},{11,3},{16,24},{17,18... | collective-permute-start | bytes 172040 | tf_op jit(solution)/shard_map/ppermute | solution.py:40
  18.6 8.8 %copy-start.2 = (f32[8,8,1792]{2,1,0:T(8,128)S(1)}, f32[8,8,1792]{2,1,0:T(8,128)}, u32[]{:S(2)}) copy-start(f32[8,8,1792]{2,1,0:T(8,128)} %param.7) | copy-start | bytes 1376260
  21.0 1.5 %collective-permute-start.13 = (bf16[64,1792]{1,0:T(8,128)(2,1)S(1)}, bf16[64,1792]{1,0:T(8,128)(2,1)S(1)}, u32[]{:S(2)}, u32[]{:S(2)}) collective-permute-start(bf16[64,1792]{1,0:T(8,128)(2,1)S(1)} %hand_on.4.refs_1_), channel_id=1, source_target_pairs={{0,8},{8,0},{16,24},{24,16},{1,9},{9,1},{17,25},{25,17},{2,10},{10... | collective-permute-start | bytes 688136 | tf_op jit(solution)/shard_map/ppermute | solution.py:47
  22.9 7.7 %collective-permute-start.14 = (bf16[64,1792]{1,0:T(8,128)(2,1)S(1)}, bf16[64,1792]{1,0:T(8,128)(2,1)S(1)}, u32[]{:S(2)}, u32[]{:S(2)}) collective-permute-start(bf16[64,1792]{1,0:T(8,128)(2,1)S(1)} %get-tuple-element.45.refs_1_), channel_id=1, source_target_pairs={{0,16},{8,24},{16,0},{24,8},{1,17},{9,25},{17,1},{25,9},{2,18},{10... | collective-permute-start | bytes 688136 | tf_op jit(solution)/shard_map/ppermute | solution.py:47
  23.8 3.6 %collective-permute-start.15 = (bf16[32,1792]{1,0:T(8,128)(2,1)S(1)}, bf16[32,1792]{1,0:T(8,128)(2,1)S(1)}, u32[]{:S(2)}, u32[]{:S(2)}) collective-permute-start(bf16[32,1792]{1,0:T(8,128)(2,1)S(1)} %get-tuple-element.46), channel_id=1, source_target_pairs={{0,8},{8,0},{16,24},{24,16},{1,9},{9,1},{17,25},{25,17},{2,10},{10... | collective-permute-start | bytes 344072 | tf_op jit(solution)/shard_map/ppermute | solution.py:47
  23.8 3.6 %collective-permute-start.16 = (bf16[32,1792]{1,0:T(8,128)(2,1)S(1)}, bf16[32,1792]{1,0:T(8,128)(2,1)S(1)}, u32[]{:S(2)}, u32[]{:S(2)}) collective-permute-start(bf16[32,1792]{1,0:T(8,128)(2,1)S(1)} %get-tuple-element.47), channel_id=1, source_target_pairs={{0,8},{8,0},{16,24},{24,16},{1,9},{9,1},{17,25},{25,17},{2,10},{10... | collective-permute-start | bytes 344072 | tf_op jit(solution)/shard_map/ppermute | solution.py:47
  24.3 4.2 %collective-permute-start.17 = (f32[8,1792]{1,0:T(8,128)S(1)}, f32[8,1792]{1,0:T(8,128)S(1)}, u32[]{:S(2)}, u32[]{:S(2)}) collective-permute-start(f32[8,1792]{1,0:T(8,128)S(1)} %get-tuple-element.50), channel_id=1, source_target_pairs={{0,4},{4,0},{8,12},{12,8},{16,20},{20,16},{24,28},{28,24},{1,5},{5... | collective-permute-start | bytes 172040 | tf_op jit(solution)/shard_map/ppermute | solution.py:40
  25.8 4.2 %collective-permute-start.18 = (f32[8,1792]{1,0:T(8,128)S(1)}, f32[8,1792]{1,0:T(8,128)S(1)}, u32[]{:S(2)}, u32[]{:S(2)}) collective-permute-start(f32[8,1792]{1,0:T(8,128)S(1)} %get-tuple-element.51), channel_id=1, source_target_pairs={{0,1},{1,0},{2,3},{3,2},{8,9},{9,8},{10,11},{11,10},{16,17},{17,16... | collective-permute-start | bytes 172040 | tf_op jit(solution)/shard_map/ppermute | solution.py:40
  27.4 2.6 %collective-permute-start.19 = (f32[8,1792]{1,0:T(8,128)S(1)}, f32[8,1792]{1,0:T(8,128)S(1)}, u32[]{:S(2)}, u32[]{:S(2)}) collective-permute-start(f32[8,1792]{1,0:T(8,128)S(1)} %get-tuple-element.52), channel_id=1, source_target_pairs={{0,8},{1,2},{2,1},{3,11},{8,0},{9,10},{10,9},{11,3},{16,24},{17,18... | collective-permute-start | bytes 172040 | tf_op jit(solution)/shard_map/ppermute | solution.py:40
  30.6 1.5 %collective-permute-start.20 = (bf16[64,1792]{1,0:T(8,128)(2,1)S(1)}, bf16[64,1792]{1,0:T(8,128)(2,1)S(1)}, u32[]{:S(2)}, u32[]{:S(2)}) collective-permute-start(bf16[64,1792]{1,0:T(8,128)(2,1)S(1)} %hand_on.5.refs_1_), channel_id=1, source_target_pairs={{0,8},{8,0},{16,24},{24,16},{1,9},{9,1},{17,25},{25,17},{2,10},{10... | collective-permute-start | bytes 688136 | tf_op jit(solution)/shard_map/ppermute | solution.py:47

commit v13 on v12

--- a/solution.py
+++ b/solution.py
@@ -328,7 +328,7 @@
             for j in range(size):
                 if left[i] is None or right[j] is None:
                     continue
-                term = left[i] * right[j] * gram[min(i, j)][max(i, j)]
+                term = left[i] * gram[min(i, j)][max(i, j)] * right[j]
                 total = term if total is None else total + term
         return total
 

time: 46 us -> 46 us (level)
  no operation moved by 1% of the time
where the time goes in v13:
time: 46 us; the launch traced here: 45.8 us
  starting transfers between devices  15.7 us (34%)
  blocking collectives  12.1 us (26%)
  waiting for transfers between devices  8.77 us (19%)
  Pallas kernels  7.43 us (16%)
  local copies, waits for them, and re-layouts  1.06 us (2%)
  between operations  0.84 us (2%)
    all_to_all x1, blocking collectives, per_device(): gram = lax.all_to_all(gram, AXES, 0, 0)  12.1 us
    ppermute x9, starting transfers between devices, move_faces(): arrived.append(lax.ppermute(face, ('mode', axis), pairs))  9.28 us
    pallas_call x12, Pallas kernels, call(): pl.pallas_call(body, out_shape=list(shapes), in_specs=[spec for spec, ope...  7.42 us
    ppermute x12, starting transfers between devices, exchange(): return lax.ppermute(array, 'mode', [(i, i ^ bit) for i in range(count)])  6.39 us
    ppermute x9, waiting for transfers between devices, move_faces(): arrived.append(lax.ppermute(face, ('mode', axis), pairs))  4.63 us
    ppermute x12, waiting for transfers between devices, exchange(): return lax.ppermute(array, 'mode', [(i, i ^ bit) for i in range(count)])  4.14 us
    unnamed x16, local copies, waits for them, and re-layouts  1.06 us
  transfers between devices with their start and end apart: 21, of which 10 were waited for; matrix products, arithmetic and copies ran while one was open for 0% of the time, Pallas kernels for 11%

profile of v13, /device:TPU:0, one launch (start us, length us, event | category | flops | bytes accessed | tf_op | source)
XLA Modules:
  0.0 45.8 jit_solution(11851731765508117290)
XLA Ops:
  0.6 0.0 copy-start.1
  0.6 1.0 %copy-done.1 = f32[8,8,1792]{2,1,0:T(8,128)S(1)} copy-done((f32[8,8,1792]{2,1,0:T(8,128)S(1)}, f32[8,8,1792]{2,1,0:T(8,128)}, u32[]{:S(2)}) %copy-start.1) | copy-done | bytes 458776
  1.7 0.0 copy-start
  1.7 0.0 copy-start.3
  1.7 0.0 copy-start.4
  1.7 0.0 copy-start.5
  1.7 0.0 copy-start.6
  1.7 3.0 %collective-permute-start = (bf16[64,1792]{1,0:T(8,128)(2,1)S(1)}, bf16[64,1792]{1,0:T(8,128)(2,1)S(1)}, u32[]{:S(2)}, u32[]{:S(2)}) collective-permute-start(bf16[64,1792]{1,0:T(8,128)(2,1)S(1)} %get-tuple-element.29.refs_1_), channel_id=1, source_target_pairs={{0,16},{8,24},{16,0},{24,8},{1,17},{9,25},{17,1},{25,9},{2,18},{10... | collective-permute-start | bytes 688136 | tf_op jit(solution)/shard_map/ppermute | solution.py:47
  4.8 0.0 collective-permute-start.1
  4.8 0.5 %collective-permute-start.2 = (bf16[32,1792]{1,0:T(8,128)(2,1)S(1)}, bf16[32,1792]{1,0:T(8,128)(2,1)S(1)}, u32[]{:S(2)}, u32[]{:S(2)}) collective-permute-start(bf16[32,1792]{1,0:T(8,128)(2,1)S(1)} %get-tuple-element.31), channel_id=1, source_target_pairs={{0,8},{8,0},{16,24},{24,16},{1,9},{9,1},{17,25},{25,17},{2,10},{10... | collective-permute-start | bytes 344072 | tf_op jit(solution)/shard_map/ppermute | solution.py:47
  5.3 0.2 prepare.1
  5.5 1.6 %collective-permute-start.3 = (f32[8,1792]{1,0:T(8,128)S(1)}, f32[8,1792]{1,0:T(8,128)S(1)}, u32[]{:S(2)}, u32[]{:S(2)}) collective-permute-start(f32[8,1792]{1,0:T(8,128)S(1)} %get-tuple-element.34), channel_id=1, source_target_pairs={{0,4},{4,0},{8,12},{12,8},{16,20},{20,16},{24,28},{28,24},{1,5},{5... | collective-permute-start | bytes 172040 | tf_op jit(solution)/shard_map/ppermute | solution.py:40
  7.1 1.6 %collective-permute-start.4 = (f32[8,1792]{1,0:T(8,128)S(1)}, f32[8,1792]{1,0:T(8,128)S(1)}, u32[]{:S(2)}, u32[]{:S(2)}) collective-permute-start(f32[8,1792]{1,0:T(8,128)S(1)} %get-tuple-element.35), channel_id=1, source_target_pairs={{0,1},{1,0},{2,3},{3,2},{8,9},{9,8},{10,11},{11,10},{16,17},{17,16... | collective-permute-start | bytes 172040 | tf_op jit(solution)/shard_map/ppermute | solution.py:40
  8.7 0.0 collective-permute-done.2.refs_3_
  8.7 1.2 %near_0.1 = (f32[64,1792]{1,0:T(8,128)S(1)}, bf16[14,256,128]{2,1,0:T(8,128)(2,1)S(1)}) custom-call(s32[8,14]{1,0:T(8,128)S(1)} %bitcast.9, bf16[64,1792]{1,0:T(8,128)(2,1)S(1)} %get-tuple-element.29.refs_1_, bf16[32,1792]{1,0:T(8,128)(2,1)S(1)} %collective-permute-done.1.refs_2_, bf16[32,1792]{1,0:T(8,128)(2,1)S(1)} %collective-permute-done.2.refs_3_, ...), custom_call_target="tpu_custom_call" | custom-call | flops 117440512 | bytes 6032832 | tf_op jit(solution)/shard_map/near_0/pallas_call | solution.py:413
  9.9 0.0 collective-permute-done.3.refs_2_.refs_6_
  9.9 1.3 %collective-permute-done.4.refs_3_.refs_7_ = f32[8,1792]{1,0:T(8,128)S(1)} collective-permute-done((f32[8,1792]{1,0:T(8,128)S(1)}, f32[8,1792]{1,0:T(8,128)S(1)}, u32[]{:S(2)}, u32[]{:S(2)}) %collective-permute-start.4) | collective-permute-done | bytes 57376 | tf_op jit(solution)/shard_map/ppermute | solution.py:40
  11.3 0.1 collective-permute-start.6
  11.3 0.5 %middle_0.1.refs_3_ = f32[64,1792]{1,0:T(8,128)S(1)} custom-call(s32[8,14]{1,0:T(8,128)S(1)} %bitcast.10, bf16[64,1792]{1,0:T(8,128)(2,1)S(1)} %hand_on.3.refs_1_, bf16[14,8,128,128]{3,2,1,0:T(8,128)(2,1)S(1)} %copy-done, f32[64,1792]{1,0:T(8,128)S(1)} %get-tuple-element.33.refs_1_.refs_3_, f32[2,1792]{1,0:T(2,128)S(1)} %copy-done.3, ...), custom_call_target="tpu_custom_call" | custom-call | flops 58720256 | bytes 5018048 | tf_op jit(solution)/shard_map/middle_0/pallas_call | solution.py:413
  11.9 0.9 %collective-permute-done.6.refs_1_ = bf16[64,1792]{1,0:T(8,128)(2,1)S(1)} collective-permute-done((bf16[64,1792]{1,0:T(8,128)(2,1)S(1)}, bf16[64,1792]{1,0:T(8,128)(2,1)S(1)}, u32[]{:S(2)}, u32[]{:S(2)}) %collective-permute-start.6) | collective-permute-done | bytes 229408 | tf_op jit(solution)/shard_map/ppermute | solution.py:47
  12.8 0.4 last_0.1
  13.2 0.9 %collective-permute-start.7 = (bf16[64,1792]{1,0:T(8,128)(2,1)S(1)}, bf16[64,1792]{1,0:T(8,128)(2,1)S(1)}, u32[]{:S(2)}, u32[]{:S(2)}) collective-permute-start(bf16[64,1792]{1,0:T(8,128)(2,1)S(1)} %get-tuple-element.38.refs_1_), channel_id=1, source_target_pairs={{0,16},{8,24},{16,0},{24,8},{1,17},{9,25},{17,1},{25,9},{2,18},{10... | collective-permute-start | bytes 688136 | tf_op jit(solution)/shard_map/ppermute | solution.py:47
  14.1 0.0 collective-permute-start.8
  14.1 0.5 %collective-permute-start.9 = (bf16[32,1792]{1,0:T(8,128)(2,1)S(1)}, bf16[32,1792]{1,0:T(8,128)(2,1)S(1)}, u32[]{:S(2)}, u32[]{:S(2)}) collective-permute-start(bf16[32,1792]{1,0:T(8,128)(2,1)S(1)} %get-tuple-element.40), channel_id=1, source_target_pairs={{0,8},{8,0},{16,24},{24,16},{1,9},{9,1},{17,25},{25,17},{2,10},{10... | collective-permute-start | bytes 344072 | tf_op jit(solution)/shard_map/ppermute | solution.py:47
  14.6 1.5 %collective-permute-start.10 = (f32[8,1792]{1,0:T(8,128)S(1)}, f32[8,1792]{1,0:T(8,128)S(1)}, u32[]{:S(2)}, u32[]{:S(2)}) collective-permute-start(f32[8,1792]{1,0:T(8,128)S(1)} %get-tuple-element.42), channel_id=1, source_target_pairs={{0,4},{4,0},{8,12},{12,8},{16,20},{20,16},{24,28},{28,24},{1,5},{5... | collective-permute-start | bytes 172040 | tf_op jit(solution)/shard_map/ppermute | solution.py:40
  16.1 1.6 %collective-permute-start.11 = (f32[8,1792]{1,0:T(8,128)S(1)}, f32[8,1792]{1,0:T(8,128)S(1)}, u32[]{:S(2)}, u32[]{:S(2)}) collective-permute-start(f32[8,1792]{1,0:T(8,128)S(1)} %get-tuple-element.43), channel_id=1, source_target_pairs={{0,1},{1,0},{2,3},{3,2},{8,9},{9,8},{10,11},{11,10},{16,17},{17,16... | collective-permute-start | bytes 172040 | tf_op jit(solution)/shard_map/ppermute | solution.py:40
  17.7 0.0 collective-permute-done.8.refs_2_
  17.7 0.8 %near_1.1.refs_1_.refs_3_ = f32[64,1792]{1,0:T(8,128)S(1)} custom-call(s32[8,14]{1,0:T(8,128)S(1)} %bitcast.12, bf16[64,1792]{1,0:T(8,128)(2,1)S(1)} %get-tuple-element.38.refs_1_, bf16[32,1792]{1,0:T(8,128)(2,1)S(1)} %collective-permute-done.8.refs_2_, bf16[32,1792]{1,0:T(8,128)(2,1)S(1)} %collective-permute-done.9.refs_3_, ...), custom_call_target="tpu_custom_call" | custom-call | flops 117440512 | bytes 5115328 | tf_op jit(solution)/shard_map/near_1/pallas_call | solution.py:413
  18.6 0.0 copy-start.2
  18.6 0.2 collective-permute-done.10.refs_2_.refs_6_
  18.8 1.5 %collective-permute-done.11.refs_3_.refs_7_ = f32[8,1792]{1,0:T(8,128)S(1)} collective-permute-done((f32[8,1792]{1,0:T(8,128)S(1)}, f32[8,1792]{1,0:T(8,128)S(1)}, u32[]{:S(2)}, u32[]{:S(2)}) %collective-permute-start.11) | collective-permute-done | bytes 57376 | tf_op jit(solution)/shard_map/ppermute | solution.py:40
  20.3 0.6 %collective-permute-done.7.refs_0_ = bf16[64,1792]{1,0:T(8,128)(2,1)S(1)} collective-permute-done((bf16[64,1792]{1,0:T(8,128)(2,1)S(1)}, bf16[64,1792]{1,0:T(8,128)(2,1)S(1)}, u32[]{:S(2)}, u32[]{:S(2)}) %collective-permute-start.7) | collective-permute-done | bytes 229408 | tf_op jit(solution)/shard_map/ppermute | solution.py:47
  21.0 0.5 %middle_1.1.refs_3_ = f32[64,1792]{1,0:T(8,128)S(1)} custom-call(s32[8,14]{1,0:T(8,128)S(1)} %bitcast.13, bf16[64,1792]{1,0:T(8,128)(2,1)S(1)} %hand_on.4.refs_1_, bf16[14,8,128,128]{3,2,1,0:T(8,128)(2,1)S(1)} %copy-done, f32[64,1792]{1,0:T(8,128)S(1)} %near_1.1.refs_1_.refs_3_, f32[2,1792]{1,0:T(2,128)S(1)} %copy-done.3, s32[2,1792]{1,0:T(2,128)S(1)} %copy-done.4, ...), custom_call_target="tpu_custom_call" | custom-call | flops 58720256 | bytes 5018048 | tf_op jit(solution)/shard_map/middle_1/pallas_call | solution.py:413
  21.5 0.9 %collective-permute-done.13.refs_1_ = bf16[64,1792]{1,0:T(8,128)(2,1)S(1)} collective-permute-done((bf16[64,1792]{1,0:T(8,128)(2,1)S(1)}, bf16[64,1792]{1,0:T(8,128)(2,1)S(1)}, u32[]{:S(2)}, u32[]{:S(2)}) %collective-permute-start.13) | collective-permute-done | bytes 229408 | tf_op jit(solution)/shard_map/ppermute | solution.py:47
  22.4 0.4 last_1.1
  22.9 0.9 %collective-permute-start.14 = (bf16[64,1792]{1,0:T(8,128)(2,1)S(1)}, bf16[64,1792]{1,0:T(8,128)(2,1)S(1)}, u32[]{:S(2)}, u32[]{:S(2)}) collective-permute-start(bf16[64,1792]{1,0:T(8,128)(2,1)S(1)} %get-tuple-element.45.refs_1_), channel_id=1, source_target_pairs={{0,16},{8,24},{16,0},{24,8},{1,17},{9,25},{17,1},{25,9},{2,18},{10... | collective-permute-start | bytes 688136 | tf_op jit(solution)/shard_map/ppermute | solution.py:47
  23.8 0.5 %collective-permute-start.16 = (bf16[32,1792]{1,0:T(8,128)(2,1)S(1)}, bf16[32,1792]{1,0:T(8,128)(2,1)S(1)}, u32[]{:S(2)}, u32[]{:S(2)}) collective-permute-start(bf16[32,1792]{1,0:T(8,128)(2,1)S(1)} %get-tuple-element.47), channel_id=1, source_target_pairs={{0,8},{8,0},{16,24},{24,16},{1,9},{9,1},{17,25},{25,17},{2,10},{10... | collective-permute-start | bytes 344072 | tf_op jit(solution)/shard_map/ppermute | solution.py:47
  24.3 1.5 %collective-permute-start.17 = (f32[8,1792]{1,0:T(8,128)S(1)}, f32[8,1792]{1,0:T(8,128)S(1)}, u32[]{:S(2)}, u32[]{:S(2)}) collective-permute-start(f32[8,1792]{1,0:T(8,128)S(1)} %get-tuple-element.50), channel_id=1, source_target_pairs={{0,4},{4,0},{8,12},{12,8},{16,20},{20,16},{24,28},{28,24},{1,5},{5... | collective-permute-start | bytes 172040 | tf_op jit(solution)/shard_map/ppermute | solution.py:40
  25.8 1.6 %collective-permute-start.18 = (f32[8,1792]{1,0:T(8,128)S(1)}, f32[8,1792]{1,0:T(8,128)S(1)}, u32[]{:S(2)}, u32[]{:S(2)}) collective-permute-start(f32[8,1792]{1,0:T(8,128)S(1)} %get-tuple-element.51), channel_id=1, source_target_pairs={{0,1},{1,0},{2,3},{3,2},{8,9},{9,8},{10,11},{11,10},{16,17},{17,16... | collective-permute-start | bytes 172040 | tf_op jit(solution)/shard_map/ppermute | solution.py:40
  27.4 1.0 %near_2.1 = (f32[64,1792]{1,0:T(8,128)S(1)}, f32[16,128]{1,0:T(8,128)S(1)}) custom-call(s32[8,14]{1,0:T(8,128)S(1)} %bitcast.15, bf16[64,1792]{1,0:T(8,128)(2,1)S(1)} %get-tuple-element.45.refs_1_, bf16[32,1792]{1,0:T(8,128)(2,1)S(1)} %collective-permute-done.15.refs_2_, bf16[32,1792]{1,0:T(8,128)(2,1)S(1)} %collective-permute-done.16.refs_3_, ...), custom_call_target="tpu_custom_call" | custom-call | flops 117440512 | bytes 6499776 | tf_op jit(solution)/shard_map/near_2/pallas_call | solution.py:413
  28.4 0.1 collective-permute-done.17.refs_2_.refs_6_
  28.5 1.5 %collective-permute-done.18.refs_3_.refs_7_ = f32[8,1792]{1,0:T(8,128)S(1)} collective-permute-done((f32[8,1792]{1,0:T(8,128)S(1)}, f32[8,1792]{1,0:T(8,128)S(1)}, u32[]{:S(2)}, u32[]{:S(2)}) %collective-permute-start.18) | collective-permute-done | bytes 57376 | tf_op jit(solution)/shard_map/ppermute | solution.py:40
  30.0 0.7 %collective-permute-done.14.refs_0_ = bf16[64,1792]{1,0:T(8,128)(2,1)S(1)} collective-permute-done((bf16[64,1792]{1,0:T(8,128)(2,1)S(1)}, bf16[64,1792]{1,0:T(8,128)(2,1)S(1)}, u32[]{:S(2)}, u32[]{:S(2)}) %collective-permute-start.14) | collective-permute-done | bytes 229408 | tf_op jit(solution)/shard_map/ppermute | solution.py:47
  30.6 0.5 %middle_2.1.refs_3_ = f32[64,1792]{1,0:T(8,128)S(1)} custom-call(s32[8,14]{1,0:T(8,128)S(1)} %bitcast.16, bf16[64,1792]{1,0:T(8,128)(2,1)S(1)} %hand_on.5.refs_1_, bf16[14,8,128,128]{3,2,1,0:T(8,128)(2,1)S(1)} %copy-done, f32[64,1792]{1,0:T(8,128)S(1)} %get-tuple-element.49.refs_1_.refs_3_, f32[2,1792]{1,0:T(2,128)S(1)} %copy-done.3, ...), custom_call_target="tpu_custom_call" | custom-call | flops 58720256 | bytes 5018048 | tf_op jit(solution)/shard_map/middle_2/pallas_call | solution.py:413
  31.1 0.9 %collective-permute-done.20.refs_1_ = bf16[64,1792]{1,0:T(8,128)(2,1)S(1)} collective-permute-done((bf16[64,1792]{1,0:T(8,128)(2,1)S(1)}, bf16[64,1792]{1,0:T(8,128)(2,1)S(1)}, u32[]{:S(2)}, u32[]{:S(2)}) %collective-permute-start.20) | collective-permute-done | bytes 229408 | tf_op jit(solution)/shard_map/ppermute | solution.py:47
  32.1 0.5 %last_2.1 = f32[32,1,128]{2,1,0:T(1,128)S(1)} custom-call(s32[8,14]{1,0:T(8,128)S(1)} %bitcast.17, bf16[64,1792]{1,0:T(8,128)(2,1)S(1)} %collective-permute-done.20.refs_1_, bf16[14,256,128]{2,1,0:T(8,128)(2,1)S(1)} %get-tuple-element.37.refs_2_, f32[64,1792]{1,0:T(8,128)S(1)} %middle_2.1.refs_3_, f32[64,128]{1,0:T(8,128)S(1)} %get-tuple-element.32.refs_6_.refs_4_, ...), custom_call_target="tpu_custom_call" | custom-call | flops 58720256 | bytes 3039680 | tf_op jit(solution)/shard_map/last_2/pallas_call | solution.py:413
  32.6 12.1 %all_to_all.5.refs_0_ = f32[32,1,128]{2,1,0:T(1,128)S(1)} all-to-all(f32[32,1,128]{2,1,0:T(1,128)S(1)} %last_2.1), channel_id=1, replica_groups=mesh['mode'=4,'gx'=2,'gy'=4] {'mode','gx','gy'}, dimensions={0} | all-to-all | bytes 32768 | tf_op jit(solution)/shard_map/all_to_all | solution.py:572
  44.7 1.1 %finish.1 = (f32[64,1792]{1,0:T(8,128)}, f32[4,3]{1,0:T(4,128)}) custom-call(f32[32,1,128]{2,1,0:T(1,128)S(1)} %all_to_all.5.refs_0_, f32[64,1792]{1,0:T(8,128)S(1)} %bitcast.8, f32[64,1792]{1,0:T(8,128)S(1)} %get-tuple-element.41.refs_5_.refs_11_.refs_6_.refs_2_, f32[64,1792]{1,0:T(8,128)S(1)} %get-tuple-element.48.refs_5_.refs_12_.refs_7_.refs_3_), custom_call_target="tpu_custom_call" | custom-call | bytes 1851440 | tf_op jit(solution)/shard_map/finish/pallas_call | solution.py:413
  (26 shorter events, 0.1 us)
Async XLA Ops:
  0.6 1.0 %copy-start.1 = (f32[8,8,1792]{2,1,0:T(8,128)S(1)}, f32[8,8,1792]{2,1,0:T(8,128)}, u32[]{:S(2)}) copy-start(f32[8,8,1792]{2,1,0:T(8,128)} %param.7) | copy-start | bytes 1376260
  1.7 3.6 %copy-start.7 = (s32[8,8]{1,0:T(8,128)S(1)}, s32[8,8]{1,0:T(8,128)}, u32[]{:S(2)}) copy-start(s32[8,8]{1,0:T(8,128)} %refs_1_.1) | copy-start | bytes 772
  1.7 7.0 %copy-start = (bf16[14,8,128,128]{3,2,1,0:T(8,128)(2,1)S(1)}, bf16[14,8,128,128]{3,2,1,0:T(8,128)(2,1)}, u32[]{:S(2)}) copy-start(bf16[14,8,128,128]{3,2,1,0:T(8,128)(2,1)} %refs_2_.5) | copy-start | bytes 11010052
  1.7 7.0 %copy-start.3 = (f32[2,1792]{1,0:T(2,128)S(1)}, f32[2,1792]{1,0:T(2,128)}, u32[]{:S(2)}) copy-start(f32[2,1792]{1,0:T(2,128)} %refs_4_.11) | copy-start | bytes 43012
  1.7 7.0 %copy-start.4 = (s32[2,1792]{1,0:T(2,128)S(1)}, s32[2,1792]{1,0:T(2,128)}, u32[]{:S(2)}) copy-start(s32[2,1792]{1,0:T(2,128)} %refs_5_.5) | copy-start | bytes 43012
  1.7 7.0 %copy-start.5 = (s32[14,8]{0,1:T(8,128)S(1)}, s32[14,8]{0,1:T(8,128)}, u32[]{:S(2)}) copy-start(s32[14,8]{0,1:T(8,128)} %param.8) | copy-start | bytes 1348
  1.7 7.0 %copy-start.6 = (f32[1792]{0:T(1024)S(1)}, f32[1792]{0:T(1024)}, u32[]{:S(2)}) copy-start(f32[1792]{0:T(1024)} %refs_7_.5) | copy-start | bytes 21508
  1.7 9.5 %collective-permute-start = (bf16[64,1792]{1,0:T(8,128)(2,1)S(1)}, bf16[64,1792]{1,0:T(8,128)(2,1)S(1)}, u32[]{:S(2)}, u32[]{:S(2)}) collective-permute-start(bf16[64,1792]{1,0:T(8,128)(2,1)S(1)} %get-tuple-element.29.refs_1_), channel_id=1, source_target_pairs={{0,16},{8,24},{16,0},{24,8},{1,17},{9,25},{17,1},{25,9},{2,18},{10... | collective-permute-start | bytes 688136 | tf_op jit(solution)/shard_map/ppermute | solution.py:47
  4.8 3.9 %collective-permute-start.1 = (bf16[32,1792]{1,0:T(8,128)(2,1)S(1)}, bf16[32,1792]{1,0:T(8,128)(2,1)S(1)}, u32[]{:S(2)}, u32[]{:S(2)}) collective-permute-start(bf16[32,1792]{1,0:T(8,128)(2,1)S(1)} %get-tuple-element.30), channel_id=1, source_target_pairs={{0,8},{8,0},{16,24},{24,16},{1,9},{9,1},{17,25},{25,17},{2,10},{10... | collective-permute-start | bytes 344072 | tf_op jit(solution)/shard_map/ppermute | solution.py:47
  4.8 3.9 %collective-permute-start.2 = (bf16[32,1792]{1,0:T(8,128)(2,1)S(1)}, bf16[32,1792]{1,0:T(8,128)(2,1)S(1)}, u32[]{:S(2)}, u32[]{:S(2)}) collective-permute-start(bf16[32,1792]{1,0:T(8,128)(2,1)S(1)} %get-tuple-element.31), channel_id=1, source_target_pairs={{0,8},{8,0},{16,24},{24,16},{1,9},{9,1},{17,25},{25,17},{2,10},{10... | collective-permute-start | bytes 344072 | tf_op jit(solution)/shard_map/ppermute | solution.py:47
  5.5 4.4 %collective-permute-start.3 = (f32[8,1792]{1,0:T(8,128)S(1)}, f32[8,1792]{1,0:T(8,128)S(1)}, u32[]{:S(2)}, u32[]{:S(2)}) collective-permute-start(f32[8,1792]{1,0:T(8,128)S(1)} %get-tuple-element.34), channel_id=1, source_target_pairs={{0,4},{4,0},{8,12},{12,8},{16,20},{20,16},{24,28},{28,24},{1,5},{5... | collective-permute-start | bytes 172040 | tf_op jit(solution)/shard_map/ppermute | solution.py:40
  7.1 4.2 %collective-permute-start.4 = (f32[8,1792]{1,0:T(8,128)S(1)}, f32[8,1792]{1,0:T(8,128)S(1)}, u32[]{:S(2)}, u32[]{:S(2)}) collective-permute-start(f32[8,1792]{1,0:T(8,128)S(1)} %get-tuple-element.35), channel_id=1, source_target_pairs={{0,1},{1,0},{2,3},{3,2},{8,9},{9,8},{10,11},{11,10},{16,17},{17,16... | collective-permute-start | bytes 172040 | tf_op jit(solution)/shard_map/ppermute | solution.py:40
  8.6 2.6 %collective-permute-start.5 = (f32[8,1792]{1,0:T(8,128)S(1)}, f32[8,1792]{1,0:T(8,128)S(1)}, u32[]{:S(2)}, u32[]{:S(2)}) collective-permute-start(f32[8,1792]{1,0:T(8,128)S(1)} %get-tuple-element.36), channel_id=1, source_target_pairs={{0,8},{1,2},{2,1},{3,11},{8,0},{9,10},{10,9},{11,3},{16,24},{17,18... | collective-permute-start | bytes 172040 | tf_op jit(solution)/shard_map/ppermute | solution.py:40
  11.3 1.5 %collective-permute-start.6 = (bf16[64,1792]{1,0:T(8,128)(2,1)S(1)}, bf16[64,1792]{1,0:T(8,128)(2,1)S(1)}, u32[]{:S(2)}, u32[]{:S(2)}) collective-permute-start(bf16[64,1792]{1,0:T(8,128)(2,1)S(1)} %hand_on.3.refs_1_), channel_id=1, source_target_pairs={{0,8},{8,0},{16,24},{24,16},{1,9},{9,1},{17,25},{25,17},{2,10},{10... | collective-permute-start | bytes 688136 | tf_op jit(solution)/shard_map/ppermute | solution.py:47
  13.2 7.7 %collective-permute-start.7 = (bf16[64,1792]{1,0:T(8,128)(2,1)S(1)}, bf16[64,1792]{1,0:T(8,128)(2,1)S(1)}, u32[]{:S(2)}, u32[]{:S(2)}) collective-permute-start(bf16[64,1792]{1,0:T(8,128)(2,1)S(1)} %get-tuple-element.38.refs_1_), channel_id=1, source_target_pairs={{0,16},{8,24},{16,0},{24,8},{1,17},{9,25},{17,1},{25,9},{2,18},{10... | collective-permute-start | bytes 688136 | tf_op jit(solution)/shard_map/ppermute | solution.py:47
  14.1 3.6 %collective-permute-start.8 = (bf16[32,1792]{1,0:T(8,128)(2,1)S(1)}, bf16[32,1792]{1,0:T(8,128)(2,1)S(1)}, u32[]{:S(2)}, u32[]{:S(2)}) collective-permute-start(bf16[32,1792]{1,0:T(8,128)(2,1)S(1)} %get-tuple-element.39), channel_id=1, source_target_pairs={{0,8},{8,0},{16,24},{24,16},{1,9},{9,1},{17,25},{25,17},{2,10},{10... | collective-permute-start | bytes 344072 | tf_op jit(solution)/shard_map/ppermute | solution.py:47
  14.1 3.6 %collective-permute-start.9 = (bf16[32,1792]{1,0:T(8,128)(2,1)S(1)}, bf16[32,1792]{1,0:T(8,128)(2,1)S(1)}, u32[]{:S(2)}, u32[]{:S(2)}) collective-permute-start(bf16[32,1792]{1,0:T(8,128)(2,1)S(1)} %get-tuple-element.40), channel_id=1, source_target_pairs={{0,8},{8,0},{16,24},{24,16},{1,9},{9,1},{17,25},{25,17},{2,10},{10... | collective-permute-start | bytes 344072 | tf_op jit(solution)/shard_map/ppermute | solution.py:47
  14.6 4.2 %collective-permute-start.10 = (f32[8,1792]{1,0:T(8,128)S(1)}, f32[8,1792]{1,0:T(8,128)S(1)}, u32[]{:S(2)}, u32[]{:S(2)}) collective-permute-start(f32[8,1792]{1,0:T(8,128)S(1)} %get-tuple-element.42), channel_id=1, source_target_pairs={{0,4},{4,0},{8,12},{12,8},{16,20},{20,16},{24,28},{28,24},{1,5},{5... | collective-permute-start | bytes 172040 | tf_op jit(solution)/shard_map/ppermute | solution.py:40
  16.1 4.2 %collective-permute-start.11 = (f32[8,1792]{1,0:T(8,128)S(1)}, f32[8,1792]{1,0:T(8,128)S(1)}, u32[]{:S(2)}, u32[]{:S(2)}) collective-permute-start(f32[8,1792]{1,0:T(8,128)S(1)} %get-tuple-element.43), channel_id=1, source_target_pairs={{0,1},{1,0},{2,3},{3,2},{8,9},{9,8},{10,11},{11,10},{16,17},{17,16... | collective-permute-start | bytes 172040 | tf_op jit(solution)/shard_map/ppermute | solution.py:40
  17.7 2.6 %collective-permute-start.12 = (f32[8,1792]{1,0:T(8,128)S(1)}, f32[8,1792]{1,0:T(8,128)S(1)}, u32[]{:S(2)}, u32[]{:S(2)}) collective-permute-start(f32[8,1792]{1,0:T(8,128)S(1)} %get-tuple-element.44), channel_id=1, source_target_pairs={{0,8},{1,2},{2,1},{3,11},{8,0},{9,10},{10,9},{11,3},{16,24},{17,18... | collective-permute-start | bytes 172040 | tf_op jit(solution)/shard_map/ppermute | solution.py:40
  18.6 8.8 %copy-start.2 = (f32[8,8,1792]{2,1,0:T(8,128)S(1)}, f32[8,8,1792]{2,1,0:T(8,128)}, u32[]{:S(2)}) copy-start(f32[8,8,1792]{2,1,0:T(8,128)} %param.7) | copy-start | bytes 1376260
  21.0 1.5 %collective-permute-start.13 = (bf16[64,1792]{1,0:T(8,128)(2,1)S(1)}, bf16[64,1792]{1,0:T(8,128)(2,1)S(1)}, u32[]{:S(2)}, u32[]{:S(2)}) collective-permute-start(bf16[64,1792]{1,0:T(8,128)(2,1)S(1)} %hand_on.4.refs_1_), channel_id=1, source_target_pairs={{0,8},{8,0},{16,24},{24,16},{1,9},{9,1},{17,25},{25,17},{2,10},{10... | collective-permute-start | bytes 688136 | tf_op jit(solution)/shard_map/ppermute | solution.py:47
  22.9 7.7 %collective-permute-start.14 = (bf16[64,1792]{1,0:T(8,128)(2,1)S(1)}, bf16[64,1792]{1,0:T(8,128)(2,1)S(1)}, u32[]{:S(2)}, u32[]{:S(2)}) collective-permute-start(bf16[64,1792]{1,0:T(8,128)(2,1)S(1)} %get-tuple-element.45.refs_1_), channel_id=1, source_target_pairs={{0,16},{8,24},{16,0},{24,8},{1,17},{9,25},{17,1},{25,9},{2,18},{10... | collective-permute-start | bytes 688136 | tf_op jit(solution)/shard_map/ppermute | solution.py:47
  23.8 3.6 %collective-permute-start.15 = (bf16[32,1792]{1,0:T(8,128)(2,1)S(1)}, bf16[32,1792]{1,0:T(8,128)(2,1)S(1)}, u32[]{:S(2)}, u32[]{:S(2)}) collective-permute-start(bf16[32,1792]{1,0:T(8,128)(2,1)S(1)} %get-tuple-element.46), channel_id=1, source_target_pairs={{0,8},{8,0},{16,24},{24,16},{1,9},{9,1},{17,25},{25,17},{2,10},{10... | collective-permute-start | bytes 344072 | tf_op jit(solution)/shard_map/ppermute | solution.py:47
  23.8 3.6 %collective-permute-start.16 = (bf16[32,1792]{1,0:T(8,128)(2,1)S(1)}, bf16[32,1792]{1,0:T(8,128)(2,1)S(1)}, u32[]{:S(2)}, u32[]{:S(2)}) collective-permute-start(bf16[32,1792]{1,0:T(8,128)(2,1)S(1)} %get-tuple-element.47), channel_id=1, source_target_pairs={{0,8},{8,0},{16,24},{24,16},{1,9},{9,1},{17,25},{25,17},{2,10},{10... | collective-permute-start | bytes 344072 | tf_op jit(solution)/shard_map/ppermute | solution.py:47
  24.3 4.2 %collective-permute-start.17 = (f32[8,1792]{1,0:T(8,128)S(1)}, f32[8,1792]{1,0:T(8,128)S(1)}, u32[]{:S(2)}, u32[]{:S(2)}) collective-permute-start(f32[8,1792]{1,0:T(8,128)S(1)} %get-tuple-element.50), channel_id=1, source_target_pairs={{0,4},{4,0},{8,12},{12,8},{16,20},{20,16},{24,28},{28,24},{1,5},{5... | collective-permute-start | bytes 172040 | tf_op jit(solution)/shard_map/ppermute | solution.py:40
  25.8 4.2 %collective-permute-start.18 = (f32[8,1792]{1,0:T(8,128)S(1)}, f32[8,1792]{1,0:T(8,128)S(1)}, u32[]{:S(2)}, u32[]{:S(2)}) collective-permute-start(f32[8,1792]{1,0:T(8,128)S(1)} %get-tuple-element.51), channel_id=1, source_target_pairs={{0,1},{1,0},{2,3},{3,2},{8,9},{9,8},{10,11},{11,10},{16,17},{17,16... | collective-permute-start | bytes 172040 | tf_op jit(solution)/shard_map/ppermute | solution.py:40
  27.4 2.6 %collective-permute-start.19 = (f32[8,1792]{1,0:T(8,128)S(1)}, f32[8,1792]{1,0:T(8,128)S(1)}, u32[]{:S(2)}, u32[]{:S(2)}) collective-permute-start(f32[8,1792]{1,0:T(8,128)S(1)} %get-tuple-element.52), channel_id=1, source_target_pairs={{0,8},{1,2},{2,1},{3,11},{8,0},{9,10},{10,9},{11,3},{16,24},{17,18... | collective-permute-start | bytes 172040 | tf_op jit(solution)/shard_map/ppermute | solution.py:40
  30.6 1.5 %collective-permute-start.20 = (bf16[64,1792]{1,0:T(8,128)(2,1)S(1)}, bf16[64,1792]{1,0:T(8,128)(2,1)S(1)}, u32[]{:S(2)}, u32[]{:S(2)}) collective-permute-start(bf16[64,1792]{1,0:T(8,128)(2,1)S(1)} %hand_on.5.refs_1_), channel_id=1, source_target_pairs={{0,8},{8,0},{16,24},{24,16},{1,9},{9,1},{17,25},{25,17},{2,10},{10... | collective-permute-start | bytes 688136 | tf_op jit(solution)/shard_map/ppermute | solution.py:47

commit v14 on v13

--- a/solution.py
+++ b/solution.py
@@ -1,5 +1,3 @@
-import functools
-
 import jax
 import jax.numpy as jnp
 from jax import lax
@@ -58,13 +56,17 @@
     return held
 
 
-def store_packed(refs, lanes, value):
-    refs[0][:, lanes] = value.astype(jnp.bfloat16)
+def spread_kernel(sizes, value_ref, open_ref, part_refs, x_refs, y_refs):
+    first, second, local_blocks, block = sizes
     at = 0
-    for ref in refs[1:]:
+    for ref in part_refs:
         rows = ref.shape[0]
-        ref[:, lanes] = value[at : at + rows].astype(jnp.bfloat16)
+        ref[...] = value_ref[at : at + rows, :].astype(jnp.bfloat16)
         at += rows
+    for b in range(local_blocks):
+        lanes = slice(b * block, (b + 1) * block)
+        masked = (value_ref[:, lanes] * open_ref[...]).reshape(first, second, block)
+        write_faces(masked, lanes, first, second, x_refs, y_refs)
 
 
 def hand_on(arrays, after):
@@ -104,7 +106,7 @@
     return jnp.where(at == 0, zero, low), jnp.where(at == lax.axis_size(axis) - 1, zero, high)
 
 
-def prepare_kernel(sizes, rhs_ref, wall_ref, x_refs, y_refs, open_ref):
+def prepare_kernel(sizes, rhs_ref, wall_ref, part_refs, x_refs, y_refs, open_ref):
     first, second, local_blocks, block = sizes
     wall = wall_ref[...].astype(jnp.float32)
     eye = (
@@ -114,10 +116,7 @@
     for row in range(first):
         column = jnp.sum(eye * (1.0 - wall[row : row + 1, :]), axis=1, keepdims=True)
         open_ref[row * second : (row + 1) * second, :] = jnp.broadcast_to(column, (second, block))
-    for b in range(local_blocks):
-        lanes = slice(b * block, (b + 1) * block)
-        masked = (rhs_ref[:, lanes] * open_ref[...]).reshape(first, second, block)
-        write_faces(masked, lanes, first, second, x_refs, y_refs)
+    spread_kernel(sizes, rhs_ref, open_ref, part_refs, x_refs, y_refs)
 
 
 def scatter(sizes, per_owner, b, places, cols_ref, sources, blocks_ref, turned=False):
@@ -248,7 +247,7 @@
         out_ref[:, lanes] = value.reshape(cells, block)
 
 
-def last_kernel(sizes, per_owner, places, cols_ref, sources, blocks_ref, partial_ref, earlier, open_ref, outs, early_ref=None):
+def last_kernel(sizes, per_owner, places, cols_ref, sources, blocks_ref, partial_ref, earlier, outs, early_ref=None):
     first, second, local_blocks, block = sizes
     cells = first * second
     sums = {}
@@ -258,11 +257,7 @@
         result = partial_ref[:, lanes] - scattered
         if outs.gram is None:
             outs.value[:, lanes] = result
-            store_packed(outs.packed, lanes, result)
-            write_faces(
-                (result * open_ref[...]).reshape(first, second, block),
-                lanes, first, second, outs.x, outs.y,
-            )
+            outs.packed[:, lanes] = result.astype(jnp.bfloat16)
         else:
             vectors = [ref[:, lanes] for ref in earlier] + [result]
             for i, vector in enumerate(vectors):
@@ -285,8 +280,7 @@
 
 
 class Outs:
-    value = gram = None
-    x = y = packed = ()
+    value = packed = gram = None
 
 
 def least_squares(hessenberg, initial):
@@ -322,15 +316,14 @@
 def arnoldi(gram):
     size = KRYLOV + 1
 
-    def inner(left, right):
-        total = None
-        for i in range(size):
-            for j in range(size):
-                if left[i] is None or right[j] is None:
-                    continue
-                term = left[i] * gram[min(i, j)][max(i, j)] * right[j]
-                total = term if total is None else total + term
-        return total
+    def dot(left, right):
+        terms = [a * b for a, b in zip(left, right) if a is not None and b is not None]
+        while len(terms) > 1:
+            terms = [sum(terms[at + 1 : at + 2], terms[at]) for at in range(0, len(terms), 2)]
+        return terms[0]
+
+    def times_gram(vector):
+        return [dot([gram[min(i, j)][max(i, j)] for j in range(size)], vector) for i in range(size)]
 
     initial = jnp.sqrt(gram[0][0] + epsilon)
     basis = [[1.0 / initial] + [None] * KRYLOV]
@@ -347,12 +340,13 @@
                 parts.append(SHIFT * vector[k])
             image[k] = sum(parts[1:], parts[0])
         rest = list(image)
+        products = times_gram(image)
         for earlier in range(section + 1):
-            coefficient = inner(basis[earlier], image)
+            coefficient = dot(basis[earlier], products)
             hessenberg[earlier][section] = coefficient
             for k in range(earlier + 1):
                 rest[k] = rest[k] - coefficient * basis[earlier][k]
-        length = jnp.sqrt(jnp.maximum(inner(rest, rest), 0.0) + epsilon)
+        length = jnp.sqrt(jnp.maximum(dot(rest, times_gram(rest)), 0.0) + epsilon)
         hessenberg[section + 1][section] = length
         basis.append([None if part is None else part / length for part in rest])
     combo = least_squares(hessenberg, initial)
@@ -442,8 +436,8 @@
         shape_of((first, local_modes), f32)
     ] * y_moves
     parts = 2 if cells % 32 == 0 else 1
-    packed_shapes = [shape_of((cells, local_modes), jnp.bfloat16)]
-    packed_shapes += [shape_of((cells // parts, local_modes), jnp.bfloat16)] * parts
+    packed_shape = shape_of((cells, local_modes), jnp.bfloat16)
+    spread_shapes = [shape_of((cells // parts, local_modes), jnp.bfloat16)] * parts + face_shapes
     vector_shape = shape_of((cells, local_modes), f32)
     near = [place for place in (0, 1) if place < count]
     final = [place for place in range(3, count) if place % 2 == 1]
@@ -452,19 +446,22 @@
     start = right_side.reshape(cells, local_modes)
 
     def pack(ins, outs, scratch):
-        store_packed(outs, slice(None), ins[0][...])
-
-    packed = call("pack", pack, [in_vmem([start])], packed_shapes, flops=8 * 10**9)
+        outs[0][...] = ins[0][...].astype(jnp.bfloat16)
+
+    (packed,) = call("pack", pack, [in_vmem([start])], [packed_shape], flops=8 * 10**9)
+
+    def split(outs):
+        faces = outs[parts:]
+        return outs[:parts], faces[:x_moves], faces[x_moves:n_faces]
 
     def prepare(ins, outs, scratch):
-        faces, (open_ref,) = outs[:n_faces], outs[n_faces:]
-        prepare_kernel(sizes, *ins, faces[:x_moves], faces[x_moves:], open_ref)
-
-    *faces, open_cells = call(
+        prepare_kernel(sizes, *ins, *split(outs), outs[-1])
+
+    *spread, open_cells = call(
         "prepare",
         prepare,
         [in_vmem([start, wall_mask])],
-        face_shapes + [shape_of((cells, block), f32)],
+        spread_shapes + [shape_of((cells, block), f32)],
         flops=1 * 10**9,
     )
     columns = col_block.T
@@ -473,10 +470,11 @@
     work = 2 * cells * local_modes * per_owner * block
     vectors = [start]
     for section in range(KRYLOV):
-        sources = {0: packed[0]}
-        held = gather_far(packed[0])
-        neighbour = [exchange(part, 1) for part in packed[1:]] if count > 1 else []
-        y_in, x_in = move_faces({"gx": faces[:x_moves], "gy": faces[x_moves:]})
+        sources = {0: packed}
+        held = gather_far(packed)
+        halves, x_faces, y_faces = split(spread)
+        neighbour = [exchange(part, 1) for part in halves] if count > 1 else []
+        y_in, x_in = move_faces({"gx": x_faces, "gy": y_faces})
 
         last = section == KRYLOV - 1
 
@@ -497,7 +495,7 @@
             near_step,
             [
                 in_vmem([columns]),
-                in_vmem([packed[0], *neighbour]),
+                in_vmem([packed, *neighbour]),
                 in_vmem([blocks, vectors[-1], open_cells]),
                 in_vmem([relax_rate, drift_speed, upwind_sign]),
                 in_vmem(vectors if last else []),
@@ -534,29 +532,28 @@
         )
 
         def last_step(cols, sources, rest, earlier, early, outs, scratch, last=last):
-            blocks_ref, partial_ref, open_ref = rest
+            blocks_ref, partial_ref = rest
             named = Outs()
             if last:
                 named.gram = outs[0]
             else:
-                named.x, named.y = outs[:x_moves], outs[x_moves:n_faces]
-                *named.packed, named.value = outs[n_faces:]
+                named.packed, named.value = outs
             last_kernel(
                 sizes, per_owner, final, cols[0], [[ref] for ref in sources], blocks_ref, partial_ref,
-                earlier, open_ref, named, early[0] if last else None,
+                earlier, named, early[0] if last else None,
             )
 
         if last:
             shapes = [shape_of((devices, 1, block), f32)]
         else:
-            shapes = face_shapes + packed_shapes + [vector_shape]
+            shapes = [packed_shape, vector_shape]
         results = call(
             "last_%d" % section,
             last_step,
             [
                 in_vmem([columns]),
                 in_vmem([sources[place] for place in final]),
-                in_vmem([turned, partial, open_cells]),
+                in_vmem([turned, partial]),
                 in_vmem(vectors if last else []),
                 in_vmem(early),
             ],
@@ -566,8 +563,14 @@
         if last:
             (gram,) = results
         else:
-            faces, packed, value = results[:n_faces], results[n_faces:-1], results[-1]
+            packed, value = results
             vectors.append(value)
+            spread = call(
+                "spread_%d" % section,
+                lambda ins, outs, scratch: spread_kernel(sizes, *ins, *split(outs)),
+                [in_vmem([value, open_cells])],
+                spread_shapes,
+            )
 
     gram = lax.all_to_all(gram, AXES, 0, 0)
 

time: 46 us -> 45.8 us (level)
  waiting for transfers between devices: 8.77 us -> 8.15 us
    pallas_call x12 -> x14, Pallas kernels: 7.42 us -> 7.59 us  [call(): pl.pallas_call(body, out_shape=list(shapes), in_specs=[spec for spec, ope...]
  transfers between devices with their start and end apart: 21 -> 21, of which waited for: 10 -> 9; matrix products, arithmetic and copies ran while one was open for 0% -> 0% of each run, Pallas kernels for 11% -> 11%
where the time goes in v14:
time: 45.8 us; the launch traced here: 45.7 us
  starting transfers between devices  16 us (35%)
  blocking collectives  12.1 us (26%)
  waiting for transfers between devices  8.15 us (18%)
  Pallas kernels  7.59 us (17%)
  local copies, waits for them, and re-layouts  1.05 us (2%)
  between operations  0.85 us (2%)
    all_to_all x1, blocking collectives, per_device(): gram = lax.all_to_all(gram, AXES, 0, 0)  12.1 us
    ppermute x9, starting transfers between devices, move_faces(): arrived.append(lax.ppermute(face, ('mode', axis), pairs))  9.4 us
    pallas_call x14, Pallas kernels, call(): pl.pallas_call(body, out_shape=list(shapes), in_specs=[spec for spec, ope...  7.59 us
    ppermute x12, starting transfers between devices, exchange(): return lax.ppermute(array, 'mode', [(i, i ^ bit) for i in range(count)])  6.56 us
    ppermute x9, waiting for transfers between devices, move_faces(): arrived.append(lax.ppermute(face, ('mode', axis), pairs))  4.43 us
    ppermute x12, waiting for transfers between devices, exchange(): return lax.ppermute(array, 'mode', [(i, i ^ bit) for i in range(count)])  3.71 us
    unnamed x16, local copies, waits for them, and re-layouts  1.05 us
  transfers between devices with their start and end apart: 21, of which 9 were waited for; matrix products, arithmetic and copies ran while one was open for 0% of the time, Pallas kernels for 11%

profile of v14, /device:TPU:0, one launch (start us, length us, event | category | flops | bytes accessed | tf_op | source)
XLA Modules:
  0.0 45.7 jit_solution(2441351080541328790)
XLA Ops:
  0.6 0.0 copy-start.1
  0.6 1.0 %copy-done.1 = f32[8,8,1792]{2,1,0:T(8,128)S(1)} copy-done((f32[8,8,1792]{2,1,0:T(8,128)S(1)}, f32[8,8,1792]{2,1,0:T(8,128)}, u32[]{:S(2)}) %copy-start.1) | copy-done | bytes 458776
  1.7 0.0 copy-start
  1.7 0.0 copy-start.3
  1.7 0.0 copy-start.4
  1.7 0.0 copy-start.5
  1.7 0.0 copy-start.6
  1.7 3.0 %collective-permute-start = (bf16[64,1792]{1,0:T(8,128)(2,1)S(1)}, bf16[64,1792]{1,0:T(8,128)(2,1)S(1)}, u32[]{:S(2)}, u32[]{:S(2)}) collective-permute-start(bf16[64,1792]{1,0:T(8,128)(2,1)S(1)} %pack.1.refs_1_), channel_id=1, source_target_pairs={{0,16},{8,24},{16,0},{24,8},{1,17},{9,25},{17,1},{25,9},{2,18},{10... | collective-permute-start | bytes 688136 | tf_op jit(solution)/shard_map/ppermute | solution.py:45
  4.8 0.2 prepare.1
  5.0 0.1 collective-permute-start.1
  5.1 0.5 %collective-permute-start.2 = (bf16[32,1792]{1,0:T(8,128)(2,1)S(1)}, bf16[32,1792]{1,0:T(8,128)(2,1)S(1)}, u32[]{:S(2)}, u32[]{:S(2)}) collective-permute-start(bf16[32,1792]{1,0:T(8,128)(2,1)S(1)} %get-tuple-element.29), channel_id=1, source_target_pairs={{0,8},{8,0},{16,24},{24,16},{1,9},{9,1},{17,25},{25,17},{2,10},{10... | collective-permute-start | bytes 344072 | tf_op jit(solution)/shard_map/ppermute | solution.py:45
  5.6 1.5 %collective-permute-start.3 = (f32[8,1792]{1,0:T(8,128)S(1)}, f32[8,1792]{1,0:T(8,128)S(1)}, u32[]{:S(2)}, u32[]{:S(2)}) collective-permute-start(f32[8,1792]{1,0:T(8,128)S(1)} %get-tuple-element.32), channel_id=1, source_target_pairs={{0,4},{4,0},{8,12},{12,8},{16,20},{20,16},{24,28},{28,24},{1,5},{5... | collective-permute-start | bytes 172040 | tf_op jit(solution)/shard_map/ppermute | solution.py:38
  7.1 1.6 %collective-permute-start.4 = (f32[8,1792]{1,0:T(8,128)S(1)}, f32[8,1792]{1,0:T(8,128)S(1)}, u32[]{:S(2)}, u32[]{:S(2)}) collective-permute-start(f32[8,1792]{1,0:T(8,128)S(1)} %get-tuple-element.33), channel_id=1, source_target_pairs={{0,1},{1,0},{2,3},{3,2},{8,9},{9,8},{10,11},{11,10},{16,17},{17,16... | collective-permute-start | bytes 172040 | tf_op jit(solution)/shard_map/ppermute | solution.py:38
  8.6 0.0 collective-permute-done.1.refs_2_
  8.6 0.0 collective-permute-start.5
  8.7 1.2 %near_0.1 = (f32[64,1792]{1,0:T(8,128)S(1)}, bf16[14,256,128]{2,1,0:T(8,128)(2,1)S(1)}) custom-call(s32[8,14]{1,0:T(8,128)S(1)} %bitcast.9, bf16[64,1792]{1,0:T(8,128)(2,1)S(1)} %pack.1.refs_1_, bf16[32,1792]{1,0:T(8,128)(2,1)S(1)} %collective-permute-done.1.refs_2_, bf16[32,1792]{1,0:T(8,128)(2,1)S(1)} %collective-permute-done.2.refs_3_, ...), custom_call_target="tpu_custom_call" | custom-call | flops 117440512 | bytes 6032832 | tf_op jit(solution)/shard_map/near_0/pallas_call | solution.py:407
  9.9 1.3 %collective-permute-done.4.refs_3_.refs_7_ = f32[8,1792]{1,0:T(8,128)S(1)} collective-permute-done((f32[8,1792]{1,0:T(8,128)S(1)}, f32[8,1792]{1,0:T(8,128)S(1)}, u32[]{:S(2)}, u32[]{:S(2)}) %collective-permute-start.4) | collective-permute-done | bytes 57376 | tf_op jit(solution)/shard_map/ppermute | solution.py:38
  11.2 0.1 collective-permute-start.6
  11.3 0.5 %middle_0.1.refs_3_ = f32[64,1792]{1,0:T(8,128)S(1)} custom-call(s32[8,14]{1,0:T(8,128)S(1)} %bitcast.10, bf16[64,1792]{1,0:T(8,128)(2,1)S(1)} %hand_on.3.refs_1_, bf16[14,8,128,128]{3,2,1,0:T(8,128)(2,1)S(1)} %copy-done, f32[64,1792]{1,0:T(8,128)S(1)} %get-tuple-element.31.refs_1_.refs_3_, f32[2,1792]{1,0:T(2,128)S(1)} %copy-done.3, ...), custom_call_target="tpu_custom_call" | custom-call | flops 58720256 | bytes 5018048 | tf_op jit(solution)/shard_map/middle_0/pallas_call | solution.py:407
  11.9 0.9 %collective-permute-done.6.refs_1_ = bf16[64,1792]{1,0:T(8,128)(2,1)S(1)} collective-permute-done((bf16[64,1792]{1,0:T(8,128)(2,1)S(1)}, bf16[64,1792]{1,0:T(8,128)(2,1)S(1)}, u32[]{:S(2)}, u32[]{:S(2)}) %collective-permute-start.6) | collective-permute-done | bytes 229408 | tf_op jit(solution)/shard_map/ppermute | solution.py:45
  12.8 0.4 last_0.1
  13.2 0.9 %collective-permute-start.7 = (bf16[64,1792]{1,0:T(8,128)(2,1)S(1)}, bf16[64,1792]{1,0:T(8,128)(2,1)S(1)}, u32[]{:S(2)}, u32[]{:S(2)}) collective-permute-start(bf16[64,1792]{1,0:T(8,128)(2,1)S(1)} %get-tuple-element.36.refs_1_), channel_id=1, source_target_pairs={{0,16},{8,24},{16,0},{24,8},{1,17},{9,25},{17,1},{25,9},{2,18},{10... | collective-permute-start | bytes 688136 | tf_op jit(solution)/shard_map/ppermute | solution.py:45
  14.1 0.2 spread_0.1
  14.2 0.1 collective-permute-start.8
  14.3 0.5 %collective-permute-start.9 = (bf16[32,1792]{1,0:T(8,128)(2,1)S(1)}, bf16[32,1792]{1,0:T(8,128)(2,1)S(1)}, u32[]{:S(2)}, u32[]{:S(2)}) collective-permute-start(bf16[32,1792]{1,0:T(8,128)(2,1)S(1)} %get-tuple-element.39), channel_id=1, source_target_pairs={{0,8},{8,0},{16,24},{24,16},{1,9},{9,1},{17,25},{25,17},{2,10},{10... | collective-permute-start | bytes 344072 | tf_op jit(solution)/shard_map/ppermute | solution.py:45
  14.8 1.5 %collective-permute-start.10 = (f32[8,1792]{1,0:T(8,128)S(1)}, f32[8,1792]{1,0:T(8,128)S(1)}, u32[]{:S(2)}, u32[]{:S(2)}) collective-permute-start(f32[8,1792]{1,0:T(8,128)S(1)} %get-tuple-element.40), channel_id=1, source_target_pairs={{0,4},{4,0},{8,12},{12,8},{16,20},{20,16},{24,28},{28,24},{1,5},{5... | collective-permute-start | bytes 172040 | tf_op jit(solution)/shard_map/ppermute | solution.py:38
  16.3 1.6 %collective-permute-start.11 = (f32[8,1792]{1,0:T(8,128)S(1)}, f32[8,1792]{1,0:T(8,128)S(1)}, u32[]{:S(2)}, u32[]{:S(2)}) collective-permute-start(f32[8,1792]{1,0:T(8,128)S(1)} %get-tuple-element.41), channel_id=1, source_target_pairs={{0,1},{1,0},{2,3},{3,2},{8,9},{9,8},{10,11},{11,10},{16,17},{17,16... | collective-permute-start | bytes 172040 | tf_op jit(solution)/shard_map/ppermute | solution.py:38
  17.9 0.8 %near_1.1.refs_1_.refs_3_ = f32[64,1792]{1,0:T(8,128)S(1)} custom-call(s32[8,14]{1,0:T(8,128)S(1)} %bitcast.12, bf16[64,1792]{1,0:T(8,128)(2,1)S(1)} %get-tuple-element.36.refs_1_, bf16[32,1792]{1,0:T(8,128)(2,1)S(1)} %collective-permute-done.8.refs_2_, bf16[32,1792]{1,0:T(8,128)(2,1)S(1)} %collective-permute-done.9.refs_3_, ...), custom_call_target="tpu_custom_call" | custom-call | flops 117440512 | bytes 5115328 | tf_op jit(solution)/shard_map/near_1/pallas_call | solution.py:407
  18.7 0.2 collective-permute-done.10.refs_2_.refs_6_
  19.0 1.5 %collective-permute-done.11.refs_3_.refs_7_ = f32[8,1792]{1,0:T(8,128)S(1)} collective-permute-done((f32[8,1792]{1,0:T(8,128)S(1)}, f32[8,1792]{1,0:T(8,128)S(1)}, u32[]{:S(2)}, u32[]{:S(2)}) %collective-permute-start.11) | collective-permute-done | bytes 57376 | tf_op jit(solution)/shard_map/ppermute | solution.py:38
  20.5 0.4 collective-permute-done.7.refs_0_
  20.9 0.5 %middle_1.1.refs_3_ = f32[64,1792]{1,0:T(8,128)S(1)} custom-call(s32[8,14]{1,0:T(8,128)S(1)} %bitcast.13, bf16[64,1792]{1,0:T(8,128)(2,1)S(1)} %hand_on.4.refs_1_, bf16[14,8,128,128]{3,2,1,0:T(8,128)(2,1)S(1)} %copy-done, f32[64,1792]{1,0:T(8,128)S(1)} %near_1.1.refs_1_.refs_3_, f32[2,1792]{1,0:T(2,128)S(1)} %copy-done.3, s32[2,1792]{1,0:T(2,128)S(1)} %copy-done.4, ...), custom_call_target="tpu_custom_call" | custom-call | flops 58720256 | bytes 5018048 | tf_op jit(solution)/shard_map/middle_1/pallas_call | solution.py:407
  21.4 1.0 %collective-permute-done.13.refs_1_ = bf16[64,1792]{1,0:T(8,128)(2,1)S(1)} collective-permute-done((bf16[64,1792]{1,0:T(8,128)(2,1)S(1)}, bf16[64,1792]{1,0:T(8,128)(2,1)S(1)}, u32[]{:S(2)}, u32[]{:S(2)}) %collective-permute-start.13) | collective-permute-done | bytes 229408 | tf_op jit(solution)/shard_map/ppermute | solution.py:45
  22.4 0.4 last_1.1
  22.8 0.9 %collective-permute-start.14 = (bf16[64,1792]{1,0:T(8,128)(2,1)S(1)}, bf16[64,1792]{1,0:T(8,128)(2,1)S(1)}, u32[]{:S(2)}, u32[]{:S(2)}) collective-permute-start(bf16[64,1792]{1,0:T(8,128)(2,1)S(1)} %get-tuple-element.43.refs_1_), channel_id=1, source_target_pairs={{0,16},{8,24},{16,0},{24,8},{1,17},{9,25},{17,1},{25,9},{2,18},{10... | collective-permute-start | bytes 688136 | tf_op jit(solution)/shard_map/ppermute | solution.py:45
  23.6 0.2 spread_1.1
  23.8 0.1 collective-permute-start.15
  23.9 0.5 %collective-permute-start.16 = (bf16[32,1792]{1,0:T(8,128)(2,1)S(1)}, bf16[32,1792]{1,0:T(8,128)(2,1)S(1)}, u32[]{:S(2)}, u32[]{:S(2)}) collective-permute-start(bf16[32,1792]{1,0:T(8,128)(2,1)S(1)} %get-tuple-element.46), channel_id=1, source_target_pairs={{0,8},{8,0},{16,24},{24,16},{1,9},{9,1},{17,25},{25,17},{2,10},{10... | collective-permute-start | bytes 344072 | tf_op jit(solution)/shard_map/ppermute | solution.py:45
  24.4 1.5 %collective-permute-start.17 = (f32[8,1792]{1,0:T(8,128)S(1)}, f32[8,1792]{1,0:T(8,128)S(1)}, u32[]{:S(2)}, u32[]{:S(2)}) collective-permute-start(f32[8,1792]{1,0:T(8,128)S(1)} %get-tuple-element.48), channel_id=1, source_target_pairs={{0,4},{4,0},{8,12},{12,8},{16,20},{20,16},{24,28},{28,24},{1,5},{5... | collective-permute-start | bytes 172040 | tf_op jit(solution)/shard_map/ppermute | solution.py:38
  25.9 1.8 %collective-permute-start.18 = (f32[8,1792]{1,0:T(8,128)S(1)}, f32[8,1792]{1,0:T(8,128)S(1)}, u32[]{:S(2)}, u32[]{:S(2)}) collective-permute-start(f32[8,1792]{1,0:T(8,128)S(1)} %get-tuple-element.49), channel_id=1, source_target_pairs={{0,1},{1,0},{2,3},{3,2},{8,9},{9,8},{10,11},{11,10},{16,17},{17,16... | collective-permute-start | bytes 172040 | tf_op jit(solution)/shard_map/ppermute | solution.py:38
  27.7 1.0 %near_2.1 = (f32[64,1792]{1,0:T(8,128)S(1)}, f32[16,128]{1,0:T(8,128)S(1)}) custom-call(s32[8,14]{1,0:T(8,128)S(1)} %bitcast.15, bf16[64,1792]{1,0:T(8,128)(2,1)S(1)} %get-tuple-element.43.refs_1_, bf16[32,1792]{1,0:T(8,128)(2,1)S(1)} %collective-permute-done.15.refs_2_, bf16[32,1792]{1,0:T(8,128)(2,1)S(1)} %collective-permute-done.16.refs_3_, ...), custom_call_target="tpu_custom_call" | custom-call | flops 117440512 | bytes 6499776 | tf_op jit(solution)/shard_map/near_2/pallas_call | solution.py:407
  28.7 1.3 %collective-permute-done.18.refs_3_.refs_7_ = f32[8,1792]{1,0:T(8,128)S(1)} collective-permute-done((f32[8,1792]{1,0:T(8,128)S(1)}, f32[8,1792]{1,0:T(8,128)S(1)}, u32[]{:S(2)}, u32[]{:S(2)}) %collective-permute-start.18) | collective-permute-done | bytes 57376 | tf_op jit(solution)/shard_map/ppermute | solution.py:38
  30.0 0.4 collective-permute-done.14.refs_0_
  30.5 0.5 %middle_2.1.refs_3_ = f32[64,1792]{1,0:T(8,128)S(1)} custom-call(s32[8,14]{1,0:T(8,128)S(1)} %bitcast.16, bf16[64,1792]{1,0:T(8,128)(2,1)S(1)} %hand_on.5.refs_1_, bf16[14,8,128,128]{3,2,1,0:T(8,128)(2,1)S(1)} %copy-done, f32[64,1792]{1,0:T(8,128)S(1)} %get-tuple-element.47.refs_1_.refs_3_, f32[2,1792]{1,0:T(2,128)S(1)} %copy-done.3, ...), custom_call_target="tpu_custom_call" | custom-call | flops 58720256 | bytes 5018048 | tf_op jit(solution)/shard_map/middle_2/pallas_call | solution.py:407
  31.0 1.0 %collective-permute-done.20.refs_1_ = bf16[64,1792]{1,0:T(8,128)(2,1)S(1)} collective-permute-done((bf16[64,1792]{1,0:T(8,128)(2,1)S(1)}, bf16[64,1792]{1,0:T(8,128)(2,1)S(1)}, u32[]{:S(2)}, u32[]{:S(2)}) %collective-permute-start.20) | collective-permute-done | bytes 229408 | tf_op jit(solution)/shard_map/ppermute | solution.py:45
  32.0 0.5 %last_2.1 = f32[32,1,128]{2,1,0:T(1,128)S(1)} custom-call(s32[8,14]{1,0:T(8,128)S(1)} %bitcast.17, bf16[64,1792]{1,0:T(8,128)(2,1)S(1)} %collective-permute-done.20.refs_1_, bf16[14,256,128]{2,1,0:T(8,128)(2,1)S(1)} %get-tuple-element.35.refs_2_, f32[64,1792]{1,0:T(8,128)S(1)} %middle_2.1.refs_3_, f32[64,1792]{1,0:T(8,128)S(1)} %bitcast.7, ...), custom_call_target="tpu_custom_call" | custom-call | flops 58720256 | bytes 3006912 | tf_op jit(solution)/shard_map/last_2/pallas_call | solution.py:407
  32.5 12.1 %all_to_all.5.refs_0_ = f32[32,1,128]{2,1,0:T(1,128)S(1)} all-to-all(f32[32,1,128]{2,1,0:T(1,128)S(1)} %last_2.1), channel_id=1, replica_groups=mesh['mode'=4,'gx'=2,'gy'=4] {'mode','gx','gy'}, dimensions={0} | all-to-all | bytes 32768 | tf_op jit(solution)/shard_map/all_to_all | solution.py:575
  44.6 1.1 %finish.1 = (f32[64,1792]{1,0:T(8,128)}, f32[4,3]{1,0:T(4,128)}) custom-call(f32[32,1,128]{2,1,0:T(1,128)S(1)} %all_to_all.5.refs_0_, f32[64,1792]{1,0:T(8,128)S(1)} %bitcast.8, f32[64,1792]{1,0:T(8,128)S(1)} %get-tuple-element.37.refs_0_.refs_5_.refs_11_.refs_2_, f32[64,1792]{1,0:T(8,128)S(1)} %get-tuple-element.44.refs_0_.refs_5_.refs_12_.refs_6_.refs_3_), custom_call_target="tpu_custom_call" | custom-call | bytes 1851440 | tf_op jit(solution)/shard_map/finish/pallas_call | solution.py:407
  (28 shorter events, 0.1 us)
Async XLA Ops:
  0.6 1.0 %copy-start.1 = (f32[8,8,1792]{2,1,0:T(8,128)S(1)}, f32[8,8,1792]{2,1,0:T(8,128)}, u32[]{:S(2)}) copy-start(f32[8,8,1792]{2,1,0:T(8,128)} %param.7) | copy-start | bytes 1376260
  1.7 3.1 %copy-start.7 = (s32[8,8]{1,0:T(8,128)S(1)}, s32[8,8]{1,0:T(8,128)}, u32[]{:S(2)}) copy-start(s32[8,8]{1,0:T(8,128)} %refs_1_.1) | copy-start | bytes 772
  1.7 7.0 %copy-start = (bf16[14,8,128,128]{3,2,1,0:T(8,128)(2,1)S(1)}, bf16[14,8,128,128]{3,2,1,0:T(8,128)(2,1)}, u32[]{:S(2)}) copy-start(bf16[14,8,128,128]{3,2,1,0:T(8,128)(2,1)} %refs_2_.5) | copy-start | bytes 11010052
  1.7 7.0 %copy-start.3 = (f32[2,1792]{1,0:T(2,128)S(1)}, f32[2,1792]{1,0:T(2,128)}, u32[]{:S(2)}) copy-start(f32[2,1792]{1,0:T(2,128)} %refs_4_.11) | copy-start | bytes 43012
  1.7 7.0 %copy-start.4 = (s32[2,1792]{1,0:T(2,128)S(1)}, s32[2,1792]{1,0:T(2,128)}, u32[]{:S(2)}) copy-start(s32[2,1792]{1,0:T(2,128)} %refs_5_.5) | copy-start | bytes 43012
  1.7 7.0 %copy-start.5 = (s32[14,8]{0,1:T(8,128)S(1)}, s32[14,8]{0,1:T(8,128)}, u32[]{:S(2)}) copy-start(s32[14,8]{0,1:T(8,128)} %param.8) | copy-start | bytes 1348
  1.7 7.0 %copy-start.6 = (f32[1792]{0:T(1024)S(1)}, f32[1792]{0:T(1024)}, u32[]{:S(2)}) copy-start(f32[1792]{0:T(1024)} %refs_7_.5) | copy-start | bytes 21508
  1.7 9.5 %collective-permute-start = (bf16[64,1792]{1,0:T(8,128)(2,1)S(1)}, bf16[64,1792]{1,0:T(8,128)(2,1)S(1)}, u32[]{:S(2)}, u32[]{:S(2)}) collective-permute-start(bf16[64,1792]{1,0:T(8,128)(2,1)S(1)} %pack.1.refs_1_), channel_id=1, source_target_pairs={{0,16},{8,24},{16,0},{24,8},{1,17},{9,25},{17,1},{25,9},{2,18},{10... | collective-permute-start | bytes 688136 | tf_op jit(solution)/shard_map/ppermute | solution.py:45
  5.0 3.6 %collective-permute-start.1 = (bf16[32,1792]{1,0:T(8,128)(2,1)S(1)}, bf16[32,1792]{1,0:T(8,128)(2,1)S(1)}, u32[]{:S(2)}, u32[]{:S(2)}) collective-permute-start(bf16[32,1792]{1,0:T(8,128)(2,1)S(1)} %get-tuple-element.28), channel_id=1, source_target_pairs={{0,8},{8,0},{16,24},{24,16},{1,9},{9,1},{17,25},{25,17},{2,10},{10... | collective-permute-start | bytes 344072 | tf_op jit(solution)/shard_map/ppermute | solution.py:45
  5.1 3.6 %collective-permute-start.2 = (bf16[32,1792]{1,0:T(8,128)(2,1)S(1)}, bf16[32,1792]{1,0:T(8,128)(2,1)S(1)}, u32[]{:S(2)}, u32[]{:S(2)}) collective-permute-start(bf16[32,1792]{1,0:T(8,128)(2,1)S(1)} %get-tuple-element.29), channel_id=1, source_target_pairs={{0,8},{8,0},{16,24},{24,16},{1,9},{9,1},{17,25},{25,17},{2,10},{10... | collective-permute-start | bytes 344072 | tf_op jit(solution)/shard_map/ppermute | solution.py:45
  5.6 4.3 %collective-permute-start.3 = (f32[8,1792]{1,0:T(8,128)S(1)}, f32[8,1792]{1,0:T(8,128)S(1)}, u32[]{:S(2)}, u32[]{:S(2)}) collective-permute-start(f32[8,1792]{1,0:T(8,128)S(1)} %get-tuple-element.32), channel_id=1, source_target_pairs={{0,4},{4,0},{8,12},{12,8},{16,20},{20,16},{24,28},{28,24},{1,5},{5... | collective-permute-start | bytes 172040 | tf_op jit(solution)/shard_map/ppermute | solution.py:38
  7.1 4.2 %collective-permute-start.4 = (f32[8,1792]{1,0:T(8,128)S(1)}, f32[8,1792]{1,0:T(8,128)S(1)}, u32[]{:S(2)}, u32[]{:S(2)}) collective-permute-start(f32[8,1792]{1,0:T(8,128)S(1)} %get-tuple-element.33), channel_id=1, source_target_pairs={{0,1},{1,0},{2,3},{3,2},{8,9},{9,8},{10,11},{11,10},{16,17},{17,16... | collective-permute-start | bytes 172040 | tf_op jit(solution)/shard_map/ppermute | solution.py:38
  8.6 2.6 %collective-permute-start.5 = (f32[8,1792]{1,0:T(8,128)S(1)}, f32[8,1792]{1,0:T(8,128)S(1)}, u32[]{:S(2)}, u32[]{:S(2)}) collective-permute-start(f32[8,1792]{1,0:T(8,128)S(1)} %get-tuple-element.34), channel_id=1, source_target_pairs={{0,8},{1,2},{2,1},{3,11},{8,0},{9,10},{10,9},{11,3},{16,24},{17,18... | collective-permute-start | bytes 172040 | tf_op jit(solution)/shard_map/ppermute | solution.py:38
  11.2 1.5 %collective-permute-start.6 = (bf16[64,1792]{1,0:T(8,128)(2,1)S(1)}, bf16[64,1792]{1,0:T(8,128)(2,1)S(1)}, u32[]{:S(2)}, u32[]{:S(2)}) collective-permute-start(bf16[64,1792]{1,0:T(8,128)(2,1)S(1)} %hand_on.3.refs_1_), channel_id=1, source_target_pairs={{0,8},{8,0},{16,24},{24,16},{1,9},{9,1},{17,25},{25,17},{2,10},{10... | collective-permute-start | bytes 688136 | tf_op jit(solution)/shard_map/ppermute | solution.py:45
  13.2 7.7 %collective-permute-start.7 = (bf16[64,1792]{1,0:T(8,128)(2,1)S(1)}, bf16[64,1792]{1,0:T(8,128)(2,1)S(1)}, u32[]{:S(2)}, u32[]{:S(2)}) collective-permute-start(bf16[64,1792]{1,0:T(8,128)(2,1)S(1)} %get-tuple-element.36.refs_1_), channel_id=1, source_target_pairs={{0,16},{8,24},{16,0},{24,8},{1,17},{9,25},{17,1},{25,9},{2,18},{10... | collective-permute-start | bytes 688136 | tf_op jit(solution)/shard_map/ppermute | solution.py:45
  14.2 3.6 %collective-permute-start.8 = (bf16[32,1792]{1,0:T(8,128)(2,1)S(1)}, bf16[32,1792]{1,0:T(8,128)(2,1)S(1)}, u32[]{:S(2)}, u32[]{:S(2)}) collective-permute-start(bf16[32,1792]{1,0:T(8,128)(2,1)S(1)} %get-tuple-element.38), channel_id=1, source_target_pairs={{0,8},{8,0},{16,24},{24,16},{1,9},{9,1},{17,25},{25,17},{2,10},{10... | collective-permute-start | bytes 344072 | tf_op jit(solution)/shard_map/ppermute | solution.py:45
  14.3 3.6 %collective-permute-start.9 = (bf16[32,1792]{1,0:T(8,128)(2,1)S(1)}, bf16[32,1792]{1,0:T(8,128)(2,1)S(1)}, u32[]{:S(2)}, u32[]{:S(2)}) collective-permute-start(bf16[32,1792]{1,0:T(8,128)(2,1)S(1)} %get-tuple-element.39), channel_id=1, source_target_pairs={{0,8},{8,0},{16,24},{24,16},{1,9},{9,1},{17,25},{25,17},{2,10},{10... | collective-permute-start | bytes 344072 | tf_op jit(solution)/shard_map/ppermute | solution.py:45
  14.8 4.2 %collective-permute-start.10 = (f32[8,1792]{1,0:T(8,128)S(1)}, f32[8,1792]{1,0:T(8,128)S(1)}, u32[]{:S(2)}, u32[]{:S(2)}) collective-permute-start(f32[8,1792]{1,0:T(8,128)S(1)} %get-tuple-element.40), channel_id=1, source_target_pairs={{0,4},{4,0},{8,12},{12,8},{16,20},{20,16},{24,28},{28,24},{1,5},{5... | collective-permute-start | bytes 172040 | tf_op jit(solution)/shard_map/ppermute | solution.py:38
  16.3 4.2 %collective-permute-start.11 = (f32[8,1792]{1,0:T(8,128)S(1)}, f32[8,1792]{1,0:T(8,128)S(1)}, u32[]{:S(2)}, u32[]{:S(2)}) collective-permute-start(f32[8,1792]{1,0:T(8,128)S(1)} %get-tuple-element.41), channel_id=1, source_target_pairs={{0,1},{1,0},{2,3},{3,2},{8,9},{9,8},{10,11},{11,10},{16,17},{17,16... | collective-permute-start | bytes 172040 | tf_op jit(solution)/shard_map/ppermute | solution.py:38
  17.9 2.6 %collective-permute-start.12 = (f32[8,1792]{1,0:T(8,128)S(1)}, f32[8,1792]{1,0:T(8,128)S(1)}, u32[]{:S(2)}, u32[]{:S(2)}) collective-permute-start(f32[8,1792]{1,0:T(8,128)S(1)} %get-tuple-element.42), channel_id=1, source_target_pairs={{0,8},{1,2},{2,1},{3,11},{8,0},{9,10},{10,9},{11,3},{16,24},{17,18... | collective-permute-start | bytes 172040 | tf_op jit(solution)/shard_map/ppermute | solution.py:38
  20.9 6.8 %copy-start.2 = (f32[8,8,1792]{2,1,0:T(8,128)S(1)}, f32[8,8,1792]{2,1,0:T(8,128)}, u32[]{:S(2)}) copy-start(f32[8,8,1792]{2,1,0:T(8,128)} %param.7) | copy-start | bytes 1376260
  20.9 1.5 %collective-permute-start.13 = (bf16[64,1792]{1,0:T(8,128)(2,1)S(1)}, bf16[64,1792]{1,0:T(8,128)(2,1)S(1)}, u32[]{:S(2)}, u32[]{:S(2)}) collective-permute-start(bf16[64,1792]{1,0:T(8,128)(2,1)S(1)} %hand_on.4.refs_1_), channel_id=1, source_target_pairs={{0,8},{8,0},{16,24},{24,16},{1,9},{9,1},{17,25},{25,17},{2,10},{10... | collective-permute-start | bytes 688136 | tf_op jit(solution)/shard_map/ppermute | solution.py:45
  22.8 7.7 %collective-permute-start.14 = (bf16[64,1792]{1,0:T(8,128)(2,1)S(1)}, bf16[64,1792]{1,0:T(8,128)(2,1)S(1)}, u32[]{:S(2)}, u32[]{:S(2)}) collective-permute-start(bf16[64,1792]{1,0:T(8,128)(2,1)S(1)} %get-tuple-element.43.refs_1_), channel_id=1, source_target_pairs={{0,16},{8,24},{16,0},{24,8},{1,17},{9,25},{17,1},{25,9},{2,18},{10... | collective-permute-start | bytes 688136 | tf_op jit(solution)/shard_map/ppermute | solution.py:45
  23.8 3.8 %collective-permute-start.15 = (bf16[32,1792]{1,0:T(8,128)(2,1)S(1)}, bf16[32,1792]{1,0:T(8,128)(2,1)S(1)}, u32[]{:S(2)}, u32[]{:S(2)}) collective-permute-start(bf16[32,1792]{1,0:T(8,128)(2,1)S(1)} %get-tuple-element.45), channel_id=1, source_target_pairs={{0,8},{8,0},{16,24},{24,16},{1,9},{9,1},{17,25},{25,17},{2,10},{10... | collective-permute-start | bytes 344072 | tf_op jit(solution)/shard_map/ppermute | solution.py:45
  23.9 3.8 %collective-permute-start.16 = (bf16[32,1792]{1,0:T(8,128)(2,1)S(1)}, bf16[32,1792]{1,0:T(8,128)(2,1)S(1)}, u32[]{:S(2)}, u32[]{:S(2)}) collective-permute-start(bf16[32,1792]{1,0:T(8,128)(2,1)S(1)} %get-tuple-element.46), channel_id=1, source_target_pairs={{0,8},{8,0},{16,24},{24,16},{1,9},{9,1},{17,25},{25,17},{2,10},{10... | collective-permute-start | bytes 344072 | tf_op jit(solution)/shard_map/ppermute | solution.py:45
  24.4 4.3 %collective-permute-start.17 = (f32[8,1792]{1,0:T(8,128)S(1)}, f32[8,1792]{1,0:T(8,128)S(1)}, u32[]{:S(2)}, u32[]{:S(2)}) collective-permute-start(f32[8,1792]{1,0:T(8,128)S(1)} %get-tuple-element.48), channel_id=1, source_target_pairs={{0,4},{4,0},{8,12},{12,8},{16,20},{20,16},{24,28},{28,24},{1,5},{5... | collective-permute-start | bytes 172040 | tf_op jit(solution)/shard_map/ppermute | solution.py:38
  25.9 4.2 %collective-permute-start.18 = (f32[8,1792]{1,0:T(8,128)S(1)}, f32[8,1792]{1,0:T(8,128)S(1)}, u32[]{:S(2)}, u32[]{:S(2)}) collective-permute-start(f32[8,1792]{1,0:T(8,128)S(1)} %get-tuple-element.49), channel_id=1, source_target_pairs={{0,1},{1,0},{2,3},{3,2},{8,9},{9,8},{10,11},{11,10},{16,17},{17,16... | collective-permute-start | bytes 172040 | tf_op jit(solution)/shard_map/ppermute | solution.py:38
  27.6 2.4 %collective-permute-start.19 = (f32[8,1792]{1,0:T(8,128)S(1)}, f32[8,1792]{1,0:T(8,128)S(1)}, u32[]{:S(2)}, u32[]{:S(2)}) collective-permute-start(f32[8,1792]{1,0:T(8,128)S(1)} %get-tuple-element.50), channel_id=1, source_target_pairs={{0,8},{1,2},{2,1},{3,11},{8,0},{9,10},{10,9},{11,3},{16,24},{17,18... | collective-permute-start | bytes 172040 | tf_op jit(solution)/shard_map/ppermute | solution.py:38
  30.5 1.5 %collective-permute-start.20 = (bf16[64,1792]{1,0:T(8,128)(2,1)S(1)}, bf16[64,1792]{1,0:T(8,128)(2,1)S(1)}, u32[]{:S(2)}, u32[]{:S(2)}) collective-permute-start(bf16[64,1792]{1,0:T(8,128)(2,1)S(1)} %hand_on.5.refs_1_), channel_id=1, source_target_pairs={{0,8},{8,0},{16,24},{24,16},{1,9},{9,1},{17,25},{25,17},{2,10},{10... | collective-permute-start | bytes 688136 | tf_op jit(solution)/shard_map/ppermute | solution.py:45

commit v15 on v14

--- a/solution.py
+++ b/solution.py
@@ -313,42 +313,56 @@
     return combo
 
 
+def dot(left, right):
+    terms = [a * b for a, b in zip(left, right)]
+    while len(terms) > 1:
+        terms = [sum(terms[at + 1 : at + 2], terms[at]) for at in range(0, len(terms), 2)]
+    return terms[0]
+
+
+def factor(gram):
+    size = len(gram)
+    rows = [[] for k in range(size)]
+    for j in range(size):
+        pivot = gram[j][j] - dot(rows[j], rows[j]) if j else gram[j][j]
+        edge = jnp.sqrt(jnp.maximum(pivot, 0.0))
+        inverse = jnp.where(edge > 1e-18, 1.0 / jnp.maximum(edge, 1e-18), 0.0)
+        for k in range(j + 1, size):
+            value = gram[j][k] - dot(rows[k], rows[j]) if j else gram[j][k]
+            rows[k].append(value * inverse)
+        rows[j].append(edge)
+    return rows
+
+
 def arnoldi(gram):
-    size = KRYLOV + 1
-
-    def dot(left, right):
-        terms = [a * b for a, b in zip(left, right) if a is not None and b is not None]
-        while len(terms) > 1:
-            terms = [sum(terms[at + 1 : at + 2], terms[at]) for at in range(0, len(terms), 2)]
-        return terms[0]
-
-    def times_gram(vector):
-        return [dot([gram[min(i, j)][max(i, j)] for j in range(size)], vector) for i in range(size)]
+    rows = factor(gram)
+
+    def coordinates(vector):
+        return [
+            dot(vector[i:], [rows[k][i] for k in range(i, len(vector))]) for i in range(len(vector))
+        ]
 
     initial = jnp.sqrt(gram[0][0] + epsilon)
-    basis = [[1.0 / initial] + [None] * KRYLOV]
+    basis = [[1.0 / initial]]
+    places = [coordinates(basis[0])]
     zero = jnp.zeros_like(initial)
-    hessenberg = [[zero] * KRYLOV for row_index in range(size)]
+    hessenberg = [[zero] * KRYLOV for row_index in range(KRYLOV + 1)]
     for section in range(KRYLOV):
         vector = basis[section]
-        image = [None] * size
-        for k in range(section + 2):
-            parts = []
-            if k > 0 and vector[k - 1] is not None:
-                parts.append(vector[k - 1])
-            if vector[k] is not None:
-                parts.append(SHIFT * vector[k])
-            image[k] = sum(parts[1:], parts[0])
-        rest = list(image)
-        products = times_gram(image)
+        shifted = [SHIFT * part for part in vector] + [zero]
+        image = [shifted[0]] + [a + b for a, b in zip(vector, shifted[1:])]
+        spot = coordinates(image)
+        rest, rest_spot = list(image), list(spot)
         for earlier in range(section + 1):
-            coefficient = dot(basis[earlier], products)
+            coefficient = dot(places[earlier], spot)
             hessenberg[earlier][section] = coefficient
             for k in range(earlier + 1):
                 rest[k] = rest[k] - coefficient * basis[earlier][k]
-        length = jnp.sqrt(jnp.maximum(dot(rest, times_gram(rest)), 0.0) + epsilon)
+                rest_spot[k] = rest_spot[k] - coefficient * places[earlier][k]
+        length = jnp.sqrt(dot(rest_spot, rest_spot) + epsilon)
         hessenberg[section + 1][section] = length
-        basis.append([None if part is None else part / length for part in rest])
+        basis.append([part / length for part in rest])
+        places.append([part / length for part in rest_spot])
     combo = least_squares(hessenberg, initial)
     weights = []
     for k in range(KRYLOV):

time: 45.8 us -> 45.8 us (level)
  no operation moved by 1% of the time
where the time goes in v15:
time: 45.8 us; the launch traced here: 45.7 us
  starting transfers between devices  16 us (35%)
  blocking collectives  12.1 us (26%)
  waiting for transfers between devices  8.15 us (18%)
  Pallas kernels  7.57 us (17%)
  local copies, waits for them, and re-layouts  1.05 us (2%)
  between operations  0.85 us (2%)
    all_to_all x1, blocking collectives, per_device(): gram = lax.all_to_all(gram, AXES, 0, 0)  12.1 us
    ppermute x9, starting transfers between devices, move_faces(): arrived.append(lax.ppermute(face, ('mode', axis), pairs))  9.4 us
    pallas_call x14, Pallas kernels, call(): pl.pallas_call(body, out_shape=list(shapes), in_specs=[spec for spec, ope...  7.57 us
    ppermute x12, starting transfers between devices, exchange(): return lax.ppermute(array, 'mode', [(i, i ^ bit) for i in range(count)])  6.56 us
    ppermute x9, waiting for transfers between devices, move_faces(): arrived.append(lax.ppermute(face, ('mode', axis), pairs))  4.44 us
    ppermute x12, waiting for transfers between devices, exchange(): return lax.ppermute(array, 'mode', [(i, i ^ bit) for i in range(count)])  3.7 us
    unnamed x16, local copies, waits for them, and re-layouts  1.05 us
  transfers between devices with their start and end apart: 21, of which 9 were waited for; matrix products, arithmetic and copies ran while one was open for 0% of the time, Pallas kernels for 11%

profile of v15, /device:TPU:0, one launch (start us, length us, event | category | flops | bytes accessed | tf_op | source)
XLA Modules:
  0.0 45.7 jit_solution(8278650846121834978)
XLA Ops:
  0.6 0.0 copy-start.1
  0.6 1.0 %copy-done.1 = f32[8,8,1792]{2,1,0:T(8,128)S(1)} copy-done((f32[8,8,1792]{2,1,0:T(8,128)S(1)}, f32[8,8,1792]{2,1,0:T(8,128)}, u32[]{:S(2)}) %copy-start.1) | copy-done | bytes 458776
  1.7 0.0 copy-start
  1.7 0.0 copy-start.3
  1.7 0.0 copy-start.4
  1.7 0.0 copy-start.5
  1.7 0.0 copy-start.6
  1.7 3.0 %collective-permute-start = (bf16[64,1792]{1,0:T(8,128)(2,1)S(1)}, bf16[64,1792]{1,0:T(8,128)(2,1)S(1)}, u32[]{:S(2)}, u32[]{:S(2)}) collective-permute-start(bf16[64,1792]{1,0:T(8,128)(2,1)S(1)} %pack.1.refs_1_), channel_id=1, source_target_pairs={{0,16},{8,24},{16,0},{24,8},{1,17},{9,25},{17,1},{25,9},{2,18},{10... | collective-permute-start | bytes 688136 | tf_op jit(solution)/shard_map/ppermute | solution.py:45
  4.8 0.2 prepare.1
  5.0 0.1 collective-permute-start.1
  5.1 0.5 %collective-permute-start.2 = (bf16[32,1792]{1,0:T(8,128)(2,1)S(1)}, bf16[32,1792]{1,0:T(8,128)(2,1)S(1)}, u32[]{:S(2)}, u32[]{:S(2)}) collective-permute-start(bf16[32,1792]{1,0:T(8,128)(2,1)S(1)} %get-tuple-element.29), channel_id=1, source_target_pairs={{0,8},{8,0},{16,24},{24,16},{1,9},{9,1},{17,25},{25,17},{2,10},{10... | collective-permute-start | bytes 344072 | tf_op jit(solution)/shard_map/ppermute | solution.py:45
  5.6 1.5 %collective-permute-start.3 = (f32[8,1792]{1,0:T(8,128)S(1)}, f32[8,1792]{1,0:T(8,128)S(1)}, u32[]{:S(2)}, u32[]{:S(2)}) collective-permute-start(f32[8,1792]{1,0:T(8,128)S(1)} %get-tuple-element.32), channel_id=1, source_target_pairs={{0,4},{4,0},{8,12},{12,8},{16,20},{20,16},{24,28},{28,24},{1,5},{5... | collective-permute-start | bytes 172040 | tf_op jit(solution)/shard_map/ppermute | solution.py:38
  7.1 1.6 %collective-permute-start.4 = (f32[8,1792]{1,0:T(8,128)S(1)}, f32[8,1792]{1,0:T(8,128)S(1)}, u32[]{:S(2)}, u32[]{:S(2)}) collective-permute-start(f32[8,1792]{1,0:T(8,128)S(1)} %get-tuple-element.33), channel_id=1, source_target_pairs={{0,1},{1,0},{2,3},{3,2},{8,9},{9,8},{10,11},{11,10},{16,17},{17,16... | collective-permute-start | bytes 172040 | tf_op jit(solution)/shard_map/ppermute | solution.py:38
  8.6 0.0 collective-permute-done.1.refs_2_
  8.6 0.0 collective-permute-start.5
  8.7 1.2 %near_0.1 = (f32[64,1792]{1,0:T(8,128)S(1)}, bf16[14,256,128]{2,1,0:T(8,128)(2,1)S(1)}) custom-call(s32[8,14]{1,0:T(8,128)S(1)} %bitcast.9, bf16[64,1792]{1,0:T(8,128)(2,1)S(1)} %pack.1.refs_1_, bf16[32,1792]{1,0:T(8,128)(2,1)S(1)} %collective-permute-done.1.refs_2_, bf16[32,1792]{1,0:T(8,128)(2,1)S(1)} %collective-permute-done.2.refs_3_, ...), custom_call_target="tpu_custom_call" | custom-call | flops 117440512 | bytes 6032832 | tf_op jit(solution)/shard_map/near_0/pallas_call | solution.py:421
  9.9 1.3 %collective-permute-done.4.refs_3_.refs_7_ = f32[8,1792]{1,0:T(8,128)S(1)} collective-permute-done((f32[8,1792]{1,0:T(8,128)S(1)}, f32[8,1792]{1,0:T(8,128)S(1)}, u32[]{:S(2)}, u32[]{:S(2)}) %collective-permute-start.4) | collective-permute-done | bytes 57376 | tf_op jit(solution)/shard_map/ppermute | solution.py:38
  11.2 0.1 collective-permute-start.6
  11.3 0.5 %middle_0.1.refs_3_ = f32[64,1792]{1,0:T(8,128)S(1)} custom-call(s32[8,14]{1,0:T(8,128)S(1)} %bitcast.10, bf16[64,1792]{1,0:T(8,128)(2,1)S(1)} %hand_on.3.refs_1_, bf16[14,8,128,128]{3,2,1,0:T(8,128)(2,1)S(1)} %copy-done, f32[64,1792]{1,0:T(8,128)S(1)} %get-tuple-element.31.refs_1_.refs_3_, f32[2,1792]{1,0:T(2,128)S(1)} %copy-done.3, ...), custom_call_target="tpu_custom_call" | custom-call | flops 58720256 | bytes 5018048 | tf_op jit(solution)/shard_map/middle_0/pallas_call | solution.py:421
  11.9 0.9 %collective-permute-done.6.refs_1_ = bf16[64,1792]{1,0:T(8,128)(2,1)S(1)} collective-permute-done((bf16[64,1792]{1,0:T(8,128)(2,1)S(1)}, bf16[64,1792]{1,0:T(8,128)(2,1)S(1)}, u32[]{:S(2)}, u32[]{:S(2)}) %collective-permute-start.6) | collective-permute-done | bytes 229408 | tf_op jit(solution)/shard_map/ppermute | solution.py:45
  12.8 0.4 last_0.1
  13.2 0.9 %collective-permute-start.7 = (bf16[64,1792]{1,0:T(8,128)(2,1)S(1)}, bf16[64,1792]{1,0:T(8,128)(2,1)S(1)}, u32[]{:S(2)}, u32[]{:S(2)}) collective-permute-start(bf16[64,1792]{1,0:T(8,128)(2,1)S(1)} %get-tuple-element.36.refs_1_), channel_id=1, source_target_pairs={{0,16},{8,24},{16,0},{24,8},{1,17},{9,25},{17,1},{25,9},{2,18},{10... | collective-permute-start | bytes 688136 | tf_op jit(solution)/shard_map/ppermute | solution.py:45
  14.1 0.2 spread_0.1
  14.2 0.1 collective-permute-start.8
  14.3 0.5 %collective-permute-start.9 = (bf16[32,1792]{1,0:T(8,128)(2,1)S(1)}, bf16[32,1792]{1,0:T(8,128)(2,1)S(1)}, u32[]{:S(2)}, u32[]{:S(2)}) collective-permute-start(bf16[32,1792]{1,0:T(8,128)(2,1)S(1)} %get-tuple-element.39), channel_id=1, source_target_pairs={{0,8},{8,0},{16,24},{24,16},{1,9},{9,1},{17,25},{25,17},{2,10},{10... | collective-permute-start | bytes 344072 | tf_op jit(solution)/shard_map/ppermute | solution.py:45
  14.8 1.5 %collective-permute-start.10 = (f32[8,1792]{1,0:T(8,128)S(1)}, f32[8,1792]{1,0:T(8,128)S(1)}, u32[]{:S(2)}, u32[]{:S(2)}) collective-permute-start(f32[8,1792]{1,0:T(8,128)S(1)} %get-tuple-element.40), channel_id=1, source_target_pairs={{0,4},{4,0},{8,12},{12,8},{16,20},{20,16},{24,28},{28,24},{1,5},{5... | collective-permute-start | bytes 172040 | tf_op jit(solution)/shard_map/ppermute | solution.py:38
  16.3 1.6 %collective-permute-start.11 = (f32[8,1792]{1,0:T(8,128)S(1)}, f32[8,1792]{1,0:T(8,128)S(1)}, u32[]{:S(2)}, u32[]{:S(2)}) collective-permute-start(f32[8,1792]{1,0:T(8,128)S(1)} %get-tuple-element.41), channel_id=1, source_target_pairs={{0,1},{1,0},{2,3},{3,2},{8,9},{9,8},{10,11},{11,10},{16,17},{17,16... | collective-permute-start | bytes 172040 | tf_op jit(solution)/shard_map/ppermute | solution.py:38
  17.9 0.8 %near_1.1.refs_1_.refs_3_ = f32[64,1792]{1,0:T(8,128)S(1)} custom-call(s32[8,14]{1,0:T(8,128)S(1)} %bitcast.12, bf16[64,1792]{1,0:T(8,128)(2,1)S(1)} %get-tuple-element.36.refs_1_, bf16[32,1792]{1,0:T(8,128)(2,1)S(1)} %collective-permute-done.8.refs_2_, bf16[32,1792]{1,0:T(8,128)(2,1)S(1)} %collective-permute-done.9.refs_3_, ...), custom_call_target="tpu_custom_call" | custom-call | flops 117440512 | bytes 5115328 | tf_op jit(solution)/shard_map/near_1/pallas_call | solution.py:421
  18.7 0.3 collective-permute-done.10.refs_2_.refs_6_
  19.0 1.5 %collective-permute-done.11.refs_3_.refs_7_ = f32[8,1792]{1,0:T(8,128)S(1)} collective-permute-done((f32[8,1792]{1,0:T(8,128)S(1)}, f32[8,1792]{1,0:T(8,128)S(1)}, u32[]{:S(2)}, u32[]{:S(2)}) %collective-permute-start.11) | collective-permute-done | bytes 57376 | tf_op jit(solution)/shard_map/ppermute | solution.py:38
  20.5 0.4 collective-permute-done.7.refs_0_
  20.9 0.5 %middle_1.1.refs_3_ = f32[64,1792]{1,0:T(8,128)S(1)} custom-call(s32[8,14]{1,0:T(8,128)S(1)} %bitcast.13, bf16[64,1792]{1,0:T(8,128)(2,1)S(1)} %hand_on.4.refs_1_, bf16[14,8,128,128]{3,2,1,0:T(8,128)(2,1)S(1)} %copy-done, f32[64,1792]{1,0:T(8,128)S(1)} %near_1.1.refs_1_.refs_3_, f32[2,1792]{1,0:T(2,128)S(1)} %copy-done.3, s32[2,1792]{1,0:T(2,128)S(1)} %copy-done.4, ...), custom_call_target="tpu_custom_call" | custom-call | flops 58720256 | bytes 5018048 | tf_op jit(solution)/shard_map/middle_1/pallas_call | solution.py:421
  21.4 1.0 %collective-permute-done.13.refs_1_ = bf16[64,1792]{1,0:T(8,128)(2,1)S(1)} collective-permute-done((bf16[64,1792]{1,0:T(8,128)(2,1)S(1)}, bf16[64,1792]{1,0:T(8,128)(2,1)S(1)}, u32[]{:S(2)}, u32[]{:S(2)}) %collective-permute-start.13) | collective-permute-done | bytes 229408 | tf_op jit(solution)/shard_map/ppermute | solution.py:45
  22.4 0.4 last_1.1
  22.8 0.9 %collective-permute-start.14 = (bf16[64,1792]{1,0:T(8,128)(2,1)S(1)}, bf16[64,1792]{1,0:T(8,128)(2,1)S(1)}, u32[]{:S(2)}, u32[]{:S(2)}) collective-permute-start(bf16[64,1792]{1,0:T(8,128)(2,1)S(1)} %get-tuple-element.43.refs_1_), channel_id=1, source_target_pairs={{0,16},{8,24},{16,0},{24,8},{1,17},{9,25},{17,1},{25,9},{2,18},{10... | collective-permute-start | bytes 688136 | tf_op jit(solution)/shard_map/ppermute | solution.py:45
  23.6 0.2 spread_1.1
  23.8 0.1 collective-permute-start.15
  23.9 0.5 %collective-permute-start.16 = (bf16[32,1792]{1,0:T(8,128)(2,1)S(1)}, bf16[32,1792]{1,0:T(8,128)(2,1)S(1)}, u32[]{:S(2)}, u32[]{:S(2)}) collective-permute-start(bf16[32,1792]{1,0:T(8,128)(2,1)S(1)} %get-tuple-element.46), channel_id=1, source_target_pairs={{0,8},{8,0},{16,24},{24,16},{1,9},{9,1},{17,25},{25,17},{2,10},{10... | collective-permute-start | bytes 344072 | tf_op jit(solution)/shard_map/ppermute | solution.py:45
  24.4 1.5 %collective-permute-start.17 = (f32[8,1792]{1,0:T(8,128)S(1)}, f32[8,1792]{1,0:T(8,128)S(1)}, u32[]{:S(2)}, u32[]{:S(2)}) collective-permute-start(f32[8,1792]{1,0:T(8,128)S(1)} %get-tuple-element.48), channel_id=1, source_target_pairs={{0,4},{4,0},{8,12},{12,8},{16,20},{20,16},{24,28},{28,24},{1,5},{5... | collective-permute-start | bytes 172040 | tf_op jit(solution)/shard_map/ppermute | solution.py:38
  25.9 1.8 %collective-permute-start.18 = (f32[8,1792]{1,0:T(8,128)S(1)}, f32[8,1792]{1,0:T(8,128)S(1)}, u32[]{:S(2)}, u32[]{:S(2)}) collective-permute-start(f32[8,1792]{1,0:T(8,128)S(1)} %get-tuple-element.49), channel_id=1, source_target_pairs={{0,1},{1,0},{2,3},{3,2},{8,9},{9,8},{10,11},{11,10},{16,17},{17,16... | collective-permute-start | bytes 172040 | tf_op jit(solution)/shard_map/ppermute | solution.py:38
  27.7 1.0 %near_2.1 = (f32[64,1792]{1,0:T(8,128)S(1)}, f32[16,128]{1,0:T(8,128)S(1)}) custom-call(s32[8,14]{1,0:T(8,128)S(1)} %bitcast.15, bf16[64,1792]{1,0:T(8,128)(2,1)S(1)} %get-tuple-element.43.refs_1_, bf16[32,1792]{1,0:T(8,128)(2,1)S(1)} %collective-permute-done.15.refs_2_, bf16[32,1792]{1,0:T(8,128)(2,1)S(1)} %collective-permute-done.16.refs_3_, ...), custom_call_target="tpu_custom_call" | custom-call | flops 117440512 | bytes 6499776 | tf_op jit(solution)/shard_map/near_2/pallas_call | solution.py:421
  28.7 1.3 %collective-permute-done.18.refs_3_.refs_7_ = f32[8,1792]{1,0:T(8,128)S(1)} collective-permute-done((f32[8,1792]{1,0:T(8,128)S(1)}, f32[8,1792]{1,0:T(8,128)S(1)}, u32[]{:S(2)}, u32[]{:S(2)}) %collective-permute-start.18) | collective-permute-done | bytes 57376 | tf_op jit(solution)/shard_map/ppermute | solution.py:38
  30.1 0.4 collective-permute-done.14.refs_0_
  30.5 0.5 %middle_2.1.refs_3_ = f32[64,1792]{1,0:T(8,128)S(1)} custom-call(s32[8,14]{1,0:T(8,128)S(1)} %bitcast.16, bf16[64,1792]{1,0:T(8,128)(2,1)S(1)} %hand_on.5.refs_1_, bf16[14,8,128,128]{3,2,1,0:T(8,128)(2,1)S(1)} %copy-done, f32[64,1792]{1,0:T(8,128)S(1)} %get-tuple-element.47.refs_1_.refs_3_, f32[2,1792]{1,0:T(2,128)S(1)} %copy-done.3, ...), custom_call_target="tpu_custom_call" | custom-call | flops 58720256 | bytes 5018048 | tf_op jit(solution)/shard_map/middle_2/pallas_call | solution.py:421
  31.0 1.0 %collective-permute-done.20.refs_1_ = bf16[64,1792]{1,0:T(8,128)(2,1)S(1)} collective-permute-done((bf16[64,1792]{1,0:T(8,128)(2,1)S(1)}, bf16[64,1792]{1,0:T(8,128)(2,1)S(1)}, u32[]{:S(2)}, u32[]{:S(2)}) %collective-permute-start.20) | collective-permute-done | bytes 229408 | tf_op jit(solution)/shard_map/ppermute | solution.py:45
  32.0 0.5 %last_2.1 = f32[32,1,128]{2,1,0:T(1,128)S(1)} custom-call(s32[8,14]{1,0:T(8,128)S(1)} %bitcast.17, bf16[64,1792]{1,0:T(8,128)(2,1)S(1)} %collective-permute-done.20.refs_1_, bf16[14,256,128]{2,1,0:T(8,128)(2,1)S(1)} %get-tuple-element.35.refs_2_, f32[64,1792]{1,0:T(8,128)S(1)} %middle_2.1.refs_3_, f32[64,1792]{1,0:T(8,128)S(1)} %bitcast.7, ...), custom_call_target="tpu_custom_call" | custom-call | flops 58720256 | bytes 3006912 | tf_op jit(solution)/shard_map/last_2/pallas_call | solution.py:421
  32.5 12.1 %all_to_all.5.refs_0_ = f32[32,1,128]{2,1,0:T(1,128)S(1)} all-to-all(f32[32,1,128]{2,1,0:T(1,128)S(1)} %last_2.1), channel_id=1, replica_groups=mesh['mode'=4,'gx'=2,'gy'=4] {'mode','gx','gy'}, dimensions={0} | all-to-all | bytes 32768 | tf_op jit(solution)/shard_map/all_to_all | solution.py:589
  44.6 1.1 %finish.1 = (f32[64,1792]{1,0:T(8,128)}, f32[4,3]{1,0:T(4,128)}) custom-call(f32[32,1,128]{2,1,0:T(1,128)S(1)} %all_to_all.5.refs_0_, f32[64,1792]{1,0:T(8,128)S(1)} %bitcast.8, f32[64,1792]{1,0:T(8,128)S(1)} %get-tuple-element.37.refs_0_.refs_5_.refs_11_.refs_2_, f32[64,1792]{1,0:T(8,128)S(1)} %get-tuple-element.44.refs_0_.refs_5_.refs_12_.refs_6_.refs_3_), custom_call_target="tpu_custom_call" | custom-call | bytes 1851440 | tf_op jit(solution)/shard_map/finish/pallas_call | solution.py:421
  (28 shorter events, 0.1 us)
Async XLA Ops:
  0.6 1.0 %copy-start.1 = (f32[8,8,1792]{2,1,0:T(8,128)S(1)}, f32[8,8,1792]{2,1,0:T(8,128)}, u32[]{:S(2)}) copy-start(f32[8,8,1792]{2,1,0:T(8,128)} %param.7) | copy-start | bytes 1376260
  1.7 3.1 %copy-start.7 = (s32[8,8]{1,0:T(8,128)S(1)}, s32[8,8]{1,0:T(8,128)}, u32[]{:S(2)}) copy-start(s32[8,8]{1,0:T(8,128)} %refs_1_.1) | copy-start | bytes 772
  1.7 7.0 %copy-start = (bf16[14,8,128,128]{3,2,1,0:T(8,128)(2,1)S(1)}, bf16[14,8,128,128]{3,2,1,0:T(8,128)(2,1)}, u32[]{:S(2)}) copy-start(bf16[14,8,128,128]{3,2,1,0:T(8,128)(2,1)} %refs_2_.5) | copy-start | bytes 11010052
  1.7 7.0 %copy-start.3 = (f32[2,1792]{1,0:T(2,128)S(1)}, f32[2,1792]{1,0:T(2,128)}, u32[]{:S(2)}) copy-start(f32[2,1792]{1,0:T(2,128)} %refs_4_.11) | copy-start | bytes 43012
  1.7 7.0 %copy-start.4 = (s32[2,1792]{1,0:T(2,128)S(1)}, s32[2,1792]{1,0:T(2,128)}, u32[]{:S(2)}) copy-start(s32[2,1792]{1,0:T(2,128)} %refs_5_.5) | copy-start | bytes 43012
  1.7 7.0 %copy-start.5 = (s32[14,8]{0,1:T(8,128)S(1)}, s32[14,8]{0,1:T(8,128)}, u32[]{:S(2)}) copy-start(s32[14,8]{0,1:T(8,128)} %param.8) | copy-start | bytes 1348
  1.7 7.0 %copy-start.6 = (f32[1792]{0:T(1024)S(1)}, f32[1792]{0:T(1024)}, u32[]{:S(2)}) copy-start(f32[1792]{0:T(1024)} %refs_7_.5) | copy-start | bytes 21508
  1.7 9.5 %collective-permute-start = (bf16[64,1792]{1,0:T(8,128)(2,1)S(1)}, bf16[64,1792]{1,0:T(8,128)(2,1)S(1)}, u32[]{:S(2)}, u32[]{:S(2)}) collective-permute-start(bf16[64,1792]{1,0:T(8,128)(2,1)S(1)} %pack.1.refs_1_), channel_id=1, source_target_pairs={{0,16},{8,24},{16,0},{24,8},{1,17},{9,25},{17,1},{25,9},{2,18},{10... | collective-permute-start | bytes 688136 | tf_op jit(solution)/shard_map/ppermute | solution.py:45
  5.0 3.6 %collective-permute-start.1 = (bf16[32,1792]{1,0:T(8,128)(2,1)S(1)}, bf16[32,1792]{1,0:T(8,128)(2,1)S(1)}, u32[]{:S(2)}, u32[]{:S(2)}) collective-permute-start(bf16[32,1792]{1,0:T(8,128)(2,1)S(1)} %get-tuple-element.28), channel_id=1, source_target_pairs={{0,8},{8,0},{16,24},{24,16},{1,9},{9,1},{17,25},{25,17},{2,10},{10... | collective-permute-start | bytes 344072 | tf_op jit(solution)/shard_map/ppermute | solution.py:45
  5.1 3.6 %collective-permute-start.2 = (bf16[32,1792]{1,0:T(8,128)(2,1)S(1)}, bf16[32,1792]{1,0:T(8,128)(2,1)S(1)}, u32[]{:S(2)}, u32[]{:S(2)}) collective-permute-start(bf16[32,1792]{1,0:T(8,128)(2,1)S(1)} %get-tuple-element.29), channel_id=1, source_target_pairs={{0,8},{8,0},{16,24},{24,16},{1,9},{9,1},{17,25},{25,17},{2,10},{10... | collective-permute-start | bytes 344072 | tf_op jit(solution)/shard_map/ppermute | solution.py:45
  5.6 4.3 %collective-permute-start.3 = (f32[8,1792]{1,0:T(8,128)S(1)}, f32[8,1792]{1,0:T(8,128)S(1)}, u32[]{:S(2)}, u32[]{:S(2)}) collective-permute-start(f32[8,1792]{1,0:T(8,128)S(1)} %get-tuple-element.32), channel_id=1, source_target_pairs={{0,4},{4,0},{8,12},{12,8},{16,20},{20,16},{24,28},{28,24},{1,5},{5... | collective-permute-start | bytes 172040 | tf_op jit(solution)/shard_map/ppermute | solution.py:38
  7.1 4.2 %collective-permute-start.4 = (f32[8,1792]{1,0:T(8,128)S(1)}, f32[8,1792]{1,0:T(8,128)S(1)}, u32[]{:S(2)}, u32[]{:S(2)}) collective-permute-start(f32[8,1792]{1,0:T(8,128)S(1)} %get-tuple-element.33), channel_id=1, source_target_pairs={{0,1},{1,0},{2,3},{3,2},{8,9},{9,8},{10,11},{11,10},{16,17},{17,16... | collective-permute-start | bytes 172040 | tf_op jit(solution)/shard_map/ppermute | solution.py:38
  8.6 2.6 %collective-permute-start.5 = (f32[8,1792]{1,0:T(8,128)S(1)}, f32[8,1792]{1,0:T(8,128)S(1)}, u32[]{:S(2)}, u32[]{:S(2)}) collective-permute-start(f32[8,1792]{1,0:T(8,128)S(1)} %get-tuple-element.34), channel_id=1, source_target_pairs={{0,8},{1,2},{2,1},{3,11},{8,0},{9,10},{10,9},{11,3},{16,24},{17,18... | collective-permute-start | bytes 172040 | tf_op jit(solution)/shard_map/ppermute | solution.py:38
  11.2 1.5 %collective-permute-start.6 = (bf16[64,1792]{1,0:T(8,128)(2,1)S(1)}, bf16[64,1792]{1,0:T(8,128)(2,1)S(1)}, u32[]{:S(2)}, u32[]{:S(2)}) collective-permute-start(bf16[64,1792]{1,0:T(8,128)(2,1)S(1)} %hand_on.3.refs_1_), channel_id=1, source_target_pairs={{0,8},{8,0},{16,24},{24,16},{1,9},{9,1},{17,25},{25,17},{2,10},{10... | collective-permute-start | bytes 688136 | tf_op jit(solution)/shard_map/ppermute | solution.py:45
  13.2 7.7 %collective-permute-start.7 = (bf16[64,1792]{1,0:T(8,128)(2,1)S(1)}, bf16[64,1792]{1,0:T(8,128)(2,1)S(1)}, u32[]{:S(2)}, u32[]{:S(2)}) collective-permute-start(bf16[64,1792]{1,0:T(8,128)(2,1)S(1)} %get-tuple-element.36.refs_1_), channel_id=1, source_target_pairs={{0,16},{8,24},{16,0},{24,8},{1,17},{9,25},{17,1},{25,9},{2,18},{10... | collective-permute-start | bytes 688136 | tf_op jit(solution)/shard_map/ppermute | solution.py:45
  14.2 3.6 %collective-permute-start.8 = (bf16[32,1792]{1,0:T(8,128)(2,1)S(1)}, bf16[32,1792]{1,0:T(8,128)(2,1)S(1)}, u32[]{:S(2)}, u32[]{:S(2)}) collective-permute-start(bf16[32,1792]{1,0:T(8,128)(2,1)S(1)} %get-tuple-element.38), channel_id=1, source_target_pairs={{0,8},{8,0},{16,24},{24,16},{1,9},{9,1},{17,25},{25,17},{2,10},{10... | collective-permute-start | bytes 344072 | tf_op jit(solution)/shard_map/ppermute | solution.py:45
  14.3 3.6 %collective-permute-start.9 = (bf16[32,1792]{1,0:T(8,128)(2,1)S(1)}, bf16[32,1792]{1,0:T(8,128)(2,1)S(1)}, u32[]{:S(2)}, u32[]{:S(2)}) collective-permute-start(bf16[32,1792]{1,0:T(8,128)(2,1)S(1)} %get-tuple-element.39), channel_id=1, source_target_pairs={{0,8},{8,0},{16,24},{24,16},{1,9},{9,1},{17,25},{25,17},{2,10},{10... | collective-permute-start | bytes 344072 | tf_op jit(solution)/shard_map/ppermute | solution.py:45
  14.8 4.2 %collective-permute-start.10 = (f32[8,1792]{1,0:T(8,128)S(1)}, f32[8,1792]{1,0:T(8,128)S(1)}, u32[]{:S(2)}, u32[]{:S(2)}) collective-permute-start(f32[8,1792]{1,0:T(8,128)S(1)} %get-tuple-element.40), channel_id=1, source_target_pairs={{0,4},{4,0},{8,12},{12,8},{16,20},{20,16},{24,28},{28,24},{1,5},{5... | collective-permute-start | bytes 172040 | tf_op jit(solution)/shard_map/ppermute | solution.py:38
  16.3 4.2 %collective-permute-start.11 = (f32[8,1792]{1,0:T(8,128)S(1)}, f32[8,1792]{1,0:T(8,128)S(1)}, u32[]{:S(2)}, u32[]{:S(2)}) collective-permute-start(f32[8,1792]{1,0:T(8,128)S(1)} %get-tuple-element.41), channel_id=1, source_target_pairs={{0,1},{1,0},{2,3},{3,2},{8,9},{9,8},{10,11},{11,10},{16,17},{17,16... | collective-permute-start | bytes 172040 | tf_op jit(solution)/shard_map/ppermute | solution.py:38
  17.9 2.6 %collective-permute-start.12 = (f32[8,1792]{1,0:T(8,128)S(1)}, f32[8,1792]{1,0:T(8,128)S(1)}, u32[]{:S(2)}, u32[]{:S(2)}) collective-permute-start(f32[8,1792]{1,0:T(8,128)S(1)} %get-tuple-element.42), channel_id=1, source_target_pairs={{0,8},{1,2},{2,1},{3,11},{8,0},{9,10},{10,9},{11,3},{16,24},{17,18... | collective-permute-start | bytes 172040 | tf_op jit(solution)/shard_map/ppermute | solution.py:38
  20.9 6.8 %copy-start.2 = (f32[8,8,1792]{2,1,0:T(8,128)S(1)}, f32[8,8,1792]{2,1,0:T(8,128)}, u32[]{:S(2)}) copy-start(f32[8,8,1792]{2,1,0:T(8,128)} %param.7) | copy-start | bytes 1376260
  20.9 1.5 %collective-permute-start.13 = (bf16[64,1792]{1,0:T(8,128)(2,1)S(1)}, bf16[64,1792]{1,0:T(8,128)(2,1)S(1)}, u32[]{:S(2)}, u32[]{:S(2)}) collective-permute-start(bf16[64,1792]{1,0:T(8,128)(2,1)S(1)} %hand_on.4.refs_1_), channel_id=1, source_target_pairs={{0,8},{8,0},{16,24},{24,16},{1,9},{9,1},{17,25},{25,17},{2,10},{10... | collective-permute-start | bytes 688136 | tf_op jit(solution)/shard_map/ppermute | solution.py:45
  22.8 7.7 %collective-permute-start.14 = (bf16[64,1792]{1,0:T(8,128)(2,1)S(1)}, bf16[64,1792]{1,0:T(8,128)(2,1)S(1)}, u32[]{:S(2)}, u32[]{:S(2)}) collective-permute-start(bf16[64,1792]{1,0:T(8,128)(2,1)S(1)} %get-tuple-element.43.refs_1_), channel_id=1, source_target_pairs={{0,16},{8,24},{16,0},{24,8},{1,17},{9,25},{17,1},{25,9},{2,18},{10... | collective-permute-start | bytes 688136 | tf_op jit(solution)/shard_map/ppermute | solution.py:45
  23.8 3.8 %collective-permute-start.15 = (bf16[32,1792]{1,0:T(8,128)(2,1)S(1)}, bf16[32,1792]{1,0:T(8,128)(2,1)S(1)}, u32[]{:S(2)}, u32[]{:S(2)}) collective-permute-start(bf16[32,1792]{1,0:T(8,128)(2,1)S(1)} %get-tuple-element.45), channel_id=1, source_target_pairs={{0,8},{8,0},{16,24},{24,16},{1,9},{9,1},{17,25},{25,17},{2,10},{10... | collective-permute-start | bytes 344072 | tf_op jit(solution)/shard_map/ppermute | solution.py:45
  23.9 3.8 %collective-permute-start.16 = (bf16[32,1792]{1,0:T(8,128)(2,1)S(1)}, bf16[32,1792]{1,0:T(8,128)(2,1)S(1)}, u32[]{:S(2)}, u32[]{:S(2)}) collective-permute-start(bf16[32,1792]{1,0:T(8,128)(2,1)S(1)} %get-tuple-element.46), channel_id=1, source_target_pairs={{0,8},{8,0},{16,24},{24,16},{1,9},{9,1},{17,25},{25,17},{2,10},{10... | collective-permute-start | bytes 344072 | tf_op jit(solution)/shard_map/ppermute | solution.py:45
  24.4 4.3 %collective-permute-start.17 = (f32[8,1792]{1,0:T(8,128)S(1)}, f32[8,1792]{1,0:T(8,128)S(1)}, u32[]{:S(2)}, u32[]{:S(2)}) collective-permute-start(f32[8,1792]{1,0:T(8,128)S(1)} %get-tuple-element.48), channel_id=1, source_target_pairs={{0,4},{4,0},{8,12},{12,8},{16,20},{20,16},{24,28},{28,24},{1,5},{5... | collective-permute-start | bytes 172040 | tf_op jit(solution)/shard_map/ppermute | solution.py:38
  25.9 4.2 %collective-permute-start.18 = (f32[8,1792]{1,0:T(8,128)S(1)}, f32[8,1792]{1,0:T(8,128)S(1)}, u32[]{:S(2)}, u32[]{:S(2)}) collective-permute-start(f32[8,1792]{1,0:T(8,128)S(1)} %get-tuple-element.49), channel_id=1, source_target_pairs={{0,1},{1,0},{2,3},{3,2},{8,9},{9,8},{10,11},{11,10},{16,17},{17,16... | collective-permute-start | bytes 172040 | tf_op jit(solution)/shard_map/ppermute | solution.py:38
  27.6 2.4 %collective-permute-start.19 = (f32[8,1792]{1,0:T(8,128)S(1)}, f32[8,1792]{1,0:T(8,128)S(1)}, u32[]{:S(2)}, u32[]{:S(2)}) collective-permute-start(f32[8,1792]{1,0:T(8,128)S(1)} %get-tuple-element.50), channel_id=1, source_target_pairs={{0,8},{1,2},{2,1},{3,11},{8,0},{9,10},{10,9},{11,3},{16,24},{17,18... | collective-permute-start | bytes 172040 | tf_op jit(solution)/shard_map/ppermute | solution.py:38
  30.5 1.5 %collective-permute-start.20 = (bf16[64,1792]{1,0:T(8,128)(2,1)S(1)}, bf16[64,1792]{1,0:T(8,128)(2,1)S(1)}, u32[]{:S(2)}, u32[]{:S(2)}) collective-permute-start(bf16[64,1792]{1,0:T(8,128)(2,1)S(1)} %hand_on.5.refs_1_), channel_id=1, source_target_pairs={{0,8},{8,0},{16,24},{24,16},{1,9},{9,1},{17,25},{25,17},{2,10},{10... | collective-permute-start | bytes 688136 | tf_op jit(solution)/shard_map/ppermute | solution.py:45

commit v16 on v14

--- a/solution.py
+++ b/solution.py
@@ -362,7 +362,11 @@
 def finish_kernel(gram_ref, *refs):
     vectors, (solution_ref, hessenberg_ref) = refs[:KRYLOV], refs[KRYLOV:]
     block = gram_ref.shape[2]
-    total = jnp.sum(gram_ref[...], axis=0)
+    total = gram_ref[...]
+    while total.shape[0] % 2 == 0:
+        middle = total.shape[0] // 2
+        total = total[:middle] + total[middle:]
+    total = jnp.sum(total, axis=0)
     lane = lax.broadcasted_iota(jnp.int32, (1, block), 1)
     gram = [[None] * (KRYLOV + 1) for i in range(KRYLOV + 1)]
     at = 0

time: 45.8 us -> 45.8 us (level)
  no operation moved by 1% of the time
where the time goes in v16:
time: 45.8 us; the launch traced here: 45.6 us
  starting transfers between devices  16 us (35%)
  blocking collectives  12.1 us (26%)
  waiting for transfers between devices  8.15 us (18%)
  Pallas kernels  7.56 us (17%)
  local copies, waits for them, and re-layouts  1.05 us (2%)
  between operations  0.85 us (2%)
    all_to_all x1, blocking collectives, per_device(): gram = lax.all_to_all(gram, AXES, 0, 0)  12.1 us
    ppermute x9, starting transfers between devices, move_faces(): arrived.append(lax.ppermute(face, ('mode', axis), pairs))  9.4 us
    pallas_call x14, Pallas kernels, call(): pl.pallas_call(body, out_shape=list(shapes), in_specs=[spec for spec, ope...  7.56 us
    ppermute x12, starting transfers between devices, exchange(): return lax.ppermute(array, 'mode', [(i, i ^ bit) for i in range(count)])  6.57 us
    ppermute x9, waiting for transfers between devices, move_faces(): arrived.append(lax.ppermute(face, ('mode', axis), pairs))  4.43 us
    ppermute x12, waiting for transfers between devices, exchange(): return lax.ppermute(array, 'mode', [(i, i ^ bit) for i in range(count)])  3.72 us
    unnamed x16, local copies, waits for them, and re-layouts  1.05 us
  transfers between devices with their start and end apart: 21, of which 9 were waited for; matrix products, arithmetic and copies ran while one was open for 0% of the time, Pallas kernels for 11%

profile of v16, /device:TPU:0, one launch (start us, length us, event | category | flops | bytes accessed | tf_op | source)
XLA Modules:
  0.0 45.6 jit_solution(9273176917838899775)
XLA Ops:
  0.6 0.0 copy-start.1
  0.6 1.0 %copy-done.1 = f32[8,8,1792]{2,1,0:T(8,128)S(1)} copy-done((f32[8,8,1792]{2,1,0:T(8,128)S(1)}, f32[8,8,1792]{2,1,0:T(8,128)}, u32[]{:S(2)}) %copy-start.1) | copy-done | bytes 458776
  1.7 0.0 copy-start
  1.7 0.0 copy-start.3
  1.7 0.0 copy-start.4
  1.7 0.0 copy-start.5
  1.7 0.0 copy-start.6
  1.7 3.0 %collective-permute-start = (bf16[64,1792]{1,0:T(8,128)(2,1)S(1)}, bf16[64,1792]{1,0:T(8,128)(2,1)S(1)}, u32[]{:S(2)}, u32[]{:S(2)}) collective-permute-start(bf16[64,1792]{1,0:T(8,128)(2,1)S(1)} %pack.1.refs_1_), channel_id=1, source_target_pairs={{0,16},{8,24},{16,0},{24,8},{1,17},{9,25},{17,1},{25,9},{2,18},{10... | collective-permute-start | bytes 688136 | tf_op jit(solution)/shard_map/ppermute | solution.py:45
  4.8 0.2 prepare.1
  5.0 0.1 collective-permute-start.1
  5.1 0.5 %collective-permute-start.2 = (bf16[32,1792]{1,0:T(8,128)(2,1)S(1)}, bf16[32,1792]{1,0:T(8,128)(2,1)S(1)}, u32[]{:S(2)}, u32[]{:S(2)}) collective-permute-start(bf16[32,1792]{1,0:T(8,128)(2,1)S(1)} %get-tuple-element.29), channel_id=1, source_target_pairs={{0,8},{8,0},{16,24},{24,16},{1,9},{9,1},{17,25},{25,17},{2,10},{10... | collective-permute-start | bytes 344072 | tf_op jit(solution)/shard_map/ppermute | solution.py:45
  5.6 1.5 %collective-permute-start.3 = (f32[8,1792]{1,0:T(8,128)S(1)}, f32[8,1792]{1,0:T(8,128)S(1)}, u32[]{:S(2)}, u32[]{:S(2)}) collective-permute-start(f32[8,1792]{1,0:T(8,128)S(1)} %get-tuple-element.32), channel_id=1, source_target_pairs={{0,4},{4,0},{8,12},{12,8},{16,20},{20,16},{24,28},{28,24},{1,5},{5... | collective-permute-start | bytes 172040 | tf_op jit(solution)/shard_map/ppermute | solution.py:38
  7.1 1.6 %collective-permute-start.4 = (f32[8,1792]{1,0:T(8,128)S(1)}, f32[8,1792]{1,0:T(8,128)S(1)}, u32[]{:S(2)}, u32[]{:S(2)}) collective-permute-start(f32[8,1792]{1,0:T(8,128)S(1)} %get-tuple-element.33), channel_id=1, source_target_pairs={{0,1},{1,0},{2,3},{3,2},{8,9},{9,8},{10,11},{11,10},{16,17},{17,16... | collective-permute-start | bytes 172040 | tf_op jit(solution)/shard_map/ppermute | solution.py:38
  8.6 0.0 collective-permute-done.1.refs_2_
  8.6 0.0 collective-permute-start.5
  8.7 1.2 %near_0.1 = (f32[64,1792]{1,0:T(8,128)S(1)}, bf16[14,256,128]{2,1,0:T(8,128)(2,1)S(1)}) custom-call(s32[8,14]{1,0:T(8,128)S(1)} %bitcast.9, bf16[64,1792]{1,0:T(8,128)(2,1)S(1)} %pack.1.refs_1_, bf16[32,1792]{1,0:T(8,128)(2,1)S(1)} %collective-permute-done.1.refs_2_, bf16[32,1792]{1,0:T(8,128)(2,1)S(1)} %collective-permute-done.2.refs_3_, ...), custom_call_target="tpu_custom_call" | custom-call | flops 117440512 | bytes 6032832 | tf_op jit(solution)/shard_map/near_0/pallas_call | solution.py:411
  9.9 1.3 %collective-permute-done.4.refs_3_.refs_7_ = f32[8,1792]{1,0:T(8,128)S(1)} collective-permute-done((f32[8,1792]{1,0:T(8,128)S(1)}, f32[8,1792]{1,0:T(8,128)S(1)}, u32[]{:S(2)}, u32[]{:S(2)}) %collective-permute-start.4) | collective-permute-done | bytes 57376 | tf_op jit(solution)/shard_map/ppermute | solution.py:38
  11.2 0.1 collective-permute-start.6
  11.3 0.5 %middle_0.1.refs_3_ = f32[64,1792]{1,0:T(8,128)S(1)} custom-call(s32[8,14]{1,0:T(8,128)S(1)} %bitcast.10, bf16[64,1792]{1,0:T(8,128)(2,1)S(1)} %hand_on.3.refs_1_, bf16[14,8,128,128]{3,2,1,0:T(8,128)(2,1)S(1)} %copy-done, f32[64,1792]{1,0:T(8,128)S(1)} %get-tuple-element.31.refs_1_.refs_3_, f32[2,1792]{1,0:T(2,128)S(1)} %copy-done.3, ...), custom_call_target="tpu_custom_call" | custom-call | flops 58720256 | bytes 5018048 | tf_op jit(solution)/shard_map/middle_0/pallas_call | solution.py:411
  11.9 0.9 %collective-permute-done.6.refs_1_ = bf16[64,1792]{1,0:T(8,128)(2,1)S(1)} collective-permute-done((bf16[64,1792]{1,0:T(8,128)(2,1)S(1)}, bf16[64,1792]{1,0:T(8,128)(2,1)S(1)}, u32[]{:S(2)}, u32[]{:S(2)}) %collective-permute-start.6) | collective-permute-done | bytes 229408 | tf_op jit(solution)/shard_map/ppermute | solution.py:45
  12.8 0.4 last_0.1
  13.2 0.9 %collective-permute-start.7 = (bf16[64,1792]{1,0:T(8,128)(2,1)S(1)}, bf16[64,1792]{1,0:T(8,128)(2,1)S(1)}, u32[]{:S(2)}, u32[]{:S(2)}) collective-permute-start(bf16[64,1792]{1,0:T(8,128)(2,1)S(1)} %get-tuple-element.36.refs_1_), channel_id=1, source_target_pairs={{0,16},{8,24},{16,0},{24,8},{1,17},{9,25},{17,1},{25,9},{2,18},{10... | collective-permute-start | bytes 688136 | tf_op jit(solution)/shard_map/ppermute | solution.py:45
  14.1 0.2 spread_0.1
  14.2 0.1 collective-permute-start.8
  14.3 0.5 %collective-permute-start.9 = (bf16[32,1792]{1,0:T(8,128)(2,1)S(1)}, bf16[32,1792]{1,0:T(8,128)(2,1)S(1)}, u32[]{:S(2)}, u32[]{:S(2)}) collective-permute-start(bf16[32,1792]{1,0:T(8,128)(2,1)S(1)} %get-tuple-element.39), channel_id=1, source_target_pairs={{0,8},{8,0},{16,24},{24,16},{1,9},{9,1},{17,25},{25,17},{2,10},{10... | collective-permute-start | bytes 344072 | tf_op jit(solution)/shard_map/ppermute | solution.py:45
  14.8 1.5 %collective-permute-start.10 = (f32[8,1792]{1,0:T(8,128)S(1)}, f32[8,1792]{1,0:T(8,128)S(1)}, u32[]{:S(2)}, u32[]{:S(2)}) collective-permute-start(f32[8,1792]{1,0:T(8,128)S(1)} %get-tuple-element.40), channel_id=1, source_target_pairs={{0,4},{4,0},{8,12},{12,8},{16,20},{20,16},{24,28},{28,24},{1,5},{5... | collective-permute-start | bytes 172040 | tf_op jit(solution)/shard_map/ppermute | solution.py:38
  16.3 1.6 %collective-permute-start.11 = (f32[8,1792]{1,0:T(8,128)S(1)}, f32[8,1792]{1,0:T(8,128)S(1)}, u32[]{:S(2)}, u32[]{:S(2)}) collective-permute-start(f32[8,1792]{1,0:T(8,128)S(1)} %get-tuple-element.41), channel_id=1, source_target_pairs={{0,1},{1,0},{2,3},{3,2},{8,9},{9,8},{10,11},{11,10},{16,17},{17,16... | collective-permute-start | bytes 172040 | tf_op jit(solution)/shard_map/ppermute | solution.py:38
  17.9 0.8 %near_1.1.refs_1_.refs_3_ = f32[64,1792]{1,0:T(8,128)S(1)} custom-call(s32[8,14]{1,0:T(8,128)S(1)} %bitcast.12, bf16[64,1792]{1,0:T(8,128)(2,1)S(1)} %get-tuple-element.36.refs_1_, bf16[32,1792]{1,0:T(8,128)(2,1)S(1)} %collective-permute-done.8.refs_2_, bf16[32,1792]{1,0:T(8,128)(2,1)S(1)} %collective-permute-done.9.refs_3_, ...), custom_call_target="tpu_custom_call" | custom-call | flops 117440512 | bytes 5115328 | tf_op jit(solution)/shard_map/near_1/pallas_call | solution.py:411
  18.7 0.2 collective-permute-done.10.refs_2_.refs_6_
  19.0 1.5 %collective-permute-done.11.refs_3_.refs_7_ = f32[8,1792]{1,0:T(8,128)S(1)} collective-permute-done((f32[8,1792]{1,0:T(8,128)S(1)}, f32[8,1792]{1,0:T(8,128)S(1)}, u32[]{:S(2)}, u32[]{:S(2)}) %collective-permute-start.11) | collective-permute-done | bytes 57376 | tf_op jit(solution)/shard_map/ppermute | solution.py:38
  20.5 0.4 collective-permute-done.7.refs_0_
  20.9 0.5 %middle_1.1.refs_3_ = f32[64,1792]{1,0:T(8,128)S(1)} custom-call(s32[8,14]{1,0:T(8,128)S(1)} %bitcast.13, bf16[64,1792]{1,0:T(8,128)(2,1)S(1)} %hand_on.4.refs_1_, bf16[14,8,128,128]{3,2,1,0:T(8,128)(2,1)S(1)} %copy-done, f32[64,1792]{1,0:T(8,128)S(1)} %near_1.1.refs_1_.refs_3_, f32[2,1792]{1,0:T(2,128)S(1)} %copy-done.3, s32[2,1792]{1,0:T(2,128)S(1)} %copy-done.4, ...), custom_call_target="tpu_custom_call" | custom-call | flops 58720256 | bytes 5018048 | tf_op jit(solution)/shard_map/middle_1/pallas_call | solution.py:411
  21.4 1.0 %collective-permute-done.13.refs_1_ = bf16[64,1792]{1,0:T(8,128)(2,1)S(1)} collective-permute-done((bf16[64,1792]{1,0:T(8,128)(2,1)S(1)}, bf16[64,1792]{1,0:T(8,128)(2,1)S(1)}, u32[]{:S(2)}, u32[]{:S(2)}) %collective-permute-start.13) | collective-permute-done | bytes 229408 | tf_op jit(solution)/shard_map/ppermute | solution.py:45
  22.4 0.4 last_1.1
  22.8 0.9 %collective-permute-start.14 = (bf16[64,1792]{1,0:T(8,128)(2,1)S(1)}, bf16[64,1792]{1,0:T(8,128)(2,1)S(1)}, u32[]{:S(2)}, u32[]{:S(2)}) collective-permute-start(bf16[64,1792]{1,0:T(8,128)(2,1)S(1)} %get-tuple-element.43.refs_1_), channel_id=1, source_target_pairs={{0,16},{8,24},{16,0},{24,8},{1,17},{9,25},{17,1},{25,9},{2,18},{10... | collective-permute-start | bytes 688136 | tf_op jit(solution)/shard_map/ppermute | solution.py:45
  23.6 0.2 spread_1.1
  23.8 0.1 collective-permute-start.15
  23.9 0.5 %collective-permute-start.16 = (bf16[32,1792]{1,0:T(8,128)(2,1)S(1)}, bf16[32,1792]{1,0:T(8,128)(2,1)S(1)}, u32[]{:S(2)}, u32[]{:S(2)}) collective-permute-start(bf16[32,1792]{1,0:T(8,128)(2,1)S(1)} %get-tuple-element.46), channel_id=1, source_target_pairs={{0,8},{8,0},{16,24},{24,16},{1,9},{9,1},{17,25},{25,17},{2,10},{10... | collective-permute-start | bytes 344072 | tf_op jit(solution)/shard_map/ppermute | solution.py:45
  24.4 1.5 %collective-permute-start.17 = (f32[8,1792]{1,0:T(8,128)S(1)}, f32[8,1792]{1,0:T(8,128)S(1)}, u32[]{:S(2)}, u32[]{:S(2)}) collective-permute-start(f32[8,1792]{1,0:T(8,128)S(1)} %get-tuple-element.48), channel_id=1, source_target_pairs={{0,4},{4,0},{8,12},{12,8},{16,20},{20,16},{24,28},{28,24},{1,5},{5... | collective-permute-start | bytes 172040 | tf_op jit(solution)/shard_map/ppermute | solution.py:38
  25.9 1.8 %collective-permute-start.18 = (f32[8,1792]{1,0:T(8,128)S(1)}, f32[8,1792]{1,0:T(8,128)S(1)}, u32[]{:S(2)}, u32[]{:S(2)}) collective-permute-start(f32[8,1792]{1,0:T(8,128)S(1)} %get-tuple-element.49), channel_id=1, source_target_pairs={{0,1},{1,0},{2,3},{3,2},{8,9},{9,8},{10,11},{11,10},{16,17},{17,16... | collective-permute-start | bytes 172040 | tf_op jit(solution)/shard_map/ppermute | solution.py:38
  27.7 1.0 %near_2.1 = (f32[64,1792]{1,0:T(8,128)S(1)}, f32[16,128]{1,0:T(8,128)S(1)}) custom-call(s32[8,14]{1,0:T(8,128)S(1)} %bitcast.15, bf16[64,1792]{1,0:T(8,128)(2,1)S(1)} %get-tuple-element.43.refs_1_, bf16[32,1792]{1,0:T(8,128)(2,1)S(1)} %collective-permute-done.15.refs_2_, bf16[32,1792]{1,0:T(8,128)(2,1)S(1)} %collective-permute-done.16.refs_3_, ...), custom_call_target="tpu_custom_call" | custom-call | flops 117440512 | bytes 6499776 | tf_op jit(solution)/shard_map/near_2/pallas_call | solution.py:411
  28.7 1.3 %collective-permute-done.18.refs_3_.refs_7_ = f32[8,1792]{1,0:T(8,128)S(1)} collective-permute-done((f32[8,1792]{1,0:T(8,128)S(1)}, f32[8,1792]{1,0:T(8,128)S(1)}, u32[]{:S(2)}, u32[]{:S(2)}) %collective-permute-start.18) | collective-permute-done | bytes 57376 | tf_op jit(solution)/shard_map/ppermute | solution.py:38
  30.1 0.4 collective-permute-done.14.refs_0_
  30.5 0.5 %middle_2.1.refs_3_ = f32[64,1792]{1,0:T(8,128)S(1)} custom-call(s32[8,14]{1,0:T(8,128)S(1)} %bitcast.16, bf16[64,1792]{1,0:T(8,128)(2,1)S(1)} %hand_on.5.refs_1_, bf16[14,8,128,128]{3,2,1,0:T(8,128)(2,1)S(1)} %copy-done, f32[64,1792]{1,0:T(8,128)S(1)} %get-tuple-element.47.refs_1_.refs_3_, f32[2,1792]{1,0:T(2,128)S(1)} %copy-done.3, ...), custom_call_target="tpu_custom_call" | custom-call | flops 58720256 | bytes 5018048 | tf_op jit(solution)/shard_map/middle_2/pallas_call | solution.py:411
  31.0 1.0 %collective-permute-done.20.refs_1_ = bf16[64,1792]{1,0:T(8,128)(2,1)S(1)} collective-permute-done((bf16[64,1792]{1,0:T(8,128)(2,1)S(1)}, bf16[64,1792]{1,0:T(8,128)(2,1)S(1)}, u32[]{:S(2)}, u32[]{:S(2)}) %collective-permute-start.20) | collective-permute-done | bytes 229408 | tf_op jit(solution)/shard_map/ppermute | solution.py:45
  32.0 0.5 %last_2.1 = f32[32,1,128]{2,1,0:T(1,128)S(1)} custom-call(s32[8,14]{1,0:T(8,128)S(1)} %bitcast.17, bf16[64,1792]{1,0:T(8,128)(2,1)S(1)} %collective-permute-done.20.refs_1_, bf16[14,256,128]{2,1,0:T(8,128)(2,1)S(1)} %get-tuple-element.35.refs_2_, f32[64,1792]{1,0:T(8,128)S(1)} %middle_2.1.refs_3_, f32[64,1792]{1,0:T(8,128)S(1)} %bitcast.7, ...), custom_call_target="tpu_custom_call" | custom-call | flops 58720256 | bytes 3006912 | tf_op jit(solution)/shard_map/last_2/pallas_call | solution.py:411
  32.5 12.1 %all_to_all.5.refs_0_ = f32[32,1,128]{2,1,0:T(1,128)S(1)} all-to-all(f32[32,1,128]{2,1,0:T(1,128)S(1)} %last_2.1), channel_id=1, replica_groups=mesh['mode'=4,'gx'=2,'gy'=4] {'mode','gx','gy'}, dimensions={0} | all-to-all | bytes 32768 | tf_op jit(solution)/shard_map/all_to_all | solution.py:579
  44.6 1.1 %finish.1 = (f32[64,1792]{1,0:T(8,128)}, f32[4,3]{1,0:T(4,128)}) custom-call(f32[32,1,128]{2,1,0:T(1,128)S(1)} %all_to_all.5.refs_0_, f32[64,1792]{1,0:T(8,128)S(1)} %bitcast.8, f32[64,1792]{1,0:T(8,128)S(1)} %get-tuple-element.37.refs_0_.refs_5_.refs_11_.refs_2_, f32[64,1792]{1,0:T(8,128)S(1)} %get-tuple-element.44.refs_0_.refs_5_.refs_12_.refs_6_.refs_3_), custom_call_target="tpu_custom_call" | custom-call | bytes 1851440 | tf_op jit(solution)/shard_map/finish/pallas_call | solution.py:411
  (28 shorter events, 0.1 us)
Async XLA Ops:
  0.6 1.0 %copy-start.1 = (f32[8,8,1792]{2,1,0:T(8,128)S(1)}, f32[8,8,1792]{2,1,0:T(8,128)}, u32[]{:S(2)}) copy-start(f32[8,8,1792]{2,1,0:T(8,128)} %param.7) | copy-start | bytes 1376260
  1.7 3.1 %copy-start.7 = (s32[8,8]{1,0:T(8,128)S(1)}, s32[8,8]{1,0:T(8,128)}, u32[]{:S(2)}) copy-start(s32[8,8]{1,0:T(8,128)} %refs_1_.1) | copy-start | bytes 772
  1.7 7.0 %copy-start = (bf16[14,8,128,128]{3,2,1,0:T(8,128)(2,1)S(1)}, bf16[14,8,128,128]{3,2,1,0:T(8,128)(2,1)}, u32[]{:S(2)}) copy-start(bf16[14,8,128,128]{3,2,1,0:T(8,128)(2,1)} %refs_2_.5) | copy-start | bytes 11010052
  1.7 7.0 %copy-start.3 = (f32[2,1792]{1,0:T(2,128)S(1)}, f32[2,1792]{1,0:T(2,128)}, u32[]{:S(2)}) copy-start(f32[2,1792]{1,0:T(2,128)} %refs_4_.11) | copy-start | bytes 43012
  1.7 7.0 %copy-start.4 = (s32[2,1792]{1,0:T(2,128)S(1)}, s32[2,1792]{1,0:T(2,128)}, u32[]{:S(2)}) copy-start(s32[2,1792]{1,0:T(2,128)} %refs_5_.5) | copy-start | bytes 43012
  1.7 7.0 %copy-start.5 = (s32[14,8]{0,1:T(8,128)S(1)}, s32[14,8]{0,1:T(8,128)}, u32[]{:S(2)}) copy-start(s32[14,8]{0,1:T(8,128)} %param.8) | copy-start | bytes 1348
  1.7 7.0 %copy-start.6 = (f32[1792]{0:T(1024)S(1)}, f32[1792]{0:T(1024)}, u32[]{:S(2)}) copy-start(f32[1792]{0:T(1024)} %refs_7_.5) | copy-start | bytes 21508
  1.7 9.5 %collective-permute-start = (bf16[64,1792]{1,0:T(8,128)(2,1)S(1)}, bf16[64,1792]{1,0:T(8,128)(2,1)S(1)}, u32[]{:S(2)}, u32[]{:S(2)}) collective-permute-start(bf16[64,1792]{1,0:T(8,128)(2,1)S(1)} %pack.1.refs_1_), channel_id=1, source_target_pairs={{0,16},{8,24},{16,0},{24,8},{1,17},{9,25},{17,1},{25,9},{2,18},{10... | collective-permute-start | bytes 688136 | tf_op jit(solution)/shard_map/ppermute | solution.py:45
  5.0 3.6 %collective-permute-start.1 = (bf16[32,1792]{1,0:T(8,128)(2,1)S(1)}, bf16[32,1792]{1,0:T(8,128)(2,1)S(1)}, u32[]{:S(2)}, u32[]{:S(2)}) collective-permute-start(bf16[32,1792]{1,0:T(8,128)(2,1)S(1)} %get-tuple-element.28), channel_id=1, source_target_pairs={{0,8},{8,0},{16,24},{24,16},{1,9},{9,1},{17,25},{25,17},{2,10},{10... | collective-permute-start | bytes 344072 | tf_op jit(solution)/shard_map/ppermute | solution.py:45
  5.1 3.6 %collective-permute-start.2 = (bf16[32,1792]{1,0:T(8,128)(2,1)S(1)}, bf16[32,1792]{1,0:T(8,128)(2,1)S(1)}, u32[]{:S(2)}, u32[]{:S(2)}) collective-permute-start(bf16[32,1792]{1,0:T(8,128)(2,1)S(1)} %get-tuple-element.29), channel_id=1, source_target_pairs={{0,8},{8,0},{16,24},{24,16},{1,9},{9,1},{17,25},{25,17},{2,10},{10... | collective-permute-start | bytes 344072 | tf_op jit(solution)/shard_map/ppermute | solution.py:45
  5.6 4.3 %collective-permute-start.3 = (f32[8,1792]{1,0:T(8,128)S(1)}, f32[8,1792]{1,0:T(8,128)S(1)}, u32[]{:S(2)}, u32[]{:S(2)}) collective-permute-start(f32[8,1792]{1,0:T(8,128)S(1)} %get-tuple-element.32), channel_id=1, source_target_pairs={{0,4},{4,0},{8,12},{12,8},{16,20},{20,16},{24,28},{28,24},{1,5},{5... | collective-permute-start | bytes 172040 | tf_op jit(solution)/shard_map/ppermute | solution.py:38
  7.1 4.2 %collective-permute-start.4 = (f32[8,1792]{1,0:T(8,128)S(1)}, f32[8,1792]{1,0:T(8,128)S(1)}, u32[]{:S(2)}, u32[]{:S(2)}) collective-permute-start(f32[8,1792]{1,0:T(8,128)S(1)} %get-tuple-element.33), channel_id=1, source_target_pairs={{0,1},{1,0},{2,3},{3,2},{8,9},{9,8},{10,11},{11,10},{16,17},{17,16... | collective-permute-start | bytes 172040 | tf_op jit(solution)/shard_map/ppermute | solution.py:38
  8.6 2.6 %collective-permute-start.5 = (f32[8,1792]{1,0:T(8,128)S(1)}, f32[8,1792]{1,0:T(8,128)S(1)}, u32[]{:S(2)}, u32[]{:S(2)}) collective-permute-start(f32[8,1792]{1,0:T(8,128)S(1)} %get-tuple-element.34), channel_id=1, source_target_pairs={{0,8},{1,2},{2,1},{3,11},{8,0},{9,10},{10,9},{11,3},{16,24},{17,18... | collective-permute-start | bytes 172040 | tf_op jit(solution)/shard_map/ppermute | solution.py:38
  11.2 1.5 %collective-permute-start.6 = (bf16[64,1792]{1,0:T(8,128)(2,1)S(1)}, bf16[64,1792]{1,0:T(8,128)(2,1)S(1)}, u32[]{:S(2)}, u32[]{:S(2)}) collective-permute-start(bf16[64,1792]{1,0:T(8,128)(2,1)S(1)} %hand_on.3.refs_1_), channel_id=1, source_target_pairs={{0,8},{8,0},{16,24},{24,16},{1,9},{9,1},{17,25},{25,17},{2,10},{10... | collective-permute-start | bytes 688136 | tf_op jit(solution)/shard_map/ppermute | solution.py:45
  13.2 7.7 %collective-permute-start.7 = (bf16[64,1792]{1,0:T(8,128)(2,1)S(1)}, bf16[64,1792]{1,0:T(8,128)(2,1)S(1)}, u32[]{:S(2)}, u32[]{:S(2)}) collective-permute-start(bf16[64,1792]{1,0:T(8,128)(2,1)S(1)} %get-tuple-element.36.refs_1_), channel_id=1, source_target_pairs={{0,16},{8,24},{16,0},{24,8},{1,17},{9,25},{17,1},{25,9},{2,18},{10... | collective-permute-start | bytes 688136 | tf_op jit(solution)/shard_map/ppermute | solution.py:45
  14.2 3.6 %collective-permute-start.8 = (bf16[32,1792]{1,0:T(8,128)(2,1)S(1)}, bf16[32,1792]{1,0:T(8,128)(2,1)S(1)}, u32[]{:S(2)}, u32[]{:S(2)}) collective-permute-start(bf16[32,1792]{1,0:T(8,128)(2,1)S(1)} %get-tuple-element.38), channel_id=1, source_target_pairs={{0,8},{8,0},{16,24},{24,16},{1,9},{9,1},{17,25},{25,17},{2,10},{10... | collective-permute-start | bytes 344072 | tf_op jit(solution)/shard_map/ppermute | solution.py:45
  14.3 3.6 %collective-permute-start.9 = (bf16[32,1792]{1,0:T(8,128)(2,1)S(1)}, bf16[32,1792]{1,0:T(8,128)(2,1)S(1)}, u32[]{:S(2)}, u32[]{:S(2)}) collective-permute-start(bf16[32,1792]{1,0:T(8,128)(2,1)S(1)} %get-tuple-element.39), channel_id=1, source_target_pairs={{0,8},{8,0},{16,24},{24,16},{1,9},{9,1},{17,25},{25,17},{2,10},{10... | collective-permute-start | bytes 344072 | tf_op jit(solution)/shard_map/ppermute | solution.py:45
  14.8 4.2 %collective-permute-start.10 = (f32[8,1792]{1,0:T(8,128)S(1)}, f32[8,1792]{1,0:T(8,128)S(1)}, u32[]{:S(2)}, u32[]{:S(2)}) collective-permute-start(f32[8,1792]{1,0:T(8,128)S(1)} %get-tuple-element.40), channel_id=1, source_target_pairs={{0,4},{4,0},{8,12},{12,8},{16,20},{20,16},{24,28},{28,24},{1,5},{5... | collective-permute-start | bytes 172040 | tf_op jit(solution)/shard_map/ppermute | solution.py:38
  16.3 4.2 %collective-permute-start.11 = (f32[8,1792]{1,0:T(8,128)S(1)}, f32[8,1792]{1,0:T(8,128)S(1)}, u32[]{:S(2)}, u32[]{:S(2)}) collective-permute-start(f32[8,1792]{1,0:T(8,128)S(1)} %get-tuple-element.41), channel_id=1, source_target_pairs={{0,1},{1,0},{2,3},{3,2},{8,9},{9,8},{10,11},{11,10},{16,17},{17,16... | collective-permute-start | bytes 172040 | tf_op jit(solution)/shard_map/ppermute | solution.py:38
  17.9 2.6 %collective-permute-start.12 = (f32[8,1792]{1,0:T(8,128)S(1)}, f32[8,1792]{1,0:T(8,128)S(1)}, u32[]{:S(2)}, u32[]{:S(2)}) collective-permute-start(f32[8,1792]{1,0:T(8,128)S(1)} %get-tuple-element.42), channel_id=1, source_target_pairs={{0,8},{1,2},{2,1},{3,11},{8,0},{9,10},{10,9},{11,3},{16,24},{17,18... | collective-permute-start | bytes 172040 | tf_op jit(solution)/shard_map/ppermute | solution.py:38
  20.9 6.8 %copy-start.2 = (f32[8,8,1792]{2,1,0:T(8,128)S(1)}, f32[8,8,1792]{2,1,0:T(8,128)}, u32[]{:S(2)}) copy-start(f32[8,8,1792]{2,1,0:T(8,128)} %param.7) | copy-start | bytes 1376260
  20.9 1.5 %collective-permute-start.13 = (bf16[64,1792]{1,0:T(8,128)(2,1)S(1)}, bf16[64,1792]{1,0:T(8,128)(2,1)S(1)}, u32[]{:S(2)}, u32[]{:S(2)}) collective-permute-start(bf16[64,1792]{1,0:T(8,128)(2,1)S(1)} %hand_on.4.refs_1_), channel_id=1, source_target_pairs={{0,8},{8,0},{16,24},{24,16},{1,9},{9,1},{17,25},{25,17},{2,10},{10... | collective-permute-start | bytes 688136 | tf_op jit(solution)/shard_map/ppermute | solution.py:45
  22.8 7.7 %collective-permute-start.14 = (bf16[64,1792]{1,0:T(8,128)(2,1)S(1)}, bf16[64,1792]{1,0:T(8,128)(2,1)S(1)}, u32[]{:S(2)}, u32[]{:S(2)}) collective-permute-start(bf16[64,1792]{1,0:T(8,128)(2,1)S(1)} %get-tuple-element.43.refs_1_), channel_id=1, source_target_pairs={{0,16},{8,24},{16,0},{24,8},{1,17},{9,25},{17,1},{25,9},{2,18},{10... | collective-permute-start | bytes 688136 | tf_op jit(solution)/shard_map/ppermute | solution.py:45
  23.8 3.8 %collective-permute-start.15 = (bf16[32,1792]{1,0:T(8,128)(2,1)S(1)}, bf16[32,1792]{1,0:T(8,128)(2,1)S(1)}, u32[]{:S(2)}, u32[]{:S(2)}) collective-permute-start(bf16[32,1792]{1,0:T(8,128)(2,1)S(1)} %get-tuple-element.45), channel_id=1, source_target_pairs={{0,8},{8,0},{16,24},{24,16},{1,9},{9,1},{17,25},{25,17},{2,10},{10... | collective-permute-start | bytes 344072 | tf_op jit(solution)/shard_map/ppermute | solution.py:45
  23.9 3.8 %collective-permute-start.16 = (bf16[32,1792]{1,0:T(8,128)(2,1)S(1)}, bf16[32,1792]{1,0:T(8,128)(2,1)S(1)}, u32[]{:S(2)}, u32[]{:S(2)}) collective-permute-start(bf16[32,1792]{1,0:T(8,128)(2,1)S(1)} %get-tuple-element.46), channel_id=1, source_target_pairs={{0,8},{8,0},{16,24},{24,16},{1,9},{9,1},{17,25},{25,17},{2,10},{10... | collective-permute-start | bytes 344072 | tf_op jit(solution)/shard_map/ppermute | solution.py:45
  24.4 4.3 %collective-permute-start.17 = (f32[8,1792]{1,0:T(8,128)S(1)}, f32[8,1792]{1,0:T(8,128)S(1)}, u32[]{:S(2)}, u32[]{:S(2)}) collective-permute-start(f32[8,1792]{1,0:T(8,128)S(1)} %get-tuple-element.48), channel_id=1, source_target_pairs={{0,4},{4,0},{8,12},{12,8},{16,20},{20,16},{24,28},{28,24},{1,5},{5... | collective-permute-start | bytes 172040 | tf_op jit(solution)/shard_map/ppermute | solution.py:38
  25.9 4.2 %collective-permute-start.18 = (f32[8,1792]{1,0:T(8,128)S(1)}, f32[8,1792]{1,0:T(8,128)S(1)}, u32[]{:S(2)}, u32[]{:S(2)}) collective-permute-start(f32[8,1792]{1,0:T(8,128)S(1)} %get-tuple-element.49), channel_id=1, source_target_pairs={{0,1},{1,0},{2,3},{3,2},{8,9},{9,8},{10,11},{11,10},{16,17},{17,16... | collective-permute-start | bytes 172040 | tf_op jit(solution)/shard_map/ppermute | solution.py:38
  27.6 2.4 %collective-permute-start.19 = (f32[8,1792]{1,0:T(8,128)S(1)}, f32[8,1792]{1,0:T(8,128)S(1)}, u32[]{:S(2)}, u32[]{:S(2)}) collective-permute-start(f32[8,1792]{1,0:T(8,128)S(1)} %get-tuple-element.50), channel_id=1, source_target_pairs={{0,8},{1,2},{2,1},{3,11},{8,0},{9,10},{10,9},{11,3},{16,24},{17,18... | collective-permute-start | bytes 172040 | tf_op jit(solution)/shard_map/ppermute | solution.py:38
  30.5 1.5 %collective-permute-start.20 = (bf16[64,1792]{1,0:T(8,128)(2,1)S(1)}, bf16[64,1792]{1,0:T(8,128)(2,1)S(1)}, u32[]{:S(2)}, u32[]{:S(2)}) collective-permute-start(bf16[64,1792]{1,0:T(8,128)(2,1)S(1)} %hand_on.5.refs_1_), channel_id=1, source_target_pairs={{0,8},{8,0},{16,24},{24,16},{1,9},{9,1},{17,25},{25,17},{2,10},{10... | collective-permute-start | bytes 688136 | tf_op jit(solution)/shard_map/ppermute | solution.py:45
